TPU v7x, 32 devices: a whole 2x2x4 slice. The times are simulated.
32 devices in a mesh: expert: 8 (over z, x), fsdp: 4 (over y, core).
Axes of the slice: x: 2, y: 2, z: 4, core: 2. Of those that a mesh axis runs over, the one named last changes fastest.
Arguments:
- tokens: bfloat16 [16384, 1536], P(('expert', 'fsdp')), may hold values from -6 to 6
- cotangent: bfloat16 [16384, 1536], P(('expert', 'fsdp')), may hold values from -6 to 6
- routes: int32 [16384, 4], P(('expert', 'fsdp')), may hold values from 0 to 31, all different within a row; in each aligned block of 512 rows (0 to 511, 512 to 1023, ...) at most 80 rows name the same one
- gains: float32 [2, 1536], P(None, 'fsdp'), may hold values from 0.5 to 1.5
- gains_first: float32 [2, 1536], P(None, 'fsdp'), may hold values from -120.75685 to 120.75685
- gains_second: float32 [2, 1536], P(None, 'fsdp'), may hold values from 1032.192 to 31132.297
- query_weight: float32 [1536, 1536], P('fsdp'), may hold values from -0.21875 to 0.21875
- query_first: float32 [1536, 1536], P('fsdp'), may hold values from -320 to 320
- query_second: float32 [1536, 1536], P('fsdp'), may hold values from 13762.56 to 55050.24
- key_matrix: float32 [1536, 256], P('fsdp'), may hold values from -0.21875 to 0.21875
- key_moment_first: float32 [1536, 256], P('fsdp'), may hold values from -768 to 768
- key_moment_second: float32 [1536, 256], P('fsdp'), may hold values from 69795.84 to 278528
- value_matrix: float32 [1536, 256], P('fsdp'), may hold values from -0.15625 to 0.15625
- value_moment_first: float32 [1536, 256], P('fsdp'), may hold values from -160 to 160
- value_moment_second: float32 [1536, 256], P('fsdp'), may hold values from 1727.3403 to 6904.34
- output_weight: float32 [1536, 1536], P('fsdp'), may hold values from -0.875 to 0.875
- output_first: float32 [1536, 1536], P('fsdp'), may hold values from -20 to 20
- output_second: float32 [1536, 1536], P('fsdp'), may hold values from 54.0672 to 212.992
- router_weight: float32 [1536, 32], P('fsdp'), may hold values from -0.078125 to 0.078125
- router_first: float32 [1536, 32], P('fsdp'), may hold values from -512 to 512
- router_second: float32 [1536, 32], P('fsdp'), may hold values from 31129.6 to 124518.4
- expert_in: float32 [32, 1536, 1536], P('expert', 'fsdp'), may hold values from -0.15625 to 0.15625
- in_first: float32 [32, 1536, 1536], P('expert', 'fsdp'), may hold values from -16 to 16
- in_second: float32 [32, 1536, 1536], P('expert', 'fsdp'), may hold values from 26.624 to 108.544
- expert_out: float32 [32, 768, 1536], P('expert', None, 'fsdp'), may hold values from -0.625 to 0.625
- out_first: float32 [32, 768, 1536], P('expert', None, 'fsdp'), may hold values from -4 to 4
- out_second: float32 [32, 768, 1536], P('expert', None, 'fsdp'), may hold values from 2.4576 to 9.6256
Outputs:
- layer_out: bfloat16 [16384, 1536], P(('expert', 'fsdp'))
- input_grad: bfloat16 [16384, 1536], P(('expert', 'fsdp'))
- gains_new: float32 [2, 1536], P(None, 'fsdp')
- gains_first_new: float32 [2, 1536], P(None, 'fsdp')
- gains_second_new: float32 [2, 1536], P(None, 'fsdp')
- query_new: float32 [1536, 1536], P('fsdp')
- query_first_new: float32 [1536, 1536], P('fsdp')
- query_second_new: float32 [1536, 1536], P('fsdp')
- key_new: float32 [1536, 256], P('fsdp')
- key_first_new: float32 [1536, 256], P('fsdp')
- key_second_new: float32 [1536, 256], P('fsdp')
- value_new: float32 [1536, 256], P('fsdp')
- value_first_new: float32 [1536, 256], P('fsdp')
- value_second_new: float32 [1536, 256], P('fsdp')
- output_new: float32 [1536, 1536], P('fsdp')
- output_first_new: float32 [1536, 1536], P('fsdp')
- output_second_new: float32 [1536, 1536], P('fsdp')
- router_new: float32 [1536, 32], P('fsdp')
- router_first_new: float32 [1536, 32], P('fsdp')
- router_second_new: float32 [1536, 32], P('fsdp')
- expert_in_new: float32 [32, 1536, 1536], P('expert', 'fsdp')
- in_first_new: float32 [32, 1536, 1536], P('expert', 'fsdp')
- in_second_new: float32 [32, 1536, 1536], P('expert', 'fsdp')
- expert_out_new: float32 [32, 768, 1536], P('expert', None, 'fsdp')
- out_first_new: float32 [32, 768, 1536], P('expert', None, 'fsdp')
- out_second_new: float32 [32, 768, 1536], P('expert', None, 'fsdp')
Inputs may be any that keep to these rules, and one draw needn't show every extreme that they name: `routes`: within the rows of one device no expert is named more than 80 times, a bound that some block reaches.
All inputs are finite; a program needn't handle non-finite values.
Results may differ from a plain program's by a relative error of at most 0.028.
Values may be sent and summed in bfloat16 or wider, within the bound.
No kernel may reach another device: no remote copies, remote signals or barrier semaphores. Data moves between devices by JAX's collectives and lax.ppermute only.
A program may use at most 320 MiB of HBM per device.

v0:
```python
import math

import jax
import jax.numpy as jnp
from jax import lax
from jax.sharding import PartitionSpec as P

MODEL_WIDTH = 1536
QUERY_HEADS = 12
KEY_VALUE_HEADS = 2
HEAD_SIZE = 128
FF = 768
STEP = 10
CAP = 80


NORM_EPS = 1e-05
ROPE_BASE = 10000.0
BETA_ONE = 0.9
BETA_TWO = 0.95
ADAM_EPS = 1e-08
DECAY = 0.1
GAIN_RATE = 0.8
MASKED = -1e30


def rotary_apply(values, token_positions, heads, sign):
    row_count = values.shape[0]
    head_width = values.shape[1] // heads
    half_width = head_width // 2
    shaped = values.reshape(row_count, heads, head_width)
    inverse = ROPE_BASE ** (-(jnp.arange(half_width, dtype=jnp.float32) * 2.0 / head_width))
    angle_grid = token_positions[:, None] * inverse[None, :]
    cosine = jnp.cos(angle_grid)[:, None, :]
    sine_part = sign * jnp.sin(angle_grid)[:, None, :]
    front_half = shaped[..., :half_width]
    back_half = shaped[..., half_width:]
    turned = jnp.concatenate(
        [front_half * cosine - back_half * sine_part, back_half * cosine + front_half * sine_part],
        axis=-1,
    )
    return turned.reshape(row_count, heads * head_width)


def contract_rows(left, right):
    return lax.dot_general(
        left, right, (((0,), (0,)), ((), ())), preferred_element_type=jnp.float32
    )


def times_transpose(left, right):
    return lax.dot_general(
        left, right, (((1,), (1,)), ((), ())), preferred_element_type=jnp.float32
    )


def slot_tables(routes, experts_all, capacity):
    token_rows, top_count = routes.shape
    flat_routes = routes.reshape(-1)
    onehot = (flat_routes[:, None] == jnp.arange(experts_all, dtype=jnp.int32)[None, :]).astype(
        jnp.int32
    )
    before = jnp.cumsum(onehot, axis=0) - onehot
    slot_index = jnp.sum(before * onehot, axis=1)
    position = flat_routes * capacity + slot_index
    source = (
        jnp.full((experts_all * capacity,), token_rows * top_count, jnp.int32)
        .at[position]
        .set(jnp.arange(token_rows * top_count, dtype=jnp.int32))
    )
    return (position, source)


def adamw_update(weight, moment_one, moment_two, gradient, step_rate, decay_rate):
    first_new = BETA_ONE * moment_one + (1.0 - BETA_ONE) * gradient
    second_new = BETA_TWO * moment_two + (1.0 - BETA_TWO) * gradient * gradient
    first_hat = first_new / (1.0 - BETA_ONE**STEP)
    second_hat = second_new / (1.0 - BETA_TWO**STEP)
    weight_new = weight - step_rate * (
        first_hat / (jnp.sqrt(second_hat) + ADAM_EPS) + decay_rate * weight
    )
    return (weight_new, first_new, second_new)


def body(
    tokens,
    cotangent,
    routes,
    gains,
    gains_first,
    gains_second,
    query_weight,
    query_first,
    query_second,
    key_matrix,
    key_moment_first,
    key_moment_second,
    value_matrix,
    value_moment_first,
    value_moment_second,
    output_weight,
    output_first,
    output_second,
    router_weight,
    router_first,
    router_second,
    expert_in,
    in_first,
    in_second,
    expert_out,
    out_first,
    out_second,
):
    token_rows = tokens.shape[0]
    top_count = routes.shape[1]
    fsdp_count = lax.axis_size("fsdp")
    fsdp_place = lax.axis_index("fsdp")
    expert_count = lax.axis_size("expert")
    experts_local = expert_in.shape[0]
    experts_all = experts_local * expert_count
    query_group_size = QUERY_HEADS // KEY_VALUE_HEADS
    score_scaling = 1.0 / math.sqrt(HEAD_SIZE)
    gains_low, query_low, key_reduced, value_low, output_low, router_low = (
        lax.all_gather(gains.astype(jnp.bfloat16), "fsdp", axis=1, tiled=True),
        lax.all_gather(query_weight.astype(jnp.bfloat16), "fsdp", axis=0, tiled=True),
        lax.all_gather(key_matrix.astype(jnp.bfloat16), "fsdp", axis=0, tiled=True),
        lax.all_gather(value_matrix.astype(jnp.bfloat16), "fsdp", axis=0, tiled=True),
        lax.all_gather(output_weight.astype(jnp.bfloat16), "fsdp", axis=0, tiled=True),
        lax.all_gather(router_weight.astype(jnp.bfloat16), "fsdp", axis=0, tiled=True),
    )
    gain_one = gains_low[0].astype(jnp.float32)
    gain_two = gains_low[1].astype(jnp.float32)
    inputs = tokens.astype(jnp.float32)
    scale_one = lax.rsqrt(jnp.mean(inputs * inputs, axis=1, keepdims=True) + NORM_EPS)
    normed_one = inputs * scale_one
    first_hidden = (normed_one * gain_one).astype(jnp.bfloat16)
    query_places = fsdp_place * token_rows + jnp.arange(token_rows, dtype=jnp.int32)
    token_positions = query_places.astype(jnp.float32)
    query_rows = rotary_apply(
        jnp.dot(first_hidden, query_low, preferred_element_type=jnp.float32),
        token_positions,
        QUERY_HEADS,
        1.0,
    ).astype(jnp.bfloat16)
    keys_local = rotary_apply(
        jnp.dot(first_hidden, key_reduced, preferred_element_type=jnp.float32),
        token_positions,
        KEY_VALUE_HEADS,
        1.0,
    ).astype(jnp.bfloat16)
    values_local = jnp.dot(first_hidden, value_low, preferred_element_type=jnp.float32).astype(
        jnp.bfloat16
    )
    every_key, every_value = (
        lax.all_gather(keys_local, "fsdp", axis=0, tiled=True),
        lax.all_gather(values_local, "fsdp", axis=0, tiled=True),
    )
    sequence_rows = every_key.shape[0]
    key_head_rows = every_key.reshape(sequence_rows, KEY_VALUE_HEADS, HEAD_SIZE)
    value_head_rows = every_value.reshape(sequence_rows, KEY_VALUE_HEADS, HEAD_SIZE)
    query_head_rows = query_rows.reshape(token_rows, KEY_VALUE_HEADS, query_group_size, HEAD_SIZE)
    block_ratio = max(1, min(fsdp_count, 512 // token_rows))
    while fsdp_count % block_ratio:
        block_ratio -= 1
    key_block = block_ratio * token_rows
    visit_block = ((fsdp_place + 1) * token_rows - 1) // key_block + 1

    def block_scores(block_index):
        block_start = block_index * key_block
        key_portion = lax.dynamic_slice_in_dim(key_head_rows, block_start, key_block, 0)
        value_portion = lax.dynamic_slice_in_dim(value_head_rows, block_start, key_block, 0)
        scores = (
            jnp.einsum(
                "ayos,pys->yoap", query_head_rows, key_portion, preferred_element_type=jnp.float32
            )
            * score_scaling
        )
        allowed = (block_start + jnp.arange(key_block, dtype=jnp.int32))[None, :] <= query_places[
            :, None
        ]
        return (scores, allowed, key_portion, value_portion)

    def stat_step(block_index, carry_in):
        running, exp_total = carry_in
        scores, allowed, key_portion, value_portion = block_scores(block_index)
        biggest = jnp.maximum(running, jnp.max(jnp.where(allowed, scores, MASKED), axis=-1))
        exp_total = exp_total * jnp.exp(running - biggest) + jnp.sum(
            jnp.where(allowed, jnp.exp(scores - biggest[..., None]), 0.0), axis=-1
        )
        return (biggest, exp_total)

    statistic_shape = (KEY_VALUE_HEADS, query_group_size, token_rows)
    running, exp_total = lax.fori_loop(
        0,
        visit_block,
        stat_step,
        (jnp.full(statistic_shape, MASKED, jnp.float32), jnp.zeros(statistic_shape, jnp.float32)),
    )
    log_total = running + jnp.log(exp_total)

    def weights_of(scores, allowed):
        return jnp.where(allowed, jnp.exp(scores - log_total[..., None]), 0.0)

    def output_update(block_index, running_sum):
        scores, allowed, key_portion, value_portion = block_scores(block_index)
        current_weights = weights_of(scores, allowed).astype(jnp.bfloat16)
        return running_sum + jnp.einsum(
            "cljx,xcz->jclz", current_weights, value_portion, preferred_element_type=jnp.float32
        )

    attended_rows = lax.fori_loop(
        0,
        visit_block,
        output_update,
        jnp.zeros((token_rows, KEY_VALUE_HEADS, query_group_size, HEAD_SIZE), jnp.float32),
    )
    attended_rows = attended_rows.reshape(token_rows, QUERY_HEADS * HEAD_SIZE).astype(jnp.bfloat16)
    residual = inputs + jnp.dot(attended_rows, output_low, preferred_element_type=jnp.float32)
    scale_two = lax.rsqrt(jnp.mean(residual * residual, axis=1, keepdims=True) + NORM_EPS)
    normed_two = residual * scale_two
    hidden_two = (normed_two * gain_two).astype(jnp.bfloat16)
    logits = jnp.dot(hidden_two, router_low, preferred_element_type=jnp.float32)
    chosen = (routes[:, :, None] == jnp.arange(experts_all, dtype=jnp.int32)[None, None, :]).astype(
        jnp.float32
    )
    picked_logits = jnp.sum(chosen * logits[:, None, :], axis=2)
    gate_weights = jax.nn.softmax(picked_logits, axis=1)
    position, source = slot_tables(routes, experts_all, CAP)
    source_rows = source // top_count
    padded_two = jnp.concatenate([hidden_two, jnp.zeros((1, MODEL_WIDTH), jnp.bfloat16)], axis=0)
    outgoing = padded_two[source_rows].reshape(expert_count, experts_local, CAP, MODEL_WIDTH)
    arrived = lax.all_to_all(outgoing, "expert", split_axis=0, concat_axis=0, tiled=True)
    gate_up_low, down_low = (
        lax.all_gather(expert_in.astype(jnp.bfloat16), "fsdp", axis=1, tiled=True),
        lax.all_gather(expert_out.astype(jnp.bfloat16), "fsdp", axis=2, tiled=True),
    )
    gate_up = jnp.einsum("sjcd,jdf->sjcf", arrived, gate_up_low, preferred_element_type=jnp.float32)
    gate_pre = gate_up[..., :FF]
    up_part = gate_up[..., FF:]
    sigmoid_gate = jax.nn.sigmoid(gate_pre)
    silu_value = gate_pre * sigmoid_gate
    expert_hidden = (jax.nn.silu(gate_pre) * up_part).astype(jnp.bfloat16)
    expert_result = jnp.einsum(
        "sjcf,jfd->sjcd", expert_hidden, down_low, preferred_element_type=jnp.float32
    ).astype(jnp.bfloat16)
    returned = lax.all_to_all(
        expert_result, "expert", split_axis=0, concat_axis=0, tiled=True
    ).reshape(experts_all * CAP, MODEL_WIDTH)
    gathered_rows = (
        returned[position].reshape(token_rows, top_count, MODEL_WIDTH).astype(jnp.float32)
    )
    layer_out = (residual + jnp.sum(gate_weights[:, :, None] * gathered_rows, axis=1)).astype(
        jnp.bfloat16
    )
    upstream = cotangent.astype(jnp.float32)
    gate_grad = jnp.sum(upstream[:, None, :] * gathered_rows, axis=2)
    picked_grad = gate_weights * (
        gate_grad - jnp.sum(gate_weights * gate_grad, axis=1, keepdims=True)
    )
    logit_grad = jnp.sum(chosen * picked_grad[:, :, None], axis=1).astype(jnp.bfloat16)
    router_term = contract_rows(hidden_two, logit_grad)
    hidden_two_grad = times_transpose(logit_grad, router_low)
    padded_gates = jnp.concatenate([gate_weights.reshape(-1), jnp.zeros((1,), jnp.float32)])
    padded_upstream = jnp.concatenate([upstream, jnp.zeros((1, MODEL_WIDTH), jnp.float32)], axis=0)
    slot_grad = (padded_gates[source][:, None] * padded_upstream[source_rows]).astype(jnp.bfloat16)
    arrived_grad = lax.all_to_all(
        slot_grad.reshape(expert_count, experts_local, CAP, MODEL_WIDTH),
        "expert",
        split_axis=0,
        concat_axis=0,
        tiled=True,
    )
    down_term = jnp.einsum(
        "sjcf,sjcd->jfd", expert_hidden, arrived_grad, preferred_element_type=jnp.float32
    )
    inner_grad = jnp.einsum(
        "sjcd,jfd->sjcf", arrived_grad, down_low, preferred_element_type=jnp.float32
    )
    gate_pre_grad = inner_grad * up_part * (sigmoid_gate * (1.0 + gate_pre * (1.0 - sigmoid_gate)))
    up_grad = inner_grad * silu_value
    gate_up_grad = jnp.concatenate([gate_pre_grad, up_grad], axis=-1).astype(jnp.bfloat16)
    in_term = jnp.einsum(
        "sjcd,sjcf->jdf", arrived, gate_up_grad, preferred_element_type=jnp.float32
    )
    row_grad = jnp.einsum(
        "sjcf,jdf->sjcd", gate_up_grad, gate_up_low, preferred_element_type=jnp.float32
    ).astype(jnp.bfloat16)
    row_back = lax.all_to_all(row_grad, "expert", split_axis=0, concat_axis=0, tiled=True).reshape(
        experts_all * CAP, MODEL_WIDTH
    )
    hidden_two_grad = hidden_two_grad + jnp.sum(
        row_back[position].reshape(token_rows, top_count, MODEL_WIDTH).astype(jnp.float32), axis=1
    )
    in_sum, out_sum = (
        lax.psum_scatter(
            in_term.astype(jnp.bfloat16), "fsdp", scatter_dimension=1, tiled=True
        ).astype(jnp.float32),
        lax.psum_scatter(
            down_term.astype(jnp.bfloat16), "fsdp", scatter_dimension=2, tiled=True
        ).astype(jnp.float32),
    )
    gain_two_term = jnp.sum(hidden_two_grad * normed_two, axis=0)
    scaled_two = hidden_two_grad * gain_two
    residual_grad = upstream + scale_two * (
        scaled_two - normed_two * jnp.mean(scaled_two * normed_two, axis=1, keepdims=True)
    )
    branch_grad = residual_grad.astype(jnp.bfloat16)
    output_term = contract_rows(attended_rows, branch_grad)
    attended_rows_grad = (
        times_transpose(branch_grad, output_low)
        .astype(jnp.bfloat16)
        .reshape(token_rows, KEY_VALUE_HEADS, query_group_size, HEAD_SIZE)
    )

    def dot_step(block_index, running_sum):
        scores, allowed, key_portion, value_portion = block_scores(block_index)
        current_weights = weights_of(scores, allowed)
        prob_grad = jnp.einsum(
            "ayos,pys->yoap", attended_rows_grad, value_portion, preferred_element_type=jnp.float32
        )
        return running_sum + jnp.sum(current_weights * prob_grad, axis=-1)

    row_dot = lax.fori_loop(0, visit_block, dot_step, jnp.zeros(statistic_shape, jnp.float32))

    def grad_step(block_index, carry_in):
        query_acc, key_accumulator, value_accumulator = carry_in
        scores, allowed, key_portion, value_portion = block_scores(block_index)
        current_weights = weights_of(scores, allowed)
        prob_grad = jnp.einsum(
            "ayos,pys->yoap", attended_rows_grad, value_portion, preferred_element_type=jnp.float32
        )
        score_gradient = (current_weights * (prob_grad - row_dot[..., None])).astype(jnp.bfloat16)
        query_acc = query_acc + jnp.einsum(
            "cljx,xcz->jclz", score_gradient, key_portion, preferred_element_type=jnp.float32
        )
        key_block_grad = jnp.einsum(
            "qral,aqrw->lqw", score_gradient, query_head_rows, preferred_element_type=jnp.float32
        )
        value_block_grad = jnp.einsum(
            "qral,aqrw->lqw",
            current_weights.astype(jnp.bfloat16),
            attended_rows_grad,
            preferred_element_type=jnp.float32,
        )
        block_start = block_index * key_block
        key_accumulator = lax.dynamic_update_slice_in_dim(
            key_accumulator,
            lax.dynamic_slice_in_dim(key_accumulator, block_start, key_block, 0) + key_block_grad,
            block_start,
            0,
        )
        value_accumulator = lax.dynamic_update_slice_in_dim(
            value_accumulator,
            lax.dynamic_slice_in_dim(value_accumulator, block_start, key_block, 0)
            + value_block_grad,
            block_start,
            0,
        )
        return (query_acc, key_accumulator, value_accumulator)

    query_acc, key_accumulator, value_accumulator = lax.fori_loop(
        0,
        visit_block,
        grad_step,
        (
            jnp.zeros((token_rows, KEY_VALUE_HEADS, query_group_size, HEAD_SIZE), jnp.float32),
            jnp.zeros((sequence_rows, KEY_VALUE_HEADS, HEAD_SIZE), jnp.float32),
            jnp.zeros((sequence_rows, KEY_VALUE_HEADS, HEAD_SIZE), jnp.float32),
        ),
    )
    key_gradient, value_grad = (
        lax.psum_scatter(
            (
                key_accumulator.reshape(sequence_rows, KEY_VALUE_HEADS * HEAD_SIZE) * score_scaling
            ).astype(jnp.bfloat16),
            "fsdp",
            scatter_dimension=0,
            tiled=True,
        ).astype(jnp.float32),
        lax.psum_scatter(
            value_accumulator.reshape(sequence_rows, KEY_VALUE_HEADS * HEAD_SIZE).astype(
                jnp.bfloat16
            ),
            "fsdp",
            scatter_dimension=0,
            tiled=True,
        ).astype(jnp.float32),
    )
    query_pre_grad = rotary_apply(
        query_acc.reshape(token_rows, QUERY_HEADS * HEAD_SIZE) * score_scaling,
        token_positions,
        QUERY_HEADS,
        -1.0,
    ).astype(jnp.bfloat16)
    key_before_rotation_grad = rotary_apply(
        key_gradient, token_positions, KEY_VALUE_HEADS, -1.0
    ).astype(jnp.bfloat16)
    value_pre_grad = value_grad.astype(jnp.bfloat16)
    query_term = contract_rows(first_hidden, query_pre_grad)
    key_term = contract_rows(first_hidden, key_before_rotation_grad)
    value_term = contract_rows(first_hidden, value_pre_grad)
    hidden_one_grad = (
        times_transpose(query_pre_grad, query_low)
        + times_transpose(key_before_rotation_grad, key_reduced)
        + times_transpose(value_pre_grad, value_low)
    )
    gain_one_term = jnp.sum(hidden_one_grad * normed_one, axis=0)
    scaled_one = hidden_one_grad * gain_one
    input_grad = (
        residual_grad
        + scale_one
        * (scaled_one - normed_one * jnp.mean(scaled_one * normed_one, axis=1, keepdims=True))
    ).astype(jnp.bfloat16)
    gain_terms = jnp.stack([gain_one_term, gain_two_term])
    gain_part, query_part, key_part_sum, value_part_sum, output_part, router_part = (
        lax.psum_scatter(
            gain_terms.astype(jnp.bfloat16), "fsdp", scatter_dimension=1, tiled=True
        ).astype(jnp.float32),
        lax.psum_scatter(
            query_term.astype(jnp.bfloat16), "fsdp", scatter_dimension=0, tiled=True
        ).astype(jnp.float32),
        lax.psum_scatter(
            key_term.astype(jnp.bfloat16), "fsdp", scatter_dimension=0, tiled=True
        ).astype(jnp.float32),
        lax.psum_scatter(
            value_term.astype(jnp.bfloat16), "fsdp", scatter_dimension=0, tiled=True
        ).astype(jnp.float32),
        lax.psum_scatter(
            output_term.astype(jnp.bfloat16), "fsdp", scatter_dimension=0, tiled=True
        ).astype(jnp.float32),
        lax.psum_scatter(
            router_term.astype(jnp.bfloat16), "fsdp", scatter_dimension=0, tiled=True
        ).astype(jnp.float32),
    )
    gain_sum, query_sum, key_sum, value_sum, output_sum, router_sum = (
        lax.psum(gain_part.astype(jnp.bfloat16), "expert").astype(jnp.float32),
        lax.psum(query_part.astype(jnp.bfloat16), "expert").astype(jnp.float32),
        lax.psum(key_part_sum.astype(jnp.bfloat16), "expert").astype(jnp.float32),
        lax.psum(value_part_sum.astype(jnp.bfloat16), "expert").astype(jnp.float32),
        lax.psum(output_part.astype(jnp.bfloat16), "expert").astype(jnp.float32),
        lax.psum(router_part.astype(jnp.bfloat16), "expert").astype(jnp.float32),
    )
    gains_new, gains_first_new, gains_second_new = adamw_update(
        gains, gains_first, gains_second, gain_sum, GAIN_RATE, 0.0
    )
    query_new, query_first_new, query_second_new = adamw_update(
        query_weight, query_first, query_second, query_sum, 0.5 / math.sqrt(MODEL_WIDTH // 2), DECAY
    )
    key_new, key_first_new, key_second_new = adamw_update(
        key_matrix,
        key_moment_first,
        key_moment_second,
        key_sum,
        0.5 / math.sqrt(MODEL_WIDTH // 2),
        DECAY,
    )
    value_new, value_first_new, value_second_new = adamw_update(
        value_matrix,
        value_moment_first,
        value_moment_second,
        value_sum,
        0.5 / math.sqrt(MODEL_WIDTH),
        DECAY,
    )
    output_new, output_first_new, output_second_new = adamw_update(
        output_weight,
        output_first,
        output_second,
        output_sum,
        0.5 / math.sqrt(MODEL_WIDTH // 32),
        DECAY,
    )
    router_new, router_first_new, router_second_new = adamw_update(
        router_weight,
        router_first,
        router_second,
        router_sum,
        0.5 / math.sqrt(4 * MODEL_WIDTH),
        DECAY,
    )
    expert_in_new, in_first_new, in_second_new = adamw_update(
        expert_in, in_first, in_second, in_sum, 0.5 / math.sqrt(MODEL_WIDTH), DECAY
    )
    expert_out_new, out_first_new, out_second_new = adamw_update(
        expert_out, out_first, out_second, out_sum, 0.5 / math.sqrt(FF // 8), DECAY
    )
    return (
        layer_out,
        input_grad,
        gains_new,
        gains_first_new,
        gains_second_new,
        query_new,
        query_first_new,
        query_second_new,
        key_new,
        key_first_new,
        key_second_new,
        value_new,
        value_first_new,
        value_second_new,
        output_new,
        output_first_new,
        output_second_new,
        router_new,
        router_first_new,
        router_second_new,
        expert_in_new,
        in_first_new,
        in_second_new,
        expert_out_new,
        out_first_new,
        out_second_new,
    )


def solution(mesh):
    return jax.shard_map(
        body,
        mesh=mesh,
        in_specs=(
            P(("expert", "fsdp"), None),
            P(("expert", "fsdp"), None),
            P(("expert", "fsdp"), None),
            P(None, "fsdp"),
            P(None, "fsdp"),
            P(None, "fsdp"),
            P("fsdp", None),
            P("fsdp", None),
            P("fsdp", None),
            P("fsdp", None),
            P("fsdp", None),
            P("fsdp", None),
            P("fsdp", None),
            P("fsdp", None),
            P("fsdp", None),
            P("fsdp", None),
            P("fsdp", None),
            P("fsdp", None),
            P("fsdp", None),
            P("fsdp", None),
            P("fsdp", None),
            P("expert", "fsdp", None),
            P("expert", "fsdp", None),
            P("expert", "fsdp", None),
            P("expert", None, "fsdp"),
            P("expert", None, "fsdp"),
            P("expert", None, "fsdp"),
        ),
        out_specs=(
            P(("expert", "fsdp"), None),
            P(("expert", "fsdp"), None),
            P(None, "fsdp"),
            P(None, "fsdp"),
            P(None, "fsdp"),
            P("fsdp", None),
            P("fsdp", None),
            P("fsdp", None),
            P("fsdp", None),
            P("fsdp", None),
            P("fsdp", None),
            P("fsdp", None),
            P("fsdp", None),
            P("fsdp", None),
            P("fsdp", None),
            P("fsdp", None),
            P("fsdp", None),
            P("fsdp", None),
            P("fsdp", None),
            P("fsdp", None),
            P("expert", "fsdp", None),
            P("expert", "fsdp", None),
            P("expert", "fsdp", None),
            P("expert", None, "fsdp"),
            P("expert", None, "fsdp"),
            P("expert", None, "fsdp"),
        ),
        check_vma=False,
    )
```

profile of v0, /device:TPU:8, one launch (start us, length us, event | category | flops | bytes accessed | tf_op | source)
XLA Modules:
  0.0 1839.2 jit_solution(5031184081307827173)
XLA Ops:
  16.1 8.7 all_gather.33
  27.7 8.7 all_gather.31
  51.6 9.1 reduce-window.6
  61.6 8.1 scatter_custom_fusion
  74.8 29.5 %all-gather.11.cloned.1.call-done = bf16[1536,1536]{1,0:T(8,128)(2,1)} async-done(((bf16[384,1536]{1,0:T(8,128)(2,1)}), bf16[1536,1536]{1,0:T(8,128)(2,1)}) %all-gather.11.cloned.1.call-update) | async-done | bytes 4718608 | tf_op jit(solution)/shard_map/all_gather | solution.py:125
  121.2 10.7 while.51
  124.1 7.4 bitcast_add_fusion.4
  135.8 7.9 all-gather.13.cloned.1.call-done
  151.2 9.4 gather_fusion
  172.5 10.3 gather_fusion.3
  182.8 46.8 %all_gather.37 = bf16[1536,32]{0,1:T(8,128)(2,1)S(1)} all-gather(bf16[384,32]{0,1:T(8,128)(2,1)S(1)} %convert_element_type.228), channel_id=1, replica_groups=mesh['expert'=8,'fsdp'=4] {'fsdp'}, dimensions={0}, use_global_device_ids=true | all-gather | bytes 122880 | tf_op jit(solution)/shard_map/all_gather | solution.py:129
  234.5 13.6 gather_fusion.2
  248.3 8.7 multiply_convert_fusion
  256.9 80.4 %all-to-all-done = bf16[8,4,80,1536]{3,2,1,0:T(8,128)(2,1)} async-done(((bf16[8,4,80,1536]{3,2,1,0:T(8,128)(2,1)}), bf16[8,4,80,1536]{3,2,1,0:T(8,128)(2,1)}, u32[]{:S(2)}, u32[]{:S(2)}) %all-to-all-start) | async-done | bytes 7864352 | tf_op jit(solution)/shard_map/all_to_all | solution.py:232
  343.8 21.7 %fusion.88 = f32[8,4,80,1536]{3,2,0,1:T(8,128)} fusion(bf16[4,1536,1536]{2,1,0:T(8,128)(2,1)} %all-gather.15.cloned.1.call-done, bf16[8,4,80,1536]{3,2,1,0:T(8,128)(2,1)} %all-to-all-done), kind=kOutput, calls=%fused_computation.123 | convolution fusion | flops 12079595520 | bytes 42467328 | tf_op jit(solution)/shard_map/sjcd,jdf->sjcf/dot_general | solution.py:237
  365.5 149.0 %all-to-all-done.2 = bf16[8,4,80,1536]{3,2,1,0:T(8,128)(2,1)} async-done(((bf16[8,4,80,1536]{3,2,1,0:T(8,128)(2,1)}), bf16[8,4,80,1536]{3,2,1,0:T(8,128)(2,1)}, u32[]{:S(2)}, u32[]{:S(2)}) %all-to-all-start.2) | async-done | bytes 7864352 | tf_op jit(solution)/shard_map/all_to_all | solution.py:266
  514.4 17.5 fusion.83
  532.0 22.9 %convert_bitcast_fusion = bf16[8,4,80,1536]{3,2,0,1:T(8,128)(2,1)} fusion(bf16[4,1536,1536]{2,1,0:T(8,128)(2,1)} %all-gather.15.cloned.1.call-done, bf16[8,4,80,768]{3,2,0,1:T(8,128)(2,1)} %get-tuple-element.610, bf16[8,4,80,768]{3,2,0,1:T(8,128)(2,1)} %get-tuple-element.609), kind=kOutput, calls=%fused_computation.116 | convolution fusion | flops 12099256320 | bytes 34603008 | tf_op jit(solution)/shard_map/sjcf,jdf->sjcd/dot_general | solution.py:285
  562.0 7.5 all-to-all-start.3
  569.5 10.7 convert_bitcast_fusion.1
  584.0 155.6 %all-to-all-done.3 = bf16[8,4,80,1536]{3,2,1,0:T(8,128)(2,1)} async-done(((bf16[8,4,80,1536]{3,2,1,0:T(8,128)(2,1)}), bf16[8,4,80,1536]{3,2,1,0:T(8,128)(2,1)}, u32[]{:S(2)}, u32[]{:S(2)}) %all-to-all-start.3) | async-done | bytes 7864352 | tf_op jit(solution)/shard_map/all_to_all | solution.py:288
  739.6 7.3 all-to-all-start.1
  750.1 17.9 gather_fusion.4
  768.0 12.3 reshape.416
  780.3 135.9 %all-to-all-done.1 = bf16[8,4,80,1536]{3,2,1,0:T(8,128)(2,1)} async-done(((bf16[8,4,80,1536]{3,2,1,0:T(8,128)(2,1)}), bf16[8,4,80,1536]{3,2,1,0:T(8,128)(2,1)}, u32[]{:S(2)}, u32[]{:S(2)}) %all-to-all-start.1) | async-done | bytes 7864352 | tf_op jit(solution)/shard_map/all_to_all | solution.py:246
  916.2 17.5 gather_fusion.1
  933.7 12.4 reshape.415
  946.1 17.5 multiply_reduce_fusion
  964.8 12.8 reduce_sum.156
  992.8 8.6 while.52
  1006.6 36.8 %while.53 = (s32[]{:T(128)}, f32[512,2,6,128]{0,3,2,1:T(8,128)}, f32[2048,2,128]{0,2,1:T(8,128)}, f32[2048,2,128]{0,2,1:T(8,128)}, s32[]{:T(128)}, /*index=5*/bf...) while((s32[]{:T(128)}, f32[512,2,6,128]{0,3,2,1:T(8,128)}, ...), condition=%wide.region_25.26_spmd.clone, body=%wide.region_24.25_spmd.clone.sunk | while | flops 4059300864 | bytes 131678520 | solution.py:361
  1006.6 7.3 fusion.253
  1014.2 9.3 fusion.254
  1047.6 184.7 %reduce-scatter.17.cloned.1.call-done = bf16[512,256]{0,1:T(8,128)(2,1)} async-done(((bf16[2048,256]{0,1:T(8,128)(2,1)}), bf16[512,256]{0,1:T(8,128)(2,1)}) %reduce-scatter.17.cloned.1.call-update) | async-done | bytes 262160 | tf_op jit(solution)/shard_map/reduce_scatter | solution.py:372
  1236.0 24.5 %reduce-scatter.19.cloned.1.call-done = bf16[512,256]{0,1:T(8,128)(2,1)} async-done(((bf16[2048,256]{0,1:T(8,128)(2,1)}), bf16[512,256]{0,1:T(8,128)(2,1)}) %reduce-scatter.19.cloned.1.call-update) | async-done | bytes 262160 | tf_op jit(solution)/shard_map/reduce_scatter | solution.py:380
  1291.6 13.3 bitcast_convert_fusion.1
  1304.9 15.4 copy.225
  1320.2 10.5 copy.250
  1330.9 33.5 %reduce-scatter.21.cloned.1.call-done = bf16[384,1536]{1,0:T(8,128)(2,1)} async-done(((bf16[1536,1536]{1,0:T(8,128)(2,1)}), bf16[384,1536]{1,0:T(8,128)(2,1)}) %reduce-scatter.21.cloned.1.call-update) | async-done | bytes 1179664 | tf_op jit(solution)/shard_map/reduce_scatter | solution.py:419
  1364.3 51.0 %reduce-scatter.27.cloned.1.call-done = bf16[384,1536]{1,0:T(8,128)(2,1)} async-done(((bf16[1536,1536]{1,0:T(8,128)(2,1)}), bf16[384,1536]{1,0:T(8,128)(2,1)}) %reduce-scatter.27.cloned.1.call-update) | async-done | bytes 1179664 | tf_op jit(solution)/shard_map/reduce_scatter | solution.py:428
  1415.4 22.0 %bitcast_convert_fusion = bf16[4,1536,1536]{2,1,0:T(8,128)(2,1)} fusion(bf16[8,4,80,1536]{3,2,1,0:T(8,128)(2,1)} %all-to-all-done, bf16[8,4,80,768]{3,2,0,1:T(8,128)(2,1)} %get-tuple-element.610, bf16[8,4,80,768]{3,2,0,1:T(8,128)(2,1)} %get-tuple-element.609), kind=kOutput, calls=%fused_computation.90 | convolution fusion | flops 12104761344 | bytes 34603008 | tf_op jit(solution)/shard_map/sjcd,sjcf->jdf/dot_general | solution.py:282
  1445.2 17.8 reduce-scatter.31.cloned.1.call-done
  1464.0 34.8 %all-reduce.2 = (bf16[2,384]{1,0:T(2,128)(2,1)S(1)}, bf16[384,32]{0,1:T(8,128)(2,1)S(1)}) all-reduce(bf16[2,384]{1,0:T(2,128)(2,1)S(1)} %copy.222, bf16[384,32]{0,1:T(8,128)(2,1)S(1)} %copy.224), channel_id=1, replica_groups=mesh['expert'=8,'fsdp'=4] {'expert'}, use_global_device_ids=true, to_apply=%region_32.33 | all-reduce | flops 13056 | bytes 52224 | tf_op jit(solution)/shard_map/psum | solution.py:436
  1500.0 44.4 %reduce-scatter.35.cloned.1.call-done = bf16[384,3072]{1,0:T(8,128)(2,1)} async-done(((bf16[1536,3072]{1,0:T(8,128)(2,1)}), bf16[384,3072]{1,0:T(8,128)(2,1)}) %reduce-scatter.35.cloned.1.call-update) | async-done | bytes 2359312
  1552.7 12.1 multiply_subtract_fusion.1
  1564.8 101.9 %all-reduce.6.cloned.1.call-done = (bf16[384,1536]{1,0:T(8,128)(2,1)}, bf16[384,256]{1,0:T(8,128)(2,1)}, bf16[384,256]{1,0:T(8,128)(2,1)}, bf16[384,1536]{1,0:T(8,128)(2,1)}) async-done(((bf16[384,1536]{1,0:T(8,128)(2,1)}, bf16[384,256]{1,0:T(8,128)(2,1)}, bf16[384,256]{1,0:T(8,128)(2,1)}, bf16[384,1536]{1,0:T(8,128)(2,1)}), (bf16[384,1536]{1,0:T(8,128)(2,1)}, bf16[384,256]{1,0:T(8,128)(2,1)}, ...) | async-done | bytes 2752528 | tf_op jit(solution)/shard_map/psum | solution.py:437
  1683.6 125.3 %reduce-scatter.29.cloned.1.call-done = bf16[4,384,1536]{2,1,0:T(8,128)(2,1)} async-done(((bf16[4,1536,1536]{2,1,0:T(8,128)(2,1)}), bf16[4,384,1536]{2,1,0:T(8,128)(2,1)}) %reduce-scatter.29.cloned.1.call-update) | async-done | bytes 4718608 | tf_op jit(solution)/shard_map/reduce_scatter | solution.py:295
  1808.8 23.6 %multiply_subtract_fusion = (f32[4,384,1536]{2,1,0:T(8,128)}, f32[4,384,1536]{2,1,0:T(8,128)}, f32[4,384,1536]{2,1,0:T(8,128)}) fusion(f32[4,384,1536]{2,1,0:T(8,128)} %param.56, bf16[4,384,1536]{2,1,0:T(8,128)(2,1)} %reduce-scatter.29.cloned.1.call-done, f32[4,384,1536]{2,1,0:T(8,128)} %param.57, f32[4,384,1536]{2,1,0:T(8,128)} %param.58), kind=kLoop, calls=%fused_computation.107 | loop fusion | flops 37748736 | bytes 61341696 | tf_op jit(solution)/shard_map/sub | solution.py:79
  (346 shorter events, 230.7 us)
Async XLA Ops:
  7.2 18.8 %copy-start.11 = (bf16[512,1536]{1,0:T(8,128)(2,1)S(1)}, bf16[512,1536]{1,0:T(8,128)(2,1)}, u32[]{:S(2)}) copy-start(bf16[512,1536]{1,0:T(8,128)(2,1)} %param.35) | copy-start | bytes 4718596
  7.2 63.1 %all-gather.9.cloned.1.call-start = ((), (), s32[]{:S(2)}) async-start(), calls=%async_computation.15 | async-start | bytes 1310720 | tf_op jit(solution)/shard_map/all_gather | solution.py:155
  13.2 91.0 %copy-start.57 = (f32[1536]{0:T(1024)}, f32[1536]{0:T(1024)S(1)}, u32[]{:S(2)}) copy-start(f32[1536]{0:T(1024)S(1)} %get-tuple-element.496) | copy-start | bytes 18436
  13.3 135.8 %copy-start.52 = (f32[1536]{0:T(1024)}, f32[1536]{0:T(1024)S(1)}, u32[]{:S(2)}) copy-start(f32[1536]{0:T(1024)S(1)} %get-tuple-element.495) | copy-start | bytes 18436
  15.1 89.2 %copy-start.72 = (f32[512]{0:T(512)}, f32[512]{0:T(512)S(1)}, u32[]{:S(2)}) copy-start(f32[512]{0:T(512)S(1)} %add_rsqrt_fusion.1) | copy-start | bytes 6148
  26.0 83.0 %copy-start.22 = (f32[512,64]{0,1:T(8,128)}, f32[512,64]{0,1:T(8,128)S(1)}, u32[]{:S(2)}) copy-start(f32[512,64]{0,1:T(8,128)S(1)} %get-tuple-element.626) | copy-start | bytes 393220
  27.6 44.9 %all-gather.7.cloned.1.call-start = ((), (), s32[]{:S(2)}) async-start(), calls=%async_computation.14 | async-start | bytes 1310720 | tf_op jit(solution)/shard_map/all_gather | solution.py:156
  37.8 66.4 %all-gather.11.cloned.1.call-start = ((), (), s32[]{:S(2)}) async-start(), calls=%async_computation.16 | async-start | bytes 5898240 | tf_op jit(solution)/shard_map/all_gather | solution.py:125
  40.7 103.0 %all-gather.13.cloned.1.call-start = ((), (), s32[]{:S(2)}) async-start(), calls=%async_computation.17 | async-start | bytes 5898240 | tf_op jit(solution)/shard_map/all_gather | solution.py:128
  43.6 300.2 %all-gather.15.cloned.1.call-start = ((), (), s32[]{:S(2)}) async-start(), calls=%async_computation.18 | async-start | bytes 23592960 | tf_op jit(solution)/shard_map/all_gather | solution.py:234
  61.6 47.4 %copy-start.68 = (s32[2048,1]{0,1:T(1,128)}, s32[2048,1]{0,1:T(1,128)S(1)}, u32[]{:S(2)}) copy-start(s32[2048,1]{0,1:T(1,128)S(1)} %compare_select_fusion) | copy-start | bytes 24580
  160.6 176.7 %all-to-all-start = ((bf16[8,4,80,1536]{3,2,1,0:T(8,128)(2,1)}), bf16[8,4,80,1536]{3,2,1,0:T(8,128)(2,1)}, u32[]{:S(2)}, u32[]{:S(2)}) async-start(bf16[8,4,80,1536]{3,2,1,0:T(8,128)(2,1)} %bitcast.308), calls=%async_computation | async-start | bytes 15728640 | tf_op jit(solution)/shard_map/all_to_all | solution.py:232
  166.6 198.8 %all-gather.17.cloned.1.call-start = ((), (), s32[]{:S(2)}) async-start(), calls=%async_computation.19 | async-start | bytes 11796480 | tf_op jit(solution)/shard_map/all_gather | solution.py:235
  172.5 59.7 %copy-start.55 = (s32[512,4]{0,1:T(4,128)S(1)}, s32[512,4]{0,1:T(4,128)}, u32[]{:S(2)}) copy-start(s32[512,4]{0,1:T(4,128)} %param.37) | copy-start | bytes 24580
  172.5 62.0 %copy-start.63 = (s32[3072]{0:T(1024)S(1)}, s32[3072]{0:T(1024)}, u32[]{:S(2)}) copy-start(s32[3072]{0:T(1024)} %get-tuple-element.631) | copy-start | bytes 36868
  337.3 177.1 %all-to-all-start.2 = ((bf16[8,4,80,1536]{3,2,1,0:T(8,128)(2,1)}), bf16[8,4,80,1536]{3,2,1,0:T(8,128)(2,1)}, u32[]{:S(2)}, u32[]{:S(2)}) async-start(bf16[8,4,80,1536]{3,2,1,0:T(8,128)(2,1)} %multiply_convert_fusion), calls=%async_computation.2 | async-start | bytes 15728640 | tf_op jit(solution)/shard_map/all_to_all | solution.py:266
  562.0 177.5 %all-to-all-start.3 = ((bf16[8,4,80,1536]{3,2,1,0:T(8,128)(2,1)}), bf16[8,4,80,1536]{3,2,1,0:T(8,128)(2,1)}, u32[]{:S(2)}, u32[]{:S(2)}) async-start(bf16[8,4,80,1536]{3,2,1,0:T(8,128)(2,1)} %copy.188), calls=%async_computation.3 | async-start | bytes 15728640 | tf_op jit(solution)/shard_map/all_to_all | solution.py:288
  584.0 163.0 %copy-start.14 = (bf16[512,1536]{1,0:T(8,128)(2,1)S(1)}, bf16[512,1536]{1,0:T(8,128)(2,1)}, u32[]{:S(2)}) copy-start(bf16[512,1536]{1,0:T(8,128)(2,1)} %param.36) | copy-start | bytes 4718596
  739.6 176.6 %all-to-all-start.1 = ((bf16[8,4,80,1536]{3,2,1,0:T(8,128)(2,1)}), bf16[8,4,80,1536]{3,2,1,0:T(8,128)(2,1)}, u32[]{:S(2)}, u32[]{:S(2)}) async-start(bf16[8,4,80,1536]{3,2,1,0:T(8,128)(2,1)} %copy.183), calls=%async_computation.1 | async-start | bytes 15728640 | tf_op jit(solution)/shard_map/all_to_all | solution.py:246
  746.9 485.4 %reduce-scatter.17.cloned.1.call-start = ((), (), s32[]{:S(2)}) async-start(), calls=%async_computation.20 | async-start | bytes 1310720 | tf_op jit(solution)/shard_map/reduce_scatter | solution.py:372
  946.1 18.6 %copy-start.48 = (f32[512,4]{0,1:T(4,128)S(1)}, f32[512,4]{0,1:T(4,128)}, u32[]{:S(2)}) copy-start(f32[512,4]{0,1:T(4,128)} %copy-done.47) | copy-start | bytes 24580
  946.1 18.6 %copy-start.56 = (s32[512,4]{0,1:T(4,128)S(1)}, s32[512,4]{0,1:T(4,128)}, u32[]{:S(2)}) copy-start(s32[512,4]{0,1:T(4,128)} %param.37) | copy-start | bytes 24580
  1046.3 187.0 %copy-start.23 = (f32[512,64]{0,1:T(8,128)S(1)}, f32[512,64]{0,1:T(8,128)}, u32[]{:S(2)}) copy-start(f32[512,64]{0,1:T(8,128)} %copy-done.22) | copy-start | bytes 393220
  1046.3 187.0 %copy-start.38 = (f32[512,64]{0,1:T(8,128)S(1)}, f32[512,64]{0,1:T(8,128)}, u32[]{:S(2)}) copy-start(f32[512,64]{0,1:T(8,128)} %get-tuple-element.624) | copy-start | bytes 393220
  1046.4 214.1 %reduce-scatter.19.cloned.1.call-start = ((), (), s32[]{:S(2)}) async-start(), calls=%async_computation.21 | async-start | bytes 1310720 | tf_op jit(solution)/shard_map/reduce_scatter | solution.py:380
  1046.4 187.8 %copy-start.58 = (f32[1536]{0:T(1024)S(1)}, f32[1536]{0:T(1024)}, u32[]{:S(2)}) copy-start(f32[1536]{0:T(1024)} %copy-done.57) | copy-start | bytes 18436
  1046.4 187.8 %copy-start.73 = (f32[512]{0:T(512)S(1)}, f32[512]{0:T(512)}, u32[]{:S(2)}) copy-start(f32[512]{0:T(512)} %copy-done.72) | copy-start | bytes 6148
  1047.6 186.7 %copy-start.12 = (bf16[512,1536]{1,0:T(8,128)(2,1)S(1)}, bf16[512,1536]{1,0:T(8,128)(2,1)}, u32[]{:S(2)}) copy-start(bf16[512,1536]{1,0:T(8,128)(2,1)} %param.35) | copy-start | bytes 4718596
  1047.6 283.2 %reduce-scatter.23.cloned.1.call-start = ((), (), s32[]{:S(2)}) async-start(), calls=%async_computation.23 | async-start | bytes 983040 | tf_op jit(solution)/shard_map/reduce_scatter | solution.py:422
  1235.9 27.8 %copy-start.5 = (f32[512,2,6,128]{0,3,2,1:T(8,128)S(1)}, f32[512,2,6,128]{0,3,2,1:T(8,128)}, u32[]{:S(2)}) copy-start(f32[512,2,6,128]{0,3,2,1:T(8,128)} %get-tuple-element.225) | copy-start | bytes 9437188
  1235.9 94.9 %reduce-scatter.25.cloned.1.call-start = ((), (), s32[]{:S(2)}) async-start(), calls=%async_computation.24 | async-start | bytes 983040 | tf_op jit(solution)/shard_map/reduce_scatter | solution.py:425
  1263.6 100.7 %reduce-scatter.21.cloned.1.call-start = ((), (), s32[]{:S(2)}) async-start(), calls=%async_computation.22 | async-start | bytes 5898240 | tf_op jit(solution)/shard_map/reduce_scatter | solution.py:419
  1270.5 144.8 %reduce-scatter.27.cloned.1.call-start = ((), (), s32[]{:S(2)}) async-start(), calls=%async_computation.25 | async-start | bytes 5898240 | tf_op jit(solution)/shard_map/reduce_scatter | solution.py:428
  1278.1 161.1 %reduce-scatter.33.cloned.1.call-start = ((), (), s32[]{:S(2)}) async-start(), calls=%async_computation.28 | async-start | bytes 491520
  1280.9 182.1 %reduce-scatter.31.cloned.1.call-start = ((), (), s32[]{:S(2)}) async-start(), calls=%async_computation.27 | async-start | bytes 491520
  1291.4 253.1 %reduce-scatter.35.cloned.1.call-start = ((), (), s32[]{:S(2)}) async-start(), calls=%async_computation.29 | async-start | bytes 11796480
  1330.8 336.0 %all-reduce.6.cloned.1.call-start = ((), (), s32[]{:S(2)}) async-start(), calls=%async_computation.30 | async-start | bytes 5505024 | tf_op jit(solution)/shard_map/psum | solution.py:437
  1415.3 393.5 %reduce-scatter.29.cloned.1.call-start = ((), (), s32[]{:S(2)}) async-start(), calls=%async_computation.26 | async-start | bytes 23592960 | tf_op jit(solution)/shard_map/reduce_scatter | solution.py:295
  1440.2 58.5 %copy-start.75 = (f32[2,384]{1,0:T(2,128)S(1)}, f32[2,384]{1,0:T(2,128)}, u32[]{:S(2)}) copy-start(f32[2,384]{1,0:T(2,128)} %param.38) | copy-start | bytes 9220
  1440.2 58.5 %copy-start.76 = (f32[2,384]{1,0:T(2,128)S(1)}, f32[2,384]{1,0:T(2,128)}, u32[]{:S(2)}) copy-start(f32[2,384]{1,0:T(2,128)} %param.39) | copy-start | bytes 9220
  1440.2 58.5 %copy-start.77 = (f32[2,384]{1,0:T(2,128)S(1)}, f32[2,384]{1,0:T(2,128)}, u32[]{:S(2)}) copy-start(f32[2,384]{1,0:T(2,128)} %param.40) | copy-start | bytes 9220
  1440.3 59.1 %copy-start.51 = (f32[384,32]{0,1:T(8,128)S(1)}, f32[384,32]{0,1:T(8,128)}, u32[]{:S(2)}) copy-start(f32[384,32]{0,1:T(8,128)} %param.53) | copy-start | bytes 147460
  1440.3 59.1 %copy-start.61 = (f32[384,32]{0,1:T(8,128)S(1)}, f32[384,32]{0,1:T(8,128)}, u32[]{:S(2)}) copy-start(f32[384,32]{0,1:T(8,128)} %param.54) | copy-start | bytes 147460
  1440.3 59.1 %copy-start.62 = (f32[384,32]{0,1:T(8,128)S(1)}, f32[384,32]{0,1:T(8,128)}, u32[]{:S(2)}) copy-start(f32[384,32]{0,1:T(8,128)} %param.55) | copy-start | bytes 147460
  1552.7 114.0 %copy-start.34 = (f32[384,256]{1,0:T(8,128)S(1)}, f32[384,256]{1,0:T(8,128)}, u32[]{:S(2)}) copy-start(f32[384,256]{1,0:T(8,128)} %param.44) | copy-start | bytes 1179652
  1552.7 114.0 %copy-start.44 = (f32[384,256]{1,0:T(8,128)S(1)}, f32[384,256]{1,0:T(8,128)}, u32[]{:S(2)}) copy-start(f32[384,256]{1,0:T(8,128)} %param.45) | copy-start | bytes 1179652
  1552.7 116.5 %copy-start.36 = (f32[384,256]{1,0:T(8,128)S(1)}, f32[384,256]{1,0:T(8,128)}, u32[]{:S(2)}) copy-start(f32[384,256]{1,0:T(8,128)} %param.47) | copy-start | bytes 1179652
  1564.8 106.8 %copy-start.19 = (f32[384,1536]{1,0:T(8,128)S(1)}, f32[384,1536]{1,0:T(8,128)}, u32[]{:S(2)}) copy-start(f32[384,1536]{1,0:T(8,128)} %param.41) | copy-start | bytes 7077892
  (53 other events, 293.6 us)
Sparse Core Ops, SparseCore 0:
  27.7 17.9 all-gather.8
  47.8 16.7 all-gather.6
  66.8 37.3 all-gather.10
  106.2 37.4 all-gather.12
  145.7 119.7 all-gather.14
  267.5 64.0 all-gather.16
  1046.5 185.8 reduce-scatter.16
  1235.6 24.8 reduce-scatter.18
  1263.6 23.2 reduce-scatter.22
  1290.0 23.2 reduce-scatter.24
  1316.4 47.8 reduce-scatter.20
  1367.4 47.8 reduce-scatter.26
  1418.4 20.7 reduce-scatter.32
  1442.2 20.7 reduce-scatter.30
  1466.0 78.4 reduce-scatter.34
  1548.2 118.5 all-reduce.5
  1669.2 139.6 reduce-scatter.28
where the time goes:
time: 1850 us; the launch traced here: 1840 us
  waiting for transfers between devices  1140 us (62%)
  matrix products  204 us (11%)
  local copies, waits for them, and re-layouts  193 us (10%)
  other arithmetic  151 us (8%)
  blocking collectives  104 us (6%)
  starting transfers between devices  28.1 us (2%)
    reduce_scatter x1, waiting for transfers between devices, body(): lax.psum_scatter((key_accumulator.reshape(sequence_rows, KEY_VALUE_HEADS...  185 us
    all_to_all x1, waiting for transfers between devices, body(): lax.all_to_all(row_grad, 'expert', split_axis=0, concat_axis=0, tiled=True)  156 us
    all_to_all x1, waiting for transfers between devices, body(): lax.all_to_all(slot_grad.reshape(expert_count, experts_local, CAP, MODEL_...  149 us
    all_to_all x1, waiting for transfers between devices, body(): lax.all_to_all(expert_result, 'expert', split_axis=0, concat_axis=0, tile...  136 us
    reduce_scatter x1, waiting for transfers between devices, body(): lax.psum_scatter(in_term.astype(jnp.bfloat16), 'fsdp', scatter_dimension=...  125 us
    psum x1, waiting for transfers between devices, body(): lax.psum(query_part.astype(jnp.bfloat16), 'expert').astype(jnp.float32)  102 us
    all_to_all x1, waiting for transfers between devices, body(): lax.all_to_all(outgoing, 'expert', split_axis=0, concat_axis=0, tiled=True)  80.4 us
    unnamed x20, waiting for transfers between devices  64.4 us
  transfers between devices with their start and end apart: 21, of which 15 were waited for; matrix products, arithmetic and copies ran while one was open for 18% of the time, Pallas kernels for 0%

commit v1 on v0

v1 whole, which is shorter than its diff:
```python
import math

import jax
import jax.numpy as jnp
from jax import lax
from jax.experimental import pallas as pl
from jax.experimental.pallas import tpu as pltpu
from jax.sharding import PartitionSpec as P

MODEL_WIDTH = 1536
QUERY_HEADS = 12
KEY_VALUE_HEADS = 2
HEAD_SIZE = 128
GROUP = QUERY_HEADS // KEY_VALUE_HEADS
FF = 768
STEP = 10
CAP = 80
DEPTH = 4
HALF = MODEL_WIDTH // 2
KV = KEY_VALUE_HEADS * HEAD_SIZE
QKV = MODEL_WIDTH + 2 * KV


NORM_EPS = 1e-05
ROPE_BASE = 10000.0
BETA_ONE = 0.9
BETA_TWO = 0.95
ADAM_EPS = 1e-08
DECAY = 0.1
GAIN_RATE = 0.8
MASKED = -1e30
LOG2E = 1.0 / math.log(2.0)
SCORE_SCALE = 1.0 / math.sqrt(HEAD_SIZE)

f32 = jnp.float32
bf16 = jnp.bfloat16


def dot_nn(left, right):
    return lax.dot_general(left, right, (((1,), (0,)), ((), ())), preferred_element_type=f32)


def dot_nt(left, right):
    return lax.dot_general(left, right, (((1,), (1,)), ((), ())), preferred_element_type=f32)


def dot_tn(left, right):
    return lax.dot_general(left, right, (((0,), (0,)), ((), ())), preferred_element_type=f32)


def params(megabytes, axes):
    return pltpu.CompilerParams(
        vmem_limit_bytes=megabytes * 1024 * 1024, dimension_semantics=("arbitrary",) * axes
    )


def cost(flops, nbytes, trans=0):
    return pl.CostEstimate(flops=int(flops), bytes_accessed=int(nbytes), transcendentals=int(trans))


def causal(score_t):
    key_place = lax.broadcasted_iota(jnp.int32, score_t.shape, 0)
    query_place = lax.broadcasted_iota(jnp.int32, score_t.shape, 1)
    return key_place <= query_place


def attend_kernel(place, pre, cosine, sine, keys, values, out, log_total, turned):
    rows = pre[...]
    query = rows * cosine[...] + pltpu.roll(rows, HEAD_SIZE // 2, 1) * sine[...]
    turned[...] = query.astype(bf16)
    query_t = query.T.astype(bf16)
    factor = SCORE_SCALE * LOG2E

    score = dot_nn(keys[0], query_t) * factor
    score = jnp.where(causal(score), score, MASKED)
    biggest = jnp.max(score, axis=0, keepdims=True)
    weight = jnp.exp2(score - biggest)
    total = jnp.sum(weight, axis=0, keepdims=True)
    acc = dot_nn(values[0].T, weight.astype(bf16))

    def step(back, carry):
        biggest, total, acc = carry
        score = dot_nn(keys[back], query_t) * factor
        larger = jnp.maximum(biggest, jnp.max(score, axis=0, keepdims=True))
        weight = jnp.exp2(score - larger)
        shrink = jnp.exp2(biggest - larger)
        total = total * shrink + jnp.sum(weight, axis=0, keepdims=True)
        acc = acc * shrink + dot_nn(values[back].T, weight.astype(bf16))
        return larger, total, acc

    biggest, total, acc = lax.fori_loop(1, place[0] + 1, step, (biggest, total, acc))
    out[...] = (acc / total).T.astype(bf16)
    log_total[0] = biggest + jnp.log(total) * LOG2E


def attend(place, pre, cosine, sine, kv_blocks):
    token_rows = pre.shape[0]
    blocks = kv_blocks.shape[0]
    width = (token_rows, HEAD_SIZE)
    many = (blocks, token_rows, HEAD_SIZE)
    return pl.pallas_call(
        attend_kernel,
        out_shape=(
            jax.ShapeDtypeStruct((token_rows, MODEL_WIDTH), bf16),
            jax.ShapeDtypeStruct((QUERY_HEADS, 1, token_rows), f32),
            jax.ShapeDtypeStruct((token_rows, MODEL_WIDTH), bf16),
        ),
        grid_spec=pltpu.PrefetchScalarGridSpec(
            num_scalar_prefetch=1,
            grid=(QUERY_HEADS,),
            in_specs=[
                pl.BlockSpec(width, lambda h, p: (0, h)),
                pl.BlockSpec(width, lambda h, p: (0, 0)),
                pl.BlockSpec(width, lambda h, p: (0, 0)),
                pl.BlockSpec(many, lambda h, p: (0, 0, h // GROUP)),
                pl.BlockSpec(many, lambda h, p: (0, 0, KEY_VALUE_HEADS + h // GROUP)),
            ],
            out_specs=(
                pl.BlockSpec(width, lambda h, p: (0, h)),
                pl.BlockSpec((1, 1, token_rows), lambda h, p: (h, 0, 0)),
                pl.BlockSpec(width, lambda h, p: (0, h)),
            ),
        ),
        compiler_params=params(56, 1),
        cost_estimate=cost(16e9, 8e6, 6e6),
        name="attend",
    )(place, pre, cosine, sine, kv_blocks, kv_blocks)


def attend_back_kernel(
    place, query, keys, values, out, out_grad, log_total, cosine, sine, pre_grad, key_grad, value_grad, key_acc, value_acc
):
    head = pl.program_id(0)

    @pl.when(head % GROUP == 0)
    def _():
        key_acc[...] = jnp.zeros_like(key_acc)
        value_acc[...] = jnp.zeros_like(value_acc)

    factor = SCORE_SCALE * LOG2E
    query_rows = query[...]
    grad_rows = out_grad[...]
    query_t = query_rows.astype(f32).T.astype(bf16)
    grad_t32 = grad_rows.astype(f32).T
    grad_t = grad_t32.astype(bf16)
    row_dot = jnp.sum(out[...].astype(f32).T * grad_t32, axis=0, keepdims=True)
    level = log_total[0]

    def block(back, masked):
        key = keys[back]
        score = dot_nn(key, query_t) * factor - level
        weight = jnp.exp2(score)
        if masked:
            weight = jnp.where(causal(weight), weight, 0.0)
        value_acc[back] += dot_nn(weight.astype(bf16), grad_rows)
        prob_grad = dot_nn(values[back], grad_t)
        score_grad = (weight * (prob_grad - row_dot)).astype(bf16)
        key_acc[back] += dot_nn(score_grad, query_rows)
        return dot_nn(key.T, score_grad)

    query_grad = block(0, True)
    query_grad = lax.fori_loop(1, place[0] + 1, lambda b, acc: acc + block(b, False), query_grad)
    rows = query_grad.T * SCORE_SCALE
    pre_grad[...] = (rows * cosine[...] - pltpu.roll(rows, HEAD_SIZE // 2, 1) * sine[...]).astype(bf16)

    @pl.when(head % GROUP == GROUP - 1)
    def _():
        key_grad[...] = (key_acc[...] * SCORE_SCALE).astype(bf16)
        value_grad[...] = value_acc[...].astype(bf16)


def attend_back(place, query, kv_blocks, out, out_grad, log_total, cosine, sine):
    token_rows = query.shape[0]
    blocks = kv_blocks.shape[0]
    width = (token_rows, HEAD_SIZE)
    many = (blocks, token_rows, HEAD_SIZE)
    return pl.pallas_call(
        attend_back_kernel,
        out_shape=(
            jax.ShapeDtypeStruct((token_rows, MODEL_WIDTH), bf16),
            jax.ShapeDtypeStruct((blocks, token_rows, KV), bf16),
            jax.ShapeDtypeStruct((blocks, token_rows, KV), bf16),
        ),
        grid_spec=pltpu.PrefetchScalarGridSpec(
            num_scalar_prefetch=1,
            grid=(QUERY_HEADS,),
            in_specs=[
                pl.BlockSpec(width, lambda h, p: (0, h)),
                pl.BlockSpec(many, lambda h, p: (0, 0, h // GROUP)),
                pl.BlockSpec(many, lambda h, p: (0, 0, KEY_VALUE_HEADS + h // GROUP)),
                pl.BlockSpec(width, lambda h, p: (0, h)),
                pl.BlockSpec(width, lambda h, p: (0, h)),
                pl.BlockSpec((1, 1, token_rows), lambda h, p: (h, 0, 0)),
                pl.BlockSpec(width, lambda h, p: (0, 0)),
                pl.BlockSpec(width, lambda h, p: (0, 0)),
            ],
            out_specs=(
                pl.BlockSpec(width, lambda h, p: (0, h)),
                pl.BlockSpec(many, lambda h, p: (0, 0, h // GROUP)),
                pl.BlockSpec(many, lambda h, p: (0, 0, h // GROUP)),
            ),
            scratch_shapes=[pltpu.VMEM(many, f32), pltpu.VMEM(many, f32)],
        ),
        compiler_params=params(56, 1),
        cost_estimate=cost(40e9, 12e6, 6e6),
        name="attend_back",
    )(place, query, kv_blocks, kv_blocks, out, out_grad, log_total, cosine, sine)


def inner_kernel(first, second, down, inner):
    shards, span = down.shape[0], down.shape[3]
    acc = None
    for c in range(shards):
        side = first if c < shards // 2 else second
        at = (c % (shards // 2)) * span
        term = dot_nt(side[0, :, at : at + span], down[c, 0])
        acc = term if acc is None else acc + term
    inner[0] = acc


def inner_rows(first, second, down):
    experts, rows, _ = first.shape
    shards, _, _, span = down.shape
    tile = 256
    return pl.pallas_call(
        inner_kernel,
        out_shape=jax.ShapeDtypeStruct((experts, rows, FF), f32),
        grid=(experts, FF // tile),
        in_specs=[
            pl.BlockSpec((1, rows, HALF), lambda e, n: (e, 0, 0)),
            pl.BlockSpec((1, rows, HALF), lambda e, n: (e, 0, 0)),
            pl.BlockSpec((shards, 1, tile, span), lambda e, n: (0, e, n, 0)),
        ],
        out_specs=pl.BlockSpec((1, rows, tile), lambda e, n: (e, 0, n)),
        compiler_params=params(56, 2),
        cost_estimate=cost(2 * experts * rows * FF * MODEL_WIDTH, 30e6),
        name="inner_rows",
    )(first, second, down)


def gate_kernel(first, second, gate_w, up_w, inner, weight, scaled, gate_out, up_out, gate_grad):
    shards, _, span, tile = gate_w.shape
    near, far = first[0], second[0]

    def product(ref):
        low = ref[: shards // 2, 0].reshape(HALF, tile)
        high = ref[shards // 2 :, 0].reshape(HALF, tile)
        return dot_nn(near, low) + dot_nn(far, high)

    gate_pre = product(gate_w)
    up_part = product(up_w)
    sigmoid = 1.0 / (1.0 + jnp.exp(-gate_pre))
    silu = gate_pre * sigmoid
    hidden = silu * up_part
    factor = weight[0]
    raw = inner[0]
    scaled[0] = (hidden * factor).astype(bf16)
    part = jnp.sum(raw * hidden, axis=1, keepdims=True)
    raw = raw * factor
    gate_out[0] = (raw * up_part * (sigmoid * (1.0 + gate_pre * (1.0 - sigmoid)))).astype(bf16)
    up_out[0] = (raw * silu).astype(bf16)

    @pl.when(pl.program_id(1) == 0)
    def _():
        gate_grad[0] = part

    @pl.when(pl.program_id(1) > 0)
    def _():
        gate_grad[0] += part


def gate_rows(first, second, gate_up, inner, weight):
    experts, rows, _ = first.shape
    shards, _, span, _ = gate_up.shape
    tile = 256
    tiles = FF // tile
    wide = pl.BlockSpec((1, rows, tile), lambda e, n: (e, 0, n))
    column = pl.BlockSpec((1, rows, 1), lambda e, n: (e, 0, 0))
    low = jax.ShapeDtypeStruct((experts, rows, FF), bf16)
    return pl.pallas_call(
        gate_kernel,
        out_shape=(low, low, low, jax.ShapeDtypeStruct((experts, rows, 1), f32)),
        grid=(experts, tiles),
        in_specs=[
            pl.BlockSpec((1, rows, HALF), lambda e, n: (e, 0, 0)),
            pl.BlockSpec((1, rows, HALF), lambda e, n: (e, 0, 0)),
            pl.BlockSpec((shards, 1, span, tile), lambda e, n: (0, e, 0, n)),
            pl.BlockSpec((shards, 1, span, tile), lambda e, n: (0, e, 0, n + tiles)),
            wide,
            column,
        ],
        out_specs=(wide, wide, wide, column),
        compiler_params=params(56, 2),
        cost_estimate=cost(4 * experts * rows * FF * MODEL_WIDTH, 50e6, experts * rows * FF),
        name="gate_rows",
    )(first, second, gate_up, gate_up, inner, weight)


def row_grad_kernel(gate_side, up_side, weight, out):
    block = weight[0, 0]
    out[0] = (dot_nt(gate_side[0], block[:, :FF]) + dot_nt(up_side[0], block[:, FF:])).astype(bf16)


def row_grads(gate_side, up_side, gate_up):
    experts, rows, _ = gate_side.shape
    shards, _, span, _ = gate_up.shape
    span_all = MODEL_WIDTH // shards
    whole = pl.BlockSpec((1, rows, FF), lambda e, n: (e, 0, 0))
    if span_all % 128:
        joined = gate_up.transpose(1, 0, 2, 3).reshape(1, experts, MODEL_WIDTH, 2 * FF)
        spec = pl.BlockSpec((1, 1, 384, 2 * FF), lambda e, n: (0, e, n, 0))
        span, shards = 384, MODEL_WIDTH // 384
    else:
        joined = gate_up
        spec = pl.BlockSpec((1, 1, span, 2 * FF), lambda e, n: (n, e, 0, 0))
    return pl.pallas_call(
        row_grad_kernel,
        out_shape=jax.ShapeDtypeStruct((experts, rows, MODEL_WIDTH), bf16),
        grid=(experts, shards),
        in_specs=[whole, whole, spec],
        out_specs=pl.BlockSpec((1, rows, span), lambda e, n: (e, 0, n)),
        compiler_params=params(56, 2),
        cost_estimate=cost(4 * experts * rows * FF * MODEL_WIDTH, 40e6),
        name="row_grads",
    )(gate_side, up_side, joined)


def result_kernel(scaled, down, out):
    shards, span = down.shape[0], down.shape[3]
    rows = scaled[0]
    for c in range(shards):
        out[0, :, c * span : (c + 1) * span] = dot_nn(rows, down[c, 0]).astype(bf16)


def result_rows(scaled, down):
    experts, rows, _ = scaled.shape
    shards, _, _, span = down.shape
    return pl.pallas_call(
        result_kernel,
        out_shape=jax.ShapeDtypeStruct((experts, rows, MODEL_WIDTH), bf16),
        grid=(experts,),
        in_specs=[
            pl.BlockSpec((1, rows, FF), lambda e: (e, 0, 0)),
            pl.BlockSpec((shards, 1, FF, span), lambda e: (0, e, 0, 0)),
        ],
        out_specs=pl.BlockSpec((1, rows, MODEL_WIDTH), lambda e: (e, 0, 0)),
        compiler_params=params(56, 1),
        cost_estimate=cost(2 * experts * rows * FF * MODEL_WIDTH, 22e6),
        name="result_rows",
    )(scaled, down)


def down_grad_kernel(scaled, first, second, out):
    shards, span = out.shape[0], out.shape[3]
    rows_t = scaled[0].T
    for c in range(shards):
        side = first if c < shards // 2 else second
        at = (c % (shards // 2)) * span
        out[c, 0] = dot_nn(rows_t, side[0, :, at : at + span]).astype(bf16)


def down_grads(scaled, first, second, shards):
    experts, rows, _ = scaled.shape
    span = MODEL_WIDTH // shards
    half = pl.BlockSpec((1, rows, HALF), lambda e: (e, 0, 0))
    return pl.pallas_call(
        down_grad_kernel,
        out_shape=jax.ShapeDtypeStruct((shards, experts, FF, span), bf16),
        grid=(experts,),
        in_specs=[pl.BlockSpec((1, rows, FF), lambda e: (e, 0, 0)), half, half],
        out_specs=pl.BlockSpec((shards, 1, FF, span), lambda e: (0, e, 0, 0)),
        compiler_params=params(56, 1),
        cost_estimate=cost(2 * experts * rows * FF * MODEL_WIDTH, 22e6),
        name="down_grads",
    )(scaled, first, second)


def in_grads(first, second, gate_side, up_side, shards):
    experts, rows, _ = first.shape
    span = MODEL_WIDTH // shards
    half = pl.BlockSpec((1, rows, HALF), lambda e, n: (e, 0, 0))

    def kernel(first, second, gate_side, up_side, out):
        pick = pl.program_id(1)

        def fill(column):
            for side, base in ((first, 0), (second, shards // 2)):
                rows_t = side[0].T
                for c in range(shards // 2):
                    part = rows_t[c * span : (c + 1) * span]
                    out[base + c, 0] = dot_nn(part, column[0]).astype(bf16)

        @pl.when(pick == 0)
        def _():
            fill(gate_side)

        @pl.when(pick == 1)
        def _():
            fill(up_side)

    return pl.pallas_call(
        kernel,
        out_shape=jax.ShapeDtypeStruct((shards, experts, span, 2 * FF), bf16),
        grid=(experts, 2),
        in_specs=[half, half, half, half],
        out_specs=pl.BlockSpec((shards, 1, span, FF), lambda e, n: (0, e, 0, n)),
        compiler_params=params(56, 2),
        cost_estimate=cost(4 * experts * rows * FF * MODEL_WIDTH, 35e6),
        name="in_grads",
    )(first, second, gate_side, up_side)


def pick_kernel(picks_up, picks_down, up, down, own, away):
    per = own.shape[1]
    for half, (picks, rows) in enumerate(((picks_up, up), (picks_down, down))):
        picked = dot_nn(picks[0], rows[...]).astype(bf16)
        own[half] = picked[:per]
        for r in range(away.shape[0]):
            away[r, half] = picked[(r + 1) * per : (r + 2) * per]


def pick_rows(picks, k, mirror, up, down, wide):
    _, many, token_rows = picks.shape
    per = many // wide
    return pl.pallas_call(
        pick_kernel,
        out_shape=(
            jax.ShapeDtypeStruct((2, per, HALF), bf16),
            jax.ShapeDtypeStruct((wide - 1, 2, per, HALF), bf16),
        ),
        grid=(1,),
        in_specs=[
            pl.BlockSpec((1, many, token_rows), lambda g: (k, 0, 0)),
            pl.BlockSpec((1, many, token_rows), lambda g: (mirror, 0, 0)),
            pl.BlockSpec((token_rows, HALF), lambda g: (0, 0)),
            pl.BlockSpec((token_rows, HALF), lambda g: (0, 0)),
        ],
        out_specs=(
            pl.BlockSpec((2, per, HALF), lambda g: (0, 0, 0)),
            pl.BlockSpec((wide - 1, 2, per, HALF), lambda g: (0, 0, 0, 0)),
        ),
        compiler_params=params(32, 1),
        cost_estimate=cost(4 * many * token_rows * HALF, 5e6),
        name="pick_rows",
    )(picks, picks, up, down)


def weight_grad_kernel(rows, *refs):
    *grads, extra, out = refs
    rows_t = rows[...].T
    at = 0
    for side in grads:
        columns = side.shape[1]
        out[:, at : at + columns] = dot_nn(rows_t, side[...]).astype(bf16)
        at += columns
    out[:, at:] = extra[...].T.astype(bf16)


def weight_grads(rows, grads, extra):
    token_rows = rows.shape[0]
    tile = 384
    columns = sum(g.shape[1] for g in grads) + extra.shape[0]
    return pl.pallas_call(
        weight_grad_kernel,
        out_shape=jax.ShapeDtypeStruct((MODEL_WIDTH, columns), bf16),
        grid=(MODEL_WIDTH // tile,),
        in_specs=[pl.BlockSpec((token_rows, tile), lambda n: (0, n))]
        + [pl.BlockSpec(g.shape, lambda n: (0, 0)) for g in grads]
        + [pl.BlockSpec((extra.shape[0], tile), lambda n: (0, n))],
        out_specs=pl.BlockSpec((tile, columns), lambda n: (n, 0)),
        compiler_params=params(56, 1),
        cost_estimate=cost(2 * MODEL_WIDTH * token_rows * columns, 14e6),
        name="weight_grads",
    )(rows, *grads, extra)


def adamw_update(weight, moment_one, moment_two, gradient, step_rate, decay_rate):
    first_new = BETA_ONE * moment_one + (1.0 - BETA_ONE) * gradient
    second_new = BETA_TWO * moment_two + (1.0 - BETA_TWO) * gradient * gradient
    first_hat = first_new / (1.0 - BETA_ONE**STEP)
    second_hat = second_new / (1.0 - BETA_TWO**STEP)
    weight_new = weight - step_rate * (
        first_hat / (jnp.sqrt(second_hat) + ADAM_EPS) + decay_rate * weight
    )
    return (weight_new, first_new, second_new)


def body(
    tokens,
    cotangent,
    routes,
    gains,
    gains_first,
    gains_second,
    query_weight,
    query_first,
    query_second,
    key_matrix,
    key_moment_first,
    key_moment_second,
    value_matrix,
    value_moment_first,
    value_moment_second,
    output_weight,
    output_first,
    output_second,
    router_weight,
    router_first,
    router_second,
    expert_in,
    in_first,
    in_second,
    expert_out,
    out_first,
    out_second,
):
    token_rows, top_count = routes.shape
    shards = lax.axis_size("fsdp")
    place = lax.axis_index("fsdp")
    groups = lax.axis_size("expert")
    group = lax.axis_index("expert")
    depth = DEPTH
    wide = groups // depth
    level, column = group // wide, group % wide
    experts_local = expert_in.shape[0]
    experts_all = experts_local * groups
    near = wide * experts_local
    shard_rows = query_weight.shape[0]

    def z_shift(value, by):
        return lax.ppermute(
            value,
            "expert",
            [(a * wide + b, (a + by) % depth * wide + b) for a in range(depth) for b in range(wide)],
        )

    def x_shift(value, by):
        return lax.ppermute(
            value,
            "expert",
            [(a * wide + b, a * wide + (b + by) % wide) for a in range(depth) for b in range(wide)],
        )

    def back_shift(value, by):
        pairs = [(a, a + by) for a in range(shards) if 0 <= a + by < shards]
        return lax.ppermute(value, "fsdp", pairs)

    def z_spread(value):
        up, down = [value[:, :HALF]], [value[:, HALF:]]
        for _ in range(depth - 1):
            up.append(z_shift(up[-1], 1))
            down.append(z_shift(down[-1], -1))
        return up, down

    small = jnp.concatenate(
        [
            router_weight.astype(bf16),
            gains.T.astype(bf16),
            jnp.zeros((shard_rows, 128 - experts_all - 2), bf16),
        ],
        axis=1,
    )
    front_low = lax.all_gather(
        jnp.concatenate(
            [query_weight.astype(bf16), key_matrix.astype(bf16), value_matrix.astype(bf16), small], axis=1
        ),
        "fsdp",
        axis=0,
        tiled=True,
    )
    output_low = lax.all_gather(output_weight.astype(bf16), "fsdp", axis=0, tiled=True)
    gate_up_low = lax.all_gather(expert_in.astype(bf16), "fsdp", axis=0)
    down_low = lax.all_gather(expert_out.astype(bf16), "fsdp", axis=0)
    qkv_low = front_low[:, :QKV]
    router_low = front_low[:, QKV : QKV + experts_all]
    gain_pair = front_low[:, QKV + experts_all : QKV + experts_all + 2].astype(f32).T
    gain_one, gain_two = gain_pair[0], gain_pair[1]

    routes_t = routes.T
    routes_of = jnp.stack([routes_t] + [z_shift(routes_t, i) for i in range(1, depth)])

    def expert_ids(at_level):
        columns = (column + jnp.arange(wide, dtype=jnp.int32)) % wide
        first_ids = (at_level * wide + columns) * experts_local
        return (first_ids[:, None] + jnp.arange(experts_local, dtype=jnp.int32)[None, :]).reshape(near)

    named = (routes_of[:, None] == expert_ids(level)[None, :, None, None]).astype(f32)
    chosen_here = jnp.sum(named, axis=2)
    earlier = (
        jnp.arange(token_rows, dtype=jnp.int32)[:, None] < jnp.arange(token_rows, dtype=jnp.int32)[None, :]
    ).astype(bf16)
    slots = dot_nn(chosen_here.reshape(depth * near, token_rows).astype(bf16), earlier).reshape(
        depth, near, token_rows
    )
    code = jnp.where(chosen_here > 0, slots.astype(jnp.int32), -1)
    picks = code[:, :, None, :] == jnp.arange(CAP, dtype=jnp.int32)[None, None, :, None]
    picks_low = picks.astype(bf16).reshape(depth, near * CAP, token_rows)

    def pick_all(up, down):
        return [pick_rows(picks_low, k, (depth - k) % depth, up[k], down[k], wide) for k in range(depth)]

    def swap_all(picked):
        first = [[None] * depth for _ in range(wide)]
        second = [[None] * depth for _ in range(wide)]
        for k, (own, away) in enumerate(picked):
            for r in range(wide):
                pair = x_shift(away[r - 1], r) if r else own
                pair = pair.reshape(2, experts_local, CAP, HALF)
                first[r][k] = pair[0]
                second[r][(depth - k) % depth] = pair[1]
        shape = (experts_local, wide * depth * CAP, HALF)
        return (
            jnp.stack([first[r][i] for r in range(wide) for i in range(depth)], axis=1).reshape(shape),
            jnp.stack([second[r][i] for r in range(wide) for i in range(depth)], axis=1).reshape(shape),
        )

    def swap_back(rows):
        shaped = rows.reshape(experts_local, wide, depth, CAP, MODEL_WIDTH)
        steps = []
        for m in range(depth):
            i = (m + 1) % depth
            mirror = (depth - i) % depth
            pieces = []
            for r in range(wide):
                pair = jnp.stack([shaped[:, r, i, :, :HALF], shaped[:, r, mirror, :, HALF:]])
                if r:
                    pair = x_shift(pair, -r)
                pieces.append(pair.reshape(2, experts_local * CAP, HALF))
            steps.append(jnp.concatenate(pieces, axis=1))
        return steps

    def collect(steps):
        held = []
        for m, both in enumerate(steps):
            i = (m + 1) % depth
            mirror = (depth - i) % depth
            part_up = dot_tn(picks_low[i], both[0])
            part_down = dot_tn(picks_low[mirror], both[1])
            if m:
                part_up = part_up + z_shift(held[-1][0], 1).astype(f32)
                part_down = part_down + z_shift(held[-1][1], -1).astype(f32)
            held.append((part_up.astype(bf16), part_down.astype(bf16)))
        return jnp.concatenate([part_up, part_down], axis=1), held

    upstream = cotangent.astype(f32)
    upstream_picked = pick_all(*z_spread(cotangent))

    inputs = tokens.astype(f32)
    scale_one = lax.rsqrt(jnp.mean(inputs * inputs, axis=1, keepdims=True) + NORM_EPS)
    normed_one = inputs * scale_one
    first_hidden = (normed_one * gain_one).astype(bf16)
    inverse = ROPE_BASE ** (-(jnp.arange(HEAD_SIZE // 2, dtype=f32) * 2.0 / HEAD_SIZE))
    places = (place * token_rows + jnp.arange(token_rows, dtype=jnp.int32)).astype(f32)
    angles = places[:, None] * inverse[None, :]
    half_cos, half_sin = jnp.cos(angles), jnp.sin(angles)
    cosine = jnp.concatenate([half_cos, half_cos], axis=1)
    sine = jnp.concatenate([-half_sin, half_sin], axis=1)

    def turn_keys(rows, sign):
        parts = []
        for h in range(KEY_VALUE_HEADS):
            piece = rows[:, h * HEAD_SIZE : (h + 1) * HEAD_SIZE]
            swapped = jnp.concatenate([piece[:, HEAD_SIZE // 2 :], piece[:, : HEAD_SIZE // 2]], axis=1)
            parts.append(piece * cosine + swapped * (sign * sine))
        return jnp.concatenate(parts, axis=1)

    pre = dot_nn(first_hidden, qkv_low)
    keys_local = turn_keys(pre[:, MODEL_WIDTH : MODEL_WIDTH + KV], 1.0).astype(bf16)
    kv_local = jnp.concatenate([keys_local, pre[:, MODEL_WIDTH + KV :].astype(bf16)], axis=1)
    kv_blocks = jnp.stack([kv_local] + [back_shift(kv_local, s) for s in range(1, shards)])
    kv_blocks, upstream_picked = lax.optimization_barrier((kv_blocks, upstream_picked))
    upstream_rows = swap_all(upstream_picked)
    place_arg = place.astype(jnp.int32).reshape(1)
    attended, log_total, query_rows = attend(place_arg, pre, cosine, sine, kv_blocks)
    residual = inputs + dot_nn(attended, output_low)
    scale_two = lax.rsqrt(jnp.mean(residual * residual, axis=1, keepdims=True) + NORM_EPS)
    normed_two = residual * scale_two
    hidden_two = (normed_two * gain_two).astype(bf16)

    hidden_rows = swap_all(pick_all(*z_spread(hidden_two)))
    logits_t = lax.dot_general(
        router_low, hidden_two, (((0,), (1,)), ((), ())), preferred_element_type=f32
    )
    all_ids = jnp.arange(experts_all, dtype=jnp.int32)
    chosen_t = (routes_t[:, None, :] == all_ids[None, :, None]).astype(f32)
    gate_weights = jax.nn.softmax(jnp.sum(chosen_t * logits_t[None], axis=1), axis=0)
    gates_of = jnp.stack([gate_weights] + [z_shift(gate_weights, i) for i in range(1, depth)])
    gates_near = jnp.sum(named * gates_of[:, None], axis=2)
    row_gates = jnp.sum(jnp.where(picks, gates_near[:, :, None, :], 0.0), axis=3)
    row_gates = row_gates.reshape(depth, wide, experts_local, CAP)
    row_gates = jnp.stack(
        [row_gates[:, 0]] + [x_shift(row_gates[:, r], r) for r in range(1, wide)]
    )
    row_gates = row_gates.transpose(2, 0, 1, 3).reshape(experts_local, wide * depth * CAP, 1)

    inner = inner_rows(*upstream_rows, down_low)
    scaled_hidden, gate_side, up_side, gate_dots = gate_rows(*hidden_rows, gate_up_low, inner, row_gates)
    hidden_back, held = collect(swap_back(row_grads(gate_side, up_side, gate_up_low)))

    down_term = down_grads(scaled_hidden, *upstream_rows, shards)
    in_term = in_grads(*hidden_rows, gate_side, up_side, shards)
    results = result_rows(scaled_hidden, down_low)
    out_sum = lax.psum_scatter(down_term, "fsdp", scatter_dimension=0).astype(f32)
    in_sum = lax.psum_scatter(in_term, "fsdp", scatter_dimension=0).astype(f32)
    results, _ = lax.optimization_barrier((results, held[2]))
    result_steps = swap_back(results)

    gate_dots = gate_dots.reshape(experts_local, wide, depth, CAP)
    gate_dots = jnp.stack(
        [gate_dots[:, 0]] + [x_shift(gate_dots[:, r], -r) for r in range(1, wide)]
    )
    gate_dots, _ = lax.optimization_barrier((gate_dots, held[2]))
    gate_dots = gate_dots.transpose(2, 0, 1, 3).reshape(depth, near, CAP)
    token_dots = jnp.sum(jnp.where(picks, gate_dots[:, :, :, None], 0.0), axis=2)
    home_dots = [token_dots[0]] + [z_shift(token_dots[i], -i) for i in range(1, depth)]
    gate_grad = 0.0
    for i in range(depth):
        ids = expert_ids((level + i) % depth)
        same = (routes_t[:, None, :] == ids[None, :, None]).astype(f32)
        gate_grad = gate_grad + jnp.sum(same * home_dots[i][None], axis=1)
    picked_grad = gate_weights * (
        gate_grad - jnp.sum(gate_weights * gate_grad, axis=0, keepdims=True)
    )
    logit_grad_t = jnp.sum(chosen_t * picked_grad[:, None, :], axis=0).astype(bf16)
    router_term = dot_nn(logit_grad_t, hidden_two)
    hidden_two_grad = hidden_back + lax.dot_general(
        logit_grad_t, router_low, (((0,), (1,)), ((), ())), preferred_element_type=f32
    )

    gain_two_term = jnp.sum(hidden_two_grad * normed_two, axis=0)
    scaled_two = hidden_two_grad * gain_two
    residual_grad = upstream + scale_two * (
        scaled_two - normed_two * jnp.mean(scaled_two * normed_two, axis=1, keepdims=True)
    )
    branch_grad = residual_grad.astype(bf16)
    attended_grad = dot_nt(branch_grad, output_low).astype(bf16)
    attended_grad, in_term, down_term = lax.optimization_barrier((attended_grad, in_term, down_term))
    pre_grad, key_back, value_back = attend_back(
        place_arg, query_rows, kv_blocks, attended, attended_grad, log_total, cosine, sine
    )
    kv_back = jnp.concatenate([key_back, value_back], axis=2)
    kv_grad = kv_back[0].astype(f32)
    for s in range(1, shards):
        kv_grad = kv_grad + back_shift(kv_back[s], -s).astype(f32)
    key_pre_grad = turn_keys(kv_grad[:, :KV], -1.0)
    kv_pre_grad = jnp.concatenate([key_pre_grad, kv_grad[:, KV:]], axis=1).astype(bf16)

    moe_out, _ = collect(result_steps)
    layer_out = (residual + moe_out).astype(bf16)

    hidden_one_grad = dot_nt(pre_grad, qkv_low[:, :MODEL_WIDTH]) + dot_nt(kv_pre_grad, qkv_low[:, MODEL_WIDTH:])
    gain_one_term = jnp.sum(hidden_one_grad * normed_one, axis=0)
    scaled_one = hidden_one_grad * gain_one
    input_grad = (
        residual_grad
        + scale_one
        * (scaled_one - normed_one * jnp.mean(scaled_one * normed_one, axis=1, keepdims=True))
    ).astype(bf16)

    def extra_rows(*terms):
        used = sum(t.shape[0] for t in terms)
        return jnp.concatenate(list(terms) + [jnp.zeros((128 - used, MODEL_WIDTH), f32)], axis=0)

    def spread_sum(parts, index, shift):
        count = parts.shape[0]
        total = lax.dynamic_index_in_dim(parts, index, 0, keepdims=False).astype(f32)
        for s in range(1, count):
            sent = lax.dynamic_index_in_dim(parts, (index + s) % count, 0, keepdims=False)
            total = total + shift(sent, s).astype(f32)
        return total

    def join(part, index, count, shift):
        whole = jnp.zeros((count,) + part.shape, part.dtype)
        for s in range(count):
            piece = shift(part, s) if s else part
            whole = lax.dynamic_update_index_in_dim(whole, piece, (index - s) % count, 0)
        return whole

    def core_shift(value, by):
        return lax.ppermute(value, "fsdp", [(a, a // 2 * 2 + (a + by) % 2) for a in range(shards)])

    def y_shift(value, by):
        return lax.ppermute(value, "fsdp", [(a, (a + 2 * by) % shards) for a in range(shards)])

    def total_sum(terms):
        columns = terms.shape[1]
        parts = terms.reshape(shards // 2, 2, shard_rows, columns).transpose(1, 0, 2, 3)
        part = spread_sum(parts, place % 2, core_shift).astype(bf16)
        part = spread_sum(part, place // 2, y_shift).astype(bf16)
        part = spread_sum(part.reshape(wide, shard_rows // wide, columns), column, x_shift).astype(bf16)
        part = spread_sum(part.reshape(depth, shard_rows // wide // depth, columns), level, z_shift).astype(bf16)
        part = join(part, level, depth, z_shift).reshape(shard_rows // wide, columns)
        return join(part, column, wide, x_shift).reshape(shard_rows, columns).astype(f32)

    back_sum = total_sum(weight_grads(attended, [branch_grad], extra_rows(router_term, gain_two_term[None])))
    front_sum = total_sum(weight_grads(first_hidden, [pre_grad, kv_pre_grad], extra_rows(gain_one_term[None])))
    output_sum = back_sum[:, :MODEL_WIDTH]
    router_sum = back_sum[:, MODEL_WIDTH : MODEL_WIDTH + experts_all]
    query_sum = front_sum[:, :MODEL_WIDTH]
    key_sum = front_sum[:, MODEL_WIDTH : MODEL_WIDTH + KV]
    value_sum = front_sum[:, MODEL_WIDTH + KV : QKV]
    gain_sum = jnp.stack([front_sum[:, QKV], back_sum[:, MODEL_WIDTH + experts_all]])

    rate = 0.5 / math.sqrt(MODEL_WIDTH // 2)
    return (
        layer_out,
        input_grad,
        *adamw_update(gains, gains_first, gains_second, gain_sum, GAIN_RATE, 0.0),
        *adamw_update(query_weight, query_first, query_second, query_sum, rate, DECAY),
        *adamw_update(key_matrix, key_moment_first, key_moment_second, key_sum, rate, DECAY),
        *adamw_update(
            value_matrix,
            value_moment_first,
            value_moment_second,
            value_sum,
            0.5 / math.sqrt(MODEL_WIDTH),
            DECAY,
        ),
        *adamw_update(
            output_weight, output_first, output_second, output_sum, 0.5 / math.sqrt(MODEL_WIDTH // 32), DECAY
        ),
        *adamw_update(
            router_weight, router_first, router_second, router_sum, 0.5 / math.sqrt(4 * MODEL_WIDTH), DECAY
        ),
        *adamw_update(expert_in, in_first, in_second, in_sum, 0.5 / math.sqrt(MODEL_WIDTH), DECAY),
        *adamw_update(expert_out, out_first, out_second, out_sum, 0.5 / math.sqrt(FF // 8), DECAY),
    )


def solution(mesh):
    rows = P(("expert", "fsdp"), None)
    gains = P(None, "fsdp")
    matrix = P("fsdp", None)
    wide = P("expert", "fsdp", None)
    tall = P("expert", None, "fsdp")
    return jax.shard_map(
        body,
        mesh=mesh,
        in_specs=(rows,) * 3 + (gains,) * 3 + (matrix,) * 15 + (wide,) * 3 + (tall,) * 3,
        out_specs=(rows,) * 2 + (gains,) * 3 + (matrix,) * 15 + (wide,) * 3 + (tall,) * 3,
        check_vma=False,
    )
```

time: 1850 us -> 1000 us (0.54)
  waiting for transfers between devices: 1140 us -> 422 us
  Pallas kernels: 0 us -> 183 us
  matrix products: 204 us -> 56 us
  local copies, waits for them, and re-layouts: 193 us -> 82 us
  blocking collectives: 104 us -> 0 us
  starting transfers between devices: 28.1 us -> 119 us
  other arithmetic: 151 us -> 113 us
    all_to_all x4 -> x0, waiting for transfers between devices: 521 us -> none  [the longest x1 156 us: body(): lax.all_to_all(row_grad, 'expert', split_axis=0, concat_axis=0, tiled=True)]
    ppermute x0 -> x77, waiting for transfers between devices: none -> 422 us  [the longest x45 224 us: z_shift(): lax.ppermute(value, 'expert', [(a * wide + b, (a + by) % depth * wide + b...]
    reduce_scatter x7 -> x2, waiting for transfers between devices: 419 us -> 0.01 us  [the longest x1 0.01 us: body(): in_sum = lax.psum_scatter(in_term, 'fsdp', scatter_dimension=0).astype(f32)]
    pallas_call x0 -> x18, Pallas kernels: none -> 183 us  [the longest x1 27.8 us: row_grads(): pl.pallas_call(row_grad_kernel, out_shape=jax.ShapeDtypeStruct((experts,...]
    dot_general x30 -> x25, matrix products: 204 us -> 56 us  [the longest x16 26.5 us: dot_tn(): lax.dot_general(left, right, (((0,), (0,)), ((), ())), preferred_element_...]
    ppermute x0 -> x77, starting transfers between devices: none -> 118 us  [the longest x45 74.2 us: z_shift(): lax.ppermute(value, 'expert', [(a * wide + b, (a + by) % depth * wide + b...]
    psum x1 -> x0, waiting for transfers between devices: 102 us -> none  [body(): lax.psum(query_part.astype(jnp.bfloat16), 'expert').astype(jnp.float32)]
    all_gather x4 -> x0, blocking collectives: 69.3 us -> none  [the longest x1 46.8 us: body(): lax.all_gather(router_weight.astype(jnp.bfloat16), 'fsdp', axis=0, tiled=...]
  transfers between devices with their start and end apart: 21 -> 83, of which waited for: 15 -> 37; matrix products, arithmetic and copies ran while one was open for 18% -> 21% of each run, Pallas kernels for 0% -> 15%
where the time goes in v1:
time: 1000 us; the launch traced here: 992 us
  waiting for transfers between devices  422 us (42%)
  Pallas kernels  183 us (18%)
  starting transfers between devices  119 us (12%)
  other arithmetic  113 us (11%)
  local copies, waits for them, and re-layouts  82 us (8%)
  matrix products  56 us (6%)
  between operations  16.5 us (2%)
    ppermute x45, waiting for transfers between devices, z_shift(): lax.ppermute(value, 'expert', [(a * wide + b, (a + by) % depth * wide + b...  224 us
    ppermute x22, waiting for transfers between devices, x_shift(): lax.ppermute(value, 'expert', [(a * wide + b, a * wide + (b + by) % wide)...  154 us
    ppermute x45, starting transfers between devices, z_shift(): lax.ppermute(value, 'expert', [(a * wide + b, (a + by) % depth * wide + b...  74.2 us
    sub x7, other arithmetic, adamw_update(): weight - step_rate * (first_hat / (jnp.sqrt(second_hat) + ADAM_EPS) + dec...  46.4 us
    unnamed x240, local copies, waits for them, and re-layouts  36.9 us
    pallas_call x1, Pallas kernels, row_grads(): pl.pallas_call(row_grad_kernel, out_shape=jax.ShapeDtypeStruct((experts,...  27.8 us
    ppermute x22, starting transfers between devices, x_shift(): lax.ppermute(value, 'expert', [(a * wide + b, a * wide + (b + by) % wide)...  26.7 us
    dot_general x16, matrix products, dot_tn(): lax.dot_general(left, right, (((0,), (0,)), ((), ())), preferred_element_...  26.5 us
  transfers between devices with their start and end apart: 83, of which 37 were waited for; matrix products, arithmetic and copies ran while one was open for 21% of the time, Pallas kernels for 15%

profile of v1, /device:TPU:8, one launch (start us, length us, event | category | flops | bytes accessed | tf_op | source)
XLA Modules:
  0.0 991.8 jit_solution(6457803782313021577)
XLA Ops:
  22.9 7.5 convert_element_type.319
  41.5 25.3 %collective-permute-done.6.up = bf16[512,768]{1,0:T(8,128)(2,1)S(1)} collective-permute-done((bf16[512,768]{1,0:T(8,128)(2,1)S(1)}, bf16[512,768]{1,0:T(8,128)(2,1)S(1)}, u32[]{:S(2)}, u32[]{:S(2)}) %collective-permute-start.6) | collective-permute-done | bytes 786464 | tf_op jit(solution)/shard_map/ppermute | solution.py:531
  72.8 28.6 %collective-permute-done.8.up = bf16[512,768]{1,0:T(8,128)(2,1)} collective-permute-done((bf16[512,768]{1,0:T(8,128)(2,1)S(1)}, bf16[512,768]{1,0:T(8,128)(2,1)}, u32[]{:S(2)}, u32[]{:S(2)}) %collective-permute-start.8) | collective-permute-done | bytes 786464 | tf_op jit(solution)/shard_map/ppermute | solution.py:531
  110.5 6.1 fusion.3.pre
  145.1 22.5 %collective-permute-done.1 = bf16[512,512]{1,0:T(8,128)(2,1)S(1)} collective-permute-done((bf16[512,512]{1,0:T(8,128)(2,1)S(1)}, bf16[512,512]{1,0:T(8,128)(2,1)S(1)}, u32[]{:S(2)}, u32[]{:S(2)}) %collective-permute-start.1) | collective-permute-done | bytes 524320 | tf_op jit(solution)/shard_map/ppermute | solution.py:546
  169.1 13.8 %attend.1 = (bf16[512,1536]{1,0:T(8,128)(2,1)}, f32[12,1,512]{2,1,0:T(1,128)}, bf16[512,1536]{1,0:T(8,128)(2,1)}) custom-call(s32[1]{0:T(128)} %bitcast.place, f32[512,2048]{1,0:T(8,128)} %copy-done.57, f32[512,128]{1,0:T(8,128)} %get-tuple-element.373.cosine, f32[512,128]{1,0:T(8,128)} %copy-done.36, bf16[4,512,512]{2,1,0:T(8,128)(2,1)} %pad_maximum_fusion.keys.values, ...), custom_call_target="tpu_custom_call" | custom-call | flops 16000000000 | bytes 8000000 | tf_op jit(solution)/shard_map/attend/pallas_call | solution.py:101
  182.9 6.0 multiply_reduce_fusion.2
  216.0 33.2 %collective-permute-done.29 = f32[4,4,80]{2,0,1:T(4,128)S(1)} collective-permute-done((f32[4,4,80]{2,0,1:T(4,128)S(1)}, f32[4,4,80]{2,0,1:T(4,128)S(1)}, u32[]{:S(2)}, u32[]{:S(2)}) %collective-permute-start.29) | collective-permute-done | bytes 5152 | tf_op jit(solution)/shard_map/ppermute | solution.py:538
  265.1 26.9 %collective-permute-done.24 = bf16[2,320,768]{2,1,0:T(8,128)(2,1)S(1)} collective-permute-done((bf16[2,320,768]{2,1,0:T(8,128)(2,1)}, bf16[2,320,768]{2,1,0:T(8,128)(2,1)S(1)}, u32[]{:S(2)}, u32[]{:S(2)}) %collective-permute-start.24) | collective-permute-done | bytes 983072 | tf_op jit(solution)/shard_map/ppermute | solution.py:538
  292.1 5.6 collective-permute-start.15
  298.6 14.6 %collective-permute-done.25 = bf16[2,320,768]{2,1,0:T(8,128)(2,1)S(1)} collective-permute-done((bf16[2,320,768]{2,1,0:T(8,128)(2,1)}, bf16[2,320,768]{2,1,0:T(8,128)(2,1)S(1)}, u32[]{:S(2)}, u32[]{:S(2)}) %collective-permute-start.25) | collective-permute-done | bytes 983072 | tf_op jit(solution)/shard_map/ppermute | solution.py:538
  328.7 5.5 collective-permute-done.19
  334.3 23.2 %collective-permute-done.17.down = bf16[512,768]{1,0:T(8,128)(2,1)S(1)} collective-permute-done((bf16[512,768]{1,0:T(8,128)(2,1)S(1)}, bf16[512,768]{1,0:T(8,128)(2,1)S(1)}, u32[]{:S(2)}, u32[]{:S(2)}) %collective-permute-start.17) | collective-permute-done | bytes 786464 | tf_op jit(solution)/shard_map/ppermute | solution.py:531
  366.9 15.4 %collective-permute-done.21 = bf16[2,320,768]{2,1,0:T(8,128)(2,1)S(1)} collective-permute-done((bf16[2,320,768]{2,1,0:T(8,128)(2,1)S(1)}, bf16[2,320,768]{2,1,0:T(8,128)(2,1)S(1)}, u32[]{:S(2)}, u32[]{:S(2)}) %collective-permute-start.21) | collective-permute-done | bytes 983072 | tf_op jit(solution)/shard_map/ppermute | solution.py:538
  385.6 17.0 %inner_rows.1.inner = f32[4,640,768]{2,1,0:T(8,128)} custom-call(bf16[4,640,768]{2,1,0:T(8,128)(2,1)} %bitcast.74.first, bf16[4,640,768]{2,1,0:T(8,128)(2,1)} %bitcast.91.second, bf16[4,4,768,384]{3,2,1,0:T(8,128)(2,1)} %bitcast.466), custom_call_target="tpu_custom_call" | custom-call | flops 6039797760 | bytes 30000000 | tf_op jit(solution)/shard_map/inner_rows/pallas_call | solution.py:225
  402.5 25.8 %gate_rows.1 = (bf16[4,640,768]{2,1,0:T(8,128)(2,1)}, bf16[4,640,768]{2,1,0:T(8,128)(2,1)}, bf16[4,640,768]{2,1,0:T(8,128)(2,1)}, f32[4,640,1]{2,1,0:T(8,128)}) custom-call(bf16[4,640,768]{2,1,0:T(8,128)(2,1)} %bitcast.35.first, bf16[4,640,768]{2,1,0:T(8,128)(2,1)} %bitcast.52.second, bf16[4,4,384,1536]{3,2,1,0:T(8,128)(2,1)} %bitcast.463, ...), custom_call_target="tpu_custom_call" | custom-call | flops 12079595520 | bytes 50000000 | tf_op jit(solution)/shard_map/gate_rows/pallas_call | solution.py:280
  428.4 13.3 %down_grads.1 = bf16[4,4,768,384]{3,2,1,0:T(8,128)(2,1)} custom-call(bf16[4,640,768]{2,1,0:T(8,128)(2,1)} %get-tuple-element.90.scaled, bf16[4,640,768]{2,1,0:T(8,128)(2,1)} %bitcast.74.first, bf16[4,640,768]{2,1,0:T(8,128)(2,1)} %bitcast.91.second), custom_call_target="tpu_custom_call" | custom-call | flops 6039797760 | bytes 22000000 | tf_op jit(solution)/shard_map/down_grads/pallas_call | solution.py:366
  448.1 27.8 %row_grads.1 = bf16[4,640,1536]{2,1,0:T(8,128)(2,1)} custom-call(bf16[4,640,768]{2,1,0:T(8,128)(2,1)} %get-tuple-element.91.gate_side, bf16[4,640,768]{2,1,0:T(8,128)(2,1)} %get-tuple-element.92.up_side, bf16[4,4,384,1536]{3,2,1,0:T(8,128)(2,1)} %bitcast.465), custom_call_target="tpu_custom_call" | custom-call | flops 12079595520 | bytes 40000000 | tf_op jit(solution)/shard_map/row_grads/pallas_call | solution.py:316
  475.9 5.0 fusion.98
  485.0 23.0 %in_grads.1 = bf16[4,4,384,1536]{3,2,1,0:T(8,128)(2,1)} custom-call(bf16[4,640,768]{2,1,0:T(8,128)(2,1)} %bitcast.35.first, bf16[4,640,768]{2,1,0:T(8,128)(2,1)} %bitcast.52.second, bf16[4,640,768]{2,1,0:T(8,128)(2,1)} %get-tuple-element.91.gate_side, bf16[4,640,768]{2,1,0:T(8,128)(2,1)} %get-tuple-element.92.up_side), custom_call_target="tpu_custom_call" | custom-call | flops 12079595520 | bytes 35000000 | tf_op jit(solution)/shard_map/in_grads/pallas_call | solution.py:401
  522.5 5.3 collective-permute-done.31
  536.7 15.8 %collective-permute-done.35 = bf16[512,768]{1,0:T(8,128)(2,1)} collective-permute-done((bf16[512,768]{1,0:T(8,128)(2,1)}, bf16[512,768]{1,0:T(8,128)(2,1)}, u32[]{:S(2)}, u32[]{:S(2)}) %collective-permute-start.35) | collective-permute-done | bytes 786464 | tf_op jit(solution)/shard_map/ppermute | solution.py:531
  557.7 12.9 %result_rows.1 = bf16[4,640,1536]{2,1,0:T(8,128)(2,1)} custom-call(bf16[4,640,768]{2,1,0:T(8,128)(2,1)} %get-tuple-element.90.scaled, bf16[4,4,768,384]{3,2,1,0:T(8,128)(2,1)} %bitcast.467), custom_call_target="tpu_custom_call" | custom-call | flops 6039797760 | bytes 22000000 | tf_op jit(solution)/shard_map/result_rows/pallas_call | solution.py:338
  572.3 14.6 %collective-permute-done.36 = bf16[512,768]{1,0:T(8,128)(2,1)S(1)} collective-permute-done((bf16[512,768]{1,0:T(8,128)(2,1)S(1)}, bf16[512,768]{1,0:T(8,128)(2,1)S(1)}, u32[]{:S(2)}, u32[]{:S(2)}) %collective-permute-start.36) | collective-permute-done | bytes 786464 | tf_op jit(solution)/shard_map/ppermute | solution.py:531
  603.3 22.2 %collective-permute-done.51 = f32[8,512]{1,0:T(8,128)S(1)} collective-permute-done((f32[8,512]{1,0:T(8,128)S(1)}, f32[8,512]{1,0:T(8,128)S(1)}, u32[]{:S(2)}, u32[]{:S(2)}) %collective-permute-start.51) | collective-permute-done | bytes 16416 | tf_op jit(solution)/shard_map/ppermute | solution.py:531
  640.9 17.6 %attend_back.1 = (bf16[512,1536]{1,0:T(8,128)(2,1)}, bf16[4,512,256]{2,1,0:T(8,128)(2,1)}, bf16[4,512,256]{2,1,0:T(8,128)(2,1)}) custom-call(s32[1]{0:T(128)} %bitcast.place, bf16[512,1536]{1,0:T(8,128)(2,1)} %get-tuple-element.96.query, bf16[4,512,512]{2,1,0:T(8,128)(2,1)} %pad_maximum_fusion.keys.values, bf16[4,512,512]{2,1,0:T(8,128)(2,1)} %pad_maximum_fusion.keys.values, ...), custom_call_target="tpu_custom_call" | custom-call | flops 40000000000 | bytes 12000000 | tf_op jit(solution)/shard_map/attend_back/pallas_call | solution.py:177
  664.6 6.7 weight_grads.3
  674.8 4.6 fusion.13
  685.2 4.7 collective-permute-done.38
  701.4 4.5 fusion.22
  707.8 9.2 collective-permute-done.44
  720.3 7.7 weight_grads.2
  728.0 4.1 dynamic-slice_bitcast_fusion
  738.0 14.1 %collective-permute-done.45 = bf16[512,768]{1,0:T(8,128)(2,1)} collective-permute-done((bf16[512,768]{1,0:T(8,128)(2,1)}, bf16[512,768]{1,0:T(8,128)(2,1)}, u32[]{:S(2)}, u32[]{:S(2)}) %collective-permute-start.45) | collective-permute-done | bytes 786464 | tf_op jit(solution)/shard_map/ppermute | solution.py:531
  762.5 7.1 collective-permute-done.42
  774.5 11.4 %collective-permute-done.46 = bf16[512,768]{1,0:T(8,128)(2,1)} collective-permute-done((bf16[512,768]{1,0:T(8,128)(2,1)}, bf16[512,768]{1,0:T(8,128)(2,1)}, u32[]{:S(2)}, u32[]{:S(2)}) %collective-permute-start.46) | collective-permute-done | bytes 786464 | tf_op jit(solution)/shard_map/ppermute | solution.py:531
  788.0 15.2 %collective-permute-done.43 = bf16[512,768]{1,0:T(8,128)(2,1)} collective-permute-done((bf16[512,768]{1,0:T(8,128)(2,1)}, bf16[512,768]{1,0:T(8,128)(2,1)}, u32[]{:S(2)}, u32[]{:S(2)}) %collective-permute-start.43) | collective-permute-done | bytes 786464 | tf_op jit(solution)/shard_map/ppermute | solution.py:531
  812.4 10.8 %collective-permute-done.69 = bf16[192,1664]{1,0:T(8,128)(2,1)S(1)} collective-permute-done((bf16[192,1664]{1,0:T(8,128)(2,1)S(1)}, bf16[192,1664]{1,0:T(8,128)(2,1)S(1)}, u32[]{:S(2)}, u32[]{:S(2)}) %collective-permute-start.69) | collective-permute-done | bytes 639008 | tf_op jit(solution)/shard_map/ppermute | solution.py:538
  830.9 5.7 collective-permute-done.71
  847.1 18.8 %collective-permute-done.58 = bf16[384,2176]{1,0:T(8,128)(2,1)S(1)} collective-permute-done((bf16[384,2176]{1,0:T(8,128)(2,1)S(1)}, bf16[384,2176]{1,0:T(8,128)(2,1)S(1)}, u32[]{:S(2)}, u32[]{:S(2)}) %collective-permute-start.58) | collective-permute-done | bytes 1671200 | tf_op jit(solution)/shard_map/ppermute | solution.py:783
  868.8 19.2 %collective-permute-done.59 = bf16[192,2176]{1,0:T(8,128)(2,1)S(1)} collective-permute-done((bf16[192,2176]{1,0:T(8,128)(2,1)S(1)}, bf16[192,2176]{1,0:T(8,128)(2,1)S(1)}, u32[]{:S(2)}, u32[]{:S(2)}) %collective-permute-start.59) | collective-permute-done | bytes 835616 | tf_op jit(solution)/shard_map/ppermute | solution.py:538
  892.5 5.7 collective-permute-done.76
  906.8 9.9 collective-permute-done.63
  923.5 4.2 multiply_subtract_fusion.2
  929.1 12.1 %collective-permute-done.66 = bf16[192,2176]{1,0:T(8,128)(2,1)S(1)} collective-permute-done((bf16[192,2176]{1,0:T(8,128)(2,1)S(1)}, bf16[192,2176]{1,0:T(8,128)(2,1)S(1)}, u32[]{:S(2)}, u32[]{:S(2)}) %collective-permute-start.66) | collective-permute-done | bytes 835616 | tf_op jit(solution)/shard_map/ppermute | solution.py:538
  945.4 4.2 multiply_subtract_fusion.3
  949.5 11.3 %multiply_subtract_fusion.1 = (f32[4,768,384]{2,1,0:T(8,128)}, f32[4,768,384]{2,1,0:T(8,128)}, f32[4,768,384]{2,1,0:T(8,128)}) fusion(f32[4,768,384]{2,1,0:T(8,128)} %param.51, bf16[1,4,768,384]{3,2,1,0:T(8,128)(2,1)} %reduce-scatter.5.cloned.1.call-done, f32[4,768,384]{2,1,0:T(8,128)} %param.52, f32[4,768,384]{2,1,0:T(8,128)} %param.53), kind=kLoop, calls=%fused_computation.31 | loop fusion | flops 18874368 | bytes 30670848 | tf_op jit(solution)/shard_map/sub | solution.py:482
  960.9 23.7 %multiply_subtract_fusion = (f32[4,384,1536]{2,1,0:T(8,128)}, f32[4,384,1536]{2,1,0:T(8,128)}, f32[4,384,1536]{2,1,0:T(8,128)}) fusion(f32[4,384,1536]{2,1,0:T(8,128)} %param.48, bf16[1,4,384,1536]{3,2,1,0:T(8,128)(2,1)} %reduce-scatter.3.cloned.1.call-done, f32[4,384,1536]{2,1,0:T(8,128)} %param.49, f32[4,384,1536]{2,1,0:T(8,128)} %param.50), kind=kLoop, calls=%fused_computation.5 | loop fusion | flops 37748736 | bytes 61341696 | tf_op jit(solution)/shard_map/sub | solution.py:482
  (579 shorter events, 326.0 us)
Async XLA Ops:
  7.2 100.8 %all-gather.7.cloned.1.call-start = ((), (), s32[]{:S(2)}) async-start(), calls=%async_computation.2 | async-start | bytes 8355840 | tf_op jit(solution)/shard_map/all_gather | solution.py:563
  17.5 165.4 %all-gather.9.cloned.1.call-start = ((), (), s32[]{:S(2)}) async-start(), calls=%async_computation.3 | async-start | bytes 5898240 | tf_op jit(solution)/shard_map/all_gather | solution.py:571
  18.8 366.8 %all-gather.13.cloned.1.call-start = ((), (), s32[]{:S(2)}) async-start(), calls=%async_computation.7 | async-start | bytes 11796480 | tf_op jit(solution)/shard_map/all_gather | solution.py:573
  22.8 379.7 %all-gather.11.cloned.1.call-start = ((), (), s32[]{:S(2)}) async-start(), calls=%async_computation.6 | async-start | bytes 23592960 | tf_op jit(solution)/shard_map/all_gather | solution.py:572
  30.4 919.1 %reduce-scatter.5.cloned.1.call-start = ((), (), s32[]{:S(2)}) async-start(), calls=%async_computation.5 | async-start | bytes 11796480 | tf_op jit(solution)/shard_map/reduce_scatter | solution.py:703
  32.0 34.7 %collective-permute-start.6 = (bf16[512,768]{1,0:T(8,128)(2,1)S(1)}, bf16[512,768]{1,0:T(8,128)(2,1)S(1)}, u32[]{:S(2)}, u32[]{:S(2)}) collective-permute-start(bf16[512,768]{1,0:T(8,128)(2,1)S(1)} %get-tuple-element.323.up), channel_id=1, source_target_pairs={{0,8},{4,12},{8,16},{12,20},{16,24},{20,28},{24,0},{28,4},{1,9},{5... | collective-permute-start | bytes 2359304 | tf_op jit(solution)/shard_map/ppermute | solution.py:531
  33.6 36.2 %collective-permute-start.7 = (bf16[512,768]{1,0:T(8,128)(2,1)S(1)}, bf16[512,768]{1,0:T(8,128)(2,1)S(1)}, u32[]{:S(2)}, u32[]{:S(2)}) collective-permute-start(bf16[512,768]{1,0:T(8,128)(2,1)S(1)} %get-tuple-element.322.down), channel_id=1, source_target_pairs={{0,24},{4,28},{8,0},{12,4},{16,8},{20,12},{24,16},{28,20},{1,25},{... | collective-permute-start | bytes 2359304 | tf_op jit(solution)/shard_map/ppermute | solution.py:531
  34.1 38.0 %collective-permute-start.5 = (s32[4,512]{1,0:T(4,128)S(1)}, s32[4,512]{1,0:T(4,128)S(1)}, u32[]{:S(2)}, u32[]{:S(2)}) collective-permute-start(s32[4,512]{1,0:T(4,128)S(1)} %bitcast.559), channel_id=1, source_target_pairs={{0,24},{4,28},{8,0},{12,4},{16,8},{20,12},{24,16},{28,20},{1,25},{... | collective-permute-start | bytes 24584 | tf_op jit(solution)/shard_map/ppermute | solution.py:531
  36.2 35.9 %collective-permute-start.4 = (s32[4,512]{1,0:T(4,128)S(1)}, s32[4,512]{1,0:T(4,128)S(1)}, u32[]{:S(2)}, u32[]{:S(2)}) collective-permute-start(s32[4,512]{1,0:T(4,128)S(1)} %bitcast.560), channel_id=1, source_target_pairs={{0,16},{4,20},{8,24},{12,28},{16,0},{20,4},{24,8},{28,12},{1,17},{... | collective-permute-start | bytes 24584 | tf_op jit(solution)/shard_map/ppermute | solution.py:531
  37.1 35.0 %collective-permute-start.3 = (s32[4,512]{1,0:T(4,128)S(1)}, s32[4,512]{1,0:T(4,128)S(1)}, u32[]{:S(2)}, u32[]{:S(2)}) collective-permute-start(s32[4,512]{1,0:T(4,128)S(1)} %bitcast.561), channel_id=1, source_target_pairs={{0,8},{4,12},{8,16},{12,20},{16,24},{20,28},{24,0},{28,4},{1,9},{5... | collective-permute-start | bytes 24584 | tf_op jit(solution)/shard_map/ppermute | solution.py:531
  66.8 34.7 %collective-permute-start.8 = (bf16[512,768]{1,0:T(8,128)(2,1)S(1)}, bf16[512,768]{1,0:T(8,128)(2,1)}, u32[]{:S(2)}, u32[]{:S(2)}) collective-permute-start(bf16[512,768]{1,0:T(8,128)(2,1)S(1)} %collective-permute-done.6.up), channel_id=1, source_target_pairs={{0,8},{4,12},{8,16},{12,20},{16,24},{20,28},{24,0},{28,4},{1,9},{5... | collective-permute-start | bytes 2359304 | tf_op jit(solution)/shard_map/ppermute | solution.py:531
  69.8 36.7 %collective-permute-start.9 = (bf16[512,768]{1,0:T(8,128)(2,1)S(1)}, bf16[512,768]{1,0:T(8,128)(2,1)}, u32[]{:S(2)}, u32[]{:S(2)}) collective-permute-start(bf16[512,768]{1,0:T(8,128)(2,1)S(1)} %collective-permute-done.7.down), channel_id=1, source_target_pairs={{0,24},{4,28},{8,0},{12,4},{16,8},{20,12},{24,16},{28,20},{1,25},{... | collective-permute-start | bytes 2359304 | tf_op jit(solution)/shard_map/ppermute | solution.py:531
  101.4 34.5 %collective-permute-start.10 = (bf16[512,768]{1,0:T(8,128)(2,1)}, bf16[512,768]{1,0:T(8,128)(2,1)}, u32[]{:S(2)}, u32[]{:S(2)}) collective-permute-start(bf16[512,768]{1,0:T(8,128)(2,1)} %collective-permute-done.8.up), channel_id=1, source_target_pairs={{0,8},{4,12},{8,16},{12,20},{16,24},{20,28},{24,0},{28,4},{1,9},{5... | collective-permute-start | bytes 2359304 | tf_op jit(solution)/shard_map/ppermute | solution.py:531
  121.8 45.7 %collective-permute-start.1 = (bf16[512,512]{1,0:T(8,128)(2,1)S(1)}, bf16[512,512]{1,0:T(8,128)(2,1)S(1)}, u32[]{:S(2)}, u32[]{:S(2)}) collective-permute-start(bf16[512,512]{1,0:T(8,128)(2,1)S(1)} %get-tuple-element.371), channel_id=1, source_target_pairs={{0,2},{1,3},{4,6},{5,7},{8,10},{9,11},{12,14},{13,15},{16,18},{17,... | collective-permute-start | bytes 1572872 | tf_op jit(solution)/shard_map/ppermute | solution.py:546
  123.2 44.3 %collective-permute-start = (bf16[512,512]{1,0:T(8,128)(2,1)S(1)}, bf16[512,512]{1,0:T(8,128)(2,1)S(1)}, u32[]{:S(2)}, u32[]{:S(2)}) collective-permute-start(bf16[512,512]{1,0:T(8,128)(2,1)S(1)} %get-tuple-element.371), channel_id=1, source_target_pairs={{0,1},{1,2},{2,3},{4,5},{5,6},{6,7},{8,9},{9,10},{10,11},{12,13},{... | collective-permute-start | bytes 1572872 | tf_op jit(solution)/shard_map/ppermute | solution.py:546
  197.0 55.4 %collective-permute-start.12 = (bf16[512,768]{1,0:T(8,128)(2,1)}, bf16[512,768]{1,0:T(8,128)(2,1)}, u32[]{:S(2)}, u32[]{:S(2)}) collective-permute-start(bf16[512,768]{1,0:T(8,128)(2,1)} %get-tuple-element.321.up), channel_id=1, source_target_pairs={{0,8},{4,12},{8,16},{12,20},{16,24},{20,28},{24,0},{28,4},{1,9},{5... | collective-permute-start | bytes 2359304 | tf_op jit(solution)/shard_map/ppermute | solution.py:531
  198.6 54.3 %collective-permute-start.13 = (bf16[512,768]{1,0:T(8,128)(2,1)S(1)}, bf16[512,768]{1,0:T(8,128)(2,1)}, u32[]{:S(2)}, u32[]{:S(2)}) collective-permute-start(bf16[512,768]{1,0:T(8,128)(2,1)S(1)} %get-tuple-element.320.down), channel_id=1, source_target_pairs={{0,24},{4,28},{8,0},{12,4},{16,8},{20,12},{24,16},{28,20},{1,25},{... | collective-permute-start | bytes 2359304 | tf_op jit(solution)/shard_map/ppermute | solution.py:531
  210.7 47.2 %collective-permute-start.22 = (bf16[2,320,768]{2,1,0:T(8,128)(2,1)}, bf16[2,320,768]{2,1,0:T(8,128)(2,1)}, u32[]{:S(2)}, u32[]{:S(2)}) collective-permute-start(bf16[2,320,768]{2,1,0:T(8,128)(2,1)} %bitcast.62), channel_id=1, source_target_pairs={{0,4},{4,0},{8,12},{12,8},{16,20},{20,16},{24,28},{28,24},{1,5},{5... | collective-permute-start | bytes 2949128 | tf_op jit(solution)/shard_map/ppermute | solution.py:538
  212.3 48.3 %collective-permute-start.23 = (bf16[2,320,768]{2,1,0:T(8,128)(2,1)}, bf16[2,320,768]{2,1,0:T(8,128)(2,1)}, u32[]{:S(2)}, u32[]{:S(2)}) collective-permute-start(bf16[2,320,768]{2,1,0:T(8,128)(2,1)} %bitcast.65), channel_id=1, source_target_pairs={{0,4},{4,0},{8,12},{12,8},{16,20},{20,16},{24,28},{28,24},{1,5},{5... | collective-permute-start | bytes 2949128 | tf_op jit(solution)/shard_map/ppermute | solution.py:538
  213.6 35.6 %collective-permute-start.29 = (f32[4,4,80]{2,0,1:T(4,128)S(1)}, f32[4,4,80]{2,0,1:T(4,128)S(1)}, u32[]{:S(2)}, u32[]{:S(2)}) collective-permute-start(f32[4,4,80]{2,0,1:T(4,128)S(1)} %bitcast.569), channel_id=1, source_target_pairs={{0,4},{4,0},{8,12},{12,8},{16,20},{20,16},{24,28},{28,24},{1,5},{5... | collective-permute-start | bytes 15368 | tf_op jit(solution)/shard_map/ppermute | solution.py:538
  249.2 68.1 %collective-permute-start.18 = (bf16[2,320,768]{2,1,0:T(8,128)(2,1)}, bf16[2,320,768]{2,1,0:T(8,128)(2,1)}, u32[]{:S(2)}, u32[]{:S(2)}) collective-permute-start(bf16[2,320,768]{2,1,0:T(8,128)(2,1)} %bitcast.23), channel_id=1, source_target_pairs={{0,4},{4,0},{8,12},{12,8},{16,20},{20,16},{24,28},{28,24},{1,5},{5... | collective-permute-start | bytes 2949128 | tf_op jit(solution)/shard_map/ppermute | solution.py:538
  252.4 39.7 %collective-permute-start.24 = (bf16[2,320,768]{2,1,0:T(8,128)(2,1)}, bf16[2,320,768]{2,1,0:T(8,128)(2,1)S(1)}, u32[]{:S(2)}, u32[]{:S(2)}) collective-permute-start(bf16[2,320,768]{2,1,0:T(8,128)(2,1)} %bitcast.459), channel_id=1, source_target_pairs={{0,4},{4,0},{8,12},{12,8},{16,20},{20,16},{24,28},{28,24},{1,5},{5... | collective-permute-start | bytes 2949128 | tf_op jit(solution)/shard_map/ppermute | solution.py:538
  252.9 60.2 %collective-permute-start.25 = (bf16[2,320,768]{2,1,0:T(8,128)(2,1)}, bf16[2,320,768]{2,1,0:T(8,128)(2,1)S(1)}, u32[]{:S(2)}, u32[]{:S(2)}) collective-permute-start(bf16[2,320,768]{2,1,0:T(8,128)(2,1)} %bitcast.458), channel_id=1, source_target_pairs={{0,4},{4,0},{8,12},{12,8},{16,20},{20,16},{24,28},{28,24},{1,5},{5... | collective-permute-start | bytes 2949128 | tf_op jit(solution)/shard_map/ppermute | solution.py:538
  257.9 76.3 %collective-permute-start.19 = (bf16[2,320,768]{2,1,0:T(8,128)(2,1)S(1)}, bf16[2,320,768]{2,1,0:T(8,128)(2,1)S(1)}, u32[]{:S(2)}, u32[]{:S(2)}) collective-permute-start(bf16[2,320,768]{2,1,0:T(8,128)(2,1)S(1)} %bitcast.460), channel_id=1, source_target_pairs={{0,4},{4,0},{8,12},{12,8},{16,20},{20,16},{24,28},{28,24},{1,5},{5... | collective-permute-start | bytes 2949128 | tf_op jit(solution)/shard_map/ppermute | solution.py:538
  260.6 57.9 %collective-permute-start.14 = (bf16[512,768]{1,0:T(8,128)(2,1)}, bf16[512,768]{1,0:T(8,128)(2,1)S(1)}, u32[]{:S(2)}, u32[]{:S(2)}) collective-permute-start(bf16[512,768]{1,0:T(8,128)(2,1)} %collective-permute-done.12.up), channel_id=1, source_target_pairs={{0,8},{4,12},{8,16},{12,20},{16,24},{20,28},{24,0},{28,4},{1,9},{5... | collective-permute-start | bytes 2359304 | tf_op jit(solution)/shard_map/ppermute | solution.py:531
  322.0 35.4 %collective-permute-start.17 = (bf16[512,768]{1,0:T(8,128)(2,1)S(1)}, bf16[512,768]{1,0:T(8,128)(2,1)S(1)}, u32[]{:S(2)}, u32[]{:S(2)}) collective-permute-start(bf16[512,768]{1,0:T(8,128)(2,1)S(1)} %collective-permute-done.15.down), channel_id=1, source_target_pairs={{0,24},{4,28},{8,0},{12,4},{16,8},{20,12},{24,16},{28,20},{1,25},{... | collective-permute-start | bytes 2359304 | tf_op jit(solution)/shard_map/ppermute | solution.py:531
  326.3 39.7 %collective-permute-start.20 = (bf16[2,320,768]{2,1,0:T(8,128)(2,1)S(1)}, bf16[2,320,768]{2,1,0:T(8,128)(2,1)S(1)}, u32[]{:S(2)}, u32[]{:S(2)}) collective-permute-start(bf16[2,320,768]{2,1,0:T(8,128)(2,1)S(1)} %bitcast.461), channel_id=1, source_target_pairs={{0,4},{4,0},{8,12},{12,8},{16,20},{20,16},{24,28},{28,24},{1,5},{5... | collective-permute-start | bytes 2949128 | tf_op jit(solution)/shard_map/ppermute | solution.py:538
  441.7 519.2 %reduce-scatter.3.cloned.1.call-start = ((), (), s32[]{:S(2)}) async-start(), calls=%async_computation.4 | async-start | bytes 23592960 | tf_op jit(solution)/shard_map/reduce_scatter | solution.py:704
  484.4 43.4 %collective-permute-start.31 = (bf16[2,4,80,768]{3,2,1,0:T(8,128)(2,1)}, bf16[2,4,80,768]{3,2,1,0:T(8,128)(2,1)}, u32[]{:S(2)}, u32[]{:S(2)}) collective-permute-start(bf16[2,4,80,768]{3,2,1,0:T(8,128)(2,1)} %pad_maximum_fusion.10), channel_id=1, source_target_pairs={{0,4},{4,0},{8,12},{12,8},{16,20},{20,16},{24,28},{28,24},{1,5},{5... | collective-permute-start | bytes 2949128 | tf_op jit(solution)/shard_map/ppermute | solution.py:538
  514.2 38.3 %collective-permute-start.35 = (bf16[512,768]{1,0:T(8,128)(2,1)}, bf16[512,768]{1,0:T(8,128)(2,1)}, u32[]{:S(2)}, u32[]{:S(2)}) collective-permute-start(bf16[512,768]{1,0:T(8,128)(2,1)} %convolution_convert_fusion.3), channel_id=1, source_target_pairs={{0,24},{4,28},{8,0},{12,4},{16,8},{20,12},{24,16},{28,20},{1,25},{... | collective-permute-start | bytes 2359304 | tf_op jit(solution)/shard_map/ppermute | solution.py:531
  518.3 52.3 %collective-permute-start.50 = (f32[4,4,80]{2,1,0:T(4,128)}, f32[4,4,80]{2,1,0:T(4,128)S(1)}, u32[]{:S(2)}, u32[]{:S(2)}) collective-permute-start(f32[4,4,80]{2,1,0:T(4,128)} %get-tuple-element.379), channel_id=1, source_target_pairs={{0,4},{4,0},{8,12},{12,8},{16,20},{20,16},{24,28},{28,24},{1,5},{5... | collective-permute-start | bytes 15368 | tf_op jit(solution)/shard_map/ppermute | solution.py:538
  519.3 51.3 %collective-permute-start.30 = (bf16[2,4,80,768]{3,2,1,0:T(8,128)(2,1)}, bf16[2,4,80,768]{3,2,1,0:T(8,128)(2,1)}, u32[]{:S(2)}, u32[]{:S(2)}) collective-permute-start(bf16[2,4,80,768]{3,2,1,0:T(8,128)(2,1)} %pad_maximum_fusion.9), channel_id=1, source_target_pairs={{0,4},{4,0},{8,12},{12,8},{16,20},{20,16},{24,28},{28,24},{1,5},{5... | collective-permute-start | bytes 2949128 | tf_op jit(solution)/shard_map/ppermute | solution.py:538
  527.8 44.3 %collective-permute-start.47 = (bf16[2,4,80,768]{3,2,1,0:T(8,128)(2,1)S(1)}, bf16[2,4,80,768]{3,2,1,0:T(8,128)(2,1)S(1)}, u32[]{:S(2)}, u32[]{:S(2)}) collective-permute-start(bf16[2,4,80,768]{3,2,1,0:T(8,128)(2,1)S(1)} %pad_maximum_fusion.16), channel_id=1, source_target_pairs={{0,4},{4,0},{8,12},{12,8},{16,20},{20,16},{24,28},{28,24},{1,5},{5... | collective-permute-start | bytes 2949128 | tf_op jit(solution)/shard_map/ppermute | solution.py:538
  536.6 52.8 %collective-permute-start.34 = (bf16[512,768]{1,0:T(8,128)(2,1)S(1)}, bf16[512,768]{1,0:T(8,128)(2,1)S(1)}, u32[]{:S(2)}, u32[]{:S(2)}) collective-permute-start(bf16[512,768]{1,0:T(8,128)(2,1)S(1)} %add_convert_fusion.7), channel_id=1, source_target_pairs={{0,8},{4,12},{8,16},{12,20},{16,24},{20,28},{24,0},{28,4},{1,9},{5... | collective-permute-start | bytes 2359304 | tf_op jit(solution)/shard_map/ppermute | solution.py:531
  587.8 40.5 %collective-permute-start.49 = (bf16[512,768]{1,0:T(8,128)(2,1)S(1)}, bf16[512,768]{1,0:T(8,128)(2,1)S(1)}, u32[]{:S(2)}, u32[]{:S(2)}) collective-permute-start(bf16[512,768]{1,0:T(8,128)(2,1)S(1)} %add_convert_fusion.4), channel_id=1, source_target_pairs={{0,24},{4,28},{8,0},{12,4},{16,8},{20,12},{24,16},{28,20},{1,25},{... | collective-permute-start | bytes 2359304 | tf_op jit(solution)/shard_map/ppermute | solution.py:531
  590.3 40.9 %collective-permute-start.48 = (bf16[512,768]{1,0:T(8,128)(2,1)S(1)}, bf16[512,768]{1,0:T(8,128)(2,1)S(1)}, u32[]{:S(2)}, u32[]{:S(2)}) collective-permute-start(bf16[512,768]{1,0:T(8,128)(2,1)S(1)} %add_convert_fusion.6), channel_id=1, source_target_pairs={{0,8},{4,12},{8,16},{12,20},{16,24},{20,28},{24,0},{28,4},{1,9},{5... | collective-permute-start | bytes 2359304 | tf_op jit(solution)/shard_map/ppermute | solution.py:531
  592.6 32.9 %collective-permute-start.51 = (f32[8,512]{1,0:T(8,128)S(1)}, f32[8,512]{1,0:T(8,128)S(1)}, u32[]{:S(2)}, u32[]{:S(2)}) collective-permute-start(f32[8,512]{1,0:T(8,128)S(1)} %get-tuple-element.377), channel_id=1, source_target_pairs={{0,24},{4,28},{8,0},{12,4},{16,8},{20,12},{24,16},{28,20},{1,25},{... | collective-permute-start | bytes 49160 | tf_op jit(solution)/shard_map/ppermute | solution.py:531
  625.5 53.9 %collective-permute-start.40 = (bf16[2,4,80,768]{3,2,1,0:T(8,128)(2,1)}, bf16[2,4,80,768]{3,2,1,0:T(8,128)(2,1)}, u32[]{:S(2)}, u32[]{:S(2)}) collective-permute-start(bf16[2,4,80,768]{3,2,1,0:T(8,128)(2,1)} %pad_maximum_fusion.15), channel_id=1, source_target_pairs={{0,4},{4,0},{8,12},{12,8},{16,20},{20,16},{24,28},{28,24},{1,5},{5... | collective-permute-start | bytes 2949128 | tf_op jit(solution)/shard_map/ppermute | solution.py:538
  625.5 56.8 %collective-permute-start.39 = (bf16[2,4,80,768]{3,2,1,0:T(8,128)(2,1)}, bf16[2,4,80,768]{3,2,1,0:T(8,128)(2,1)}, u32[]{:S(2)}, u32[]{:S(2)}) collective-permute-start(bf16[2,4,80,768]{3,2,1,0:T(8,128)(2,1)} %pad_maximum_fusion.14), channel_id=1, source_target_pairs={{0,4},{4,0},{8,12},{12,8},{16,20},{20,16},{24,28},{28,24},{1,5},{5... | collective-permute-start | bytes 2949128 | tf_op jit(solution)/shard_map/ppermute | solution.py:538
  627.6 62.3 %collective-permute-start.38 = (bf16[2,4,80,768]{3,2,1,0:T(8,128)(2,1)}, bf16[2,4,80,768]{3,2,1,0:T(8,128)(2,1)}, u32[]{:S(2)}, u32[]{:S(2)}) collective-permute-start(bf16[2,4,80,768]{3,2,1,0:T(8,128)(2,1)} %pad_maximum_fusion.13), channel_id=1, source_target_pairs={{0,4},{4,0},{8,12},{12,8},{16,20},{20,16},{24,28},{28,24},{1,5},{5... | collective-permute-start | bytes 2949128 | tf_op jit(solution)/shard_map/ppermute | solution.py:538
  628.3 144.7 %collective-permute-start.37 = (bf16[2,4,80,768]{3,2,1,0:T(8,128)(2,1)}, bf16[2,4,80,768]{3,2,1,0:T(8,128)(2,1)}, u32[]{:S(2)}, u32[]{:S(2)}) collective-permute-start(bf16[2,4,80,768]{3,2,1,0:T(8,128)(2,1)} %pad_maximum_fusion.12), channel_id=1, source_target_pairs={{0,4},{4,0},{8,12},{12,8},{16,20},{20,16},{24,28},{28,24},{1,5},{5... | collective-permute-start | bytes 2949128 | tf_op jit(solution)/shard_map/ppermute | solution.py:538
  662.3 34.1 %collective-permute-start.56 = (bf16[512,512]{1,0:T(8,128)(2,1)}, bf16[512,512]{1,0:T(8,128)(2,1)}, u32[]{:S(2)}, u32[]{:S(2)}) collective-permute-start(bf16[512,512]{1,0:T(8,128)(2,1)} %get-tuple-element.316), channel_id=1, source_target_pairs={{3,0},{7,4},{11,8},{15,12},{19,16},{23,20},{27,24},{31,28}} | collective-permute-start | bytes 1572872 | tf_op jit(solution)/shard_map/ppermute | solution.py:546
  689.9 66.7 %collective-permute-start.67 = (bf16[2,384,1664]{2,1,0:T(8,128)(2,1)}, bf16[2,384,1664]{2,1,0:T(8,128)(2,1)}, u32[]{:S(2)}, u32[]{:S(2)}) collective-permute-start(bf16[2,384,1664]{2,1,0:T(8,128)(2,1)} %dynamic-slice_bitcast_fusion.1), channel_id=1, source_target_pairs={{0,1},{1,0},{2,3},{3,2},{4,5},{5,4},{6,7},{7,6},{8,9},{9,8},{10,11... | collective-permute-start | bytes 7667720 | tf_op jit(solution)/shard_map/ppermute | solution.py:780
  698.0 38.0 %collective-permute-start.41 = (bf16[512,768]{1,0:T(8,128)(2,1)}, bf16[512,768]{1,0:T(8,128)(2,1)}, u32[]{:S(2)}, u32[]{:S(2)}) collective-permute-start(bf16[512,768]{1,0:T(8,128)(2,1)} %convolution_convert_fusion.2), channel_id=1, source_target_pairs={{0,8},{4,12},{8,16},{12,20},{16,24},{20,28},{24,0},{28,4},{1,9},{5... | collective-permute-start | bytes 2359304 | tf_op jit(solution)/shard_map/ppermute | solution.py:531
  718.8 33.4 %collective-permute-start.45 = (bf16[512,768]{1,0:T(8,128)(2,1)}, bf16[512,768]{1,0:T(8,128)(2,1)}, u32[]{:S(2)}, u32[]{:S(2)}) collective-permute-start(bf16[512,768]{1,0:T(8,128)(2,1)} %add_convert_fusion.1), channel_id=1, source_target_pairs={{0,24},{4,28},{8,0},{12,4},{16,8},{20,12},{24,16},{28,20},{1,25},{... | collective-permute-start | bytes 2359304 | tf_op jit(solution)/shard_map/ppermute | solution.py:531
  732.1 76.4 %collective-permute-start.57 = (bf16[2,384,2176]{2,1,0:T(8,128)(2,1)}, bf16[2,384,2176]{2,1,0:T(8,128)(2,1)}, u32[]{:S(2)}, u32[]{:S(2)}) collective-permute-start(bf16[2,384,2176]{2,1,0:T(8,128)(2,1)} %dynamic-slice_bitcast_fusion), channel_id=1, source_target_pairs={{0,1},{1,0},{2,3},{3,2},{4,5},{5,4},{6,7},{7,6},{8,9},{9,8},{10,11... | collective-permute-start | bytes 10027016 | tf_op jit(solution)/shard_map/ppermute | solution.py:780
  760.2 45.0 %collective-permute-start.68 = (bf16[384,1664]{1,0:T(8,128)(2,1)}, bf16[384,1664]{1,0:T(8,128)(2,1)}, u32[]{:S(2)}, u32[]{:S(2)}) collective-permute-start(bf16[384,1664]{1,0:T(8,128)(2,1)} %dynamic-slice_bitcast_fusion.3), channel_id=1, source_target_pairs={{0,2},{1,3},{2,0},{3,1},{4,6},{5,7},{6,4},{7,5},{8,10},{9,11},{10,... | collective-permute-start | bytes 3833864 | tf_op jit(solution)/shard_map/ppermute | solution.py:783
  829.0 36.9 %collective-permute-start.58 = (bf16[384,2176]{1,0:T(8,128)(2,1)S(1)}, bf16[384,2176]{1,0:T(8,128)(2,1)S(1)}, u32[]{:S(2)}, u32[]{:S(2)}) collective-permute-start(bf16[384,2176]{1,0:T(8,128)(2,1)S(1)} %dynamic-slice_bitcast_fusion.2), channel_id=1, source_target_pairs={{0,2},{1,3},{2,0},{3,1},{4,6},{5,7},{6,4},{7,5},{8,10},{9,11},{10,... | collective-permute-start | bytes 5013512 | tf_op jit(solution)/shard_map/ppermute | solution.py:783
  (139 other events, 2045.7 us)
Sparse Core Ops, SparseCore 0:
  17.7 49.7 all-gather.6
  69.6 37.4 all-gather.8
  109.3 83.1 all-gather.12
  194.4 123.6 all-gather.10
  441.8 83.4 reduce-scatter.4
  527.7 139.4 reduce-scatter.2

commit v2 on v1

v2 whole, which is shorter than its diff:
```python
import functools
import math

import jax
import jax.numpy as jnp
from jax import lax
from jax.experimental import pallas as pl
from jax.experimental.pallas import tpu as pltpu
from jax.sharding import PartitionSpec as P

MODEL_WIDTH = 1536
QUERY_HEADS = 12
KEY_VALUE_HEADS = 2
HEAD_SIZE = 128
GROUP = QUERY_HEADS // KEY_VALUE_HEADS
FF = 768
STEP = 10
CAP = 80
DEPTH = 4
HALF = MODEL_WIDTH // 2
KV = KEY_VALUE_HEADS * HEAD_SIZE
QKV = MODEL_WIDTH + 2 * KV


NORM_EPS = 1e-05
ROPE_BASE = 10000.0
BETA_ONE = 0.9
BETA_TWO = 0.95
ADAM_EPS = 1e-08
DECAY = 0.1
GAIN_RATE = 0.8
MASKED = -1e30
LOG2E = 1.0 / math.log(2.0)
SCORE_SCALE = 1.0 / math.sqrt(HEAD_SIZE)

f32 = jnp.float32
bf16 = jnp.bfloat16


def dot_nn(left, right):
    return lax.dot_general(left, right, (((1,), (0,)), ((), ())), preferred_element_type=f32)


def dot_nt(left, right):
    return lax.dot_general(left, right, (((1,), (1,)), ((), ())), preferred_element_type=f32)


def dot_tn(left, right):
    return lax.dot_general(left, right, (((0,), (0,)), ((), ())), preferred_element_type=f32)


def after(value, *others):
    return lax.optimization_barrier((value, others))[0]


def params(megabytes, axes):
    return pltpu.CompilerParams(
        vmem_limit_bytes=megabytes * 1024 * 1024, dimension_semantics=("arbitrary",) * axes
    )


def cost(flops, nbytes, trans=0):
    return pl.CostEstimate(flops=int(flops), bytes_accessed=int(nbytes), transcendentals=0)


def causal(score_t):
    key_place = lax.broadcasted_iota(jnp.int32, score_t.shape, 0)
    query_place = lax.broadcasted_iota(jnp.int32, score_t.shape, 1)
    return key_place <= query_place


def attend_kernel(place, pre, cosine, sine, keys, values, out, log_total, turned):
    rows = pre[...]
    query = rows * cosine[...] + pltpu.roll(rows, HEAD_SIZE // 2, 1) * sine[...]
    turned[...] = query.astype(bf16)
    query_t = query.T.astype(bf16)
    factor = SCORE_SCALE * LOG2E

    score = dot_nn(keys[0], query_t) * factor
    score = jnp.where(causal(score), score, MASKED)
    biggest = jnp.max(score, axis=0, keepdims=True)
    weight = jnp.exp2(score - biggest)
    total = jnp.sum(weight, axis=0, keepdims=True)
    acc = dot_nn(values[0].T, weight.astype(bf16))

    def step(back, carry):
        biggest, total, acc = carry
        score = dot_nn(keys[back], query_t) * factor
        larger = jnp.maximum(biggest, jnp.max(score, axis=0, keepdims=True))
        weight = jnp.exp2(score - larger)
        shrink = jnp.exp2(biggest - larger)
        total = total * shrink + jnp.sum(weight, axis=0, keepdims=True)
        acc = acc * shrink + dot_nn(values[back].T, weight.astype(bf16))
        return larger, total, acc

    biggest, total, acc = lax.fori_loop(1, place[0] + 1, step, (biggest, total, acc))
    out[...] = (acc / total).T.astype(bf16)
    log_total[0] = biggest + jnp.log(total) * LOG2E


def attend(place, pre, cosine, sine, kv_blocks):
    token_rows = pre.shape[0]
    blocks = kv_blocks.shape[0]
    width = (token_rows, HEAD_SIZE)
    many = (blocks, token_rows, HEAD_SIZE)
    return pl.pallas_call(
        attend_kernel,
        out_shape=(
            jax.ShapeDtypeStruct((token_rows, MODEL_WIDTH), bf16),
            jax.ShapeDtypeStruct((QUERY_HEADS, 1, token_rows), f32),
            jax.ShapeDtypeStruct((token_rows, MODEL_WIDTH), bf16),
        ),
        grid_spec=pltpu.PrefetchScalarGridSpec(
            num_scalar_prefetch=1,
            grid=(QUERY_HEADS,),
            in_specs=[
                pl.BlockSpec(width, lambda h, p: (0, h)),
                pl.BlockSpec(width, lambda h, p: (0, 0)),
                pl.BlockSpec(width, lambda h, p: (0, 0)),
                pl.BlockSpec(many, lambda h, p: (0, 0, h // GROUP)),
                pl.BlockSpec(many, lambda h, p: (0, 0, KEY_VALUE_HEADS + h // GROUP)),
            ],
            out_specs=(
                pl.BlockSpec(width, lambda h, p: (0, h)),
                pl.BlockSpec((1, 1, token_rows), lambda h, p: (h, 0, 0)),
                pl.BlockSpec(width, lambda h, p: (0, h)),
            ),
        ),
        compiler_params=params(56, 1),
        cost_estimate=cost(1e9, 1e6),
        name="attend",
    )(place, pre, cosine, sine, kv_blocks, kv_blocks)


def attend_back_kernel(
    place, query, keys, values, out, out_grad, log_total, cosine, sine, pre_grad, key_grad, value_grad, key_acc, value_acc
):
    head = pl.program_id(0)

    @pl.when(head % GROUP == 0)
    def _():
        key_acc[...] = jnp.zeros_like(key_acc)
        value_acc[...] = jnp.zeros_like(value_acc)

    factor = SCORE_SCALE * LOG2E
    query_rows = query[...]
    grad_rows = out_grad[...]
    query_t = query_rows.astype(f32).T.astype(bf16)
    grad_t32 = grad_rows.astype(f32).T
    grad_t = grad_t32.astype(bf16)
    row_dot = jnp.sum(out[...].astype(f32).T * grad_t32, axis=0, keepdims=True)
    level = log_total[0]

    def block(back, masked):
        key = keys[back]
        score = dot_nn(key, query_t) * factor - level
        weight = jnp.exp2(score)
        if masked:
            weight = jnp.where(causal(weight), weight, 0.0)
        value_acc[back] += dot_nn(weight.astype(bf16), grad_rows)
        prob_grad = dot_nn(values[back], grad_t)
        score_grad = (weight * (prob_grad - row_dot)).astype(bf16)
        key_acc[back] += dot_nn(score_grad, query_rows)
        return dot_nn(key.T, score_grad)

    query_grad = block(0, True)
    query_grad = lax.fori_loop(1, place[0] + 1, lambda b, acc: acc + block(b, False), query_grad)
    rows = query_grad.T * SCORE_SCALE
    pre_grad[...] = (rows * cosine[...] - pltpu.roll(rows, HEAD_SIZE // 2, 1) * sine[...]).astype(bf16)

    @pl.when(head % GROUP == GROUP - 1)
    def _():
        key_grad[...] = (key_acc[...] * SCORE_SCALE).astype(bf16)
        value_grad[...] = value_acc[...].astype(bf16)


def attend_back(place, query, kv_blocks, out, out_grad, log_total, cosine, sine):
    token_rows = query.shape[0]
    blocks = kv_blocks.shape[0]
    width = (token_rows, HEAD_SIZE)
    many = (blocks, token_rows, HEAD_SIZE)
    return pl.pallas_call(
        attend_back_kernel,
        out_shape=(
            jax.ShapeDtypeStruct((token_rows, MODEL_WIDTH), bf16),
            jax.ShapeDtypeStruct((blocks, token_rows, KV), bf16),
            jax.ShapeDtypeStruct((blocks, token_rows, KV), bf16),
        ),
        grid_spec=pltpu.PrefetchScalarGridSpec(
            num_scalar_prefetch=1,
            grid=(QUERY_HEADS,),
            in_specs=[
                pl.BlockSpec(width, lambda h, p: (0, h)),
                pl.BlockSpec(many, lambda h, p: (0, 0, h // GROUP)),
                pl.BlockSpec(many, lambda h, p: (0, 0, KEY_VALUE_HEADS + h // GROUP)),
                pl.BlockSpec(width, lambda h, p: (0, h)),
                pl.BlockSpec(width, lambda h, p: (0, h)),
                pl.BlockSpec((1, 1, token_rows), lambda h, p: (h, 0, 0)),
                pl.BlockSpec(width, lambda h, p: (0, 0)),
                pl.BlockSpec(width, lambda h, p: (0, 0)),
            ],
            out_specs=(
                pl.BlockSpec(width, lambda h, p: (0, h)),
                pl.BlockSpec(many, lambda h, p: (0, 0, h // GROUP)),
                pl.BlockSpec(many, lambda h, p: (0, 0, h // GROUP)),
            ),
            scratch_shapes=[pltpu.VMEM(many, f32), pltpu.VMEM(many, f32)],
        ),
        compiler_params=params(56, 1),
        cost_estimate=cost(1e9, 1e6),
        name="attend_back",
    )(place, query, kv_blocks, kv_blocks, out, out_grad, log_total, cosine, sine)


def gather_rows(pieces, rows):
    for p, piece in enumerate(pieces):
        rows[p * CAP : (p + 1) * CAP] = piece[...]


def scatter_rows(rows, pieces, at, span):
    low = rows.astype(bf16)
    for p, piece in enumerate(pieces):
        piece[:, at : at + span] = low[p * CAP : (p + 1) * CAP]


def piece_spec():
    return pl.BlockSpec((CAP, MODEL_WIDTH), lambda e, *_: (e, 0))


def row_scratch(count):
    return [pltpu.VMEM((count * CAP, MODEL_WIDTH), bf16)]


def inner_kernel(count, *refs):
    pieces, (down, inner, rows) = refs[:count], refs[count:]
    gather_rows(pieces, rows)
    shards, span = down.shape[0], down.shape[3]
    acc = None
    for c in range(shards):
        term = dot_nt(rows[:, c * span : (c + 1) * span], down[c, 0])
        acc = term if acc is None else acc + term
    inner[0] = acc.astype(bf16)


def inner_rows(pieces, down):
    shards, experts, _, span = down.shape
    rows = len(pieces) * CAP
    return pl.pallas_call(
        functools.partial(inner_kernel, len(pieces)),
        out_shape=jax.ShapeDtypeStruct((experts, rows, FF), bf16),
        grid=(experts,),
        in_specs=[piece_spec()] * len(pieces) + [pl.BlockSpec((shards, 1, FF, span), lambda e: (0, e, 0, 0))],
        out_specs=pl.BlockSpec((1, rows, FF), lambda e: (e, 0, 0)),
        scratch_shapes=row_scratch(len(pieces)),
        compiler_params=params(56, 1),
        cost_estimate=cost(2 * experts * rows * FF * MODEL_WIDTH, 20e6),
        name="inner_rows",
    )(*pieces, down)


def core_kernel(count, *refs):
    pieces, refs = refs[:count], refs[count:]
    gate_up, inner, weight, scaled, gate_side, up_side, gate_dots = refs[:7]
    back, (rows,) = refs[7 : 7 + count], refs[7 + count :]
    gather_rows(pieces, rows)
    span = gate_up.shape[2]
    tile = 256
    factor = weight[0]
    dots = None

    def product(at):
        return dot_nn(rows[...], gate_up[:, 0, :, at : at + tile].reshape(MODEL_WIDTH, tile))

    for n in range(FF // tile):
        at = n * tile
        gate_pre = product(at)
        up_part = product(FF + at)
        sigmoid = 1.0 / (1.0 + jnp.exp(-gate_pre))
        silu = gate_pre * sigmoid
        hidden = silu * up_part
        raw = inner[0, :, at : at + tile].astype(f32)
        part = jnp.sum(raw * hidden, axis=1, keepdims=True)
        dots = part if dots is None else dots + part
        scaled[0, :, at : at + tile] = (hidden * factor).astype(bf16)
        raw = raw * factor
        gate_side[0, :, at : at + tile] = (raw * up_part * (sigmoid + silu * (1.0 - sigmoid))).astype(bf16)
        up_side[0, :, at : at + tile] = (raw * silu).astype(bf16)
    gate_dots[0] = dots

    width = 384
    group = width // span
    for chunk in range(MODEL_WIDTH // width):
        block = gate_up[chunk * group : (chunk + 1) * group, 0].reshape(width, 2 * FF)
        grads = dot_nt(gate_side[0], block[:, :FF]) + dot_nt(up_side[0], block[:, FF:])
        scatter_rows(grads, back, chunk * width, width)


def core_rows(pieces, gate_up, inner, weight):
    count = len(pieces)
    shards, experts, span, _ = gate_up.shape
    rows = count * CAP
    whole = pl.BlockSpec((1, rows, FF), lambda e: (e, 0, 0))
    column = pl.BlockSpec((1, rows, 1), lambda e: (e, 0, 0))
    low = jax.ShapeDtypeStruct((experts, rows, FF), bf16)
    out = pl.pallas_call(
        functools.partial(core_kernel, count),
        out_shape=(low, low, low, jax.ShapeDtypeStruct((experts, rows, 1), f32))
        + (jax.ShapeDtypeStruct(pieces[0].shape, bf16),) * count,
        grid=(experts,),
        in_specs=[piece_spec()] * count
        + [pl.BlockSpec((shards, 1, span, 2 * FF), lambda e: (0, e, 0, 0)), whole, column],
        out_specs=(whole, whole, whole, column) + (piece_spec(),) * count,
        scratch_shapes=row_scratch(len(pieces)),
        compiler_params=params(60, 1),
        cost_estimate=cost(8 * experts * rows * FF * MODEL_WIDTH, 60e6),
        name="core_rows",
    )(*pieces, gate_up, inner, weight)
    return out[0], out[1], out[2], out[3], list(out[4:])


def result_kernel(scaled, down, *pieces):
    width = 384
    shards, span = down.shape[0], down.shape[3]
    group = width // span
    rows = scaled[0]
    for chunk in range(MODEL_WIDTH // width):
        parts = [down[c, 0] for c in range(chunk * group, (chunk + 1) * group)]
        block = parts[0] if group == 1 else jnp.concatenate(parts, axis=1)
        scatter_rows(dot_nn(rows, block), pieces, chunk * width, width)


def result_rows(scaled, down, count):
    experts, rows, _ = scaled.shape
    shards, _, _, span = down.shape
    return list(
        pl.pallas_call(
            result_kernel,
            out_shape=(jax.ShapeDtypeStruct((experts * CAP, MODEL_WIDTH), bf16),) * count,
            grid=(experts,),
            in_specs=[
                pl.BlockSpec((1, rows, FF), lambda e: (e, 0, 0)),
                pl.BlockSpec((shards, 1, FF, span), lambda e: (0, e, 0, 0)),
            ],
            out_specs=(piece_spec(),) * count,
            compiler_params=params(56, 1),
            cost_estimate=cost(2 * experts * rows * FF * MODEL_WIDTH, 22e6),
            name="result_rows",
        )(scaled, down)
    )


def down_grad_kernel(count, *refs):
    pieces, (scaled, out, rows) = refs[:count], refs[count:]
    gather_rows(pieces, rows)
    shards, span = out.shape[0], out.shape[3]
    scaled_t = scaled[0].T
    for c in range(shards):
        out[c, 0] = dot_nn(scaled_t, rows[:, c * span : (c + 1) * span]).astype(bf16)


def down_grads(pieces, scaled, shards):
    experts, rows, _ = scaled.shape
    span = MODEL_WIDTH // shards
    return pl.pallas_call(
        functools.partial(down_grad_kernel, len(pieces)),
        out_shape=jax.ShapeDtypeStruct((shards, experts, FF, span), bf16),
        grid=(experts,),
        in_specs=[piece_spec()] * len(pieces) + [pl.BlockSpec((1, rows, FF), lambda e: (e, 0, 0))],
        out_specs=pl.BlockSpec((shards, 1, FF, span), lambda e: (0, e, 0, 0)),
        scratch_shapes=row_scratch(len(pieces)),
        compiler_params=params(56, 1),
        cost_estimate=cost(2 * experts * rows * FF * MODEL_WIDTH, 22e6),
        name="down_grads",
    )(*pieces, scaled)


def in_grad_kernel(count, *refs):
    pieces, (gate_side, up_side, out, rows) = refs[:count], refs[count:]
    gather_rows(pieces, rows)
    shards, span = out.shape[0], out.shape[2]
    rows_t = rows[...].T
    for c in range(shards):
        part = rows_t[c * span : (c + 1) * span]
        out[c, 0, :, :FF] = dot_nn(part, gate_side[0]).astype(bf16)
        out[c, 0, :, FF:] = dot_nn(part, up_side[0]).astype(bf16)


def in_grads(pieces, gate_side, up_side, shards):
    experts, rows, _ = gate_side.shape
    span = MODEL_WIDTH // shards
    whole = pl.BlockSpec((1, rows, FF), lambda e: (e, 0, 0))
    return pl.pallas_call(
        functools.partial(in_grad_kernel, len(pieces)),
        out_shape=jax.ShapeDtypeStruct((shards, experts, span, 2 * FF), bf16),
        grid=(experts,),
        in_specs=[piece_spec()] * len(pieces) + [whole, whole],
        out_specs=pl.BlockSpec((shards, 1, span, 2 * FF), lambda e: (0, e, 0, 0)),
        scratch_shapes=row_scratch(len(pieces)),
        compiler_params=params(56, 1),
        cost_estimate=cost(4 * experts * rows * FF * MODEL_WIDTH, 35e6),
        name="in_grads",
    )(*pieces, gate_side, up_side)


def ring_kernel(wide, *refs):
    picks, pieces = refs[0], refs[1 : 1 + wide]
    arrived, out = refs[1 + wide : -1], refs[-1]
    rows = jnp.concatenate([piece[...] for piece in pieces], axis=0)
    total = dot_tn(picks[0], rows)
    if arrived:
        total = total + arrived[0][...].astype(f32)
    out[...] = total.astype(out.dtype)


def ring_rows(picks, level, pieces, arrived, last):
    _, many, token_rows = picks.shape
    tile = 512
    side = pl.BlockSpec((token_rows, tile), lambda n: (0, n))
    return pl.pallas_call(
        functools.partial(ring_kernel, len(pieces)),
        out_shape=jax.ShapeDtypeStruct((token_rows, MODEL_WIDTH), f32 if last else bf16),
        grid=(MODEL_WIDTH // tile,),
        in_specs=[pl.BlockSpec((1, many, token_rows), lambda n: (level, 0, 0))]
        + [pl.BlockSpec((p.shape[0], tile), lambda n: (0, n)) for p in pieces]
        + [side] * len(arrived),
        out_specs=side,
        compiler_params=params(48, 1),
        cost_estimate=cost(4 * many * token_rows * HALF, 8e6),
        name="ring_rows",
    )(picks, *pieces, *arrived)


def pick_kernel(picks, rows, own, away):
    per = own.shape[0]
    picked = dot_nn(picks[0], rows[...]).astype(bf16)
    own[...] = picked[:per]
    for r in range(away.shape[0]):
        away[r] = picked[(r + 1) * per : (r + 2) * per]


def pick_rows(picks, level, rows, wide):
    _, many, token_rows = picks.shape
    per = many // wide
    tile = 512
    return pl.pallas_call(
        pick_kernel,
        out_shape=(
            jax.ShapeDtypeStruct((per, MODEL_WIDTH), bf16),
            jax.ShapeDtypeStruct((wide - 1, per, MODEL_WIDTH), bf16),
        ),
        grid=(MODEL_WIDTH // tile,),
        in_specs=[
            pl.BlockSpec((1, many, token_rows), lambda n: (level, 0, 0)),
            pl.BlockSpec((token_rows, tile), lambda n: (0, n)),
        ],
        out_specs=(
            pl.BlockSpec((per, tile), lambda n: (0, n)),
            pl.BlockSpec((wide - 1, per, tile), lambda n: (0, 0, n)),
        ),
        compiler_params=params(32, 1),
        cost_estimate=cost(4 * many * token_rows * HALF, 5e6),
        name="pick_rows",
    )(picks, rows)


def weight_grad_kernel(rows, *refs):
    *grads, out = refs
    rows_t = rows[...].T
    at = 0
    for side in grads:
        if side.dtype == f32:
            out[:, at:] = side[...].T.astype(bf16)
        else:
            columns = side.shape[1]
            out[:, at : at + columns] = dot_nn(rows_t, side[...]).astype(bf16)
            at += columns


def weight_grads(rows, grads, extra=None):
    token_rows = rows.shape[0]
    tile = 384
    extras = [] if extra is None else [extra]
    columns = sum(g.shape[1] for g in grads) + sum(e.shape[0] for e in extras)
    return pl.pallas_call(
        weight_grad_kernel,
        out_shape=jax.ShapeDtypeStruct((MODEL_WIDTH, columns), bf16),
        grid=(MODEL_WIDTH // tile,),
        in_specs=[pl.BlockSpec((token_rows, tile), lambda n: (0, n))]
        + [pl.BlockSpec(g.shape, lambda n: (0, 0)) for g in grads]
        + [pl.BlockSpec((e.shape[0], tile), lambda n: (0, n)) for e in extras],
        out_specs=pl.BlockSpec((tile, columns), lambda n: (n, 0)),
        compiler_params=params(56, 1),
        cost_estimate=cost(2 * MODEL_WIDTH * token_rows * columns, 14e6),
        name="weight_grads",
    )(rows, *grads, *extras)


def adamw_update(weight, moment_one, moment_two, gradient, step_rate, decay_rate):
    first_new = BETA_ONE * moment_one + (1.0 - BETA_ONE) * gradient
    second_new = BETA_TWO * moment_two + (1.0 - BETA_TWO) * gradient * gradient
    first_hat = first_new / (1.0 - BETA_ONE**STEP)
    second_hat = second_new / (1.0 - BETA_TWO**STEP)
    weight_new = weight - step_rate * (
        first_hat / (jnp.sqrt(second_hat) + ADAM_EPS) + decay_rate * weight
    )
    return (weight_new, first_new, second_new)


def body(
    tokens,
    cotangent,
    routes,
    gains,
    gains_first,
    gains_second,
    query_weight,
    query_first,
    query_second,
    key_matrix,
    key_moment_first,
    key_moment_second,
    value_matrix,
    value_moment_first,
    value_moment_second,
    output_weight,
    output_first,
    output_second,
    router_weight,
    router_first,
    router_second,
    expert_in,
    in_first,
    in_second,
    expert_out,
    out_first,
    out_second,
):
    token_rows, top_count = routes.shape
    shards = lax.axis_size("fsdp")
    place = lax.axis_index("fsdp")
    groups = lax.axis_size("expert")
    group = lax.axis_index("expert")
    depth = DEPTH
    wide = groups // depth
    level, column = group // wide, group % wide
    experts_local = expert_in.shape[0]
    experts_all = experts_local * groups
    near = wide * experts_local
    shard_rows = query_weight.shape[0]

    def z_shift(value, by):
        return lax.ppermute(
            value,
            "expert",
            [(a * wide + b, (a + by) % depth * wide + b) for a in range(depth) for b in range(wide)],
        )

    def x_shift(value, by):
        return lax.ppermute(
            value,
            "expert",
            [(a * wide + b, a * wide + (b + by) % wide) for a in range(depth) for b in range(wide)],
        )

    def back_shift(value, by):
        pairs = [(a, a + by) for a in range(shards) if 0 <= a + by < shards]
        return lax.ppermute(value, "fsdp", pairs)

    def core_shift(value, by):
        return lax.ppermute(value, "fsdp", [(a, a // 2 * 2 + (a + by) % 2) for a in range(shards)])

    def y_shift(value, by):
        return lax.ppermute(value, "fsdp", [(a, (a + 2 * by) % shards) for a in range(shards)])

    def y_up(value, by):
        return lax.ppermute(value, "fsdp", [(a, a + 2 * by) for a in range(shards - 2 * by)])

    small = jnp.concatenate(
        [
            router_weight.astype(bf16),
            gains.T.astype(bf16),
            jnp.zeros((shard_rows, 128 - experts_all - 2), bf16),
        ],
        axis=1,
    )
    front_low = lax.all_gather(
        jnp.concatenate(
            [query_weight.astype(bf16), key_matrix.astype(bf16), value_matrix.astype(bf16), small], axis=1
        ),
        "fsdp",
        axis=0,
        tiled=True,
    )
    output_low = lax.all_gather(output_weight.astype(bf16), "fsdp", axis=0, tiled=True)
    qkv_low = front_low[:, :QKV]
    router_low = front_low[:, QKV : QKV + experts_all]
    gain_pair = front_low[:, QKV + experts_all : QKV + experts_all + 2].astype(f32).T
    gain_one, gain_two = gain_pair[0], gain_pair[1]

    routes_t = routes.T
    routes_of = jnp.stack([routes_t] + [z_shift(routes_t, i) for i in range(1, depth)])

    def expert_ids(at_level):
        columns = (column + jnp.arange(wide, dtype=jnp.int32)) % wide
        first_ids = (at_level * wide + columns) * experts_local
        return (first_ids[:, None] + jnp.arange(experts_local, dtype=jnp.int32)[None, :]).reshape(near)

    named = (routes_of[:, None] == expert_ids(level)[None, :, None, None]).astype(f32)
    chosen_here = jnp.sum(named, axis=2)
    earlier = (
        jnp.arange(token_rows, dtype=jnp.int32)[:, None] < jnp.arange(token_rows, dtype=jnp.int32)[None, :]
    ).astype(bf16)
    slots = dot_nn(chosen_here.reshape(depth * near, token_rows).astype(bf16), earlier).reshape(
        depth, near, token_rows
    )
    code = jnp.where(chosen_here > 0, slots.astype(jnp.int32), -1)
    picks = code[:, :, None, :] == jnp.arange(CAP, dtype=jnp.int32)[None, None, :, None]
    picks_low = picks.astype(bf16).reshape(depth, near * CAP, token_rows)

    def pick(rows, k):
        return pick_rows(picks_low, k, rows, wide)

    def swap(picked, *before):
        own, away = picked
        pairs = [own]
        for r in range(1, wide):
            pairs.append(x_shift(after(away[r - 1], pairs[1:], before), r))
        return pairs

    def order(swapped):
        return [swapped[k][r] for r in range(wide) for k in range(depth)]

    def swap_back(pieces, *before):
        steps = [None] * depth
        for m in range(depth):
            k = (m + 1) % depth
            steps[k] = [pieces[k]]
            for r in range(1, wide):
                piece = x_shift(after(pieces[r * depth + k], before), -r)
                steps[k].append(piece)
                if m % 2 == 0:
                    before = (piece,)
        return steps

    def ring_send(held):
        return [z_shift(held[-1], 1)]

    def ring_step(held, pieces, arrived=()):
        m = len(held)
        out = ring_rows(picks_low, (m + 1) % depth, pieces, arrived, m == depth - 1)
        if m == depth - 1:
            return out
        held.append(out)

    upstream = cotangent.astype(f32)
    level_one = z_shift(cotangent, 1)
    upstream_swapped = [swap(pick(cotangent, 0))]
    level_one = after(level_one, upstream_swapped)
    picked = pick(level_one, 1)
    upstream_swapped.append(swap(picked, upstream_swapped[-1]))

    inputs = tokens.astype(f32)
    scale_one = lax.rsqrt(jnp.mean(inputs * inputs, axis=1, keepdims=True) + NORM_EPS)
    normed_one = inputs * scale_one
    first_hidden = (normed_one * gain_one).astype(bf16)
    inverse = ROPE_BASE ** (-(jnp.arange(HEAD_SIZE // 2, dtype=f32) * 2.0 / HEAD_SIZE))
    places = (place * token_rows + jnp.arange(token_rows, dtype=jnp.int32)).astype(f32)
    angles = places[:, None] * inverse[None, :]
    half_cos, half_sin = jnp.cos(angles), jnp.sin(angles)
    cosine = jnp.concatenate([half_cos, half_cos], axis=1)
    sine = jnp.concatenate([-half_sin, half_sin], axis=1)

    def turn_keys(rows, sign):
        parts = []
        for h in range(KEY_VALUE_HEADS):
            piece = rows[:, h * HEAD_SIZE : (h + 1) * HEAD_SIZE]
            swapped = jnp.concatenate([piece[:, HEAD_SIZE // 2 :], piece[:, : HEAD_SIZE // 2]], axis=1)
            parts.append(piece * cosine + swapped * (sign * sine))
        return jnp.concatenate(parts, axis=1)

    pre = dot_nn(after(first_hidden, picked), qkv_low)
    keys_local = turn_keys(pre[:, MODEL_WIDTH : MODEL_WIDTH + KV], 1.0).astype(bf16)
    kv_local = jnp.concatenate([keys_local, pre[:, MODEL_WIDTH + KV :].astype(bf16)], axis=1)

    chips = shards // 2
    core = place % 2
    same = [kv_local] + [y_up(kv_local, s) for s in range(1, chips)]
    other = [core_shift(v, 1) for v in same]
    blocks = []
    for distance in range(shards):
        s = distance // 2
        if distance % 2 == 0:
            blocks.append(same[s])
        elif s + 1 < chips:
            blocks.append(jnp.where(core == 1, other[s], other[s + 1]))
        else:
            blocks.append(other[s])
    kv_blocks = jnp.stack(blocks)

    down_low = lax.all_gather(after(expert_out, kv_local).astype(bf16), "fsdp", axis=0)
    gate_up_low = lax.all_gather(after(expert_in, kv_local).astype(bf16), "fsdp", axis=0)

    level_two = after(z_shift(level_one, 1), kv_blocks)
    level_three = z_shift(level_two, 1)

    place_arg = place.astype(jnp.int32).reshape(1)
    attended, log_total, query_rows = attend(
        place_arg, pre, cosine, sine, after(kv_blocks, level_two)
    )
    residual = inputs + dot_nn(after(attended, level_three), output_low)
    scale_two = lax.rsqrt(jnp.mean(residual * residual, axis=1, keepdims=True) + NORM_EPS)
    normed_two = residual * scale_two
    hidden_two = (normed_two * gain_two).astype(bf16)

    upstream_swapped[1] = after(upstream_swapped[1], attended)
    upstream_swapped.append(swap(pick(after(level_two, attended), 2), upstream_swapped[1]))
    last_picked = pick(after(level_three, hidden_two), 3)

    levels = [hidden_two, z_shift(hidden_two, 1)]
    logits_t = lax.dot_general(
        router_low, hidden_two, (((0,), (1,)), ((), ())), preferred_element_type=f32
    )
    all_ids = jnp.arange(experts_all, dtype=jnp.int32)
    chosen_t = (routes_t[:, None, :] == all_ids[None, :, None]).astype(f32)
    gate_weights = jax.nn.softmax(jnp.sum(chosen_t * logits_t[None], axis=1), axis=0)
    gates_of = [gate_weights, z_shift(gate_weights, 1)]
    picked = pick(hidden_two, 0)
    hidden_swapped = [swap(picked, upstream_swapped[-1])]
    levels[1] = after(levels[1], picked)
    picked = pick(levels[1], 1)
    hidden_swapped.append(swap(picked, hidden_swapped[-1]))
    upstream_swapped.append(swap(last_picked, hidden_swapped[-1]))
    for k in range(2, depth):
        levels.append(after(z_shift(levels[-1], 1), picked, gates_of[1]))
        if k == depth - 1:
            upstream_pieces = order(after(upstream_swapped, levels[k - 1]))
            inner = inner_rows(upstream_pieces, down_low)
            gates_of[-1] = after(gates_of[-1], inner)
            levels[k] = after(levels[k], gates_of[-1])
        gates_of.append(z_shift(gates_of[-1], 1))
        picked = pick(levels[k], k)
        hidden_swapped.append(swap(picked, hidden_swapped[-1], upstream_swapped[-1]))
    gates_near = jnp.sum(named * jnp.stack(gates_of)[:, None], axis=2)
    row_gates = jnp.sum(jnp.where(picks, gates_near[:, :, None, :], 0.0), axis=3)
    row_gates = row_gates.reshape(depth, wide, experts_local, CAP)
    away_gates = [x_shift(row_gates[:, r], r) for r in range(1, wide)]
    hidden_swapped, away_gates = after((hidden_swapped, away_gates), levels[-1])
    hidden_pieces = order(hidden_swapped)
    row_gates = jnp.stack([row_gates[:, 0]] + away_gates)
    row_gates = row_gates.transpose(2, 0, 1, 3).reshape(experts_local, wide * depth * CAP, 1)

    scaled_hidden, gate_side, up_side, gate_dots, back_pieces = core_rows(
        hidden_pieces, gate_up_low, inner, row_gates
    )
    steps = swap_back(back_pieces)
    gate_dots = gate_dots.reshape(experts_local, wide, depth, CAP)
    away_dots = [x_shift(gate_dots[:, r], -r) for r in range(1, wide)]
    down_term = down_grads(upstream_pieces, scaled_hidden, shards)
    held = []
    ring_step(held, after(steps[1], down_term))
    out_part = lax.psum_scatter(after(down_term, held[0]), "fsdp", scatter_dimension=0)
    arrived = ring_send(held)
    in_term = in_grads(hidden_pieces, *after((gate_side, up_side), held[0]), shards)
    gate_dots = jnp.stack([gate_dots[:, 0]] + after(away_dots, in_term))
    gate_dots = gate_dots.transpose(2, 0, 1, 3).reshape(depth, near, CAP)
    token_dots = jnp.sum(jnp.where(picks, gate_dots[:, :, :, None], 0.0), axis=2)
    choice_dots = jnp.sum(named * token_dots[:, :, None, :], axis=1)
    lane = z_shift(choice_dots[1], 1)
    ring_step(held, after(steps[2], in_term, lane), arrived)
    in_part = lax.psum_scatter(after(in_term, held[1]), "fsdp", scatter_dimension=0)
    lane = z_shift(lane + choice_dots[2], 1)
    arrived = ring_send(held)
    results = result_rows(after(scaled_hidden, held[1]), down_low, len(back_pieces))
    ring_step(held, after(steps[3], results, lane), arrived)
    result_steps = swap_back(results, steps[0])
    lane = z_shift(lane + choice_dots[3], 1)
    arrived = ring_send(held)
    gate_grad = lane + choice_dots[0]
    picked_grad = gate_weights * (
        gate_grad - jnp.sum(gate_weights * gate_grad, axis=0, keepdims=True)
    )
    logit_grad_t = jnp.sum(chosen_t * picked_grad[:, None, :], axis=0).astype(bf16)
    router_term = dot_nn(logit_grad_t, hidden_two)
    hidden_back = ring_step(held, after(steps[0], router_term), arrived)
    hidden_two_grad = hidden_back + lax.dot_general(
        logit_grad_t, router_low, (((0,), (1,)), ((), ())), preferred_element_type=f32
    )

    gain_two_term = jnp.sum(hidden_two_grad * normed_two, axis=0)
    scaled_two = hidden_two_grad * gain_two
    residual_grad = upstream + scale_two * (
        scaled_two - normed_two * jnp.mean(scaled_two * normed_two, axis=1, keepdims=True)
    )
    branch_grad = residual_grad.astype(bf16)
    attended_grad = dot_nt(branch_grad, output_low).astype(bf16)
    result_held = []
    ring_step(result_held, after(result_steps[1], hidden_back))
    attended_grad = after(attended_grad, result_held[0], out_part)
    arrived = ring_send(result_held)
    pre_grad, key_back, value_back = attend_back(
        place_arg, query_rows, kv_blocks, attended, attended_grad, log_total, cosine, sine
    )

    def extra_rows(*terms):
        used = sum(t.shape[0] for t in terms)
        return jnp.concatenate(list(terms) + [jnp.zeros((128 - used, MODEL_WIDTH), f32)], axis=0)

    def send_parts(parts, index, shift):
        count = parts.shape[0]
        return [lax.dynamic_index_in_dim(parts, index, 0, keepdims=False)] + [
            shift(lax.dynamic_index_in_dim(parts, (index + s) % count, 0, keepdims=False), s)
            for s in range(1, count)
        ]

    def add_parts(parts):
        return functools.reduce(lambda total, part: total + part.astype(f32), parts[1:], parts[0].astype(f32)).astype(bf16)

    def join(part, index, count, shift):
        whole = jnp.zeros((count,) + part.shape, part.dtype)
        for s in range(count):
            piece = shift(part, s) if s else part
            whole = lax.dynamic_update_index_in_dim(whole, piece, (index - s) % count, 0)
        return whole

    def core_parts(terms):
        parts = terms.reshape(chips, 2, shard_rows, terms.shape[1]).transpose(1, 0, 2, 3)
        return send_parts(parts, core, core_shift)

    def y_parts(part):
        return send_parts(part, place // 2, y_shift)

    def x_parts(part):
        return send_parts(part.reshape(wide, shard_rows // wide, part.shape[1]), column, x_shift)

    def z_total(part):
        columns = part.shape[1]
        part = add_parts(send_parts(part.reshape(depth, shard_rows // wide // depth, columns), level, z_shift))
        part = join(part, level, depth, z_shift).reshape(shard_rows // wide, columns)
        return join(part, column, wide, x_shift).reshape(shard_rows, columns).astype(f32)

    kv_back = jnp.concatenate([key_back, value_back], axis=2)
    none = jnp.zeros_like(kv_back[:1])
    mate = jnp.where(core == 1, kv_back[1::2], jnp.concatenate([none, kv_back[1:-1:2]], axis=0))
    mate = core_shift(mate, 1)
    kv_chip = kv_back[0::2].astype(f32) + mate.astype(f32)
    kv_low = kv_chip.astype(bf16)
    kv_parts = [
        lax.ppermute(kv_low[s], "fsdp", [(a + 2 * s, a) for a in range(shards - 2 * s)]) for s in range(1, chips)
    ]
    kv_grad = functools.reduce(lambda total, part: total + part.astype(f32), kv_parts, kv_chip[0])
    key_pre_grad = turn_keys(kv_grad[:, :KV], -1.0)
    kv_pre_grad = jnp.concatenate([key_pre_grad, kv_grad[:, KV:]], axis=1).astype(bf16)

    front_terms = weight_grads(first_hidden, [pre_grad, kv_pre_grad])
    front_part = lax.psum_scatter(after(front_terms, in_part), "fsdp", scatter_dimension=0, tiled=True)
    front_sum = lax.psum(front_part, "expert").astype(f32)

    ring_step(result_held, after(result_steps[2], front_terms), arrived)
    arrived = ring_send(result_held)
    pre_late, kv_late = after((pre_grad, kv_pre_grad), result_held[1])
    hidden_one_grad = dot_nt(pre_late, qkv_low[:, :MODEL_WIDTH]) + dot_nt(kv_late, qkv_low[:, MODEL_WIDTH:])
    gain_one_term = jnp.sum(hidden_one_grad * normed_one, axis=0)
    scaled_one = hidden_one_grad * gain_one
    input_grad = (
        residual_grad
        + scale_one
        * (scaled_one - normed_one * jnp.mean(scaled_one * normed_one, axis=1, keepdims=True))
    ).astype(bf16)
    back_terms = weight_grads(
        attended, [branch_grad], extra_rows(router_term, gain_one_term[None], gain_two_term[None])
    )
    back_parts = core_parts(back_terms)
    ring_step(result_held, after(result_steps[3], back_terms), arrived)
    arrived = ring_send(result_held)
    out_state = adamw_update(
        expert_out,
        out_first,
        out_second,
        after(out_part, result_held[2]).astype(f32),
        0.5 / math.sqrt(FF // 8),
        DECAY,
    )
    back_part = add_parts(after(back_parts, out_state))
    back_parts = y_parts(back_part)
    in_state = adamw_update(
        expert_in,
        in_first,
        in_second,
        after(in_part, back_part).astype(f32),
        0.5 / math.sqrt(MODEL_WIDTH),
        DECAY,
    )
    moe_out = ring_step(result_held, after(result_steps[0], in_state), arrived)
    layer_out = (residual + moe_out).astype(bf16)
    back_sum = z_total(add_parts(x_parts(add_parts(after(back_parts, layer_out)))))
    output_sum = back_sum[:, :MODEL_WIDTH]
    router_sum = back_sum[:, MODEL_WIDTH : MODEL_WIDTH + experts_all]
    query_sum = front_sum[:, :MODEL_WIDTH]
    key_sum = front_sum[:, MODEL_WIDTH : MODEL_WIDTH + KV]
    value_sum = front_sum[:, MODEL_WIDTH + KV : QKV]
    at = MODEL_WIDTH + experts_all
    gain_sum = back_sum[:, at : at + 2].T

    rate = 0.5 / math.sqrt(MODEL_WIDTH // 2)
    return (
        layer_out,
        input_grad,
        *adamw_update(gains, gains_first, gains_second, gain_sum, GAIN_RATE, 0.0),
        *adamw_update(query_weight, query_first, query_second, query_sum, rate, DECAY),
        *adamw_update(key_matrix, key_moment_first, key_moment_second, key_sum, rate, DECAY),
        *adamw_update(
            value_matrix,
            value_moment_first,
            value_moment_second,
            value_sum,
            0.5 / math.sqrt(MODEL_WIDTH),
            DECAY,
        ),
        *adamw_update(
            output_weight, output_first, output_second, output_sum, 0.5 / math.sqrt(MODEL_WIDTH // 32), DECAY
        ),
        *adamw_update(
            router_weight, router_first, router_second, router_sum, 0.5 / math.sqrt(4 * MODEL_WIDTH), DECAY
        ),
        *in_state,
        *out_state,
    )


def solution(mesh):
    rows = P(("expert", "fsdp"), None)
    gains = P(None, "fsdp")
    matrix = P("fsdp", None)
    wide = P("expert", "fsdp", None)
    tall = P("expert", None, "fsdp")
    return jax.shard_map(
        body,
        mesh=mesh,
        in_specs=(rows,) * 3 + (gains,) * 3 + (matrix,) * 15 + (wide,) * 3 + (tall,) * 3,
        out_specs=(rows,) * 2 + (gains,) * 3 + (matrix,) * 15 + (wide,) * 3 + (tall,) * 3,
        check_vma=False,
    )
```

time: 1000 us -> 895 us (0.90)
  starting transfers between devices: 119 us -> 68.4 us
  local copies, waits for them, and re-layouts: 82 us -> 48.4 us
  matrix products: 56 us -> 32.9 us
  Pallas kernels: 183 us -> 197 us
    ppermute x45 -> x27, waiting for transfers between devices: 224 us -> 126 us  [z_shift(): lax.ppermute(value, 'expert', [(a * wide + b, (a + by) % depth * wide + b...]
    psum x0 -> x1, waiting for transfers between devices: none -> 72.3 us  [body(): front_sum = lax.psum(front_part, 'expert').astype(f32)]
    ppermute x6 -> x2, waiting for transfers between devices: 25.8 us -> 82 us  [the longest x1 59.4 us: body(): lax.ppermute(kv_low[s], 'fsdp', [(a + 2 * s, a) for a in range(shards - 2...]
    ppermute x45 -> x27, starting transfers between devices: 74.2 us -> 35.9 us  [z_shift(): lax.ppermute(value, 'expert', [(a * wide + b, (a + by) % depth * wide + b...]
    ppermute x22 -> x20, waiting for transfers between devices: 154 us -> 115 us  [x_shift(): lax.ppermute(value, 'expert', [(a * wide + b, a * wide + (b + by) % wide)...]
    dot_general x16 -> x0, matrix products: 26.5 us -> none  [dot_tn(): lax.dot_general(left, right, (((0,), (0,)), ((), ())), preferred_element_...]
    slice x23 -> x2, local copies, waits for them, and re-layouts: 15.2 us -> 0.04 us  [the longest x1 0.04 us: body(): kv_back[1:-1:2]]
    pallas_call x14 -> x21, Pallas kernels: 137 us -> 151 us  [the longest x1 36.4 us: core_rows(): pl.pallas_call(functools.partial(core_kernel, count), out_shape=(low, low...]
  transfers between devices with their start and end apart: 83 -> 62, of which waited for: 37 -> 34; matrix products, arithmetic and copies ran while one was open for 21% -> 17% of each run, Pallas kernels for 15% -> 18%
where the time goes in v2:
time: 895 us; the launch traced here: 885 us
  waiting for transfers between devices  418 us (47%)
  Pallas kernels  197 us (22%)
  other arithmetic  104 us (12%)
  starting transfers between devices  68.4 us (8%)
  local copies, waits for them, and re-layouts  48.4 us (5%)
  matrix products  32.9 us (4%)
  between operations  16.3 us (2%)
    ppermute x27, waiting for transfers between devices, z_shift(): lax.ppermute(value, 'expert', [(a * wide + b, (a + by) % depth * wide + b...  126 us
    ppermute x20, waiting for transfers between devices, x_shift(): lax.ppermute(value, 'expert', [(a * wide + b, a * wide + (b + by) % wide)...  115 us
    psum x1, waiting for transfers between devices, body(): front_sum = lax.psum(front_part, 'expert').astype(f32)  72.3 us
    ppermute x1, waiting for transfers between devices, body(): lax.ppermute(kv_low[s], 'fsdp', [(a + 2 * s, a) for a in range(shards - 2...  59.4 us
    sub x7, other arithmetic, adamw_update(): weight - step_rate * (first_hat / (jnp.sqrt(second_hat) + ADAM_EPS) + dec...  50.9 us
    pallas_call x1, Pallas kernels, core_rows(): pl.pallas_call(functools.partial(core_kernel, count), out_shape=(low, low...  36.4 us
    ppermute x27, starting transfers between devices, z_shift(): lax.ppermute(value, 'expert', [(a * wide + b, (a + by) % depth * wide + b...  35.9 us
    pallas_call x8, Pallas kernels, ring_rows(): pl.pallas_call(functools.partial(ring_kernel, len(pieces)), out_shape=jax...  29.8 us
  transfers between devices with their start and end apart: 62, of which 34 were waited for; matrix products, arithmetic and copies ran while one was open for 17% of the time, Pallas kernels for 18%

profile of v2, /device:TPU:8, one launch (start us, length us, event | category | flops | bytes accessed | tf_op | source)
XLA Modules:
  0.0 885.0 jit_solution(1608002321602535069)
XLA Ops:
  26.0 4.5 pick_rows.8
  36.8 17.1 %collective-permute-done.4.refs_4_ = bf16[320,1536]{1,0:T(8,128)(2,1)} collective-permute-done((bf16[320,1536]{1,0:T(8,128)(2,1)}, bf16[320,1536]{1,0:T(8,128)(2,1)}, u32[]{:S(2)}, u32[]{:S(2)}) %collective-permute-start.4) | collective-permute-done | bytes 983072 | tf_op jit(solution)/shard_map/ppermute | solution.py:559
  53.8 5.4 collective-permute-done.3.rows
  70.0 6.1 fusion.2.pre
  80.9 6.5 convert_element_type.172
  92.2 22.6 %collective-permute-done.6 = bf16[512,512]{1,0:T(8,128)(2,1)} collective-permute-done((bf16[512,512]{1,0:T(8,128)(2,1)}, bf16[512,512]{1,0:T(8,128)(2,1)}, u32[]{:S(2)}, u32[]{:S(2)}) %collective-permute-start.6) | collective-permute-done | bytes 524320 | tf_op jit(solution)/shard_map/ppermute | solution.py:576
  127.5 14.3 %attend.1 = (bf16[512,1536]{1,0:T(8,128)(2,1)}, f32[12,1,512]{2,1,0:T(1,128)}, bf16[512,1536]{1,0:T(8,128)(2,1)}) custom-call(s32[1]{0:T(128)} %bitcast.place, f32[512,2048]{1,0:T(8,128)} %copy-done.39, f32[512,128]{1,0:T(8,128)} %get-tuple-element.460.cosine, f32[512,128]{1,0:T(8,128)} %copy-done.40, bf16[4,512,512]{2,1,0:T(8,128)(2,1)} %pad_maximum_fusion.keys.values, ...), custom_call_target="tpu_custom_call" | custom-call | flops 1000000000 | bytes 1000000 | tf_op jit(solution)/shard_map/attend/pallas_call | solution.py:106
  141.8 19.3 %collective-permute-done.9.rows = bf16[512,1536]{1,0:T(8,128)(2,1)S(1)} collective-permute-done((bf16[512,1536]{1,0:T(8,128)(2,1)}, bf16[512,1536]{1,0:T(8,128)(2,1)S(1)}, u32[]{:S(2)}, u32[]{:S(2)}) %collective-permute-start.9) | collective-permute-done | bytes 1572896 | tf_op jit(solution)/shard_map/ppermute | solution.py:552
  162.3 6.0 multiply_reduce_fusion.2
  176.5 19.4 %collective-permute-done.11.refs_6_ = bf16[320,1536]{1,0:T(8,128)(2,1)S(1)} collective-permute-done((bf16[320,1536]{1,0:T(8,128)(2,1)S(1)}, bf16[320,1536]{1,0:T(8,128)(2,1)S(1)}, u32[]{:S(2)}, u32[]{:S(2)}) %collective-permute-start.11) | collective-permute-done | bytes 983072 | tf_op jit(solution)/shard_map/ppermute | solution.py:559
  197.4 8.2 collective-permute-done.13.rows
  205.6 4.1 pick_rows.12
  209.7 8.1 collective-permute-done.12.refs_4_
  221.3 20.6 %collective-permute-done.16 = f32[4,512]{1,0:T(4,128)S(1)} collective-permute-done((f32[4,512]{1,0:T(4,128)S(1)}, f32[4,512]{1,0:T(4,128)S(1)}, u32[]{:S(2)}, u32[]{:S(2)}) %collective-permute-start.16) | collective-permute-done | bytes 8224 | tf_op jit(solution)/shard_map/ppermute | solution.py:552
  251.6 15.2 %collective-permute-done.17.refs_7_ = bf16[320,1536]{1,0:T(8,128)(2,1)S(1)} collective-permute-done((bf16[320,1536]{1,0:T(8,128)(2,1)S(1)}, bf16[320,1536]{1,0:T(8,128)(2,1)S(1)}, u32[]{:S(2)}, u32[]{:S(2)}) %collective-permute-start.17) | collective-permute-done | bytes 983072 | tf_op jit(solution)/shard_map/ppermute | solution.py:559
  270.5 6.7 collective-permute-done.19.rows
  278.4 12.9 %inner_rows.1.refs_9_ = bf16[4,640,768]{2,1,0:T(8,128)(2,1)} custom-call(bf16[320,1536]{1,0:T(8,128)(2,1)} %copy-done.20, bf16[320,1536]{1,0:T(8,128)(2,1)} %copy-done.21, bf16[320,1536]{1,0:T(8,128)(2,1)} %copy-done.24, bf16[320,1536]{1,0:T(8,128)(2,1)} %copy-done.27, bf16[320,1536]{1,0:T(8,128)(2,1)} %collective-permute-done.4.refs_4_, ...), custom_call_target="tpu_custom_call" | custom-call | flops 6039797760 | bytes 20000000 | tf_op jit(solution)/shard_map/inner_rows/pallas_call | solution.py:248
  295.8 5.1 collective-permute-done.22
  302.3 11.9 %collective-permute-done.23 = f32[4,4,80]{2,0,1:T(4,128)S(1)} collective-permute-done((f32[4,4,80]{2,0,1:T(4,128)S(1)}, f32[4,4,80]{2,0,1:T(4,128)S(1)}, u32[]{:S(2)}, u32[]{:S(2)}) %collective-permute-start.23) | collective-permute-done | bytes 5152 | tf_op jit(solution)/shard_map/ppermute | solution.py:559
  316.9 36.4 %core_rows.1 = (bf16[4,640,768]{2,1,0:T(8,128)(2,1)}, bf16[4,640,768]{2,1,0:T(8,128)(2,1)}, bf16[4,640,768]{2,1,0:T(8,128)(2,1)}, f32[4,640,1]{2,1,0:T(8,128)}, ...) custom-call(bf16[320,1536]{1,0:T(8,128)(2,1)} %copy-done.22, ...), custom_call_target="tpu_custom_call" | custom-call | flops 24159191040 | bytes 60000000 | tf_op jit(solution)/shard_map/core_rows/pallas_call | solution.py:305
  354.8 13.8 %down_grads.1 = bf16[4,4,768,384]{3,2,1,0:T(8,128)(2,1)} custom-call(bf16[320,1536]{1,0:T(8,128)(2,1)} %copy-done.20, bf16[320,1536]{1,0:T(8,128)(2,1)} %copy-done.21, bf16[320,1536]{1,0:T(8,128)(2,1)} %copy-done.24, bf16[320,1536]{1,0:T(8,128)(2,1)} %copy-done.27, bf16[320,1536]{1,0:T(8,128)(2,1)} %collective-permute-done.4.refs_4_, ...), custom_call_target="tpu_custom_call" | custom-call | flops 6039797760 | bytes 22000000 | tf_op jit(solution)/shard_map/down_grads/pallas_call | solution.py:364
  368.6 4.2 collective-permute-done.24.refs_2_
  383.4 20.9 %in_grads.1 = bf16[4,4,384,1536]{3,2,1,0:T(8,128)(2,1)} custom-call(bf16[320,1536]{1,0:T(8,128)(2,1)} %copy-done.22, bf16[320,1536]{1,0:T(8,128)(2,1)} %copy-done.23, bf16[320,1536]{1,0:T(8,128)(2,1)} %copy-done.25, bf16[320,1536]{1,0:T(8,128)(2,1)} %copy-done.26, bf16[320,1536]{1,0:T(8,128)(2,1)} %copy-done.89, ...), custom_call_target="tpu_custom_call" | custom-call | flops 12079595520 | bytes 35000000 | tf_op jit(solution)/shard_map/in_grads/pallas_call | solution.py:392
  423.9 18.0 %collective-permute-done.29.refs_2_ = bf16[320,1536]{1,0:T(8,128)(2,1)S(1)} collective-permute-done((bf16[320,1536]{1,0:T(8,128)(2,1)S(1)}, bf16[320,1536]{1,0:T(8,128)(2,1)S(1)}, u32[]{:S(2)}, u32[]{:S(2)}) %collective-permute-start.29) | collective-permute-done | bytes 983072 | tf_op jit(solution)/shard_map/ppermute | solution.py:559
  442.8 12.4 %result_rows.1 = (bf16[320,1536]{1,0:T(8,128)(2,1)}, bf16[320,1536]{1,0:T(8,128)(2,1)}, bf16[320,1536]{1,0:T(8,128)(2,1)}, bf16[320,1536]{1,0:T(8,128)(2,1)}, bf...) custom-call(bf16[4,640,768]{2,1,0:T(8,128)(2,1)} %get-tuple-element., ...), custom_call_target="tpu_custom_call" | custom-call | flops 6039797760 | bytes 22000000 | tf_op jit(solution)/shard_map/result_rows/pallas_call | solution.py:336
  467.6 16.5 %collective-permute-done.35 = f32[4,512]{1,0:T(4,128)S(1)} collective-permute-done((f32[4,512]{1,0:T(4,128)S(1)}, f32[4,512]{1,0:T(4,128)S(1)}, u32[]{:S(2)}, u32[]{:S(2)}) %collective-permute-start.35) | collective-permute-done | bytes 8224 | tf_op jit(solution)/shard_map/ppermute | solution.py:552
  491.3 4.7 multiply_reduce_fusion
  504.4 17.8 %attend_back.1 = (bf16[512,1536]{1,0:T(8,128)(2,1)}, bf16[4,512,256]{2,1,0:T(8,128)(2,1)}, bf16[4,512,256]{2,1,0:T(8,128)(2,1)}) custom-call(s32[1]{0:T(128)} %bitcast.place, bf16[512,1536]{1,0:T(8,128)(2,1)} %get-tuple-element.243.query, bf16[4,512,512]{2,1,0:T(8,128)(2,1)} %pad_maximum_fusion.keys.values, ...), custom_call_target="tpu_custom_call" | custom-call | flops 1000000000 | bytes 1000000 | tf_op jit(solution)/shard_map/attend_back/pallas_call | solution.py:182
  533.1 59.4 %collective-permute-done.39 = bf16[512,512]{1,0:T(8,128)(2,1)} collective-permute-done((bf16[512,512]{1,0:T(8,128)(2,1)}, bf16[512,512]{1,0:T(8,128)(2,1)}, u32[]{:S(2)}, u32[]{:S(2)}) %collective-permute-start.39) | collective-permute-done | bytes 524320 | tf_op jit(solution)/shard_map/ppermute | solution.py:848
  595.5 7.4 weight_grads.2
  610.6 7.0 fusion.18
  618.6 6.7 weight_grads.3
  625.3 5.2 dynamic-slice_bitcast_fusion
  631.5 14.7 %collective-permute-done.43.refs_3_ = bf16[512,1536]{1,0:T(8,128)(2,1)S(1)} collective-permute-done((bf16[512,1536]{1,0:T(8,128)(2,1)S(1)}, bf16[512,1536]{1,0:T(8,128)(2,1)S(1)}, u32[]{:S(2)}, u32[]{:S(2)}) %collective-permute-start.43) | collective-permute-done | bytes 1572896 | tf_op jit(solution)/shard_map/ppermute | solution.py:552
  647.4 4.4 ring_rows.14
  651.9 11.5 %multiply_subtract_fusion.1 = (f32[4,768,384]{2,1,0:T(8,128)}, f32[4,768,384]{2,1,0:T(8,128)}, f32[4,768,384]{2,1,0:T(8,128)}) fusion(f32[4,768,384]{2,1,0:T(8,128)} %param.51, bf16[4,768,384]{2,1,0:T(8,128)(2,1)} %bitcast.166, f32[4,768,384]{2,1,0:T(8,128)} %param.52, f32[4,768,384]{2,1,0:T(8,128)} %param.53), kind=kLoop, calls=%fused_computation.26 | loop fusion | flops 18874368 | bytes 30670848 | tf_op jit(solution)/shard_map/sub | solution.py:503
  667.9 4.7 collective-permute-start.45
  672.6 22.9 %multiply_subtract_fusion = (f32[4,384,1536]{2,1,0:T(8,128)}, f32[4,384,1536]{2,1,0:T(8,128)}, f32[4,384,1536]{2,1,0:T(8,128)}) fusion(f32[4,384,1536]{2,1,0:T(8,128)} %param.48, bf16[4,384,1536]{2,1,0:T(8,128)(2,1)S(1)} %bitcast.161, f32[4,384,1536]{2,1,0:T(8,128)} %param.49, f32[4,384,1536]{2,1,0:T(8,128)} %param.50), kind=kLoop, calls=%fused_computation.4 | loop fusion | flops 37748736 | bytes 61341696 | tf_op jit(solution)/shard_map/sub | solution.py:503
  695.5 5.8 ring_rows.15
  701.3 5.5 fusion.22
  706.8 14.3 %collective-permute-done.45 = bf16[384,1664]{1,0:T(8,128)(2,1)} collective-permute-done((bf16[384,1664]{1,0:T(8,128)(2,1)}, bf16[384,1664]{1,0:T(8,128)(2,1)}, u32[]{:S(2)}, u32[]{:S(2)}) %collective-permute-start.45) | collective-permute-done | bytes 1277984 | tf_op jit(solution)/shard_map/ppermute | solution.py:573
  723.0 10.8 %collective-permute-done.46 = bf16[192,1664]{1,0:T(8,128)(2,1)S(1)} collective-permute-done((bf16[192,1664]{1,0:T(8,128)(2,1)S(1)}, bf16[192,1664]{1,0:T(8,128)(2,1)S(1)}, u32[]{:S(2)}, u32[]{:S(2)}) %collective-permute-start.46) | collective-permute-done | bytes 639008 | tf_op jit(solution)/shard_map/ppermute | solution.py:559
  735.6 6.8 collective-permute-start.48
  744.4 9.3 %collective-permute-done.48 = bf16[48,1664]{1,0:T(8,128)(2,1)S(1)} collective-permute-done((bf16[48,1664]{1,0:T(8,128)(2,1)S(1)}, bf16[48,1664]{1,0:T(8,128)(2,1)S(1)}, u32[]{:S(2)}, u32[]{:S(2)}) %collective-permute-start.48) | collective-permute-done | bytes 159776 | tf_op jit(solution)/shard_map/ppermute | solution.py:552
  770.7 8.2 collective-permute-done.53
  788.0 7.3 multiply_subtract_fusion.2
  795.3 72.3 %all-reduce.3.cloned.1.call-done = bf16[384,2048]{1,0:T(8,128)(2,1)} async-done(((bf16[384,2048]{1,0:T(8,128)(2,1)}), bf16[384,2048]{1,0:T(8,128)(2,1)}) %all-reduce.3.cloned.1.call-update) | async-done | bytes 1572880 | tf_op jit(solution)/shard_map/psum | solution.py:856
  869.7 6.1 multiply_subtract_fusion.3
  (451 shorter events, 219.7 us)
Async XLA Ops:
  7.2 60.3 %all-gather.7.cloned.1.call-start = ((), (), s32[]{:S(2)}) async-start(), calls=%async_computation.3 | async-start | bytes 8355840 | tf_op jit(solution)/shard_map/all_gather | solution.py:586
  17.6 144.8 %all-gather.9.cloned.1.call-start = ((), (), s32[]{:S(2)}) async-start(), calls=%async_computation.4 | async-start | bytes 5898240 | tf_op jit(solution)/shard_map/all_gather | solution.py:594
  18.8 259.6 %all-gather.11.cloned.1.call-start = ((), (), s32[]{:S(2)}) async-start(), calls=%async_computation.9 | async-start | bytes 11796480 | tf_op jit(solution)/shard_map/all_gather | solution.py:700
  23.5 35.7 %collective-permute-start.3 = (bf16[512,1536]{1,0:T(8,128)(2,1)}, bf16[512,1536]{1,0:T(8,128)(2,1)}, u32[]{:S(2)}, u32[]{:S(2)}) collective-permute-start(bf16[512,1536]{1,0:T(8,128)(2,1)} %rows.1), channel_id=1, source_target_pairs={{0,8},{4,12},{8,16},{12,20},{16,24},{20,28},{24,0},{28,4},{1,9},{5... | collective-permute-start | bytes 4718600 | tf_op jit(solution)/shard_map/ppermute | solution.py:552
  31.4 22.4 %collective-permute-start.4 = (bf16[320,1536]{1,0:T(8,128)(2,1)}, bf16[320,1536]{1,0:T(8,128)(2,1)}, u32[]{:S(2)}, u32[]{:S(2)}) collective-permute-start(bf16[320,1536]{1,0:T(8,128)(2,1)} %bitcast.10), channel_id=1, source_target_pairs={{0,4},{4,0},{8,12},{12,8},{16,20},{20,16},{24,28},{28,24},{1,5},{5... | collective-permute-start | bytes 2949128 | tf_op jit(solution)/shard_map/ppermute | solution.py:559
  80.8 236.1 %all-gather.13.cloned.1.call-start = ((), (), s32[]{:S(2)}) async-start(), calls=%async_computation.10 | async-start | bytes 23592960 | tf_op jit(solution)/shard_map/all_gather | solution.py:701
  87.3 417.1 %reduce-scatter.6.cloned.1.call-start = ((), (), s32[]{:S(2)}) async-start(), calls=%async_computation.6 | async-start | bytes 11796480 | tf_op jit(solution)/shard_map/reduce_scatter | solution.py:761
  87.4 37.0 %collective-permute-start.8 = (bf16[512,1536]{1,0:T(8,128)(2,1)}, bf16[512,1536]{1,0:T(8,128)(2,1)}, u32[]{:S(2)}, u32[]{:S(2)}) collective-permute-start(bf16[512,1536]{1,0:T(8,128)(2,1)} %collective-permute-done.3.rows), channel_id=1, source_target_pairs={{0,8},{4,12},{8,16},{12,20},{16,24},{20,28},{24,0},{28,4},{1,9},{5... | collective-permute-start | bytes 4718600 | tf_op jit(solution)/shard_map/ppermute | solution.py:552
  88.9 25.9 %collective-permute-start.6 = (bf16[512,512]{1,0:T(8,128)(2,1)}, bf16[512,512]{1,0:T(8,128)(2,1)}, u32[]{:S(2)}, u32[]{:S(2)}) collective-permute-start(bf16[512,512]{1,0:T(8,128)(2,1)} %get-tuple-element.458), channel_id=1, source_target_pairs={{0,2},{1,3},{4,6},{5,7},{8,10},{9,11},{12,14},{13,15},{16,18},{17,... | collective-permute-start | bytes 1572872 | tf_op jit(solution)/shard_map/ppermute | solution.py:576
  92.2 22.6 %collective-permute-start.5 = (bf16[512,512]{1,0:T(8,128)(2,1)}, bf16[512,512]{1,0:T(8,128)(2,1)}, u32[]{:S(2)}, u32[]{:S(2)}) collective-permute-start(bf16[512,512]{1,0:T(8,128)(2,1)} %get-tuple-element.458), channel_id=1, source_target_pairs={{0,1},{1,0},{2,3},{3,2},{4,5},{5,4},{6,7},{7,6},{8,9},{9,8},{10,11... | collective-permute-start | bytes 1572872 | tf_op jit(solution)/shard_map/ppermute | solution.py:570
  124.4 36.8 %collective-permute-start.9 = (bf16[512,1536]{1,0:T(8,128)(2,1)}, bf16[512,1536]{1,0:T(8,128)(2,1)S(1)}, u32[]{:S(2)}, u32[]{:S(2)}) collective-permute-start(bf16[512,1536]{1,0:T(8,128)(2,1)} %collective-permute-done.8.rows), channel_id=1, source_target_pairs={{0,8},{4,12},{8,16},{12,20},{16,24},{20,28},{24,0},{28,4},{1,9},{5... | collective-permute-start | bytes 4718600 | tf_op jit(solution)/shard_map/ppermute | solution.py:552
  126.0 43.9 %collective-permute-start.10 = (bf16[320,1536]{1,0:T(8,128)(2,1)}, bf16[320,1536]{1,0:T(8,128)(2,1)}, u32[]{:S(2)}, u32[]{:S(2)}) collective-permute-start(bf16[320,1536]{1,0:T(8,128)(2,1)} %bitcast.17), channel_id=1, source_target_pairs={{0,4},{4,0},{8,12},{12,8},{16,20},{20,16},{24,28},{28,24},{1,5},{5... | collective-permute-start | bytes 2949128 | tf_op jit(solution)/shard_map/ppermute | solution.py:559
  168.7 36.9 %collective-permute-start.13 = (bf16[512,1536]{1,0:T(8,128)(2,1)S(1)}, bf16[512,1536]{1,0:T(8,128)(2,1)}, u32[]{:S(2)}, u32[]{:S(2)}) collective-permute-start(bf16[512,1536]{1,0:T(8,128)(2,1)S(1)} %multiply_convert_fusion.rows), channel_id=1, source_target_pairs={{0,8},{4,12},{8,16},{12,20},{16,24},{20,28},{24,0},{28,4},{1,9},{5... | collective-permute-start | bytes 4718600 | tf_op jit(solution)/shard_map/ppermute | solution.py:552
  173.2 22.8 %collective-permute-start.11 = (bf16[320,1536]{1,0:T(8,128)(2,1)S(1)}, bf16[320,1536]{1,0:T(8,128)(2,1)S(1)}, u32[]{:S(2)}, u32[]{:S(2)}) collective-permute-start(bf16[320,1536]{1,0:T(8,128)(2,1)S(1)} %bitcast.153), channel_id=1, source_target_pairs={{0,4},{4,0},{8,12},{12,8},{16,20},{20,16},{24,28},{28,24},{1,5},{5... | collective-permute-start | bytes 2949128 | tf_op jit(solution)/shard_map/ppermute | solution.py:559
  195.9 21.9 %collective-permute-start.12 = (bf16[320,1536]{1,0:T(8,128)(2,1)S(1)}, bf16[320,1536]{1,0:T(8,128)(2,1)S(1)}, u32[]{:S(2)}, u32[]{:S(2)}) collective-permute-start(bf16[320,1536]{1,0:T(8,128)(2,1)S(1)} %bitcast.151), channel_id=1, source_target_pairs={{0,4},{4,0},{8,12},{12,8},{16,20},{20,16},{24,28},{28,24},{1,5},{5... | collective-permute-start | bytes 2949128 | tf_op jit(solution)/shard_map/ppermute | solution.py:559
  205.6 36.3 %collective-permute-start.15 = (bf16[512,1536]{1,0:T(8,128)(2,1)}, bf16[512,1536]{1,0:T(8,128)(2,1)}, u32[]{:S(2)}, u32[]{:S(2)}) collective-permute-start(bf16[512,1536]{1,0:T(8,128)(2,1)} %collective-permute-done.13.rows), channel_id=1, source_target_pairs={{0,8},{4,12},{8,16},{12,20},{16,24},{20,28},{24,0},{28,4},{1,9},{5... | collective-permute-start | bytes 4718600 | tf_op jit(solution)/shard_map/ppermute | solution.py:552
  217.8 27.4 %collective-permute-start.14 = (bf16[320,1536]{1,0:T(8,128)(2,1)}, bf16[320,1536]{1,0:T(8,128)(2,1)}, u32[]{:S(2)}, u32[]{:S(2)}) collective-permute-start(bf16[320,1536]{1,0:T(8,128)(2,1)} %bitcast.18), channel_id=1, source_target_pairs={{0,4},{4,0},{8,12},{12,8},{16,20},{20,16},{24,28},{28,24},{1,5},{5... | collective-permute-start | bytes 2949128 | tf_op jit(solution)/shard_map/ppermute | solution.py:559
  221.0 20.8 %collective-permute-start.16 = (f32[4,512]{1,0:T(4,128)S(1)}, f32[4,512]{1,0:T(4,128)S(1)}, u32[]{:S(2)}, u32[]{:S(2)}) collective-permute-start(f32[4,512]{1,0:T(4,128)S(1)} %fusion.65), channel_id=1, source_target_pairs={{0,8},{4,12},{8,16},{12,20},{16,24},{20,28},{24,0},{28,4},{1,9},{5... | collective-permute-start | bytes 24584 | tf_op jit(solution)/shard_map/ppermute | solution.py:552
  241.9 35.3 %collective-permute-start.19 = (bf16[512,1536]{1,0:T(8,128)(2,1)}, bf16[512,1536]{1,0:T(8,128)(2,1)S(1)}, u32[]{:S(2)}, u32[]{:S(2)}) collective-permute-start(bf16[512,1536]{1,0:T(8,128)(2,1)} %collective-permute-done.15.rows), channel_id=1, source_target_pairs={{0,8},{4,12},{8,16},{12,20},{16,24},{20,28},{24,0},{28,4},{1,9},{5... | collective-permute-start | bytes 4718600 | tf_op jit(solution)/shard_map/ppermute | solution.py:552
  245.2 21.7 %collective-permute-start.17 = (bf16[320,1536]{1,0:T(8,128)(2,1)S(1)}, bf16[320,1536]{1,0:T(8,128)(2,1)S(1)}, u32[]{:S(2)}, u32[]{:S(2)}) collective-permute-start(bf16[320,1536]{1,0:T(8,128)(2,1)S(1)} %bitcast.152), channel_id=1, source_target_pairs={{0,4},{4,0},{8,12},{12,8},{16,20},{20,16},{24,28},{28,24},{1,5},{5... | collective-permute-start | bytes 2949128 | tf_op jit(solution)/shard_map/ppermute | solution.py:559
  266.9 27.2 %collective-permute-start.18 = (bf16[320,1536]{1,0:T(8,128)(2,1)}, bf16[320,1536]{1,0:T(8,128)(2,1)}, u32[]{:S(2)}, u32[]{:S(2)}) collective-permute-start(bf16[320,1536]{1,0:T(8,128)(2,1)} %bitcast.19), channel_id=1, source_target_pairs={{0,4},{4,0},{8,12},{12,8},{16,20},{20,16},{24,28},{28,24},{1,5},{5... | collective-permute-start | bytes 2949128 | tf_op jit(solution)/shard_map/ppermute | solution.py:559
  268.3 22.9 %collective-permute-start.20 = (f32[4,512]{1,0:T(4,128)S(1)}, f32[4,512]{1,0:T(4,128)S(1)}, u32[]{:S(2)}, u32[]{:S(2)}) collective-permute-start(f32[4,512]{1,0:T(4,128)S(1)} %collective-permute-done.16), channel_id=1, source_target_pairs={{0,8},{4,12},{8,16},{12,20},{16,24},{20,28},{24,0},{28,4},{1,9},{5... | collective-permute-start | bytes 24584 | tf_op jit(solution)/shard_map/ppermute | solution.py:552
  294.0 20.2 %collective-permute-start.21 = (bf16[320,1536]{1,0:T(8,128)(2,1)S(1)}, bf16[320,1536]{1,0:T(8,128)(2,1)S(1)}, u32[]{:S(2)}, u32[]{:S(2)}) collective-permute-start(bf16[320,1536]{1,0:T(8,128)(2,1)S(1)} %bitcast.150), channel_id=1, source_target_pairs={{0,4},{4,0},{8,12},{12,8},{16,20},{20,16},{24,28},{28,24},{1,5},{5... | collective-permute-start | bytes 2949128 | tf_op jit(solution)/shard_map/ppermute | solution.py:559
  353.3 19.5 %collective-permute-start.24 = (bf16[320,1536]{1,0:T(8,128)(2,1)}, bf16[320,1536]{1,0:T(8,128)(2,1)}, u32[]{:S(2)}, u32[]{:S(2)}) collective-permute-start(bf16[320,1536]{1,0:T(8,128)(2,1)} %get-tuple-element.207), channel_id=1, source_target_pairs={{0,4},{4,0},{8,12},{12,8},{16,20},{20,16},{24,28},{28,24},{1,5},{5... | collective-permute-start | bytes 2949128 | tf_op jit(solution)/shard_map/ppermute | solution.py:559
  378.4 273.3 %reduce-scatter.4.cloned.1.call-start = ((), (), s32[]{:S(2)}) async-start(), calls=%async_computation.5 | async-start | bytes 23592960 | tf_op jit(solution)/shard_map/reduce_scatter | solution.py:770
  380.9 23.5 %collective-permute-start.26 = (f32[4,4,80]{2,1,0:T(4,128)}, f32[4,4,80]{2,1,0:T(4,128)}, u32[]{:S(2)}, u32[]{:S(2)}) collective-permute-start(f32[4,4,80]{2,1,0:T(4,128)} %get-tuple-element.462), channel_id=1, source_target_pairs={{0,4},{4,0},{8,12},{12,8},{16,20},{20,16},{24,28},{28,24},{1,5},{5... | collective-permute-start | bytes 15368 | tf_op jit(solution)/shard_map/ppermute | solution.py:559
  382.3 32.4 %collective-permute-start.28 = (bf16[512,1536]{1,0:T(8,128)(2,1)}, bf16[512,1536]{1,0:T(8,128)(2,1)S(1)}, u32[]{:S(2)}, u32[]{:S(2)}) collective-permute-start(bf16[512,1536]{1,0:T(8,128)(2,1)} %copy-done.9), channel_id=1, source_target_pairs={{0,8},{4,12},{8,16},{12,20},{16,24},{20,28},{24,0},{28,4},{1,9},{5... | collective-permute-start | bytes 4718600 | tf_op jit(solution)/shard_map/ppermute | solution.py:552
  382.8 31.3 %collective-permute-start.25 = (bf16[320,1536]{1,0:T(8,128)(2,1)}, bf16[320,1536]{1,0:T(8,128)(2,1)S(1)}, u32[]{:S(2)}, u32[]{:S(2)}) collective-permute-start(bf16[320,1536]{1,0:T(8,128)(2,1)} %get-tuple-element.208), channel_id=1, source_target_pairs={{0,4},{4,0},{8,12},{12,8},{16,20},{20,16},{24,28},{28,24},{1,5},{5... | collective-permute-start | bytes 2949128 | tf_op jit(solution)/shard_map/ppermute | solution.py:559
  418.7 360.6 %reduce-scatter.8.cloned.1.call-start = ((), (), s32[]{:S(2)}) async-start(), calls=%async_computation.7 | async-start | bytes 7864320 | tf_op jit(solution)/shard_map/reduce_scatter | solution.py:855
  418.8 36.5 %collective-permute-start.36 = (bf16[512,1536]{1,0:T(8,128)(2,1)}, bf16[512,1536]{1,0:T(8,128)(2,1)S(1)}, u32[]{:S(2)}, u32[]{:S(2)}) collective-permute-start(bf16[512,1536]{1,0:T(8,128)(2,1)} %ring_rows.9), channel_id=1, source_target_pairs={{0,8},{4,12},{8,16},{12,20},{16,24},{20,28},{24,0},{28,4},{1,9},{5... | collective-permute-start | bytes 4718600 | tf_op jit(solution)/shard_map/ppermute | solution.py:552
  420.0 21.8 %collective-permute-start.29 = (bf16[320,1536]{1,0:T(8,128)(2,1)S(1)}, bf16[320,1536]{1,0:T(8,128)(2,1)S(1)}, u32[]{:S(2)}, u32[]{:S(2)}) collective-permute-start(bf16[320,1536]{1,0:T(8,128)(2,1)S(1)} %copy-done.92), channel_id=1, source_target_pairs={{0,4},{4,0},{8,12},{12,8},{16,20},{20,16},{24,28},{28,24},{1,5},{5... | collective-permute-start | bytes 2949128 | tf_op jit(solution)/shard_map/ppermute | solution.py:559
  421.5 33.7 %collective-permute-start.34 = (f32[4,512]{1,0:T(4,128)S(1)}, f32[4,512]{1,0:T(4,128)S(1)}, u32[]{:S(2)}, u32[]{:S(2)}) collective-permute-start(f32[4,512]{1,0:T(4,128)S(1)} %fusion.62), channel_id=1, source_target_pairs={{0,8},{4,12},{8,16},{12,20},{16,24},{20,28},{24,0},{28,4},{1,9},{5... | collective-permute-start | bytes 24584 | tf_op jit(solution)/shard_map/ppermute | solution.py:552
  441.9 21.8 %collective-permute-start.30 = (bf16[320,1536]{1,0:T(8,128)(2,1)S(1)}, bf16[320,1536]{1,0:T(8,128)(2,1)S(1)}, u32[]{:S(2)}, u32[]{:S(2)}) collective-permute-start(bf16[320,1536]{1,0:T(8,128)(2,1)S(1)} %copy-done.91), channel_id=1, source_target_pairs={{0,4},{4,0},{8,12},{12,8},{16,20},{20,16},{24,28},{28,24},{1,5},{5... | collective-permute-start | bytes 2949128 | tf_op jit(solution)/shard_map/ppermute | solution.py:559
  458.6 26.6 %collective-permute-start.37 = (bf16[512,1536]{1,0:T(8,128)(2,1)S(1)}, bf16[512,1536]{1,0:T(8,128)(2,1)S(1)}, u32[]{:S(2)}, u32[]{:S(2)}) collective-permute-start(bf16[512,1536]{1,0:T(8,128)(2,1)S(1)} %ring_rows.10), channel_id=1, source_target_pairs={{0,8},{4,12},{8,16},{12,20},{16,24},{20,28},{24,0},{28,4},{1,9},{5... | collective-permute-start | bytes 4718600 | tf_op jit(solution)/shard_map/ppermute | solution.py:552
  463.7 24.9 %collective-permute-start.31 = (bf16[320,1536]{1,0:T(8,128)(2,1)S(1)}, bf16[320,1536]{1,0:T(8,128)(2,1)S(1)}, u32[]{:S(2)}, u32[]{:S(2)}) collective-permute-start(bf16[320,1536]{1,0:T(8,128)(2,1)S(1)} %copy-done.95), channel_id=1, source_target_pairs={{0,4},{4,0},{8,12},{12,8},{16,20},{20,16},{24,28},{28,24},{1,5},{5... | collective-permute-start | bytes 2949128 | tf_op jit(solution)/shard_map/ppermute | solution.py:559
  464.6 19.5 %collective-permute-start.35 = (f32[4,512]{1,0:T(4,128)S(1)}, f32[4,512]{1,0:T(4,128)S(1)}, u32[]{:S(2)}, u32[]{:S(2)}) collective-permute-start(f32[4,512]{1,0:T(4,128)S(1)} %fusion.61), channel_id=1, source_target_pairs={{0,8},{4,12},{8,16},{12,20},{16,24},{20,28},{24,0},{28,4},{1,9},{5... | collective-permute-start | bytes 24584 | tf_op jit(solution)/shard_map/ppermute | solution.py:552
  529.6 63.0 %collective-permute-start.39 = (bf16[512,512]{1,0:T(8,128)(2,1)}, bf16[512,512]{1,0:T(8,128)(2,1)}, u32[]{:S(2)}, u32[]{:S(2)}) collective-permute-start(bf16[512,512]{1,0:T(8,128)(2,1)} %fusion.33), channel_id=1, source_target_pairs={{2,0},{3,1},{6,4},{7,5},{10,8},{11,9},{14,12},{15,13},{18,16},{19,... | collective-permute-start | bytes 1572872 | tf_op jit(solution)/shard_map/ppermute | solution.py:848
  530.9 71.9 %collective-permute-start.41 = (bf16[512,1536]{1,0:T(8,128)(2,1)S(1)}, bf16[512,1536]{1,0:T(8,128)(2,1)S(1)}, u32[]{:S(2)}, u32[]{:S(2)}) collective-permute-start(bf16[512,1536]{1,0:T(8,128)(2,1)S(1)} %copy-done.6), channel_id=1, source_target_pairs={{0,8},{4,12},{8,16},{12,20},{16,24},{20,28},{24,0},{28,4},{1,9},{5... | collective-permute-start | bytes 4718600 | tf_op jit(solution)/shard_map/ppermute | solution.py:552
  531.1 71.8 %collective-permute-start.40 = (bf16[320,1536]{1,0:T(8,128)(2,1)}, bf16[320,1536]{1,0:T(8,128)(2,1)}, u32[]{:S(2)}, u32[]{:S(2)}) collective-permute-start(bf16[320,1536]{1,0:T(8,128)(2,1)} %get-tuple-element.252), channel_id=1, source_target_pairs={{0,4},{4,0},{8,12},{12,8},{16,20},{20,16},{24,28},{28,24},{1,5},{5... | collective-permute-start | bytes 2949128 | tf_op jit(solution)/shard_map/ppermute | solution.py:559
  531.8 98.6 %collective-permute-start.32 = (bf16[320,1536]{1,0:T(8,128)(2,1)}, bf16[320,1536]{1,0:T(8,128)(2,1)}, u32[]{:S(2)}, u32[]{:S(2)}) collective-permute-start(bf16[320,1536]{1,0:T(8,128)(2,1)} %get-tuple-element.231), channel_id=1, source_target_pairs={{0,4},{4,0},{8,12},{12,8},{16,20},{20,16},{24,28},{28,24},{1,5},{5... | collective-permute-start | bytes 2949128 | tf_op jit(solution)/shard_map/ppermute | solution.py:559
  607.6 38.5 %collective-permute-start.43 = (bf16[512,1536]{1,0:T(8,128)(2,1)S(1)}, bf16[512,1536]{1,0:T(8,128)(2,1)S(1)}, u32[]{:S(2)}, u32[]{:S(2)}) collective-permute-start(bf16[512,1536]{1,0:T(8,128)(2,1)S(1)} %ring_rows.13), channel_id=1, source_target_pairs={{0,8},{4,12},{8,16},{12,20},{16,24},{20,28},{24,0},{28,4},{1,9},{5... | collective-permute-start | bytes 4718600 | tf_op jit(solution)/shard_map/ppermute | solution.py:552
  630.4 33.0 %collective-permute-start.42 = (bf16[2,384,1664]{2,1,0:T(8,128)(2,1)}, bf16[2,384,1664]{2,1,0:T(8,128)(2,1)}, u32[]{:S(2)}, u32[]{:S(2)}) collective-permute-start(bf16[2,384,1664]{2,1,0:T(8,128)(2,1)} %get-tuple-element.433), channel_id=1, source_target_pairs={{0,1},{1,0},{2,3},{3,2},{4,5},{5,4},{6,7},{7,6},{8,9},{9,8},{10,11... | collective-permute-start | bytes 7667720 | tf_op jit(solution)/shard_map/ppermute | solution.py:570
  630.4 65.0 %collective-permute-start.33 = (bf16[320,1536]{1,0:T(8,128)(2,1)}, bf16[320,1536]{1,0:T(8,128)(2,1)}, u32[]{:S(2)}, u32[]{:S(2)}) collective-permute-start(bf16[320,1536]{1,0:T(8,128)(2,1)} %get-tuple-element.232), channel_id=1, source_target_pairs={{0,4},{4,0},{8,12},{12,8},{16,20},{20,16},{24,28},{28,24},{1,5},{5... | collective-permute-start | bytes 2949128 | tf_op jit(solution)/shard_map/ppermute | solution.py:559
  651.8 43.7 %collective-permute-start.44 = (bf16[512,1536]{1,0:T(8,128)(2,1)}, bf16[512,1536]{1,0:T(8,128)(2,1)S(1)}, u32[]{:S(2)}, u32[]{:S(2)}) collective-permute-start(bf16[512,1536]{1,0:T(8,128)(2,1)} %ring_rows.14), channel_id=1, source_target_pairs={{0,8},{4,12},{8,16},{12,20},{16,24},{20,28},{24,0},{28,4},{1,9},{5... | collective-permute-start | bytes 4718600 | tf_op jit(solution)/shard_map/ppermute | solution.py:552
  651.8 215.7 %all-reduce.3.cloned.1.call-start = ((), (), s32[]{:S(2)}) async-start(), calls=%async_computation.8 | async-start | bytes 3145728 | tf_op jit(solution)/shard_map/psum | solution.py:856
  667.9 53.2 %collective-permute-start.45 = (bf16[384,1664]{1,0:T(8,128)(2,1)}, bf16[384,1664]{1,0:T(8,128)(2,1)}, u32[]{:S(2)}, u32[]{:S(2)}) collective-permute-start(bf16[384,1664]{1,0:T(8,128)(2,1)} %get-tuple-element.446), channel_id=1, source_target_pairs={{0,2},{1,3},{2,0},{3,1},{4,6},{5,7},{6,4},{7,5},{8,10},{9,11},{10,... | collective-permute-start | bytes 3833864 | tf_op jit(solution)/shard_map/ppermute | solution.py:573
  735.6 18.1 %collective-permute-start.48 = (bf16[48,1664]{1,0:T(8,128)(2,1)S(1)}, bf16[48,1664]{1,0:T(8,128)(2,1)S(1)}, u32[]{:S(2)}, u32[]{:S(2)}) collective-permute-start(bf16[48,1664]{1,0:T(8,128)(2,1)S(1)} %get-tuple-element.456), channel_id=1, source_target_pairs={{0,16},{4,20},{8,24},{12,28},{16,0},{20,4},{24,8},{28,12},{1,17},{... | collective-permute-start | bytes 479240 | tf_op jit(solution)/shard_map/ppermute | solution.py:552
  742.4 15.1 %collective-permute-start.49 = (bf16[48,1664]{1,0:T(8,128)(2,1)S(1)}, bf16[48,1664]{1,0:T(8,128)(2,1)S(1)}, u32[]{:S(2)}, u32[]{:S(2)}) collective-permute-start(bf16[48,1664]{1,0:T(8,128)(2,1)S(1)} %get-tuple-element.455), channel_id=1, source_target_pairs={{0,24},{4,28},{8,0},{12,4},{16,8},{20,12},{24,16},{28,20},{1,25},{... | collective-permute-start | bytes 479240 | tf_op jit(solution)/shard_map/ppermute | solution.py:552
  (116 other events, 2458.2 us)
Sparse Core Ops, SparseCore 0:
  17.7 49.7 all-gather.6
  69.6 45.2 all-gather.8
  117.0 67.6 all-gather.10
  186.8 120.0 all-gather.12
  378.6 88.4 reduce-scatter.5
  469.5 150.7 reduce-scatter.3
  651.9 83.6 reduce-scatter.7
  779.4 88.0 all-reduce.2

commit v3 on v2

--- a/solution.py
+++ b/solution.py
@@ -349,57 +349,76 @@
     )
 
 
-def down_grad_kernel(count, *refs):
-    pieces, (scaled, out, rows) = refs[:count], refs[count:]
+def keep_and_send(core, pair, mine, theirs):
+    first, second = (p.astype(bf16) for p in pair)
+    mine(jnp.where(core == 0, first, second))
+    theirs(jnp.where(core == 0, second, first))
+
+
+def down_grad_kernel(count, core, *refs):
+    pieces, (scaled, mine, theirs, rows) = refs[:count], refs[count:]
     gather_rows(pieces, rows)
-    shards, span = out.shape[0], out.shape[3]
+    chips, span = mine.shape[0], mine.shape[3]
     scaled_t = scaled[0].T
-    for c in range(shards):
-        out[c, 0] = dot_nn(scaled_t, rows[:, c * span : (c + 1) * span]).astype(bf16)
-
-
-def down_grads(pieces, scaled, shards):
-    experts, rows, _ = scaled.shape
-    span = MODEL_WIDTH // shards
+    for y in range(chips):
+        pair = [
+            dot_nn(scaled_t, rows[:, c * span : (c + 1) * span]) for c in (2 * y, 2 * y + 1)
+        ]
+        keep_and_send(
+            core[0],
+            pair,
+            functools.partial(mine.__setitem__, (y, 0)),
+            functools.partial(theirs.__setitem__, (y, 0)),
+        )
+
+
+def in_grad_kernel(count, core, *refs):
+    pieces, (gate_side, up_side, mine, theirs, rows) = refs[:count], refs[count:]
+    gather_rows(pieces, rows)
+    chips, span = mine.shape[0], mine.shape[2]
+    rows_t = rows[...].T
+    for y in range(chips):
+        for side, at in ((gate_side, 0), (up_side, FF)):
+            pair = [dot_nn(rows_t[c * span : (c + 1) * span], side[0]) for c in (2 * y, 2 * y + 1)]
+            where = (y, 0, slice(None), slice(at, at + FF))
+            keep_and_send(
+                core[0],
+                pair,
+                functools.partial(mine.__setitem__, where),
+                functools.partial(theirs.__setitem__, where),
+            )
+
+
+def grads_by_core(kernel, name, core, pieces, sides, shape):
+    experts, rows, _ = sides[0].shape
+    count = len(pieces)
+    out = jax.ShapeDtypeStruct(shape, bf16)
+    whole = pl.BlockSpec((1, rows, FF), lambda e, *_: (e, 0, 0))
+    block = pl.BlockSpec((shape[0], 1, shape[2], shape[3]), lambda e, *_: (0, e, 0, 0))
     return pl.pallas_call(
-        functools.partial(down_grad_kernel, len(pieces)),
-        out_shape=jax.ShapeDtypeStruct((shards, experts, FF, span), bf16),
-        grid=(experts,),
-        in_specs=[piece_spec()] * len(pieces) + [pl.BlockSpec((1, rows, FF), lambda e: (e, 0, 0))],
-        out_specs=pl.BlockSpec((shards, 1, FF, span), lambda e: (0, e, 0, 0)),
-        scratch_shapes=row_scratch(len(pieces)),
+        functools.partial(kernel, count),
+        out_shape=(out, out),
+        grid_spec=pltpu.PrefetchScalarGridSpec(
+            num_scalar_prefetch=1,
+            grid=(experts,),
+            in_specs=[piece_spec()] * count + [whole] * len(sides),
+            out_specs=(block, block),
+            scratch_shapes=row_scratch(count),
+        ),
         compiler_params=params(56, 1),
-        cost_estimate=cost(2 * experts * rows * FF * MODEL_WIDTH, 22e6),
-        name="down_grads",
-    )(*pieces, scaled)
-
-
-def in_grad_kernel(count, *refs):
-    pieces, (gate_side, up_side, out, rows) = refs[:count], refs[count:]
-    gather_rows(pieces, rows)
-    shards, span = out.shape[0], out.shape[2]
-    rows_t = rows[...].T
-    for c in range(shards):
-        part = rows_t[c * span : (c + 1) * span]
-        out[c, 0, :, :FF] = dot_nn(part, gate_side[0]).astype(bf16)
-        out[c, 0, :, FF:] = dot_nn(part, up_side[0]).astype(bf16)
-
-
-def in_grads(pieces, gate_side, up_side, shards):
-    experts, rows, _ = gate_side.shape
-    span = MODEL_WIDTH // shards
-    whole = pl.BlockSpec((1, rows, FF), lambda e: (e, 0, 0))
-    return pl.pallas_call(
-        functools.partial(in_grad_kernel, len(pieces)),
-        out_shape=jax.ShapeDtypeStruct((shards, experts, span, 2 * FF), bf16),
-        grid=(experts,),
-        in_specs=[piece_spec()] * len(pieces) + [whole, whole],
-        out_specs=pl.BlockSpec((shards, 1, span, 2 * FF), lambda e: (0, e, 0, 0)),
-        scratch_shapes=row_scratch(len(pieces)),
-        compiler_params=params(56, 1),
-        cost_estimate=cost(4 * experts * rows * FF * MODEL_WIDTH, 35e6),
-        name="in_grads",
-    )(*pieces, gate_side, up_side)
+        cost_estimate=cost(2 * len(sides) * experts * rows * FF * MODEL_WIDTH, 25e6),
+        name=name,
+    )(core, *pieces, *sides)
+
+
+def down_grads(core, pieces, scaled, shards):
+    shape = (shards // 2, scaled.shape[0], FF, MODEL_WIDTH // shards)
+    return grads_by_core(down_grad_kernel, "down_grads", core, pieces, [scaled], shape)
+
+
+def in_grads(core, pieces, gate_side, up_side, shards):
+    shape = (shards // 2, gate_side.shape[0], MODEL_WIDTH // shards, 2 * FF)
+    return grads_by_core(in_grad_kernel, "in_grads", core, pieces, [gate_side, up_side], shape)
 
 
 def ring_kernel(wide, *refs):
@@ -463,36 +482,44 @@
     )(picks, rows)
 
 
-def weight_grad_kernel(rows, *refs):
-    *grads, out = refs
+def weight_grad_kernel(core, rows, *refs):
+    *grads, mine, theirs = refs
+    span = mine.shape[1]
     rows_t = rows[...].T
     at = 0
     for side in grads:
-        if side.dtype == f32:
-            out[:, at:] = side[...].T.astype(bf16)
-        else:
-            columns = side.shape[1]
-            out[:, at : at + columns] = dot_nn(rows_t, side[...]).astype(bf16)
-            at += columns
-
-
-def weight_grads(rows, grads, extra=None):
+        columns = side.shape[1]
+        pair = [dot_nn(rows_t[c * span : (c + 1) * span], side[...]) for c in range(2)]
+        where = (0, slice(None), slice(at, at + columns))
+        keep_and_send(
+            core[0],
+            pair,
+            functools.partial(mine.__setitem__, where),
+            functools.partial(theirs.__setitem__, where),
+        )
+        at += columns
+
+
+def weight_grads(core, rows, grads, shards):
     token_rows = rows.shape[0]
-    tile = 384
-    extras = [] if extra is None else [extra]
-    columns = sum(g.shape[1] for g in grads) + sum(e.shape[0] for e in extras)
+    span = MODEL_WIDTH // shards
+    columns = sum(g.shape[1] for g in grads)
+    out = jax.ShapeDtypeStruct((shards // 2, span, columns), bf16)
+    block = pl.BlockSpec((1, span, columns), lambda n, c: (n, 0, 0))
     return pl.pallas_call(
         weight_grad_kernel,
-        out_shape=jax.ShapeDtypeStruct((MODEL_WIDTH, columns), bf16),
-        grid=(MODEL_WIDTH // tile,),
-        in_specs=[pl.BlockSpec((token_rows, tile), lambda n: (0, n))]
-        + [pl.BlockSpec(g.shape, lambda n: (0, 0)) for g in grads]
-        + [pl.BlockSpec((e.shape[0], tile), lambda n: (0, n)) for e in extras],
-        out_specs=pl.BlockSpec((tile, columns), lambda n: (n, 0)),
+        out_shape=(out, out),
+        grid_spec=pltpu.PrefetchScalarGridSpec(
+            num_scalar_prefetch=1,
+            grid=(shards // 2,),
+            in_specs=[pl.BlockSpec((token_rows, 2 * span), lambda n, c: (0, n))]
+            + [pl.BlockSpec(g.shape, lambda n, c: (0, 0)) for g in grads],
+            out_specs=(block, block),
+        ),
         compiler_params=params(56, 1),
         cost_estimate=cost(2 * MODEL_WIDTH * token_rows * columns, 14e6),
         name="weight_grads",
-    )(rows, *grads, *extras)
+    )(core, rows, *grads)
 
 
 def adamw_update(weight, moment_one, moment_two, gradient, step_rate, decay_rate):
@@ -566,6 +593,9 @@
         pairs = [(a, a + by) for a in range(shards) if 0 <= a + by < shards]
         return lax.ppermute(value, "fsdp", pairs)
 
+    chips = shards // 2
+    chip, core = place // 2, place % 2
+
     def core_shift(value, by):
         return lax.ppermute(value, "fsdp", [(a, a // 2 * 2 + (a + by) % 2) for a in range(shards)])
 
@@ -642,6 +672,20 @@
                     before = (piece,)
         return steps
 
+    def chip_sum(mine, mate, chip):
+        return lax.dynamic_index_in_dim(mine, chip, 0, keepdims=False).astype(
+            f32
+        ) + lax.dynamic_index_in_dim(mate, chip, 0, keepdims=False).astype(f32)
+
+    def chip_low(mine, mate):
+        return [chip_sum(mine, mate, (chip + s) % chips).astype(bf16) for s in range(1, chips)]
+
+    def chip_send(low):
+        return [y_shift(part, s) for s, part in enumerate(low, 1)]
+
+    def chip_total(mine, mate, sent):
+        return functools.reduce(lambda total, part: total + part.astype(f32), sent, chip_sum(mine, mate, chip))
+
     def ring_send(held):
         return [z_shift(held[-1], 1)]
 
@@ -682,8 +726,6 @@
     keys_local = turn_keys(pre[:, MODEL_WIDTH : MODEL_WIDTH + KV], 1.0).astype(bf16)
     kv_local = jnp.concatenate([keys_local, pre[:, MODEL_WIDTH + KV :].astype(bf16)], axis=1)
 
-    chips = shards // 2
-    core = place % 2
     same = [kv_local] + [y_up(kv_local, s) for s in range(1, chips)]
     other = [core_shift(v, 1) for v in same]
     blocks = []
@@ -755,23 +797,31 @@
     steps = swap_back(back_pieces)
     gate_dots = gate_dots.reshape(experts_local, wide, depth, CAP)
     away_dots = [x_shift(gate_dots[:, r], -r) for r in range(1, wide)]
-    down_term = down_grads(upstream_pieces, scaled_hidden, shards)
+    core_arg = core.astype(jnp.int32).reshape(1)
+    in_term = in_grads(core_arg, hidden_pieces, gate_side, up_side, shards)
+    in_mate = core_shift(in_term[1], 1)
     held = []
-    ring_step(held, after(steps[1], down_term))
-    out_part = lax.psum_scatter(after(down_term, held[0]), "fsdp", scatter_dimension=0)
+    ring_step(held, after(steps[1], in_term))
     arrived = ring_send(held)
-    in_term = in_grads(hidden_pieces, *after((gate_side, up_side), held[0]), shards)
-    gate_dots = jnp.stack([gate_dots[:, 0]] + after(away_dots, in_term))
+    down_term = down_grads(core_arg, upstream_pieces, after(scaled_hidden, held[0]), shards)
+    down_mate = core_shift(down_term[1], 1)
+    in_mate = after(in_mate, down_term)
+    in_low = chip_low(in_term[0], in_mate)
+    in_sent = []
+    for e in range(experts_local):
+        in_sent.append(chip_send(after([low[e : e + 1] for low in in_low], in_sent[max(min(e, 2) - 1, 0) : min(e, 2)])))
+    gate_dots = jnp.stack([gate_dots[:, 0]] + after(away_dots, down_term))
     gate_dots = gate_dots.transpose(2, 0, 1, 3).reshape(depth, near, CAP)
     token_dots = jnp.sum(jnp.where(picks, gate_dots[:, :, :, None], 0.0), axis=2)
     choice_dots = jnp.sum(named * token_dots[:, :, None, :], axis=1)
     lane = z_shift(choice_dots[1], 1)
-    ring_step(held, after(steps[2], in_term, lane), arrived)
-    in_part = lax.psum_scatter(after(in_term, held[1]), "fsdp", scatter_dimension=0)
+    ring_step(held, after(steps[2], in_low, lane), arrived)
     lane = z_shift(lane + choice_dots[2], 1)
     arrived = ring_send(held)
     results = result_rows(after(scaled_hidden, held[1]), down_low, len(back_pieces))
-    ring_step(held, after(steps[3], results, lane), arrived)
+    ring_step(held, after(steps[3], results, lane, in_sent[0]), arrived)
+    down_mate = after(down_mate, held[1])
+    down_low_sum = chip_low(down_term[0], down_mate)
     result_steps = swap_back(results, steps[0])
     lane = z_shift(lane + choice_dots[3], 1)
     arrived = ring_send(held)
@@ -781,7 +831,7 @@
     )
     logit_grad_t = jnp.sum(chosen_t * picked_grad[:, None, :], axis=0).astype(bf16)
     router_term = dot_nn(logit_grad_t, hidden_two)
-    hidden_back = ring_step(held, after(steps[0], router_term), arrived)
+    hidden_back = ring_step(held, after(steps[0], router_term, down_low_sum, in_sent[1]), arrived)
     hidden_two_grad = hidden_back + lax.dot_general(
         logit_grad_t, router_low, (((0,), (1,)), ((), ())), preferred_element_type=f32
     )
@@ -795,15 +845,11 @@
     attended_grad = dot_nt(branch_grad, output_low).astype(bf16)
     result_held = []
     ring_step(result_held, after(result_steps[1], hidden_back))
-    attended_grad = after(attended_grad, result_held[0], out_part)
+    attended_grad = after(attended_grad, result_held[0])
     arrived = ring_send(result_held)
     pre_grad, key_back, value_back = attend_back(
         place_arg, query_rows, kv_blocks, attended, attended_grad, log_total, cosine, sine
     )
-
-    def extra_rows(*terms):
-        used = sum(t.shape[0] for t in terms)
-        return jnp.concatenate(list(terms) + [jnp.zeros((128 - used, MODEL_WIDTH), f32)], axis=0)
 
     def send_parts(parts, index, shift):
         count = parts.shape[0]
@@ -822,42 +868,40 @@
             whole = lax.dynamic_update_index_in_dim(whole, piece, (index - s) % count, 0)
         return whole
 
-    def core_parts(terms):
-        parts = terms.reshape(chips, 2, shard_rows, terms.shape[1]).transpose(1, 0, 2, 3)
-        return send_parts(parts, core, core_shift)
-
-    def y_parts(part):
-        return send_parts(part, place // 2, y_shift)
-
     def x_parts(part):
         return send_parts(part.reshape(wide, shard_rows // wide, part.shape[1]), column, x_shift)
 
-    def z_total(part):
-        columns = part.shape[1]
-        part = add_parts(send_parts(part.reshape(depth, shard_rows // wide // depth, columns), level, z_shift))
-        part = join(part, level, depth, z_shift).reshape(shard_rows // wide, columns)
-        return join(part, column, wide, x_shift).reshape(shard_rows, columns).astype(f32)
+    def z_parts(part):
+        return send_parts(part.reshape(depth, shard_rows // wide // depth, part.shape[1]), level, z_shift)
+
+    def z_join(part):
+        return join(part, level, depth, z_shift).reshape(shard_rows // wide, part.shape[1])
+
+    def x_join(part):
+        return join(part, column, wide, x_shift).reshape(shard_rows, part.shape[1]).astype(f32)
 
     kv_back = jnp.concatenate([key_back, value_back], axis=2)
     none = jnp.zeros_like(kv_back[:1])
     mate = jnp.where(core == 1, kv_back[1::2], jnp.concatenate([none, kv_back[1:-1:2]], axis=0))
     mate = core_shift(mate, 1)
     kv_chip = kv_back[0::2].astype(f32) + mate.astype(f32)
-    kv_low = kv_chip.astype(bf16)
+    kv_low = after(kv_chip.astype(bf16), in_sent)
+    in_sent = [jnp.concatenate(parts, axis=0) for parts in zip(*in_sent)]
     kv_parts = [
         lax.ppermute(kv_low[s], "fsdp", [(a + 2 * s, a) for a in range(shards - 2 * s)]) for s in range(1, chips)
     ]
+    back_mine, back_mate = weight_grads(core_arg, attended, [after(branch_grad, kv_chip)], shards)
+    back_mate = core_shift(back_mate, 1)
+    kv_parts = after(kv_parts, back_mine)
     kv_grad = functools.reduce(lambda total, part: total + part.astype(f32), kv_parts, kv_chip[0])
     key_pre_grad = turn_keys(kv_grad[:, :KV], -1.0)
     kv_pre_grad = jnp.concatenate([key_pre_grad, kv_grad[:, KV:]], axis=1).astype(bf16)
 
-    front_terms = weight_grads(first_hidden, [pre_grad, kv_pre_grad])
-    front_part = lax.psum_scatter(after(front_terms, in_part), "fsdp", scatter_dimension=0, tiled=True)
-    front_sum = lax.psum(front_part, "expert").astype(f32)
-
-    ring_step(result_held, after(result_steps[2], front_terms), arrived)
-    arrived = ring_send(result_held)
-    pre_late, kv_late = after((pre_grad, kv_pre_grad), result_held[1])
+    front_mine, front_mate = weight_grads(core_arg, first_hidden, [pre_grad, kv_pre_grad], shards)
+    front_mate = core_shift(front_mate, 1)
+    back_mate = after(back_mate, front_mine)
+    back_sent = chip_send(chip_low(back_mine, back_mate))
+    pre_late, kv_late = after((pre_grad, kv_pre_grad), front_mine)
     hidden_one_grad = dot_nt(pre_late, qkv_low[:, :MODEL_WIDTH]) + dot_nt(kv_late, qkv_low[:, MODEL_WIDTH:])
     gain_one_term = jnp.sum(hidden_one_grad * normed_one, axis=0)
     scaled_one = hidden_one_grad * gain_one
@@ -866,40 +910,65 @@
         + scale_one
         * (scaled_one - normed_one * jnp.mean(scaled_one * normed_one, axis=1, keepdims=True))
     ).astype(bf16)
-    back_terms = weight_grads(
-        attended, [branch_grad], extra_rows(router_term, gain_one_term[None], gain_two_term[None])
-    )
-    back_parts = core_parts(back_terms)
-    ring_step(result_held, after(result_steps[3], back_terms), arrived)
+    extra = jnp.concatenate(
+        [
+            router_term,
+            gain_one_term[None],
+            gain_two_term[None],
+            jnp.zeros((126 - experts_all, MODEL_WIDTH), f32),
+        ],
+        axis=0,
+    )
+    extra = extra.T.astype(bf16).reshape(chips, 2, shard_rows, 128)
+    extra_mine = jnp.where(core == 0, extra[:, 0], extra[:, 1])
+    extra_mate = core_shift(jnp.where(core == 0, extra[:, 1], extra[:, 0]), 1)
+    ring_step(result_held, after(result_steps[2], front_mine), arrived)
     arrived = ring_send(result_held)
+    front_mate, extra_mate = after((front_mate, extra_mate), extra_mine, result_held[1])
+    front_mine = jnp.concatenate([front_mine, extra_mine], axis=2)
+    front_mate = jnp.concatenate([front_mate, extra_mate], axis=2)
+    front_low = chip_low(front_mine, front_mate)
+    front_sent = chip_send(front_low)
+    back_sent = after(back_sent, front_low)
+    back_low = chip_total(back_mine, back_mate, back_sent).astype(bf16)
+    back_parts = x_parts(back_low)
+    in_state = adamw_update(
+        expert_in,
+        in_first,
+        in_second,
+        chip_total(after(in_term[0], back_low), in_mate, in_sent),
+        0.5 / math.sqrt(MODEL_WIDTH),
+        DECAY,
+    )
+    back_low = add_parts(after(back_parts, in_state))
+    back_parts = z_parts(back_low)
+    ring_step(result_held, after(result_steps[3], in_state), arrived)
+    arrived = ring_send(result_held)
+    front_sent = after(front_sent, back_low, result_held[2])
+    front_low = chip_total(front_mine, front_mate, front_sent).astype(bf16)
+    front_parts = x_parts(front_low)
+    back_low = z_join(add_parts(after(back_parts, front_low)))
+    down_sent = chip_send(after(down_low_sum, front_low))
+    front_low = add_parts(after(front_parts, back_low))
+    front_low = add_parts(z_parts(front_low))
+    back_sum = x_join(back_low)
+    moe_out = ring_step(result_held, after(result_steps[0], front_low), arrived)
+    layer_out = (residual + moe_out).astype(bf16)
+    front_sum = x_join(z_join(front_low))
     out_state = adamw_update(
         expert_out,
         out_first,
         out_second,
-        after(out_part, result_held[2]).astype(f32),
+        chip_total(after(down_term[0], layer_out), down_mate, down_sent),
         0.5 / math.sqrt(FF // 8),
         DECAY,
     )
-    back_part = add_parts(after(back_parts, out_state))
-    back_parts = y_parts(back_part)
-    in_state = adamw_update(
-        expert_in,
-        in_first,
-        in_second,
-        after(in_part, back_part).astype(f32),
-        0.5 / math.sqrt(MODEL_WIDTH),
-        DECAY,
-    )
-    moe_out = ring_step(result_held, after(result_steps[0], in_state), arrived)
-    layer_out = (residual + moe_out).astype(bf16)
-    back_sum = z_total(add_parts(x_parts(add_parts(after(back_parts, layer_out)))))
-    output_sum = back_sum[:, :MODEL_WIDTH]
-    router_sum = back_sum[:, MODEL_WIDTH : MODEL_WIDTH + experts_all]
+    output_sum = back_sum
+    router_sum = front_sum[:, QKV : QKV + experts_all]
     query_sum = front_sum[:, :MODEL_WIDTH]
     key_sum = front_sum[:, MODEL_WIDTH : MODEL_WIDTH + KV]
     value_sum = front_sum[:, MODEL_WIDTH + KV : QKV]
-    at = MODEL_WIDTH + experts_all
-    gain_sum = back_sum[:, at : at + 2].T
+    gain_sum = front_sum[:, QKV + experts_all : QKV + experts_all + 2].T
 
     rate = 0.5 / math.sqrt(MODEL_WIDTH // 2)
     return (

time: 895 us -> 935 us (1.045)
  starting transfers between devices: 68.4 us -> 118 us
  local copies, waits for them, and re-layouts: 48.4 us -> 37.3 us
  other arithmetic: 104 us -> 114 us
    psum x1 -> x0, waiting for transfers between devices: 72.3 us -> none  [body(): front_sum = lax.psum(front_part, 'expert').astype(f32)]
    ppermute x27 -> x33, waiting for transfers between devices: 126 us -> 186 us  [z_shift(): lax.ppermute(value, 'expert', [(a * wide + b, (a + by) % depth * wide + b...]
    ppermute x1, waiting for transfers between devices: 59.4 us -> 6.29 us  [body(): lax.ppermute(kv_low[s], 'fsdp', [(a + 2 * s, a) for a in range(shards - 2...]
    ppermute x1 -> x7, waiting for transfers between devices: 14.3 us -> 54.7 us  [y_shift(): lax.ppermute(value, 'fsdp', [(a, (a + 2 * by) % shards) for a in range(sh...]
    ppermute x1 -> x7, starting transfers between devices: 4.69 us -> 38.1 us  [y_shift(): lax.ppermute(value, 'fsdp', [(a, (a + 2 * by) % shards) for a in range(sh...]
    ppermute x20 -> x22, waiting for transfers between devices: 115 us -> 142 us  [x_shift(): lax.ppermute(value, 'expert', [(a * wide + b, a * wide + (b + by) % wide)...]
    convert_element_type x2 -> x8, other arithmetic: 2.2 us -> 18.9 us  [the longest x4 13.9 us: chip_low(): chip_sum(mine, mate, (chip + s) % chips).astype(bf16)]
    ppermute x20 -> x22, starting transfers between devices: 22.9 us -> 31.8 us  [x_shift(): lax.ppermute(value, 'expert', [(a * wide + b, a * wide + (b + by) % wide)...]
  transfers between devices with their start and end apart: 62 -> 76, of which waited for: 34 -> 41; matrix products, arithmetic and copies ran while one was open for 17% -> 15% of each run, Pallas kernels for 18% -> 12%
where the time goes in v3:
time: 935 us; the launch traced here: 927 us
  waiting for transfers between devices  417 us (45%)
  Pallas kernels  190 us (20%)
  starting transfers between devices  118 us (13%)
  other arithmetic  114 us (12%)
  local copies, waits for them, and re-layouts  37.3 us (4%)
  matrix products  33.9 us (4%)
  between operations  16 us (2%)
    ppermute x33, waiting for transfers between devices, z_shift(): lax.ppermute(value, 'expert', [(a * wide + b, (a + by) % depth * wide + b...  186 us
    ppermute x22, waiting for transfers between devices, x_shift(): lax.ppermute(value, 'expert', [(a * wide + b, a * wide + (b + by) % wide)...  142 us
    ppermute x7, waiting for transfers between devices, y_shift(): lax.ppermute(value, 'fsdp', [(a, (a + 2 * by) % shards) for a in range(sh...  54.7 us
    sub x7, other arithmetic, adamw_update(): weight - step_rate * (first_hat / (jnp.sqrt(second_hat) + ADAM_EPS) + dec...  52 us
    ppermute x7, starting transfers between devices, y_shift(): lax.ppermute(value, 'fsdp', [(a, (a + 2 * by) % shards) for a in range(sh...  38.1 us
    ppermute x33, starting transfers between devices, z_shift(): lax.ppermute(value, 'expert', [(a * wide + b, (a + by) % depth * wide + b...  37 us
    pallas_call x1, Pallas kernels, core_rows(): pl.pallas_call(functools.partial(core_kernel, count), out_shape=(low, low...  36.4 us
    pallas_call x2, Pallas kernels, grads_by_core(): pl.pallas_call(functools.partial(kernel, count), out_shape=(out, out), gr...  34.1 us
  transfers between devices with their start and end apart: 76, of which 41 were waited for; matrix products, arithmetic and copies ran while one was open for 15% of the time, Pallas kernels for 12%

profile of v3, /device:TPU:8, one launch (start us, length us, event | category | flops | bytes accessed | tf_op | source)
XLA Modules:
  0.0 926.5 jit_solution(5291864006078629788)
XLA Ops:
  36.8 17.1 %collective-permute-done.4.refs_4_ = bf16[320,1536]{1,0:T(8,128)(2,1)} collective-permute-done((bf16[320,1536]{1,0:T(8,128)(2,1)}, bf16[320,1536]{1,0:T(8,128)(2,1)}, u32[]{:S(2)}, u32[]{:S(2)}) %collective-permute-start.4) | collective-permute-done | bytes 983072 | tf_op jit(solution)/shard_map/ppermute | solution.py:586
  53.9 5.3 collective-permute-done.3.rows
  70.0 6.1 fusion.1.pre
  80.9 6.5 convert_element_type.280
  92.2 22.6 %collective-permute-done.6 = bf16[512,512]{1,0:T(8,128)(2,1)} collective-permute-done((bf16[512,512]{1,0:T(8,128)(2,1)}, bf16[512,512]{1,0:T(8,128)(2,1)}, u32[]{:S(2)}, u32[]{:S(2)}) %collective-permute-start.6) | collective-permute-done | bytes 524320 | tf_op jit(solution)/shard_map/ppermute | solution.py:606
  127.4 14.3 %attend.1 = (bf16[512,1536]{1,0:T(8,128)(2,1)}, f32[12,1,512]{2,1,0:T(1,128)}, bf16[512,1536]{1,0:T(8,128)(2,1)}) custom-call(s32[1]{0:T(128)} %bitcast.place, f32[512,2048]{1,0:T(8,128)} %copy-done.44, f32[512,128]{1,0:T(8,128)} %get-tuple-element.515.cosine, f32[512,128]{1,0:T(8,128)} %copy-done.45, bf16[4,512,512]{2,1,0:T(8,128)(2,1)} %pad_maximum_fusion.1.keys.values, ...), custom_call_target="tpu_custom_call" | custom-call | flops 1000000000 | bytes 1000000 | tf_op jit(solution)/shard_map/attend/pallas_call | solution.py:106
  141.8 19.3 %collective-permute-done.9.rows = bf16[512,1536]{1,0:T(8,128)(2,1)S(1)} collective-permute-done((bf16[512,1536]{1,0:T(8,128)(2,1)}, bf16[512,1536]{1,0:T(8,128)(2,1)S(1)}, u32[]{:S(2)}, u32[]{:S(2)}) %collective-permute-start.9) | collective-permute-done | bytes 1572896 | tf_op jit(solution)/shard_map/ppermute | solution.py:579
  162.2 6.0 multiply_reduce_fusion.2
  177.4 19.5 %collective-permute-done.11.refs_6_ = bf16[320,1536]{1,0:T(8,128)(2,1)S(1)} collective-permute-done((bf16[320,1536]{1,0:T(8,128)(2,1)S(1)}, bf16[320,1536]{1,0:T(8,128)(2,1)S(1)}, u32[]{:S(2)}, u32[]{:S(2)}) %collective-permute-start.11) | collective-permute-done | bytes 983072 | tf_op jit(solution)/shard_map/ppermute | solution.py:586
  198.3 7.2 collective-permute-done.13.rows
  209.6 9.2 collective-permute-done.12.refs_4_
  222.3 19.5 %collective-permute-done.16 = f32[4,512]{1,0:T(4,128)S(1)} collective-permute-done((f32[4,512]{1,0:T(4,128)S(1)}, f32[4,512]{1,0:T(4,128)S(1)}, u32[]{:S(2)}, u32[]{:S(2)}) %collective-permute-start.16) | collective-permute-done | bytes 8224 | tf_op jit(solution)/shard_map/ppermute | solution.py:579
  251.5 15.2 %collective-permute-done.17.refs_7_ = bf16[320,1536]{1,0:T(8,128)(2,1)S(1)} collective-permute-done((bf16[320,1536]{1,0:T(8,128)(2,1)S(1)}, bf16[320,1536]{1,0:T(8,128)(2,1)S(1)}, u32[]{:S(2)}, u32[]{:S(2)}) %collective-permute-start.17) | collective-permute-done | bytes 983072 | tf_op jit(solution)/shard_map/ppermute | solution.py:586
  270.4 6.7 collective-permute-done.19.rows
  278.2 12.9 %inner_rows.1.refs_9_ = bf16[4,640,768]{2,1,0:T(8,128)(2,1)} custom-call(bf16[320,1536]{1,0:T(8,128)(2,1)} %copy-done.23, bf16[320,1536]{1,0:T(8,128)(2,1)} %copy-done.24, bf16[320,1536]{1,0:T(8,128)(2,1)} %copy-done.25, bf16[320,1536]{1,0:T(8,128)(2,1)} %copy-done.27, bf16[320,1536]{1,0:T(8,128)(2,1)} %collective-permute-done.4.refs_4_, ...), custom_call_target="tpu_custom_call" | custom-call | flops 6039797760 | bytes 20000000 | tf_op jit(solution)/shard_map/inner_rows/pallas_call | solution.py:248
  302.2 12.0 %collective-permute-done.23 = f32[4,4,80]{2,0,1:T(4,128)S(1)} collective-permute-done((f32[4,4,80]{2,0,1:T(4,128)S(1)}, f32[4,4,80]{2,0,1:T(4,128)S(1)}, u32[]{:S(2)}, u32[]{:S(2)}) %collective-permute-start.23) | collective-permute-done | bytes 5152 | tf_op jit(solution)/shard_map/ppermute | solution.py:586
  316.8 36.4 %core_rows.1 = (bf16[4,640,768]{2,1,0:T(8,128)(2,1)}, bf16[4,640,768]{2,1,0:T(8,128)(2,1)}, bf16[4,640,768]{2,1,0:T(8,128)(2,1)}, f32[4,640,1]{2,1,0:T(8,128)}, ...) custom-call(bf16[320,1536]{1,0:T(8,128)(2,1)} %copy-done.26, ...), custom_call_target="tpu_custom_call" | custom-call | flops 24159191040 | bytes 60000000 | tf_op jit(solution)/shard_map/core_rows/pallas_call | solution.py:305
  353.2 20.2 %in_grads.1 = (bf16[2,4,384,1536]{3,2,1,0:T(8,128)(2,1)}, bf16[2,4,384,1536]{3,2,1,0:T(8,128)(2,1)}) custom-call(s32[1]{0:T(128)} %bitcast.35.core, bf16[320,1536]{1,0:T(8,128)(2,1)} %copy-done.26, bf16[320,1536]{1,0:T(8,128)(2,1)} %copy-done.28, bf16[320,1536]{1,0:T(8,128)(2,1)} %copy-done.29, bf16[320,1536]{1,0:T(8,128)(2,1)} %copy-done.30, ...), custom_call_target="tpu_custom_call" | custom-call | flops 12079595520 | bytes 25000000 | tf_op jit(solution)/shard_map/in_grads/pallas_call | solution.py:398
  375.0 22.6 %collective-permute-done.24.refs_2_ = bf16[320,1536]{1,0:T(8,128)(2,1)S(1)} collective-permute-done((bf16[320,1536]{1,0:T(8,128)(2,1)S(1)}, bf16[320,1536]{1,0:T(8,128)(2,1)S(1)}, u32[]{:S(2)}, u32[]{:S(2)}) %collective-permute-start.24) | collective-permute-done | bytes 983072 | tf_op jit(solution)/shard_map/ppermute | solution.py:586
  404.9 14.0 %down_grads.1 = (bf16[2,4,768,384]{3,2,1,0:T(8,128)(2,1)}, bf16[2,4,768,384]{3,2,1,0:T(8,128)(2,1)}) custom-call(s32[1]{0:T(128)} %bitcast.35.core, bf16[320,1536]{1,0:T(8,128)(2,1)} %copy-done.23, bf16[320,1536]{1,0:T(8,128)(2,1)} %copy-done.24, bf16[320,1536]{1,0:T(8,128)(2,1)} %copy-done.25, bf16[320,1536]{1,0:T(8,128)(2,1)} %copy-done.27, ...), custom_call_target="tpu_custom_call" | custom-call | flops 6039797760 | bytes 25000000 | tf_op jit(solution)/shard_map/down_grads/pallas_call | solution.py:398
  419.5 7.6 collective-permute-done.26
  431.9 6.8 collective-permute-done.27
  443.4 5.2 add_convert_fusion
  450.5 8.3 collective-permute-start.38
  463.4 12.4 %result_rows.1 = (bf16[320,1536]{1,0:T(8,128)(2,1)}, bf16[320,1536]{1,0:T(8,128)(2,1)}, bf16[320,1536]{1,0:T(8,128)(2,1)}, bf16[320,1536]{1,0:T(8,128)(2,1)}, bf...) custom-call(bf16[4,640,768]{2,1,0:T(8,128)(2,1)} %get-tuple-element., ...), custom_call_target="tpu_custom_call" | custom-call | flops 6039797760 | bytes 22000000 | tf_op jit(solution)/shard_map/result_rows/pallas_call | solution.py:336
  498.8 25.3 %collective-permute-done.35 = f32[4,512]{1,0:T(4,128)S(1)} collective-permute-done((f32[4,512]{1,0:T(4,128)S(1)}, f32[4,512]{1,0:T(4,128)S(1)}, u32[]{:S(2)}, u32[]{:S(2)}) %collective-permute-start.35) | collective-permute-done | bytes 8224 | tf_op jit(solution)/shard_map/ppermute | solution.py:579
  540.9 6.6 convolution_convert_fusion.out_grad
  547.6 17.3 %attend_back.1 = (bf16[512,1536]{1,0:T(8,128)(2,1)}, bf16[4,512,256]{2,1,0:T(8,128)(2,1)}, bf16[4,512,256]{2,1,0:T(8,128)(2,1)}) custom-call(s32[1]{0:T(128)} %bitcast.place, bf16[512,1536]{1,0:T(8,128)(2,1)} %get-tuple-element.258.query, bf16[4,512,512]{2,1,0:T(8,128)(2,1)} %pad_maximum_fusion.1.keys.values, ...), custom_call_target="tpu_custom_call" | custom-call | flops 1000000000 | bytes 1000000 | tf_op jit(solution)/shard_map/attend_back/pallas_call | solution.py:182
  567.9 6.8 collective-permute-start.42
  574.6 23.0 %collective-permute-start.44 = (bf16[1,384,1536]{2,1,0:T(8,128)(2,1)S(1)}, bf16[1,384,1536]{2,1,0:T(8,128)(2,1)S(1)}, u32[]{:S(2)}, u32[]{:S(2)}) collective-permute-start(bf16[1,384,1536]{2,1,0:T(8,128)(2,1)S(1)} %copy-done.59), channel_id=1, source_target_pairs={{0,2},{1,3},{2,0},{3,1},{4,6},{5,7},{6,4},{7,5},{8,10},{9,11},{10,... | collective-permute-start | bytes 3538952 | tf_op jit(solution)/shard_map/ppermute | solution.py:603
  598.1 26.3 %collective-permute-done.44 = bf16[1,384,1536]{2,1,0:T(8,128)(2,1)S(1)} collective-permute-done((bf16[1,384,1536]{2,1,0:T(8,128)(2,1)S(1)}, bf16[1,384,1536]{2,1,0:T(8,128)(2,1)S(1)}, u32[]{:S(2)}, u32[]{:S(2)}) %collective-permute-start.44) | collective-permute-done | bytes 1179680 | tf_op jit(solution)/shard_map/ppermute | solution.py:603
  624.4 24.7 %collective-permute-done.43 = bf16[1,384,1536]{2,1,0:T(8,128)(2,1)S(1)} collective-permute-done((bf16[1,384,1536]{2,1,0:T(8,128)(2,1)S(1)}, bf16[1,384,1536]{2,1,0:T(8,128)(2,1)S(1)}, u32[]{:S(2)}, u32[]{:S(2)}) %collective-permute-start.43) | collective-permute-done | bytes 1179680 | tf_op jit(solution)/shard_map/ppermute | solution.py:603
  652.3 5.9 weight_grads.2
  658.2 6.3 collective-permute-done.45
  666.0 7.3 weight_grads.3
  676.3 5.1 fusion.9
  691.8 6.7 collective-permute-done.48.refs_2_
  698.5 15.3 %collective-permute-done.49.refs_3_ = bf16[512,1536]{1,0:T(8,128)(2,1)S(1)} collective-permute-done((bf16[512,1536]{1,0:T(8,128)(2,1)S(1)}, bf16[512,1536]{1,0:T(8,128)(2,1)S(1)}, u32[]{:S(2)}, u32[]{:S(2)}) %collective-permute-start.49) | collective-permute-done | bytes 1572896 | tf_op jit(solution)/shard_map/ppermute | solution.py:579
  726.8 26.3 %multiply_subtract_fusion = (f32[4,384,1536]{2,1,0:T(8,128)}, f32[4,384,1536]{2,1,0:T(8,128)}, f32[4,384,1536]{2,1,0:T(8,128)}) fusion(f32[4,384,1536]{2,1,0:T(8,128)} %param.48, bf16[1,384,1536]{2,1,0:T(8,128)(2,1)} %copy-done.62, bf16[1,384,1536]{2,1,0:T(8,128)(2,1)} %copy-done.63, bf16[1,384,1536]{2,1,0:T(8,128)(2,1)S(1)} %copy-done.61, ...), kind=kLoop, calls=%fused_computation.3 | loop fusion | flops 54263808 | bytes 70778880 | tf_op jit(solution)/shard_map/sub | solution.py:530
  768.3 31.3 %collective-permute-done.56 = bf16[48,1536]{1,0:T(8,128)(2,1)S(1)} collective-permute-done((bf16[48,1536]{1,0:T(8,128)(2,1)S(1)}, bf16[48,1536]{1,0:T(8,128)(2,1)S(1)}, u32[]{:S(2)}, u32[]{:S(2)}) %collective-permute-start.56) | collective-permute-done | bytes 147488 | tf_op jit(solution)/shard_map/ppermute | solution.py:579
  824.6 12.5 %collective-permute-done.55 = bf16[192,2176]{1,0:T(8,128)(2,1)S(1)} collective-permute-done((bf16[192,2176]{1,0:T(8,128)(2,1)S(1)}, bf16[192,2176]{1,0:T(8,128)(2,1)S(1)}, u32[]{:S(2)}, u32[]{:S(2)}) %collective-permute-start.55) | collective-permute-done | bytes 835616 | tf_op jit(solution)/shard_map/ppermute | solution.py:586
  839.8 7.1 collective-permute-done.70
  847.8 5.1 collective-permute-done.64
  864.4 7.0 collective-permute-done.67
  875.9 6.3 fusion.18
  882.5 12.4 %collective-permute-done.69 = bf16[192,2176]{1,0:T(8,128)(2,1)S(1)} collective-permute-done((bf16[192,2176]{1,0:T(8,128)(2,1)S(1)}, bf16[192,2176]{1,0:T(8,128)(2,1)S(1)}, u32[]{:S(2)}, u32[]{:S(2)}) %collective-permute-start.69) | collective-permute-done | bytes 835616 | tf_op jit(solution)/shard_map/ppermute | solution.py:586
  904.0 6.7 multiply_subtract_fusion.3
  910.8 8.8 multiply_subtract_fusion.1
  (488 shorter events, 277.7 us)
Async XLA Ops:
  7.2 60.3 %all-gather.7.cloned.1.call-start = ((), (), s32[]{:S(2)}) async-start(), calls=%async_computation | async-start | bytes 8355840 | tf_op jit(solution)/shard_map/all_gather | solution.py:616
  17.6 144.7 %all-gather.9.cloned.1.call-start = ((), (), s32[]{:S(2)}) async-start(), calls=%async_computation.1 | async-start | bytes 5898240 | tf_op jit(solution)/shard_map/all_gather | solution.py:624
  18.8 259.5 %all-gather.11.cloned.1.call-start = ((), (), s32[]{:S(2)}) async-start(), calls=%async_computation.2 | async-start | bytes 11796480 | tf_op jit(solution)/shard_map/all_gather | solution.py:742
  23.5 35.7 %collective-permute-start.3 = (bf16[512,1536]{1,0:T(8,128)(2,1)}, bf16[512,1536]{1,0:T(8,128)(2,1)}, u32[]{:S(2)}, u32[]{:S(2)}) collective-permute-start(bf16[512,1536]{1,0:T(8,128)(2,1)} %rows.1), channel_id=1, source_target_pairs={{0,8},{4,12},{8,16},{12,20},{16,24},{20,28},{24,0},{28,4},{1,9},{5... | collective-permute-start | bytes 4718600 | tf_op jit(solution)/shard_map/ppermute | solution.py:579
  80.8 236.0 %all-gather.13.cloned.1.call-start = ((), (), s32[]{:S(2)}) async-start(), calls=%async_computation.3 | async-start | bytes 23592960 | tf_op jit(solution)/shard_map/all_gather | solution.py:743
  87.3 37.0 %collective-permute-start.8 = (bf16[512,1536]{1,0:T(8,128)(2,1)}, bf16[512,1536]{1,0:T(8,128)(2,1)}, u32[]{:S(2)}, u32[]{:S(2)}) collective-permute-start(bf16[512,1536]{1,0:T(8,128)(2,1)} %collective-permute-done.3.rows), channel_id=1, source_target_pairs={{0,8},{4,12},{8,16},{12,20},{16,24},{20,28},{24,0},{28,4},{1,9},{5... | collective-permute-start | bytes 4718600 | tf_op jit(solution)/shard_map/ppermute | solution.py:579
  88.9 25.9 %collective-permute-start.6 = (bf16[512,512]{1,0:T(8,128)(2,1)}, bf16[512,512]{1,0:T(8,128)(2,1)}, u32[]{:S(2)}, u32[]{:S(2)}) collective-permute-start(bf16[512,512]{1,0:T(8,128)(2,1)} %get-tuple-element.511), channel_id=1, source_target_pairs={{0,2},{1,3},{4,6},{5,7},{8,10},{9,11},{12,14},{13,15},{16,18},{17,... | collective-permute-start | bytes 1572872 | tf_op jit(solution)/shard_map/ppermute | solution.py:606
  124.3 36.8 %collective-permute-start.9 = (bf16[512,1536]{1,0:T(8,128)(2,1)}, bf16[512,1536]{1,0:T(8,128)(2,1)S(1)}, u32[]{:S(2)}, u32[]{:S(2)}) collective-permute-start(bf16[512,1536]{1,0:T(8,128)(2,1)} %collective-permute-done.8.rows), channel_id=1, source_target_pairs={{0,8},{4,12},{8,16},{12,20},{16,24},{20,28},{24,0},{28,4},{1,9},{5... | collective-permute-start | bytes 4718600 | tf_op jit(solution)/shard_map/ppermute | solution.py:579
  125.9 44.0 %collective-permute-start.10 = (bf16[320,1536]{1,0:T(8,128)(2,1)}, bf16[320,1536]{1,0:T(8,128)(2,1)}, u32[]{:S(2)}, u32[]{:S(2)}) collective-permute-start(bf16[320,1536]{1,0:T(8,128)(2,1)} %bitcast.17), channel_id=1, source_target_pairs={{0,4},{4,0},{8,12},{12,8},{16,20},{20,16},{24,28},{28,24},{1,5},{5... | collective-permute-start | bytes 2949128 | tf_op jit(solution)/shard_map/ppermute | solution.py:586
  168.6 36.9 %collective-permute-start.13 = (bf16[512,1536]{1,0:T(8,128)(2,1)S(1)}, bf16[512,1536]{1,0:T(8,128)(2,1)}, u32[]{:S(2)}, u32[]{:S(2)}) collective-permute-start(bf16[512,1536]{1,0:T(8,128)(2,1)S(1)} %multiply_convert_fusion.rows), channel_id=1, source_target_pairs={{0,8},{4,12},{8,16},{12,20},{16,24},{20,28},{24,0},{28,4},{1,9},{5... | collective-permute-start | bytes 4718600 | tf_op jit(solution)/shard_map/ppermute | solution.py:579
  174.2 22.7 %collective-permute-start.11 = (bf16[320,1536]{1,0:T(8,128)(2,1)S(1)}, bf16[320,1536]{1,0:T(8,128)(2,1)S(1)}, u32[]{:S(2)}, u32[]{:S(2)}) collective-permute-start(bf16[320,1536]{1,0:T(8,128)(2,1)S(1)} %bitcast.232), channel_id=1, source_target_pairs={{0,4},{4,0},{8,12},{12,8},{16,20},{20,16},{24,28},{28,24},{1,5},{5... | collective-permute-start | bytes 2949128 | tf_op jit(solution)/shard_map/ppermute | solution.py:586
  205.5 36.3 %collective-permute-start.15 = (bf16[512,1536]{1,0:T(8,128)(2,1)}, bf16[512,1536]{1,0:T(8,128)(2,1)}, u32[]{:S(2)}, u32[]{:S(2)}) collective-permute-start(bf16[512,1536]{1,0:T(8,128)(2,1)} %collective-permute-done.13.rows), channel_id=1, source_target_pairs={{0,8},{4,12},{8,16},{12,20},{16,24},{20,28},{24,0},{28,4},{1,9},{5... | collective-permute-start | bytes 4718600 | tf_op jit(solution)/shard_map/ppermute | solution.py:579
  218.8 26.3 %collective-permute-start.14 = (bf16[320,1536]{1,0:T(8,128)(2,1)}, bf16[320,1536]{1,0:T(8,128)(2,1)}, u32[]{:S(2)}, u32[]{:S(2)}) collective-permute-start(bf16[320,1536]{1,0:T(8,128)(2,1)} %bitcast.18), channel_id=1, source_target_pairs={{0,4},{4,0},{8,12},{12,8},{16,20},{20,16},{24,28},{28,24},{1,5},{5... | collective-permute-start | bytes 2949128 | tf_op jit(solution)/shard_map/ppermute | solution.py:586
  241.8 35.3 %collective-permute-start.19 = (bf16[512,1536]{1,0:T(8,128)(2,1)}, bf16[512,1536]{1,0:T(8,128)(2,1)S(1)}, u32[]{:S(2)}, u32[]{:S(2)}) collective-permute-start(bf16[512,1536]{1,0:T(8,128)(2,1)} %collective-permute-done.15.rows), channel_id=1, source_target_pairs={{0,8},{4,12},{8,16},{12,20},{16,24},{20,28},{24,0},{28,4},{1,9},{5... | collective-permute-start | bytes 4718600 | tf_op jit(solution)/shard_map/ppermute | solution.py:579
  266.7 27.2 %collective-permute-start.18 = (bf16[320,1536]{1,0:T(8,128)(2,1)}, bf16[320,1536]{1,0:T(8,128)(2,1)}, u32[]{:S(2)}, u32[]{:S(2)}) collective-permute-start(bf16[320,1536]{1,0:T(8,128)(2,1)} %bitcast.19), channel_id=1, source_target_pairs={{0,4},{4,0},{8,12},{12,8},{16,20},{20,16},{24,28},{28,24},{1,5},{5... | collective-permute-start | bytes 2949128 | tf_op jit(solution)/shard_map/ppermute | solution.py:586
  268.2 22.9 %collective-permute-start.20 = (f32[4,512]{1,0:T(4,128)S(1)}, f32[4,512]{1,0:T(4,128)S(1)}, u32[]{:S(2)}, u32[]{:S(2)}) collective-permute-start(f32[4,512]{1,0:T(4,128)S(1)} %collective-permute-done.16), channel_id=1, source_target_pairs={{0,8},{4,12},{8,16},{12,20},{16,24},{20,28},{24,0},{28,4},{1,9},{5... | collective-permute-start | bytes 24584 | tf_op jit(solution)/shard_map/ppermute | solution.py:579
  373.4 70.0 %collective-permute-start.37 = (bf16[2,4,384,1536]{3,2,1,0:T(8,128)(2,1)}, bf16[2,4,384,1536]{3,2,1,0:T(8,128)(2,1)}, u32[]{:S(2)}, u32[]{:S(2)}) collective-permute-start(bf16[2,4,384,1536]{3,2,1,0:T(8,128)(2,1)} %get-tuple-element.236), channel_id=1, source_target_pairs={{0,1},{1,0},{2,3},{3,2},{4,5},{5,4},{6,7},{7,6},{8,9},{9,8},{10,11... | collective-permute-start | bytes 28311560 | tf_op jit(solution)/shard_map/ppermute | solution.py:600
  373.5 24.2 %collective-permute-start.24 = (bf16[320,1536]{1,0:T(8,128)(2,1)S(1)}, bf16[320,1536]{1,0:T(8,128)(2,1)S(1)}, u32[]{:S(2)}, u32[]{:S(2)}) collective-permute-start(bf16[320,1536]{1,0:T(8,128)(2,1)S(1)} %copy-done.98), channel_id=1, source_target_pairs={{0,4},{4,0},{8,12},{12,8},{16,20},{20,16},{24,28},{28,24},{1,5},{5... | collective-permute-start | bytes 2949128 | tf_op jit(solution)/shard_map/ppermute | solution.py:586
  400.5 39.6 %collective-permute-start.28 = (bf16[512,1536]{1,0:T(8,128)(2,1)}, bf16[512,1536]{1,0:T(8,128)(2,1)S(1)}, u32[]{:S(2)}, u32[]{:S(2)}) collective-permute-start(bf16[512,1536]{1,0:T(8,128)(2,1)} %ring_rows.8), channel_id=1, source_target_pairs={{0,8},{4,12},{8,16},{12,20},{16,24},{20,28},{24,0},{28,4},{1,9},{5... | collective-permute-start | bytes 4718600 | tf_op jit(solution)/shard_map/ppermute | solution.py:579
  403.4 36.8 %collective-permute-start.25 = (bf16[320,1536]{1,0:T(8,128)(2,1)}, bf16[320,1536]{1,0:T(8,128)(2,1)S(1)}, u32[]{:S(2)}, u32[]{:S(2)}) collective-permute-start(bf16[320,1536]{1,0:T(8,128)(2,1)} %get-tuple-element.230), channel_id=1, source_target_pairs={{0,4},{4,0},{8,12},{12,8},{16,20},{20,16},{24,28},{28,24},{1,5},{5... | collective-permute-start | bytes 2949128 | tf_op jit(solution)/shard_map/ppermute | solution.py:586
  418.8 105.8 %collective-permute-start.36 = (bf16[2,4,768,384]{3,2,1,0:T(8,128)(2,1)}, bf16[2,4,768,384]{3,2,1,0:T(8,128)(2,1)}, u32[]{:S(2)}, u32[]{:S(2)}) collective-permute-start(bf16[2,4,768,384]{3,2,1,0:T(8,128)(2,1)} %get-tuple-element.241), channel_id=1, source_target_pairs={{0,1},{1,0},{2,3},{3,2},{4,5},{5,4},{6,7},{7,6},{8,9},{9,8},{10,11... | collective-permute-start | bytes 14155784 | tf_op jit(solution)/shard_map/ppermute | solution.py:600
  438.6 23.0 %collective-permute-start.29 = (bf16[320,1536]{1,0:T(8,128)(2,1)}, bf16[320,1536]{1,0:T(8,128)(2,1)S(1)}, u32[]{:S(2)}, u32[]{:S(2)}) collective-permute-start(bf16[320,1536]{1,0:T(8,128)(2,1)} %get-tuple-element.253), channel_id=1, source_target_pairs={{0,4},{4,0},{8,12},{12,8},{16,20},{20,16},{24,28},{28,24},{1,5},{5... | collective-permute-start | bytes 2949128 | tf_op jit(solution)/shard_map/ppermute | solution.py:586
  443.3 40.4 %collective-permute-start.40 = (bf16[512,1536]{1,0:T(8,128)(2,1)S(1)}, bf16[512,1536]{1,0:T(8,128)(2,1)S(1)}, u32[]{:S(2)}, u32[]{:S(2)}) collective-permute-start(bf16[512,1536]{1,0:T(8,128)(2,1)S(1)} %ring_rows.9), channel_id=1, source_target_pairs={{0,8},{4,12},{8,16},{12,20},{16,24},{20,28},{24,0},{28,4},{1,9},{5... | collective-permute-start | bytes 4718600 | tf_op jit(solution)/shard_map/ppermute | solution.py:579
  450.5 33.3 %collective-permute-start.38 = (bf16[1,384,1536]{2,1,0:T(8,128)(2,1)S(1)}, bf16[1,384,1536]{2,1,0:T(8,128)(2,1)}, u32[]{:S(2)}, u32[]{:S(2)}) collective-permute-start(bf16[1,384,1536]{2,1,0:T(8,128)(2,1)S(1)} %get-tuple-element.480), channel_id=1, source_target_pairs={{0,2},{1,3},{2,0},{3,1},{4,6},{5,7},{6,4},{7,5},{8,10},{9,11},{10,... | collective-permute-start | bytes 3538952 | tf_op jit(solution)/shard_map/ppermute | solution.py:603
  461.6 34.6 %collective-permute-start.30 = (bf16[320,1536]{1,0:T(8,128)(2,1)}, bf16[320,1536]{1,0:T(8,128)(2,1)S(1)}, u32[]{:S(2)}, u32[]{:S(2)}) collective-permute-start(bf16[320,1536]{1,0:T(8,128)(2,1)} %get-tuple-element.254), channel_id=1, source_target_pairs={{0,4},{4,0},{8,12},{12,8},{16,20},{20,16},{24,28},{28,24},{1,5},{5... | collective-permute-start | bytes 2949128 | tf_op jit(solution)/shard_map/ppermute | solution.py:586
  488.4 40.9 %collective-permute-start.41 = (bf16[512,1536]{1,0:T(8,128)(2,1)S(1)}, bf16[512,1536]{1,0:T(8,128)(2,1)S(1)}, u32[]{:S(2)}, u32[]{:S(2)}) collective-permute-start(bf16[512,1536]{1,0:T(8,128)(2,1)S(1)} %ring_rows.10), channel_id=1, source_target_pairs={{0,8},{4,12},{8,16},{12,20},{16,24},{20,28},{24,0},{28,4},{1,9},{5... | collective-permute-start | bytes 4718600 | tf_op jit(solution)/shard_map/ppermute | solution.py:579
  490.0 39.2 %collective-permute-start.39 = (bf16[1,384,1536]{2,1,0:T(8,128)(2,1)}, bf16[1,384,1536]{2,1,0:T(8,128)(2,1)S(1)}, u32[]{:S(2)}, u32[]{:S(2)}) collective-permute-start(bf16[1,384,1536]{2,1,0:T(8,128)(2,1)} %get-tuple-element.261), channel_id=1, source_target_pairs={{0,2},{1,3},{2,0},{3,1},{4,6},{5,7},{6,4},{7,5},{8,10},{9,11},{10,... | collective-permute-start | bytes 3538952 | tf_op jit(solution)/shard_map/ppermute | solution.py:603
  493.2 31.0 %collective-permute-start.35 = (f32[4,512]{1,0:T(4,128)S(1)}, f32[4,512]{1,0:T(4,128)S(1)}, u32[]{:S(2)}, u32[]{:S(2)}) collective-permute-start(f32[4,512]{1,0:T(4,128)S(1)} %fusion.60), channel_id=1, source_target_pairs={{0,8},{4,12},{8,16},{12,20},{16,24},{20,28},{24,0},{28,4},{1,9},{5... | collective-permute-start | bytes 24584 | tf_op jit(solution)/shard_map/ppermute | solution.py:579
  497.1 35.5 %collective-permute-start.31 = (bf16[320,1536]{1,0:T(8,128)(2,1)S(1)}, bf16[320,1536]{1,0:T(8,128)(2,1)S(1)}, u32[]{:S(2)}, u32[]{:S(2)}) collective-permute-start(bf16[320,1536]{1,0:T(8,128)(2,1)S(1)} %copy-done.96), channel_id=1, source_target_pairs={{0,4},{4,0},{8,12},{12,8},{16,20},{20,16},{24,28},{28,24},{1,5},{5... | collective-permute-start | bytes 2949128 | tf_op jit(solution)/shard_map/ppermute | solution.py:586
  567.9 29.9 %collective-permute-start.42 = (bf16[2,512,512]{2,1,0:T(8,128)(2,1)S(1)}, bf16[2,512,512]{2,1,0:T(8,128)(2,1)S(1)}, u32[]{:S(2)}, u32[]{:S(2)}) collective-permute-start(bf16[2,512,512]{2,1,0:T(8,128)(2,1)S(1)} %pad_select_fusion), channel_id=1, source_target_pairs={{0,1},{1,0},{2,3},{3,2},{4,5},{5,4},{6,7},{7,6},{8,9},{9,8},{10,11... | collective-permute-start | bytes 3145736 | tf_op jit(solution)/shard_map/ppermute | solution.py:600
  574.6 49.8 %collective-permute-start.44 = (bf16[1,384,1536]{2,1,0:T(8,128)(2,1)S(1)}, bf16[1,384,1536]{2,1,0:T(8,128)(2,1)S(1)}, u32[]{:S(2)}, u32[]{:S(2)}) collective-permute-start(bf16[1,384,1536]{2,1,0:T(8,128)(2,1)S(1)} %copy-done.59), channel_id=1, source_target_pairs={{0,2},{1,3},{2,0},{3,1},{4,6},{5,7},{6,4},{7,5},{8,10},{9,11},{10,... | collective-permute-start | bytes 3538952 | tf_op jit(solution)/shard_map/ppermute | solution.py:603
  597.6 51.5 %collective-permute-start.43 = (bf16[1,384,1536]{2,1,0:T(8,128)(2,1)S(1)}, bf16[1,384,1536]{2,1,0:T(8,128)(2,1)S(1)}, u32[]{:S(2)}, u32[]{:S(2)}) collective-permute-start(bf16[1,384,1536]{2,1,0:T(8,128)(2,1)S(1)} %copy-done.58), channel_id=1, source_target_pairs={{0,2},{1,3},{2,0},{3,1},{4,6},{5,7},{6,4},{7,5},{8,10},{9,11},{10,... | collective-permute-start | bytes 3538952 | tf_op jit(solution)/shard_map/ppermute | solution.py:603
  650.5 24.9 %collective-permute-start.32 = (bf16[320,1536]{1,0:T(8,128)(2,1)}, bf16[320,1536]{1,0:T(8,128)(2,1)S(1)}, u32[]{:S(2)}, u32[]{:S(2)}) collective-permute-start(bf16[320,1536]{1,0:T(8,128)(2,1)} %get-tuple-element.256), channel_id=1, source_target_pairs={{0,4},{4,0},{8,12},{12,8},{16,20},{20,16},{24,28},{28,24},{1,5},{5... | collective-permute-start | bytes 2949128 | tf_op jit(solution)/shard_map/ppermute | solution.py:586
  658.2 28.6 %collective-permute-start.51 = (bf16[2,384,1536]{2,1,0:T(8,128)(2,1)}, bf16[2,384,1536]{2,1,0:T(8,128)(2,1)}, u32[]{:S(2)}, u32[]{:S(2)}) collective-permute-start(bf16[2,384,1536]{2,1,0:T(8,128)(2,1)} %get-tuple-element.293), channel_id=1, source_target_pairs={{0,1},{1,0},{2,3},{3,2},{4,5},{5,4},{6,7},{7,6},{8,9},{9,8},{10,11... | collective-permute-start | bytes 7077896 | tf_op jit(solution)/shard_map/ppermute | solution.py:600
  673.3 43.7 %collective-permute-start.46 = (bf16[2,384,2048]{2,1,0:T(8,128)(2,1)}, bf16[2,384,2048]{2,1,0:T(8,128)(2,1)}, u32[]{:S(2)}, u32[]{:S(2)}) collective-permute-start(bf16[2,384,2048]{2,1,0:T(8,128)(2,1)} %get-tuple-element.287), channel_id=1, source_target_pairs={{0,1},{1,0},{2,3},{3,2},{4,5},{5,4},{6,7},{7,6},{8,9},{9,8},{10,11... | collective-permute-start | bytes 9437192 | tf_op jit(solution)/shard_map/ppermute | solution.py:600
  673.6 24.8 %collective-permute-start.48 = (bf16[320,1536]{1,0:T(8,128)(2,1)}, bf16[320,1536]{1,0:T(8,128)(2,1)S(1)}, u32[]{:S(2)}, u32[]{:S(2)}) collective-permute-start(bf16[320,1536]{1,0:T(8,128)(2,1)} %get-tuple-element.288), channel_id=1, source_target_pairs={{0,4},{4,0},{8,12},{12,8},{16,20},{20,16},{24,28},{28,24},{1,5},{5... | collective-permute-start | bytes 2949128 | tf_op jit(solution)/shard_map/ppermute | solution.py:586
  675.4 185.6 %collective-permute-start.33 = (bf16[320,1536]{1,0:T(8,128)(2,1)}, bf16[320,1536]{1,0:T(8,128)(2,1)S(1)}, u32[]{:S(2)}, u32[]{:S(2)}) collective-permute-start(bf16[320,1536]{1,0:T(8,128)(2,1)} %get-tuple-element.257), channel_id=1, source_target_pairs={{0,4},{4,0},{8,12},{12,8},{16,20},{20,16},{24,28},{28,24},{1,5},{5... | collective-permute-start | bytes 2949128 | tf_op jit(solution)/shard_map/ppermute | solution.py:586
  675.7 38.0 %collective-permute-start.49 = (bf16[512,1536]{1,0:T(8,128)(2,1)S(1)}, bf16[512,1536]{1,0:T(8,128)(2,1)S(1)}, u32[]{:S(2)}, u32[]{:S(2)}) collective-permute-start(bf16[512,1536]{1,0:T(8,128)(2,1)S(1)} %copy-done.6), channel_id=1, source_target_pairs={{0,8},{4,12},{8,16},{12,20},{16,24},{20,28},{24,0},{28,4},{1,9},{5... | collective-permute-start | bytes 4718600 | tf_op jit(solution)/shard_map/ppermute | solution.py:579
  689.3 33.6 %collective-permute-start.52 = (bf16[384,1536]{1,0:T(8,128)(2,1)}, bf16[384,1536]{1,0:T(8,128)(2,1)S(1)}, u32[]{:S(2)}, u32[]{:S(2)}) collective-permute-start(bf16[384,1536]{1,0:T(8,128)(2,1)} %fusion.29), channel_id=1, source_target_pairs={{0,2},{1,3},{2,0},{3,1},{4,6},{5,7},{6,4},{7,5},{8,10},{9,11},{10,... | collective-permute-start | bytes 3538952 | tf_op jit(solution)/shard_map/ppermute | solution.py:603
  716.9 37.3 %collective-permute-start.54 = (bf16[512,1536]{1,0:T(8,128)(2,1)S(1)}, bf16[512,1536]{1,0:T(8,128)(2,1)S(1)}, u32[]{:S(2)}, u32[]{:S(2)}) collective-permute-start(bf16[512,1536]{1,0:T(8,128)(2,1)S(1)} %ring_rows.13), channel_id=1, source_target_pairs={{0,8},{4,12},{8,16},{12,20},{16,24},{20,28},{24,0},{28,4},{1,9},{5... | collective-permute-start | bytes 4718600 | tf_op jit(solution)/shard_map/ppermute | solution.py:579
  722.4 41.5 %collective-permute-start.50 = (bf16[384,2176]{1,0:T(8,128)(2,1)}, bf16[384,2176]{1,0:T(8,128)(2,1)}, u32[]{:S(2)}, u32[]{:S(2)}) collective-permute-start(bf16[384,2176]{1,0:T(8,128)(2,1)} %fusion.27), channel_id=1, source_target_pairs={{0,2},{1,3},{2,0},{3,1},{4,6},{5,7},{6,4},{7,5},{8,10},{9,11},{10,... | collective-permute-start | bytes 5013512 | tf_op jit(solution)/shard_map/ppermute | solution.py:603
  725.1 33.6 %collective-permute-start.53 = (bf16[192,1536]{1,0:T(8,128)(2,1)S(1)}, bf16[192,1536]{1,0:T(8,128)(2,1)S(1)}, u32[]{:S(2)}, u32[]{:S(2)}) collective-permute-start(bf16[192,1536]{1,0:T(8,128)(2,1)S(1)} %get-tuple-element.497), channel_id=1, source_target_pairs={{0,4},{4,0},{8,12},{12,8},{16,20},{20,16},{24,28},{28,24},{1,5},{5... | collective-permute-start | bytes 1769480 | tf_op jit(solution)/shard_map/ppermute | solution.py:586
  757.6 103.5 %collective-permute-start.65 = (bf16[512,1536]{1,0:T(8,128)(2,1)S(1)}, bf16[512,1536]{1,0:T(8,128)(2,1)S(1)}, u32[]{:S(2)}, u32[]{:S(2)}) collective-permute-start(bf16[512,1536]{1,0:T(8,128)(2,1)S(1)} %ring_rows.14), channel_id=1, source_target_pairs={{0,8},{4,12},{8,16},{12,20},{16,24},{20,28},{24,0},{28,4},{1,9},{5... | collective-permute-start | bytes 4718600 | tf_op jit(solution)/shard_map/ppermute | solution.py:579
  758.9 40.7 %collective-permute-start.56 = (bf16[48,1536]{1,0:T(8,128)(2,1)S(1)}, bf16[48,1536]{1,0:T(8,128)(2,1)S(1)}, u32[]{:S(2)}, u32[]{:S(2)}) collective-permute-start(bf16[48,1536]{1,0:T(8,128)(2,1)S(1)} %get-tuple-element.508), channel_id=1, source_target_pairs={{0,8},{4,12},{8,16},{12,20},{16,24},{20,28},{24,0},{28,4},{1,9},{5... | collective-permute-start | bytes 442376 | tf_op jit(solution)/shard_map/ppermute | solution.py:579
  763.2 40.7 %collective-permute-start.57 = (bf16[48,1536]{1,0:T(8,128)(2,1)S(1)}, bf16[48,1536]{1,0:T(8,128)(2,1)S(1)}, u32[]{:S(2)}, u32[]{:S(2)}) collective-permute-start(bf16[48,1536]{1,0:T(8,128)(2,1)S(1)} %get-tuple-element.507), channel_id=1, source_target_pairs={{0,16},{4,20},{8,24},{12,28},{16,0},{20,4},{24,8},{28,12},{1,17},{... | collective-permute-start | bytes 442376 | tf_op jit(solution)/shard_map/ppermute | solution.py:579
  763.9 44.8 %collective-permute-start.58 = (bf16[48,1536]{1,0:T(8,128)(2,1)S(1)}, bf16[48,1536]{1,0:T(8,128)(2,1)S(1)}, u32[]{:S(2)}, u32[]{:S(2)}) collective-permute-start(bf16[48,1536]{1,0:T(8,128)(2,1)S(1)} %get-tuple-element.506), channel_id=1, source_target_pairs={{0,24},{4,28},{8,0},{12,4},{16,8},{20,12},{24,16},{28,20},{1,25},{... | collective-permute-start | bytes 442376 | tf_op jit(solution)/shard_map/ppermute | solution.py:579
  822.7 24.2 %collective-permute-start.70 = (bf16[192,1536]{1,0:T(8,128)(2,1)S(1)}, bf16[192,1536]{1,0:T(8,128)(2,1)S(1)}, u32[]{:S(2)}, u32[]{:S(2)}) collective-permute-start(bf16[192,1536]{1,0:T(8,128)(2,1)S(1)} %bitcast.248), channel_id=1, source_target_pairs={{0,4},{4,0},{8,12},{12,8},{16,20},{20,16},{24,28},{28,24},{1,5},{5... | collective-permute-start | bytes 1769480 | tf_op jit(solution)/shard_map/ppermute | solution.py:586
  847.2 63.5 %collective-permute-start.71 = (bf16[4,768,384]{2,1,0:T(8,128)(2,1)}, bf16[4,768,384]{2,1,0:T(8,128)(2,1)}, u32[]{:S(2)}, u32[]{:S(2)}) collective-permute-start(bf16[4,768,384]{2,1,0:T(8,128)(2,1)} %fusion.23), channel_id=1, source_target_pairs={{0,2},{1,3},{2,0},{3,1},{4,6},{5,7},{6,4},{7,5},{8,10},{9,11},{10,... | collective-permute-start | bytes 7077896 | tf_op jit(solution)/shard_map/ppermute | solution.py:603
  (135 other events, 2620.9 us)
Sparse Core Ops, SparseCore 0:
  17.7 49.7 all-gather.6
  69.6 45.2 all-gather.8
  117.0 67.6 all-gather.10
  186.8 120.0 all-gather.12

commit v4 on v2

--- a/solution.py
+++ b/solution.py
@@ -493,6 +493,52 @@
         cost_estimate=cost(2 * MODEL_WIDTH * token_rows * columns, 14e6),
         name="weight_grads",
     )(rows, *grads, *extras)
+
+
+def keep_and_send(core, pair, mine, theirs):
+    first, second = (p.astype(bf16) for p in pair)
+    mine(jnp.where(core == 0, first, second))
+    theirs(jnp.where(core == 0, second, first))
+
+
+def core_grad_kernel(core, rows, *refs):
+    *grads, mine, theirs = refs
+    span = mine.shape[1]
+    rows_t = rows[...].T
+    at = 0
+    for side in grads:
+        columns = side.shape[1]
+        pair = [dot_nn(rows_t[c * span : (c + 1) * span], side[...]) for c in range(2)]
+        where = (0, slice(None), slice(at, at + columns))
+        keep_and_send(
+            core[0],
+            pair,
+            functools.partial(mine.__setitem__, where),
+            functools.partial(theirs.__setitem__, where),
+        )
+        at += columns
+
+
+def core_grads(core, rows, grads, shards):
+    token_rows = rows.shape[0]
+    span = MODEL_WIDTH // shards
+    columns = sum(g.shape[1] for g in grads)
+    out = jax.ShapeDtypeStruct((shards // 2, span, columns), bf16)
+    block = pl.BlockSpec((1, span, columns), lambda n, c: (n, 0, 0))
+    return pl.pallas_call(
+        core_grad_kernel,
+        out_shape=(out, out),
+        grid_spec=pltpu.PrefetchScalarGridSpec(
+            num_scalar_prefetch=1,
+            grid=(shards // 2,),
+            in_specs=[pl.BlockSpec((token_rows, 2 * span), lambda n, c: (0, n))]
+            + [pl.BlockSpec(g.shape, lambda n, c: (0, 0)) for g in grads],
+            out_specs=(block, block),
+        ),
+        compiler_params=params(56, 1),
+        cost_estimate=cost(2 * MODEL_WIDTH * token_rows * columns, 14e6),
+        name="core_grads",
+    )(core, rows, *grads)
 
 
 def adamw_update(weight, moment_one, moment_two, gradient, step_rate, decay_rate):
@@ -566,6 +612,10 @@
         pairs = [(a, a + by) for a in range(shards) if 0 <= a + by < shards]
         return lax.ppermute(value, "fsdp", pairs)
 
+    chips = shards // 2
+    chip, core = place // 2, place % 2
+    core_arg = core.astype(jnp.int32).reshape(1)
+
     def core_shift(value, by):
         return lax.ppermute(value, "fsdp", [(a, a // 2 * 2 + (a + by) % 2) for a in range(shards)])
 
@@ -642,6 +692,20 @@
                     before = (piece,)
         return steps
 
+    def chip_sum(mine, mate, chip):
+        return lax.dynamic_index_in_dim(mine, chip, 0, keepdims=False).astype(
+            f32
+        ) + lax.dynamic_index_in_dim(mate, chip, 0, keepdims=False).astype(f32)
+
+    def chip_low(mine, mate):
+        return [chip_sum(mine, mate, (chip + s) % chips).astype(bf16) for s in range(1, chips)]
+
+    def chip_send(low):
+        return [y_shift(part, s) for s, part in enumerate(low, 1)]
+
+    def chip_total(mine, mate, sent):
+        return functools.reduce(lambda total, part: total + part.astype(f32), sent, chip_sum(mine, mate, chip))
+
     def ring_send(held):
         return [z_shift(held[-1], 1)]
 
@@ -682,8 +746,6 @@
     keys_local = turn_keys(pre[:, MODEL_WIDTH : MODEL_WIDTH + KV], 1.0).astype(bf16)
     kv_local = jnp.concatenate([keys_local, pre[:, MODEL_WIDTH + KV :].astype(bf16)], axis=1)
 
-    chips = shards // 2
-    core = place % 2
     same = [kv_local] + [y_up(kv_local, s) for s in range(1, chips)]
     other = [core_shift(v, 1) for v in same]
     blocks = []
@@ -801,10 +863,6 @@
         place_arg, query_rows, kv_blocks, attended, attended_grad, log_total, cosine, sine
     )
 
-    def extra_rows(*terms):
-        used = sum(t.shape[0] for t in terms)
-        return jnp.concatenate(list(terms) + [jnp.zeros((128 - used, MODEL_WIDTH), f32)], axis=0)
-
     def send_parts(parts, index, shift):
         count = parts.shape[0]
         return [lax.dynamic_index_in_dim(parts, index, 0, keepdims=False)] + [
@@ -822,21 +880,17 @@
             whole = lax.dynamic_update_index_in_dim(whole, piece, (index - s) % count, 0)
         return whole
 
-    def core_parts(terms):
-        parts = terms.reshape(chips, 2, shard_rows, terms.shape[1]).transpose(1, 0, 2, 3)
-        return send_parts(parts, core, core_shift)
-
-    def y_parts(part):
-        return send_parts(part, place // 2, y_shift)
-
     def x_parts(part):
         return send_parts(part.reshape(wide, shard_rows // wide, part.shape[1]), column, x_shift)
 
-    def z_total(part):
-        columns = part.shape[1]
-        part = add_parts(send_parts(part.reshape(depth, shard_rows // wide // depth, columns), level, z_shift))
-        part = join(part, level, depth, z_shift).reshape(shard_rows // wide, columns)
-        return join(part, column, wide, x_shift).reshape(shard_rows, columns).astype(f32)
+    def z_parts(part):
+        return send_parts(part.reshape(depth, shard_rows // wide // depth, part.shape[1]), level, z_shift)
+
+    def z_join(part):
+        return join(part, level, depth, z_shift).reshape(shard_rows // wide, part.shape[1])
+
+    def x_join(part):
+        return join(part, column, wide, x_shift).reshape(shard_rows, part.shape[1]).astype(f32)
 
     kv_back = jnp.concatenate([key_back, value_back], axis=2)
     none = jnp.zeros_like(kv_back[:1])
@@ -847,17 +901,26 @@
     kv_parts = [
         lax.ppermute(kv_low[s], "fsdp", [(a + 2 * s, a) for a in range(shards - 2 * s)]) for s in range(1, chips)
     ]
+    back_mine, back_mate = core_grads(core_arg, attended, [after(branch_grad, kv_chip)], shards)
+    back_mate = core_shift(back_mate, 1)
+    out_state = adamw_update(
+        expert_out,
+        out_first,
+        out_second,
+        after(out_part, back_mine).astype(f32),
+        0.5 / math.sqrt(FF // 8),
+        DECAY,
+    )
+    ring_step(result_held, after(result_steps[2], out_state), arrived)
+    arrived = ring_send(result_held)
+    kv_parts = after(kv_parts, result_held[1])
     kv_grad = functools.reduce(lambda total, part: total + part.astype(f32), kv_parts, kv_chip[0])
     key_pre_grad = turn_keys(kv_grad[:, :KV], -1.0)
     kv_pre_grad = jnp.concatenate([key_pre_grad, kv_grad[:, KV:]], axis=1).astype(bf16)
 
     front_terms = weight_grads(first_hidden, [pre_grad, kv_pre_grad])
-    front_part = lax.psum_scatter(after(front_terms, in_part), "fsdp", scatter_dimension=0, tiled=True)
-    front_sum = lax.psum(front_part, "expert").astype(f32)
-
-    ring_step(result_held, after(result_steps[2], front_terms), arrived)
-    arrived = ring_send(result_held)
-    pre_late, kv_late = after((pre_grad, kv_pre_grad), result_held[1])
+    front_part = lax.psum_scatter(front_terms, "fsdp", scatter_dimension=0, tiled=True)
+    pre_late, kv_late = after((pre_grad, kv_pre_grad), front_terms)
     hidden_one_grad = dot_nt(pre_late, qkv_low[:, :MODEL_WIDTH]) + dot_nt(kv_late, qkv_low[:, MODEL_WIDTH:])
     gain_one_term = jnp.sum(hidden_one_grad * normed_one, axis=0)
     scaled_one = hidden_one_grad * gain_one
@@ -866,33 +929,46 @@
         + scale_one
         * (scaled_one - normed_one * jnp.mean(scaled_one * normed_one, axis=1, keepdims=True))
     ).astype(bf16)
-    back_terms = weight_grads(
-        attended, [branch_grad], extra_rows(router_term, gain_one_term[None], gain_two_term[None])
-    )
-    back_parts = core_parts(back_terms)
-    ring_step(result_held, after(result_steps[3], back_terms), arrived)
+    extra = jnp.concatenate(
+        [
+            router_term,
+            gain_one_term[None],
+            gain_two_term[None],
+            jnp.zeros((126 - experts_all, MODEL_WIDTH), f32),
+        ],
+        axis=0,
+    )
+    extra = extra.T.astype(bf16).reshape(chips, 2, shard_rows, 128)
+    extra_mine = jnp.where(core == 0, extra[:, 0], extra[:, 1])
+    extra_mate = core_shift(jnp.where(core == 0, extra[:, 1], extra[:, 0]), 1)
+    ring_step(result_held, after(result_steps[3], extra_mine), arrived)
     arrived = ring_send(result_held)
-    out_state = adamw_update(
-        expert_out,
-        out_first,
-        out_second,
-        after(out_part, result_held[2]).astype(f32),
-        0.5 / math.sqrt(FF // 8),
-        DECAY,
-    )
-    back_part = add_parts(after(back_parts, out_state))
-    back_parts = y_parts(back_part)
+    back_mate, extra_mate = after((back_mate, extra_mate), result_held[2])
+    back_mine = jnp.concatenate([back_mine, extra_mine], axis=2)
+    back_mate = jnp.concatenate([back_mate, extra_mate], axis=2)
+    back_low = chip_low(back_mine, back_mate)
+    back_sent = chip_send(back_low)
     in_state = adamw_update(
         expert_in,
         in_first,
         in_second,
-        after(in_part, back_part).astype(f32),
+        after(in_part, back_low).astype(f32),
         0.5 / math.sqrt(MODEL_WIDTH),
         DECAY,
     )
     moe_out = ring_step(result_held, after(result_steps[0], in_state), arrived)
     layer_out = (residual + moe_out).astype(bf16)
-    back_sum = z_total(add_parts(x_parts(add_parts(after(back_parts, layer_out)))))
+    back_sent = after(back_sent, moe_out)
+    back_parts = x_parts(chip_total(back_mine, back_mate, back_sent).astype(bf16))
+    back_parts = z_parts(add_parts(back_parts))
+    back_low = add_parts(back_parts)
+    front_low = after(front_part, back_low)
+    front_parts = x_parts(front_low)
+    back_low = z_join(after(back_low, front_low))
+    front_low = add_parts(after(front_parts, back_low))
+    front_low = add_parts(z_parts(front_low))
+    back_sum = x_join(after(back_low, front_low))
+    front_sum = x_join(z_join(front_low))
     output_sum = back_sum[:, :MODEL_WIDTH]
     router_sum = back_sum[:, MODEL_WIDTH : MODEL_WIDTH + experts_all]
     query_sum = front_sum[:, :MODEL_WIDTH]

time: 895 us -> 854 us (0.954)
  waiting for transfers between devices: 418 us -> 384 us
    psum x1 -> x0, waiting for transfers between devices: 72.3 us -> none  [body(): front_sum = lax.psum(front_part, 'expert').astype(f32)]
    ppermute x27 -> x33, waiting for transfers between devices: 126 us -> 166 us  [z_shift(): lax.ppermute(value, 'expert', [(a * wide + b, (a + by) % depth * wide + b...]
    ppermute x20 -> x22, waiting for transfers between devices: 115 us -> 145 us  [x_shift(): lax.ppermute(value, 'expert', [(a * wide + b, a * wide + (b + by) % wide)...]
    ppermute x1, waiting for transfers between devices: 59.4 us -> 30.9 us  [body(): lax.ppermute(kv_low[s], 'fsdp', [(a + 2 * s, a) for a in range(shards - 2...]
    ppermute x20 -> x22, starting transfers between devices: 22.9 us -> 27.4 us  [x_shift(): lax.ppermute(value, 'expert', [(a * wide + b, a * wide + (b + by) % wide)...]
    unnamed x217 -> x206, local copies, waits for them, and re-layouts: 26.7 us -> 29.6 us
    sub x7 -> x6, other arithmetic: 50.9 us -> 49.4 us  [adamw_update(): weight - step_rate * (first_hat / (jnp.sqrt(second_hat) + ADAM_EPS) + dec...]
    ppermute x27 -> x33, starting transfers between devices: 35.9 us -> 35.1 us  [z_shift(): lax.ppermute(value, 'expert', [(a * wide + b, (a + by) % depth * wide + b...]
  transfers between devices with their start and end apart: 62 -> 70, of which waited for: 34 -> 45; matrix products, arithmetic and copies ran while one was open for 17% -> 15% of each run, Pallas kernels for 18% -> 18%
where the time goes in v4:
time: 854 us; the launch traced here: 844 us
  waiting for transfers between devices  384 us (45%)
  Pallas kernels  195 us (23%)
  other arithmetic  95.6 us (11%)
  starting transfers between devices  76.1 us (9%)
  local copies, waits for them, and re-layouts  45.5 us (5%)
  matrix products  32.7 us (4%)
  between operations  16.3 us (2%)
    ppermute x33, waiting for transfers between devices, z_shift(): lax.ppermute(value, 'expert', [(a * wide + b, (a + by) % depth * wide + b...  166 us
    ppermute x22, waiting for transfers between devices, x_shift(): lax.ppermute(value, 'expert', [(a * wide + b, a * wide + (b + by) % wide)...  145 us
    sub x6, other arithmetic, adamw_update(): weight - step_rate * (first_hat / (jnp.sqrt(second_hat) + ADAM_EPS) + dec...  49.4 us
    pallas_call x1, Pallas kernels, core_rows(): pl.pallas_call(functools.partial(core_kernel, count), out_shape=(low, low...  36.4 us
    ppermute x33, starting transfers between devices, z_shift(): lax.ppermute(value, 'expert', [(a * wide + b, (a + by) % depth * wide + b...  35.1 us
    ppermute x1, waiting for transfers between devices, body(): lax.ppermute(kv_low[s], 'fsdp', [(a + 2 * s, a) for a in range(shards - 2...  30.9 us
    unnamed x206, local copies, waits for them, and re-layouts  29.6 us
    pallas_call x8, Pallas kernels, ring_rows(): pl.pallas_call(functools.partial(ring_kernel, len(pieces)), out_shape=jax...  27.5 us
  transfers between devices with their start and end apart: 70, of which 45 were waited for; matrix products, arithmetic and copies ran while one was open for 15% of the time, Pallas kernels for 18%

profile of v4, /device:TPU:8, one launch (start us, length us, event | category | flops | bytes accessed | tf_op | source)
XLA Modules:
  0.0 844.5 jit_solution(10952099055725991168)
XLA Ops:
  35.6 17.1 %collective-permute-done.4.refs_4_ = bf16[320,1536]{1,0:T(8,128)(2,1)} collective-permute-done((bf16[320,1536]{1,0:T(8,128)(2,1)}, bf16[320,1536]{1,0:T(8,128)(2,1)}, u32[]{:S(2)}, u32[]{:S(2)}) %collective-permute-start.4) | collective-permute-done | bytes 983072 | tf_op jit(solution)/shard_map/ppermute | solution.py:605
  52.7 5.3 collective-permute-done.3.rows
  68.8 6.1 fusion.2.pre
  79.9 6.5 convert_element_type.216
  91.3 22.4 %collective-permute-done.6 = bf16[512,512]{1,0:T(8,128)(2,1)} collective-permute-done((bf16[512,512]{1,0:T(8,128)(2,1)}, bf16[512,512]{1,0:T(8,128)(2,1)}, u32[]{:S(2)}, u32[]{:S(2)}) %collective-permute-start.6) | collective-permute-done | bytes 524320 | tf_op jit(solution)/shard_map/ppermute | solution.py:626
  126.6 14.3 %attend.1 = (bf16[512,1536]{1,0:T(8,128)(2,1)}, f32[12,1,512]{2,1,0:T(1,128)}, bf16[512,1536]{1,0:T(8,128)(2,1)}) custom-call(s32[1]{0:T(128)} %bitcast.place, f32[512,2048]{1,0:T(8,128)} %copy-done.46, f32[512,128]{1,0:T(8,128)} %get-tuple-element.474.cosine, f32[512,128]{1,0:T(8,128)} %copy-done.47, bf16[4,512,512]{2,1,0:T(8,128)(2,1)} %pad_maximum_fusion.keys.values, ...), custom_call_target="tpu_custom_call" | custom-call | flops 1000000000 | bytes 1000000 | tf_op jit(solution)/shard_map/attend/pallas_call | solution.py:106
  140.9 19.4 %collective-permute-done.9.rows = bf16[512,1536]{1,0:T(8,128)(2,1)S(1)} collective-permute-done((bf16[512,1536]{1,0:T(8,128)(2,1)}, bf16[512,1536]{1,0:T(8,128)(2,1)S(1)}, u32[]{:S(2)}, u32[]{:S(2)}) %collective-permute-start.9) | collective-permute-done | bytes 1572896 | tf_op jit(solution)/shard_map/ppermute | solution.py:598
  161.4 6.1 multiply_reduce_fusion.2
  175.7 19.4 %collective-permute-done.11.refs_6_ = bf16[320,1536]{1,0:T(8,128)(2,1)S(1)} collective-permute-done((bf16[320,1536]{1,0:T(8,128)(2,1)S(1)}, bf16[320,1536]{1,0:T(8,128)(2,1)S(1)}, u32[]{:S(2)}, u32[]{:S(2)}) %collective-permute-start.11) | collective-permute-done | bytes 983072 | tf_op jit(solution)/shard_map/ppermute | solution.py:605
  196.5 8.2 collective-permute-done.13.rows
  208.8 8.1 collective-permute-done.12.refs_4_
  220.5 20.6 %collective-permute-done.16 = f32[4,512]{1,0:T(4,128)S(1)} collective-permute-done((f32[4,512]{1,0:T(4,128)S(1)}, f32[4,512]{1,0:T(4,128)S(1)}, u32[]{:S(2)}, u32[]{:S(2)}) %collective-permute-start.16) | collective-permute-done | bytes 8224 | tf_op jit(solution)/shard_map/ppermute | solution.py:598
  250.8 15.3 %collective-permute-done.17.refs_7_ = bf16[320,1536]{1,0:T(8,128)(2,1)S(1)} collective-permute-done((bf16[320,1536]{1,0:T(8,128)(2,1)S(1)}, bf16[320,1536]{1,0:T(8,128)(2,1)S(1)}, u32[]{:S(2)}, u32[]{:S(2)}) %collective-permute-start.17) | collective-permute-done | bytes 983072 | tf_op jit(solution)/shard_map/ppermute | solution.py:605
  269.6 6.8 collective-permute-done.19.rows
  277.6 13.0 %inner_rows.1.refs_9_ = bf16[4,640,768]{2,1,0:T(8,128)(2,1)} custom-call(bf16[320,1536]{1,0:T(8,128)(2,1)} %copy-done.22, bf16[320,1536]{1,0:T(8,128)(2,1)} %copy-done.23, bf16[320,1536]{1,0:T(8,128)(2,1)} %copy-done.26, bf16[320,1536]{1,0:T(8,128)(2,1)} %copy-done.29, bf16[320,1536]{1,0:T(8,128)(2,1)} %collective-permute-done.4.refs_4_, ...), custom_call_target="tpu_custom_call" | custom-call | flops 6039797760 | bytes 20000000 | tf_op jit(solution)/shard_map/inner_rows/pallas_call | solution.py:248
  295.1 5.0 collective-permute-done.22
  301.5 11.9 %collective-permute-done.23 = f32[4,4,80]{2,0,1:T(4,128)S(1)} collective-permute-done((f32[4,4,80]{2,0,1:T(4,128)S(1)}, f32[4,4,80]{2,0,1:T(4,128)S(1)}, u32[]{:S(2)}, u32[]{:S(2)}) %collective-permute-start.23) | collective-permute-done | bytes 5152 | tf_op jit(solution)/shard_map/ppermute | solution.py:605
  316.1 36.4 %core_rows.1 = (bf16[4,640,768]{2,1,0:T(8,128)(2,1)}, bf16[4,640,768]{2,1,0:T(8,128)(2,1)}, bf16[4,640,768]{2,1,0:T(8,128)(2,1)}, f32[4,640,1]{2,1,0:T(8,128)}, ...) custom-call(bf16[320,1536]{1,0:T(8,128)(2,1)} %copy-done.24, ...), custom_call_target="tpu_custom_call" | custom-call | flops 24159191040 | bytes 60000000 | tf_op jit(solution)/shard_map/core_rows/pallas_call | solution.py:305
  354.0 13.8 %down_grads.1 = bf16[4,4,768,384]{3,2,1,0:T(8,128)(2,1)} custom-call(bf16[320,1536]{1,0:T(8,128)(2,1)} %copy-done.22, bf16[320,1536]{1,0:T(8,128)(2,1)} %copy-done.23, bf16[320,1536]{1,0:T(8,128)(2,1)} %copy-done.26, bf16[320,1536]{1,0:T(8,128)(2,1)} %copy-done.29, bf16[320,1536]{1,0:T(8,128)(2,1)} %collective-permute-done.4.refs_4_, ...), custom_call_target="tpu_custom_call" | custom-call | flops 6039797760 | bytes 22000000 | tf_op jit(solution)/shard_map/down_grads/pallas_call | solution.py:364
  381.9 20.8 %in_grads.1 = bf16[4,4,384,1536]{3,2,1,0:T(8,128)(2,1)} custom-call(bf16[320,1536]{1,0:T(8,128)(2,1)} %copy-done.24, bf16[320,1536]{1,0:T(8,128)(2,1)} %copy-done.25, bf16[320,1536]{1,0:T(8,128)(2,1)} %copy-done.27, bf16[320,1536]{1,0:T(8,128)(2,1)} %copy-done.28, bf16[320,1536]{1,0:T(8,128)(2,1)} %copy-done.89, ...), custom_call_target="tpu_custom_call" | custom-call | flops 12079595520 | bytes 35000000 | tf_op jit(solution)/shard_map/in_grads/pallas_call | solution.py:392
  406.7 6.1 collective-permute-done.27
  422.5 19.7 %collective-permute-done.29.refs_2_ = bf16[320,1536]{1,0:T(8,128)(2,1)S(1)} collective-permute-done((bf16[320,1536]{1,0:T(8,128)(2,1)S(1)}, bf16[320,1536]{1,0:T(8,128)(2,1)S(1)}, u32[]{:S(2)}, u32[]{:S(2)}) %collective-permute-start.29) | collective-permute-done | bytes 983072 | tf_op jit(solution)/shard_map/ppermute | solution.py:605
  442.8 12.4 %result_rows.1 = (bf16[320,1536]{1,0:T(8,128)(2,1)}, bf16[320,1536]{1,0:T(8,128)(2,1)}, bf16[320,1536]{1,0:T(8,128)(2,1)}, bf16[320,1536]{1,0:T(8,128)(2,1)}, bf...) custom-call(bf16[4,640,768]{2,1,0:T(8,128)(2,1)} %get-tuple-element., ...), custom_call_target="tpu_custom_call" | custom-call | flops 6039797760 | bytes 22000000 | tf_op jit(solution)/shard_map/result_rows/pallas_call | solution.py:336
  465.8 19.0 %collective-permute-done.35 = f32[4,512]{1,0:T(4,128)S(1)} collective-permute-done((f32[4,512]{1,0:T(4,128)S(1)}, f32[4,512]{1,0:T(4,128)S(1)}, u32[]{:S(2)}, u32[]{:S(2)}) %collective-permute-start.35) | collective-permute-done | bytes 8224 | tf_op jit(solution)/shard_map/ppermute | solution.py:598
  491.3 4.7 multiply_reduce_fusion
  503.3 17.8 %attend_back.1 = (bf16[512,1536]{1,0:T(8,128)(2,1)}, bf16[4,512,256]{2,1,0:T(8,128)(2,1)}, bf16[4,512,256]{2,1,0:T(8,128)(2,1)}) custom-call(s32[1]{0:T(128)} %bitcast.place, bf16[512,1536]{1,0:T(8,128)(2,1)} %get-tuple-element.250.query, bf16[4,512,512]{2,1,0:T(8,128)(2,1)} %pad_maximum_fusion.keys.values, ...), custom_call_target="tpu_custom_call" | custom-call | flops 1000000000 | bytes 1000000 | tf_op jit(solution)/shard_map/attend_back/pallas_call | solution.py:182
  525.9 6.7 core_grads.1
  534.3 12.2 %multiply_subtract_fusion.1 = (f32[4,768,384]{2,1,0:T(8,128)}, f32[4,768,384]{2,1,0:T(8,128)}, f32[4,768,384]{2,1,0:T(8,128)}) fusion(f32[4,768,384]{2,1,0:T(8,128)} %param.51, bf16[4,768,384]{2,1,0:T(8,128)(2,1)} %bitcast.214, f32[4,768,384]{2,1,0:T(8,128)} %param.52, f32[4,768,384]{2,1,0:T(8,128)} %param.53), kind=kLoop, calls=%fused_computation.25 | loop fusion | flops 18874368 | bytes 30670848 | tf_op jit(solution)/shard_map/sub | solution.py:549
  547.1 14.3 %collective-permute-done.41.refs_3_ = bf16[512,1536]{1,0:T(8,128)(2,1)S(1)} collective-permute-done((bf16[512,1536]{1,0:T(8,128)(2,1)S(1)}, bf16[512,1536]{1,0:T(8,128)(2,1)S(1)}, u32[]{:S(2)}, u32[]{:S(2)}) %collective-permute-start.41) | collective-permute-done | bytes 1572896 | tf_op jit(solution)/shard_map/ppermute | solution.py:598
  564.6 30.9 %collective-permute-done.39 = bf16[512,512]{1,0:T(8,128)(2,1)S(1)} collective-permute-done((bf16[512,512]{1,0:T(8,128)(2,1)S(1)}, bf16[512,512]{1,0:T(8,128)(2,1)S(1)}, u32[]{:S(2)}, u32[]{:S(2)}) %collective-permute-start.39) | collective-permute-done | bytes 524320 | tf_op jit(solution)/shard_map/ppermute | solution.py:902
  597.1 7.3 weight_grads.1
  607.7 5.0 fusion.11
  612.7 5.1 fusion.15
  619.2 10.7 %collective-permute-done.32.refs_2_ = bf16[320,1536]{1,0:T(8,128)(2,1)} collective-permute-done((bf16[320,1536]{1,0:T(8,128)(2,1)}, bf16[320,1536]{1,0:T(8,128)(2,1)}, u32[]{:S(2)}, u32[]{:S(2)}) %collective-permute-start.32) | collective-permute-done | bytes 983072 | tf_op jit(solution)/shard_map/ppermute | solution.py:605
  630.8 14.1 %collective-permute-done.44.refs_3_ = bf16[512,1536]{1,0:T(8,128)(2,1)S(1)} collective-permute-done((bf16[512,1536]{1,0:T(8,128)(2,1)S(1)}, bf16[512,1536]{1,0:T(8,128)(2,1)S(1)}, u32[]{:S(2)}, u32[]{:S(2)}) %collective-permute-start.44) | collective-permute-done | bytes 1572896 | tf_op jit(solution)/shard_map/ppermute | solution.py:598
  655.5 8.2 collective-permute-start.46
  663.7 24.4 %multiply_subtract_fusion = (f32[4,384,1536]{2,1,0:T(8,128)}, f32[4,384,1536]{2,1,0:T(8,128)}, f32[4,384,1536]{2,1,0:T(8,128)}) fusion(f32[4,384,1536]{2,1,0:T(8,128)} %param.48, bf16[4,384,1536]{2,1,0:T(8,128)(2,1)} %bitcast.205, f32[4,384,1536]{2,1,0:T(8,128)} %param.49, f32[4,384,1536]{2,1,0:T(8,128)} %param.50), kind=kLoop, calls=%fused_computation.4 | loop fusion | flops 37748736 | bytes 61341696 | tf_op jit(solution)/shard_map/sub | solution.py:549
  688.5 4.7 ring_rows.15
  693.1 12.7 %collective-permute-done.46 = bf16[384,1664]{1,0:T(8,128)(2,1)S(1)} collective-permute-done((bf16[384,1664]{1,0:T(8,128)(2,1)}, bf16[384,1664]{1,0:T(8,128)(2,1)S(1)}, u32[]{:S(2)}, u32[]{:S(2)}) %collective-permute-start.46) | collective-permute-done | bytes 1277984 | tf_op jit(solution)/shard_map/ppermute | solution.py:623
  709.0 14.8 %collective-permute-done.47 = bf16[192,1664]{1,0:T(8,128)(2,1)} collective-permute-done((bf16[192,1664]{1,0:T(8,128)(2,1)S(1)}, bf16[192,1664]{1,0:T(8,128)(2,1)}, u32[]{:S(2)}, u32[]{:S(2)}) %collective-permute-start.47) | collective-permute-done | bytes 639008 | tf_op jit(solution)/shard_map/ppermute | solution.py:605
  730.2 7.2 collective-permute-done.48
  748.4 7.1 collective-permute-done.52
  756.2 7.9 collective-permute-done.54
  769.4 5.0 fusion.19
  774.4 4.9 collective-permute-done.55
  792.6 8.5 %collective-permute-done.60 = bf16[48,2048]{1,0:T(8,128)(2,1)S(1)} collective-permute-done((bf16[48,2048]{1,0:T(8,128)(2,1)S(1)}, bf16[48,2048]{1,0:T(8,128)(2,1)S(1)}, u32[]{:S(2)}, u32[]{:S(2)}) %collective-permute-start.60) | collective-permute-done | bytes 196640 | tf_op jit(solution)/shard_map/ppermute | solution.py:598
  809.8 11.6 %collective-permute-done.62 = bf16[192,2048]{1,0:T(8,128)(2,1)} collective-permute-done((bf16[192,2048]{1,0:T(8,128)(2,1)S(1)}, bf16[192,2048]{1,0:T(8,128)(2,1)}, u32[]{:S(2)}, u32[]{:S(2)}) %collective-permute-start.62) | collective-permute-done | bytes 786464 | tf_op jit(solution)/shard_map/ppermute | solution.py:605
  826.4 8.9 %multiply_subtract_fusion.2 = (f32[384,1536]{1,0:T(8,128)}, f32[384,1536]{1,0:T(8,128)}, f32[384,1536]{1,0:T(8,128)}, f32[384,1536]{1,0:T(8,128)}, f32[384,1536]{1,0:T(8,128)}, /*index=5*/f32[384,1536]{1,0:T(8,128)}) fusion(f32[384,1536]{1,0:T(8,128)S(1)} %copy-done.43, f32[384,1664]{1,0:T(8,128)S(1)} %bitcast_convert_fusion.1, f32[384,1536]{1,0:T(8,128)} %param.43, ...), kind=kLoop, calls=%fused_computation.52 | loop fusion | flops 17694720 | bytes 33030144 | tf_op jit(solution)/shard_map/sub | solution.py:549
  (459 shorter events, 240.0 us)
Async XLA Ops:
  7.2 59.0 %all-gather.7.cloned.1.call-start = ((), (), s32[]{:S(2)}) async-start(), calls=%async_computation.3 | async-start | bytes 8355840 | tf_op jit(solution)/shard_map/all_gather | solution.py:636
  16.4 145.1 %all-gather.9.cloned.1.call-start = ((), (), s32[]{:S(2)}) async-start(), calls=%async_computation.4 | async-start | bytes 5898240 | tf_op jit(solution)/shard_map/all_gather | solution.py:644
  17.6 260.0 %all-gather.11.cloned.1.call-start = ((), (), s32[]{:S(2)}) async-start(), calls=%async_computation.8 | async-start | bytes 11796480 | tf_op jit(solution)/shard_map/all_gather | solution.py:762
  22.3 35.7 %collective-permute-start.3 = (bf16[512,1536]{1,0:T(8,128)(2,1)}, bf16[512,1536]{1,0:T(8,128)(2,1)}, u32[]{:S(2)}, u32[]{:S(2)}) collective-permute-start(bf16[512,1536]{1,0:T(8,128)(2,1)} %rows.1), channel_id=1, source_target_pairs={{0,8},{4,12},{8,16},{12,20},{16,24},{20,28},{24,0},{28,4},{1,9},{5... | collective-permute-start | bytes 4718600 | tf_op jit(solution)/shard_map/ppermute | solution.py:598
  30.3 22.4 %collective-permute-start.4 = (bf16[320,1536]{1,0:T(8,128)(2,1)}, bf16[320,1536]{1,0:T(8,128)(2,1)}, u32[]{:S(2)}, u32[]{:S(2)}) collective-permute-start(bf16[320,1536]{1,0:T(8,128)(2,1)} %bitcast.10), channel_id=1, source_target_pairs={{0,4},{4,0},{8,12},{12,8},{16,20},{20,16},{24,28},{28,24},{1,5},{5... | collective-permute-start | bytes 2949128 | tf_op jit(solution)/shard_map/ppermute | solution.py:605
  79.9 236.2 %all-gather.13.cloned.1.call-start = ((), (), s32[]{:S(2)}) async-start(), calls=%async_computation.9 | async-start | bytes 23592960 | tf_op jit(solution)/shard_map/all_gather | solution.py:763
  86.4 416.9 %reduce-scatter.6.cloned.1.call-start = ((), (), s32[]{:S(2)}) async-start(), calls=%async_computation.6 | async-start | bytes 11796480 | tf_op jit(solution)/shard_map/reduce_scatter | solution.py:823
  86.4 37.0 %collective-permute-start.8 = (bf16[512,1536]{1,0:T(8,128)(2,1)}, bf16[512,1536]{1,0:T(8,128)(2,1)}, u32[]{:S(2)}, u32[]{:S(2)}) collective-permute-start(bf16[512,1536]{1,0:T(8,128)(2,1)} %collective-permute-done.3.rows), channel_id=1, source_target_pairs={{0,8},{4,12},{8,16},{12,20},{16,24},{20,28},{24,0},{28,4},{1,9},{5... | collective-permute-start | bytes 4718600 | tf_op jit(solution)/shard_map/ppermute | solution.py:598
  88.0 25.7 %collective-permute-start.6 = (bf16[512,512]{1,0:T(8,128)(2,1)}, bf16[512,512]{1,0:T(8,128)(2,1)}, u32[]{:S(2)}, u32[]{:S(2)}) collective-permute-start(bf16[512,512]{1,0:T(8,128)(2,1)} %get-tuple-element.470), channel_id=1, source_target_pairs={{0,2},{1,3},{4,6},{5,7},{8,10},{9,11},{12,14},{13,15},{16,18},{17,... | collective-permute-start | bytes 1572872 | tf_op jit(solution)/shard_map/ppermute | solution.py:626
  91.3 22.5 %collective-permute-start.5 = (bf16[512,512]{1,0:T(8,128)(2,1)}, bf16[512,512]{1,0:T(8,128)(2,1)}, u32[]{:S(2)}, u32[]{:S(2)}) collective-permute-start(bf16[512,512]{1,0:T(8,128)(2,1)} %get-tuple-element.470), channel_id=1, source_target_pairs={{0,1},{1,0},{2,3},{3,2},{4,5},{5,4},{6,7},{7,6},{8,9},{9,8},{10,11... | collective-permute-start | bytes 1572872 | tf_op jit(solution)/shard_map/ppermute | solution.py:620
  123.5 36.8 %collective-permute-start.9 = (bf16[512,1536]{1,0:T(8,128)(2,1)}, bf16[512,1536]{1,0:T(8,128)(2,1)S(1)}, u32[]{:S(2)}, u32[]{:S(2)}) collective-permute-start(bf16[512,1536]{1,0:T(8,128)(2,1)} %collective-permute-done.8.rows), channel_id=1, source_target_pairs={{0,8},{4,12},{8,16},{12,20},{16,24},{20,28},{24,0},{28,4},{1,9},{5... | collective-permute-start | bytes 4718600 | tf_op jit(solution)/shard_map/ppermute | solution.py:598
  125.1 44.1 %collective-permute-start.10 = (bf16[320,1536]{1,0:T(8,128)(2,1)}, bf16[320,1536]{1,0:T(8,128)(2,1)}, u32[]{:S(2)}, u32[]{:S(2)}) collective-permute-start(bf16[320,1536]{1,0:T(8,128)(2,1)} %bitcast.17), channel_id=1, source_target_pairs={{0,4},{4,0},{8,12},{12,8},{16,20},{20,16},{24,28},{28,24},{1,5},{5... | collective-permute-start | bytes 2949128 | tf_op jit(solution)/shard_map/ppermute | solution.py:605
  167.9 36.9 %collective-permute-start.13 = (bf16[512,1536]{1,0:T(8,128)(2,1)S(1)}, bf16[512,1536]{1,0:T(8,128)(2,1)}, u32[]{:S(2)}, u32[]{:S(2)}) collective-permute-start(bf16[512,1536]{1,0:T(8,128)(2,1)S(1)} %multiply_convert_fusion.rows), channel_id=1, source_target_pairs={{0,8},{4,12},{8,16},{12,20},{16,24},{20,28},{24,0},{28,4},{1,9},{5... | collective-permute-start | bytes 4718600 | tf_op jit(solution)/shard_map/ppermute | solution.py:598
  172.4 22.7 %collective-permute-start.11 = (bf16[320,1536]{1,0:T(8,128)(2,1)S(1)}, bf16[320,1536]{1,0:T(8,128)(2,1)S(1)}, u32[]{:S(2)}, u32[]{:S(2)}) collective-permute-start(bf16[320,1536]{1,0:T(8,128)(2,1)S(1)} %bitcast.200), channel_id=1, source_target_pairs={{0,4},{4,0},{8,12},{12,8},{16,20},{20,16},{24,28},{28,24},{1,5},{5... | collective-permute-start | bytes 2949128 | tf_op jit(solution)/shard_map/ppermute | solution.py:605
  195.1 21.8 %collective-permute-start.12 = (bf16[320,1536]{1,0:T(8,128)(2,1)S(1)}, bf16[320,1536]{1,0:T(8,128)(2,1)S(1)}, u32[]{:S(2)}, u32[]{:S(2)}) collective-permute-start(bf16[320,1536]{1,0:T(8,128)(2,1)S(1)} %bitcast.198), channel_id=1, source_target_pairs={{0,4},{4,0},{8,12},{12,8},{16,20},{20,16},{24,28},{28,24},{1,5},{5... | collective-permute-start | bytes 2949128 | tf_op jit(solution)/shard_map/ppermute | solution.py:605
  204.8 36.3 %collective-permute-start.15 = (bf16[512,1536]{1,0:T(8,128)(2,1)}, bf16[512,1536]{1,0:T(8,128)(2,1)}, u32[]{:S(2)}, u32[]{:S(2)}) collective-permute-start(bf16[512,1536]{1,0:T(8,128)(2,1)} %collective-permute-done.13.rows), channel_id=1, source_target_pairs={{0,8},{4,12},{8,16},{12,20},{16,24},{20,28},{24,0},{28,4},{1,9},{5... | collective-permute-start | bytes 4718600 | tf_op jit(solution)/shard_map/ppermute | solution.py:598
  216.9 27.5 %collective-permute-start.14 = (bf16[320,1536]{1,0:T(8,128)(2,1)}, bf16[320,1536]{1,0:T(8,128)(2,1)}, u32[]{:S(2)}, u32[]{:S(2)}) collective-permute-start(bf16[320,1536]{1,0:T(8,128)(2,1)} %bitcast.18), channel_id=1, source_target_pairs={{0,4},{4,0},{8,12},{12,8},{16,20},{20,16},{24,28},{28,24},{1,5},{5... | collective-permute-start | bytes 2949128 | tf_op jit(solution)/shard_map/ppermute | solution.py:605
  220.1 21.0 %collective-permute-start.16 = (f32[4,512]{1,0:T(4,128)S(1)}, f32[4,512]{1,0:T(4,128)S(1)}, u32[]{:S(2)}, u32[]{:S(2)}) collective-permute-start(f32[4,512]{1,0:T(4,128)S(1)} %fusion.67), channel_id=1, source_target_pairs={{0,8},{4,12},{8,16},{12,20},{16,24},{20,28},{24,0},{28,4},{1,9},{5... | collective-permute-start | bytes 24584 | tf_op jit(solution)/shard_map/ppermute | solution.py:598
  241.1 35.3 %collective-permute-start.19 = (bf16[512,1536]{1,0:T(8,128)(2,1)}, bf16[512,1536]{1,0:T(8,128)(2,1)S(1)}, u32[]{:S(2)}, u32[]{:S(2)}) collective-permute-start(bf16[512,1536]{1,0:T(8,128)(2,1)} %collective-permute-done.15.rows), channel_id=1, source_target_pairs={{0,8},{4,12},{8,16},{12,20},{16,24},{20,28},{24,0},{28,4},{1,9},{5... | collective-permute-start | bytes 4718600 | tf_op jit(solution)/shard_map/ppermute | solution.py:598
  244.4 21.7 %collective-permute-start.17 = (bf16[320,1536]{1,0:T(8,128)(2,1)S(1)}, bf16[320,1536]{1,0:T(8,128)(2,1)S(1)}, u32[]{:S(2)}, u32[]{:S(2)}) collective-permute-start(bf16[320,1536]{1,0:T(8,128)(2,1)S(1)} %bitcast.199), channel_id=1, source_target_pairs={{0,4},{4,0},{8,12},{12,8},{16,20},{20,16},{24,28},{28,24},{1,5},{5... | collective-permute-start | bytes 2949128 | tf_op jit(solution)/shard_map/ppermute | solution.py:605
  266.1 27.3 %collective-permute-start.18 = (bf16[320,1536]{1,0:T(8,128)(2,1)}, bf16[320,1536]{1,0:T(8,128)(2,1)}, u32[]{:S(2)}, u32[]{:S(2)}) collective-permute-start(bf16[320,1536]{1,0:T(8,128)(2,1)} %bitcast.19), channel_id=1, source_target_pairs={{0,4},{4,0},{8,12},{12,8},{16,20},{20,16},{24,28},{28,24},{1,5},{5... | collective-permute-start | bytes 2949128 | tf_op jit(solution)/shard_map/ppermute | solution.py:605
  267.5 23.1 %collective-permute-start.20 = (f32[4,512]{1,0:T(4,128)S(1)}, f32[4,512]{1,0:T(4,128)S(1)}, u32[]{:S(2)}, u32[]{:S(2)}) collective-permute-start(f32[4,512]{1,0:T(4,128)S(1)} %collective-permute-done.16), channel_id=1, source_target_pairs={{0,8},{4,12},{8,16},{12,20},{16,24},{20,28},{24,0},{28,4},{1,9},{5... | collective-permute-start | bytes 24584 | tf_op jit(solution)/shard_map/ppermute | solution.py:598
  293.4 20.1 %collective-permute-start.21 = (bf16[320,1536]{1,0:T(8,128)(2,1)S(1)}, bf16[320,1536]{1,0:T(8,128)(2,1)S(1)}, u32[]{:S(2)}, u32[]{:S(2)}) collective-permute-start(bf16[320,1536]{1,0:T(8,128)(2,1)S(1)} %bitcast.197), channel_id=1, source_target_pairs={{0,4},{4,0},{8,12},{12,8},{16,20},{20,16},{24,28},{28,24},{1,5},{5... | collective-permute-start | bytes 2949128 | tf_op jit(solution)/shard_map/ppermute | solution.py:605
  352.5 19.3 %collective-permute-start.24 = (bf16[320,1536]{1,0:T(8,128)(2,1)}, bf16[320,1536]{1,0:T(8,128)(2,1)}, u32[]{:S(2)}, u32[]{:S(2)}) collective-permute-start(bf16[320,1536]{1,0:T(8,128)(2,1)} %get-tuple-element.214), channel_id=1, source_target_pairs={{0,4},{4,0},{8,12},{12,8},{16,20},{20,16},{24,28},{28,24},{1,5},{5... | collective-permute-start | bytes 2949128 | tf_op jit(solution)/shard_map/ppermute | solution.py:605
  377.5 286.2 %reduce-scatter.4.cloned.1.call-start = ((), (), s32[]{:S(2)}) async-start(), calls=%async_computation.5 | async-start | bytes 23592960 | tf_op jit(solution)/shard_map/reduce_scatter | solution.py:832
  379.3 23.4 %collective-permute-start.26 = (f32[4,4,80]{2,1,0:T(4,128)S(1)}, f32[4,4,80]{2,1,0:T(4,128)S(1)}, u32[]{:S(2)}, u32[]{:S(2)}) collective-permute-start(f32[4,4,80]{2,1,0:T(4,128)S(1)} %get-tuple-element.476), channel_id=1, source_target_pairs={{0,4},{4,0},{8,12},{12,8},{16,20},{20,16},{24,28},{28,24},{1,5},{5... | collective-permute-start | bytes 15368 | tf_op jit(solution)/shard_map/ppermute | solution.py:605
  380.8 33.0 %collective-permute-start.28 = (bf16[512,1536]{1,0:T(8,128)(2,1)}, bf16[512,1536]{1,0:T(8,128)(2,1)S(1)}, u32[]{:S(2)}, u32[]{:S(2)}) collective-permute-start(bf16[512,1536]{1,0:T(8,128)(2,1)} %copy-done.9), channel_id=1, source_target_pairs={{0,8},{4,12},{8,16},{12,20},{16,24},{20,28},{24,0},{28,4},{1,9},{5... | collective-permute-start | bytes 4718600 | tf_op jit(solution)/shard_map/ppermute | solution.py:598
  381.3 31.5 %collective-permute-start.25 = (bf16[320,1536]{1,0:T(8,128)(2,1)}, bf16[320,1536]{1,0:T(8,128)(2,1)S(1)}, u32[]{:S(2)}, u32[]{:S(2)}) collective-permute-start(bf16[320,1536]{1,0:T(8,128)(2,1)} %get-tuple-element.215), channel_id=1, source_target_pairs={{0,4},{4,0},{8,12},{12,8},{16,20},{20,16},{24,28},{28,24},{1,5},{5... | collective-permute-start | bytes 2949128 | tf_op jit(solution)/shard_map/ppermute | solution.py:605
  419.4 322.0 %reduce-scatter.8.cloned.1.call-start = ((), (), s32[]{:S(2)}) async-start(), calls=%async_computation.7 | async-start | bytes 7864320 | tf_op jit(solution)/shard_map/reduce_scatter | solution.py:922
  419.5 35.7 %collective-permute-start.36 = (bf16[512,1536]{1,0:T(8,128)(2,1)S(1)}, bf16[512,1536]{1,0:T(8,128)(2,1)S(1)}, u32[]{:S(2)}, u32[]{:S(2)}) collective-permute-start(bf16[512,1536]{1,0:T(8,128)(2,1)S(1)} %ring_rows.9), channel_id=1, source_target_pairs={{0,8},{4,12},{8,16},{12,20},{16,24},{20,28},{24,0},{28,4},{1,9},{5... | collective-permute-start | bytes 4718600 | tf_op jit(solution)/shard_map/ppermute | solution.py:598
  420.6 21.6 %collective-permute-start.29 = (bf16[320,1536]{1,0:T(8,128)(2,1)S(1)}, bf16[320,1536]{1,0:T(8,128)(2,1)S(1)}, u32[]{:S(2)}, u32[]{:S(2)}) collective-permute-start(bf16[320,1536]{1,0:T(8,128)(2,1)S(1)} %copy-done.92), channel_id=1, source_target_pairs={{0,4},{4,0},{8,12},{12,8},{16,20},{20,16},{24,28},{28,24},{1,5},{5... | collective-permute-start | bytes 2949128 | tf_op jit(solution)/shard_map/ppermute | solution.py:605
  421.2 34.0 %collective-permute-start.34 = (f32[4,512]{1,0:T(4,128)S(1)}, f32[4,512]{1,0:T(4,128)S(1)}, u32[]{:S(2)}, u32[]{:S(2)}) collective-permute-start(f32[4,512]{1,0:T(4,128)S(1)} %fusion.64), channel_id=1, source_target_pairs={{0,8},{4,12},{8,16},{12,20},{16,24},{20,28},{24,0},{28,4},{1,9},{5... | collective-permute-start | bytes 24584 | tf_op jit(solution)/shard_map/ppermute | solution.py:598
  442.2 22.0 %collective-permute-start.30 = (bf16[320,1536]{1,0:T(8,128)(2,1)}, bf16[320,1536]{1,0:T(8,128)(2,1)S(1)}, u32[]{:S(2)}, u32[]{:S(2)}) collective-permute-start(bf16[320,1536]{1,0:T(8,128)(2,1)} %get-tuple-element.236), channel_id=1, source_target_pairs={{0,4},{4,0},{8,12},{12,8},{16,20},{20,16},{24,28},{28,24},{1,5},{5... | collective-permute-start | bytes 2949128 | tf_op jit(solution)/shard_map/ppermute | solution.py:605
  458.6 26.6 %collective-permute-start.37 = (bf16[512,1536]{1,0:T(8,128)(2,1)S(1)}, bf16[512,1536]{1,0:T(8,128)(2,1)S(1)}, u32[]{:S(2)}, u32[]{:S(2)}) collective-permute-start(bf16[512,1536]{1,0:T(8,128)(2,1)S(1)} %ring_rows.10), channel_id=1, source_target_pairs={{0,8},{4,12},{8,16},{12,20},{16,24},{20,28},{24,0},{28,4},{1,9},{5... | collective-permute-start | bytes 4718600 | tf_op jit(solution)/shard_map/ppermute | solution.py:598
  464.2 24.4 %collective-permute-start.31 = (bf16[320,1536]{1,0:T(8,128)(2,1)S(1)}, bf16[320,1536]{1,0:T(8,128)(2,1)S(1)}, u32[]{:S(2)}, u32[]{:S(2)}) collective-permute-start(bf16[320,1536]{1,0:T(8,128)(2,1)S(1)} %copy-done.95), channel_id=1, source_target_pairs={{0,4},{4,0},{8,12},{12,8},{16,20},{20,16},{24,28},{28,24},{1,5},{5... | collective-permute-start | bytes 2949128 | tf_op jit(solution)/shard_map/ppermute | solution.py:605
  464.9 19.9 %collective-permute-start.35 = (f32[4,512]{1,0:T(4,128)S(1)}, f32[4,512]{1,0:T(4,128)S(1)}, u32[]{:S(2)}, u32[]{:S(2)}) collective-permute-start(f32[4,512]{1,0:T(4,128)S(1)} %fusion.63), channel_id=1, source_target_pairs={{0,8},{4,12},{8,16},{12,20},{16,24},{20,28},{24,0},{28,4},{1,9},{5... | collective-permute-start | bytes 24584 | tf_op jit(solution)/shard_map/ppermute | solution.py:598
  523.8 23.3 %collective-permute-start.40 = (bf16[320,1536]{1,0:T(8,128)(2,1)S(1)}, bf16[320,1536]{1,0:T(8,128)(2,1)S(1)}, u32[]{:S(2)}, u32[]{:S(2)}) collective-permute-start(bf16[320,1536]{1,0:T(8,128)(2,1)S(1)} %copy-done.91), channel_id=1, source_target_pairs={{0,4},{4,0},{8,12},{12,8},{16,20},{20,16},{24,28},{28,24},{1,5},{5... | collective-permute-start | bytes 2949128 | tf_op jit(solution)/shard_map/ppermute | solution.py:605
  525.1 36.3 %collective-permute-start.41 = (bf16[512,1536]{1,0:T(8,128)(2,1)S(1)}, bf16[512,1536]{1,0:T(8,128)(2,1)S(1)}, u32[]{:S(2)}, u32[]{:S(2)}) collective-permute-start(bf16[512,1536]{1,0:T(8,128)(2,1)S(1)} %copy-done.8), channel_id=1, source_target_pairs={{0,8},{4,12},{8,16},{12,20},{16,24},{20,28},{24,0},{28,4},{1,9},{5... | collective-permute-start | bytes 4718600 | tf_op jit(solution)/shard_map/ppermute | solution.py:598
  532.7 62.8 %collective-permute-start.39 = (bf16[512,512]{1,0:T(8,128)(2,1)S(1)}, bf16[512,512]{1,0:T(8,128)(2,1)S(1)}, u32[]{:S(2)}, u32[]{:S(2)}) collective-permute-start(bf16[512,512]{1,0:T(8,128)(2,1)S(1)} %fusion.33), channel_id=1, source_target_pairs={{2,0},{3,1},{6,4},{7,5},{10,8},{11,9},{14,12},{15,13},{18,16},{19,... | collective-permute-start | bytes 1572872 | tf_op jit(solution)/shard_map/ppermute | solution.py:902
  604.4 47.2 %collective-permute-start.42 = (bf16[2,384,1536]{2,1,0:T(8,128)(2,1)}, bf16[2,384,1536]{2,1,0:T(8,128)(2,1)}, u32[]{:S(2)}, u32[]{:S(2)}) collective-permute-start(bf16[2,384,1536]{2,1,0:T(8,128)(2,1)} %get-tuple-element.268), channel_id=1, source_target_pairs={{0,1},{1,0},{2,3},{3,2},{4,5},{5,4},{6,7},{7,6},{8,9},{9,8},{10,11... | collective-permute-start | bytes 7077896 | tf_op jit(solution)/shard_map/ppermute | solution.py:620
  605.3 24.5 %collective-permute-start.32 = (bf16[320,1536]{1,0:T(8,128)(2,1)}, bf16[320,1536]{1,0:T(8,128)(2,1)}, u32[]{:S(2)}, u32[]{:S(2)}) collective-permute-start(bf16[320,1536]{1,0:T(8,128)(2,1)} %get-tuple-element.238), channel_id=1, source_target_pairs={{0,4},{4,0},{8,12},{12,8},{16,20},{20,16},{24,28},{28,24},{1,5},{5... | collective-permute-start | bytes 2949128 | tf_op jit(solution)/shard_map/ppermute | solution.py:605
  606.6 38.3 %collective-permute-start.44 = (bf16[512,1536]{1,0:T(8,128)(2,1)S(1)}, bf16[512,1536]{1,0:T(8,128)(2,1)S(1)}, u32[]{:S(2)}, u32[]{:S(2)}) collective-permute-start(bf16[512,1536]{1,0:T(8,128)(2,1)S(1)} %ring_rows.13), channel_id=1, source_target_pairs={{0,8},{4,12},{8,16},{12,20},{16,24},{20,28},{24,0},{28,4},{1,9},{5... | collective-permute-start | bytes 4718600 | tf_op jit(solution)/shard_map/ppermute | solution.py:598
  619.2 32.5 %collective-permute-start.43 = (bf16[2,384,128]{2,1,0:T(8,128)(2,1)}, bf16[2,384,128]{2,1,0:T(8,128)(2,1)S(1)}, u32[]{:S(2)}, u32[]{:S(2)}) collective-permute-start(bf16[2,384,128]{2,1,0:T(8,128)(2,1)} %get-tuple-element.471), channel_id=1, source_target_pairs={{0,1},{1,0},{2,3},{3,2},{4,5},{5,4},{6,7},{7,6},{8,9},{9,8},{10,11... | collective-permute-start | bytes 589832 | tf_op jit(solution)/shard_map/ppermute | solution.py:620
  629.8 58.3 %collective-permute-start.33 = (bf16[320,1536]{1,0:T(8,128)(2,1)}, bf16[320,1536]{1,0:T(8,128)(2,1)}, u32[]{:S(2)}, u32[]{:S(2)}) collective-permute-start(bf16[320,1536]{1,0:T(8,128)(2,1)} %get-tuple-element.239), channel_id=1, source_target_pairs={{0,4},{4,0},{8,12},{12,8},{16,20},{20,16},{24,28},{28,24},{1,5},{5... | collective-permute-start | bytes 2949128 | tf_op jit(solution)/shard_map/ppermute | solution.py:605
  650.5 37.9 %collective-permute-start.45 = (bf16[512,1536]{1,0:T(8,128)(2,1)}, bf16[512,1536]{1,0:T(8,128)(2,1)S(1)}, u32[]{:S(2)}, u32[]{:S(2)}) collective-permute-start(bf16[512,1536]{1,0:T(8,128)(2,1)} %ring_rows.14), channel_id=1, source_target_pairs={{0,8},{4,12},{8,16},{12,20},{16,24},{20,28},{24,0},{28,4},{1,9},{5... | collective-permute-start | bytes 4718600 | tf_op jit(solution)/shard_map/ppermute | solution.py:598
  655.5 50.3 %collective-permute-start.46 = (bf16[384,1664]{1,0:T(8,128)(2,1)}, bf16[384,1664]{1,0:T(8,128)(2,1)S(1)}, u32[]{:S(2)}, u32[]{:S(2)}) collective-permute-start(bf16[384,1664]{1,0:T(8,128)(2,1)} %fusion.27), channel_id=1, source_target_pairs={{0,2},{1,3},{2,0},{3,1},{4,6},{5,7},{6,4},{7,5},{8,10},{9,11},{10,... | collective-permute-start | bytes 3833864 | tf_op jit(solution)/shard_map/ppermute | solution.py:623
  746.4 17.8 %collective-permute-start.54 = (bf16[192,2048]{1,0:T(8,128)(2,1)S(1)}, bf16[192,2048]{1,0:T(8,128)(2,1)S(1)}, u32[]{:S(2)}, u32[]{:S(2)}) collective-permute-start(bf16[192,2048]{1,0:T(8,128)(2,1)S(1)} %get-tuple-element.455), channel_id=1, source_target_pairs={{0,4},{4,0},{8,12},{12,8},{16,20},{20,16},{24,28},{28,24},{1,5},{5... | collective-permute-start | bytes 2359304 | tf_op jit(solution)/shard_map/ppermute | solution.py:605
  801.8 19.6 %collective-permute-start.62 = (bf16[192,2048]{1,0:T(8,128)(2,1)S(1)}, bf16[192,2048]{1,0:T(8,128)(2,1)}, u32[]{:S(2)}, u32[]{:S(2)}) collective-permute-start(bf16[192,2048]{1,0:T(8,128)(2,1)S(1)} %bitcast.206), channel_id=1, source_target_pairs={{0,4},{4,0},{8,12},{12,8},{16,20},{20,16},{24,28},{28,24},{1,5},{5... | collective-permute-start | bytes 2359304 | tf_op jit(solution)/shard_map/ppermute | solution.py:605
  (122 other events, 2000.0 us)
Sparse Core Ops, SparseCore 0:
  16.5 49.7 all-gather.6
  68.4 45.2 all-gather.8
  115.8 67.7 all-gather.10
  185.6 119.9 all-gather.12
  377.6 88.1 reduce-scatter.5
  468.3 150.7 reduce-scatter.3
  621.7 72.1 reduce-scatter.7

commit v5 on v4

--- a/solution.py
+++ b/solution.py
@@ -901,7 +901,7 @@
     kv_parts = [
         lax.ppermute(kv_low[s], "fsdp", [(a + 2 * s, a) for a in range(shards - 2 * s)]) for s in range(1, chips)
     ]
-    back_mine, back_mate = core_grads(core_arg, attended, [after(branch_grad, kv_chip)], shards)
+    back_mine, back_mate = core_grads(core_arg, attended, [after(branch_grad, kv_low)], shards)
     back_mate = core_shift(back_mate, 1)
     out_state = adamw_update(
         expert_out,
@@ -913,14 +913,18 @@
     )
     ring_step(result_held, after(result_steps[2], out_state), arrived)
     arrived = ring_send(result_held)
-    kv_parts = after(kv_parts, result_held[1])
+    back_low = chip_low(back_mine, after(back_mate, result_held[1]))
+    back_sent = chip_send(back_low)
+    kv_parts = after(kv_parts, back_low)
     kv_grad = functools.reduce(lambda total, part: total + part.astype(f32), kv_parts, kv_chip[0])
     key_pre_grad = turn_keys(kv_grad[:, :KV], -1.0)
     kv_pre_grad = jnp.concatenate([key_pre_grad, kv_grad[:, KV:]], axis=1).astype(bf16)
 
     front_terms = weight_grads(first_hidden, [pre_grad, kv_pre_grad])
     front_part = lax.psum_scatter(front_terms, "fsdp", scatter_dimension=0, tiled=True)
-    pre_late, kv_late = after((pre_grad, kv_pre_grad), front_terms)
+    ring_step(result_held, after(result_steps[3], front_terms), arrived)
+    arrived = ring_send(result_held)
+    pre_late, kv_late = after((pre_grad, kv_pre_grad), result_held[2])
     hidden_one_grad = dot_nt(pre_late, qkv_low[:, :MODEL_WIDTH]) + dot_nt(kv_late, qkv_low[:, MODEL_WIDTH:])
     gain_one_term = jnp.sum(hidden_one_grad * normed_one, axis=0)
     scaled_one = hidden_one_grad * gain_one
@@ -941,13 +945,10 @@
     extra = extra.T.astype(bf16).reshape(chips, 2, shard_rows, 128)
     extra_mine = jnp.where(core == 0, extra[:, 0], extra[:, 1])
     extra_mate = core_shift(jnp.where(core == 0, extra[:, 1], extra[:, 0]), 1)
-    ring_step(result_held, after(result_steps[3], extra_mine), arrived)
-    arrived = ring_send(result_held)
-    back_mate, extra_mate = after((back_mate, extra_mate), result_held[2])
-    back_mine = jnp.concatenate([back_mine, extra_mine], axis=2)
-    back_mate = jnp.concatenate([back_mate, extra_mate], axis=2)
-    back_low = chip_low(back_mine, back_mate)
-    back_sent = chip_send(back_low)
+    extra_sent = chip_send(chip_low(extra_mine, extra_mate))
+    back_sent = after(back_sent, extra_mine)
+    back_low = chip_total(back_mine, back_mate, back_sent).astype(bf16)
+    back_parts = x_parts(back_low)
     in_state = adamw_update(
         expert_in,
         in_first,
@@ -958,24 +959,20 @@
     )
     moe_out = ring_step(result_held, after(result_steps[0], in_state), arrived)
     layer_out = (residual + moe_out).astype(bf16)
-    back_sent = after(back_sent, moe_out)
-    back_parts = x_parts(chip_total(back_mine, back_mate, back_sent).astype(bf16))
-    back_parts = z_parts(add_parts(back_parts))
-    back_low = add_parts(back_parts)
-    front_low = after(front_part, back_low)
-    front_parts = x_parts(front_low)
-    back_low = z_join(after(back_low, front_low))
-    front_low = add_parts(after(front_parts, back_low))
+    back_low = add_parts(z_parts(add_parts(after(back_parts, moe_out))))
+    back_low = z_join(back_low)
+    extra_low = chip_total(extra_mine, extra_mate, after(extra_sent, moe_out)).astype(bf16)
+    front_low = jnp.concatenate([after(front_part, back_low), extra_low], axis=1)
+    back_sum = x_join(back_low)
+    front_low = add_parts(x_parts(front_low))
     front_low = add_parts(z_parts(front_low))
-    back_sum = x_join(after(back_low, front_low))
     front_sum = x_join(z_join(front_low))
-    output_sum = back_sum[:, :MODEL_WIDTH]
-    router_sum = back_sum[:, MODEL_WIDTH : MODEL_WIDTH + experts_all]
+    output_sum = back_sum
+    router_sum = front_sum[:, QKV : QKV + experts_all]
     query_sum = front_sum[:, :MODEL_WIDTH]
     key_sum = front_sum[:, MODEL_WIDTH : MODEL_WIDTH + KV]
     value_sum = front_sum[:, MODEL_WIDTH + KV : QKV]
-    at = MODEL_WIDTH + experts_all
-    gain_sum = back_sum[:, at : at + 2].T
+    gain_sum = front_sum[:, QKV + experts_all : QKV + experts_all + 2].T
 
     rate = 0.5 / math.sqrt(MODEL_WIDTH // 2)
     return (

time: 854 us -> 875 us (1.025)
  starting transfers between devices: 76.1 us -> 110 us
  waiting for transfers between devices: 384 us -> 358 us
    ppermute x1 -> x2, starting transfers between devices: 8.22 us -> 33.6 us  [y_shift(): lax.ppermute(value, 'fsdp', [(a, (a + 2 * by) % shards) for a in range(sh...]
    ppermute x1 -> x2, waiting for transfers between devices: 12.7 us -> 0.01 us  [y_shift(): lax.ppermute(value, 'fsdp', [(a, (a + 2 * by) % shards) for a in range(sh...]
    ppermute x1, waiting for transfers between devices: 30.9 us -> 19.2 us  [body(): lax.ppermute(kv_low[s], 'fsdp', [(a + 2 * s, a) for a in range(shards - 2...]
    ppermute x22, waiting for transfers between devices: 145 us -> 135 us  [x_shift(): lax.ppermute(value, 'expert', [(a * wide + b, a * wide + (b + by) % wide)...]
    unnamed x206 -> x207, local copies, waits for them, and re-layouts: 29.6 us -> 27.8 us
    sub x6 -> x7, other arithmetic: 49.4 us -> 50.9 us  [adamw_update(): weight - step_rate * (first_hat / (jnp.sqrt(second_hat) + ADAM_EPS) + dec...]
  transfers between devices with their start and end apart: 70 -> 71, of which waited for: 45 -> 42; matrix products, arithmetic and copies ran while one was open for 15% -> 16% of each run, Pallas kernels for 18% -> 18%
where the time goes in v5:
time: 875 us; the launch traced here: 860 us
  waiting for transfers between devices  358 us (41%)
  Pallas kernels  193 us (22%)
  starting transfers between devices  110 us (13%)
  other arithmetic  104 us (12%)
  local copies, waits for them, and re-layouts  45.9 us (5%)
  matrix products  32.8 us (4%)
  between operations  16.1 us (2%)
    ppermute x33, waiting for transfers between devices, z_shift(): lax.ppermute(value, 'expert', [(a * wide + b, (a + by) % depth * wide + b...  173 us
    ppermute x22, waiting for transfers between devices, x_shift(): lax.ppermute(value, 'expert', [(a * wide + b, a * wide + (b + by) % wide)...  135 us
    sub x7, other arithmetic, adamw_update(): weight - step_rate * (first_hat / (jnp.sqrt(second_hat) + ADAM_EPS) + dec...  50.9 us
    ppermute x33, starting transfers between devices, z_shift(): lax.ppermute(value, 'expert', [(a * wide + b, (a + by) % depth * wide + b...  43.7 us
    pallas_call x1, Pallas kernels, core_rows(): pl.pallas_call(functools.partial(core_kernel, count), out_shape=(low, low...  36.3 us
    ppermute x2, starting transfers between devices, y_shift(): lax.ppermute(value, 'fsdp', [(a, (a + 2 * by) % shards) for a in range(sh...  33.6 us
    unnamed x207, local copies, waits for them, and re-layouts  27.8 us
    ppermute x22, starting transfers between devices, x_shift(): lax.ppermute(value, 'expert', [(a * wide + b, a * wide + (b + by) % wide)...  27.6 us
  transfers between devices with their start and end apart: 71, of which 42 were waited for; matrix products, arithmetic and copies ran while one was open for 16% of the time, Pallas kernels for 18%

profile of v5, /device:TPU:8, one launch (start us, length us, event | category | flops | bytes accessed | tf_op | source)
XLA Modules:
  0.0 859.8 jit_solution(5347697803492582121)
XLA Ops:
  24.8 4.5 pick_rows.8
  35.6 17.1 %collective-permute-done.4.refs_4_ = bf16[320,1536]{1,0:T(8,128)(2,1)} collective-permute-done((bf16[320,1536]{1,0:T(8,128)(2,1)}, bf16[320,1536]{1,0:T(8,128)(2,1)}, u32[]{:S(2)}, u32[]{:S(2)}) %collective-permute-start.4) | collective-permute-done | bytes 983072 | tf_op jit(solution)/shard_map/ppermute | solution.py:605
  52.7 5.3 collective-permute-done.3.rows
  68.8 6.1 fusion.2.pre
  79.9 6.5 convert_element_type.250
  91.2 22.5 %collective-permute-done.6 = bf16[512,512]{1,0:T(8,128)(2,1)} collective-permute-done((bf16[512,512]{1,0:T(8,128)(2,1)}, bf16[512,512]{1,0:T(8,128)(2,1)}, u32[]{:S(2)}, u32[]{:S(2)}) %collective-permute-start.6) | collective-permute-done | bytes 524320 | tf_op jit(solution)/shard_map/ppermute | solution.py:626
  126.6 14.3 %attend.1 = (bf16[512,1536]{1,0:T(8,128)(2,1)}, f32[12,1,512]{2,1,0:T(1,128)}, bf16[512,1536]{1,0:T(8,128)(2,1)}) custom-call(s32[1]{0:T(128)} %bitcast.place, f32[512,2048]{1,0:T(8,128)} %copy-done.41, f32[512,128]{1,0:T(8,128)} %get-tuple-element.446.cosine, f32[512,128]{1,0:T(8,128)} %copy-done.42, bf16[4,512,512]{2,1,0:T(8,128)(2,1)} %pad_maximum_fusion.keys.values, ...), custom_call_target="tpu_custom_call" | custom-call | flops 1000000000 | bytes 1000000 | tf_op jit(solution)/shard_map/attend/pallas_call | solution.py:106
  140.9 19.4 %collective-permute-done.9.rows = bf16[512,1536]{1,0:T(8,128)(2,1)S(1)} collective-permute-done((bf16[512,1536]{1,0:T(8,128)(2,1)}, bf16[512,1536]{1,0:T(8,128)(2,1)S(1)}, u32[]{:S(2)}, u32[]{:S(2)}) %collective-permute-start.9) | collective-permute-done | bytes 1572896 | tf_op jit(solution)/shard_map/ppermute | solution.py:598
  161.4 6.1 multiply_reduce_fusion.2
  176.6 19.1 %collective-permute-done.11.refs_6_ = bf16[320,1536]{1,0:T(8,128)(2,1)S(1)} collective-permute-done((bf16[320,1536]{1,0:T(8,128)(2,1)S(1)}, bf16[320,1536]{1,0:T(8,128)(2,1)S(1)}, u32[]{:S(2)}, u32[]{:S(2)}) %collective-permute-start.11) | collective-permute-done | bytes 983072 | tf_op jit(solution)/shard_map/ppermute | solution.py:605
  197.1 8.9 %collective-permute-done.13.rows = bf16[512,1536]{1,0:T(8,128)(2,1)} collective-permute-done((bf16[512,1536]{1,0:T(8,128)(2,1)S(1)}, bf16[512,1536]{1,0:T(8,128)(2,1)}, u32[]{:S(2)}, u32[]{:S(2)}) %collective-permute-start.13) | collective-permute-done | bytes 1572896 | tf_op jit(solution)/shard_map/ppermute | solution.py:598
  210.1 7.2 collective-permute-done.12.refs_4_
  221.7 20.6 %collective-permute-done.16 = f32[4,512]{1,0:T(4,128)S(1)} collective-permute-done((f32[4,512]{1,0:T(4,128)S(1)}, f32[4,512]{1,0:T(4,128)S(1)}, u32[]{:S(2)}, u32[]{:S(2)}) %collective-permute-start.16) | collective-permute-done | bytes 8224 | tf_op jit(solution)/shard_map/ppermute | solution.py:598
  252.0 15.2 %collective-permute-done.17.refs_7_ = bf16[320,1536]{1,0:T(8,128)(2,1)S(1)} collective-permute-done((bf16[320,1536]{1,0:T(8,128)(2,1)S(1)}, bf16[320,1536]{1,0:T(8,128)(2,1)S(1)}, u32[]{:S(2)}, u32[]{:S(2)}) %collective-permute-start.17) | collective-permute-done | bytes 983072 | tf_op jit(solution)/shard_map/ppermute | solution.py:605
  270.8 6.8 collective-permute-done.19.rows
  278.8 13.0 %inner_rows.1.refs_9_ = bf16[4,640,768]{2,1,0:T(8,128)(2,1)} custom-call(bf16[320,1536]{1,0:T(8,128)(2,1)} %copy-done.24, bf16[320,1536]{1,0:T(8,128)(2,1)} %copy-done.25, bf16[320,1536]{1,0:T(8,128)(2,1)} %copy-done.28, bf16[320,1536]{1,0:T(8,128)(2,1)} %copy-done.31, bf16[320,1536]{1,0:T(8,128)(2,1)} %collective-permute-done.4.refs_4_, ...), custom_call_target="tpu_custom_call" | custom-call | flops 6039797760 | bytes 20000000 | tf_op jit(solution)/shard_map/inner_rows/pallas_call | solution.py:248
  296.4 5.0 collective-permute-done.22
  302.9 11.9 %collective-permute-done.23 = f32[4,4,80]{2,0,1:T(4,128)S(1)} collective-permute-done((f32[4,4,80]{2,0,1:T(4,128)S(1)}, f32[4,4,80]{2,0,1:T(4,128)S(1)}, u32[]{:S(2)}, u32[]{:S(2)}) %collective-permute-start.23) | collective-permute-done | bytes 5152 | tf_op jit(solution)/shard_map/ppermute | solution.py:605
  317.4 36.3 %core_rows.1 = (bf16[4,640,768]{2,1,0:T(8,128)(2,1)}, bf16[4,640,768]{2,1,0:T(8,128)(2,1)}, bf16[4,640,768]{2,1,0:T(8,128)(2,1)}, f32[4,640,1]{2,1,0:T(8,128)}, ...) custom-call(bf16[320,1536]{1,0:T(8,128)(2,1)} %copy-done.26, ...), custom_call_target="tpu_custom_call" | custom-call | flops 24159191040 | bytes 60000000 | tf_op jit(solution)/shard_map/core_rows/pallas_call | solution.py:305
  355.2 13.8 %down_grads.1 = bf16[4,4,768,384]{3,2,1,0:T(8,128)(2,1)} custom-call(bf16[320,1536]{1,0:T(8,128)(2,1)} %copy-done.24, bf16[320,1536]{1,0:T(8,128)(2,1)} %copy-done.25, bf16[320,1536]{1,0:T(8,128)(2,1)} %copy-done.28, bf16[320,1536]{1,0:T(8,128)(2,1)} %copy-done.31, bf16[320,1536]{1,0:T(8,128)(2,1)} %collective-permute-done.4.refs_4_, ...), custom_call_target="tpu_custom_call" | custom-call | flops 6039797760 | bytes 22000000 | tf_op jit(solution)/shard_map/down_grads/pallas_call | solution.py:364
  383.1 20.8 %in_grads.1 = bf16[4,4,384,1536]{3,2,1,0:T(8,128)(2,1)} custom-call(bf16[320,1536]{1,0:T(8,128)(2,1)} %copy-done.26, bf16[320,1536]{1,0:T(8,128)(2,1)} %copy-done.27, bf16[320,1536]{1,0:T(8,128)(2,1)} %copy-done.29, bf16[320,1536]{1,0:T(8,128)(2,1)} %copy-done.30, bf16[320,1536]{1,0:T(8,128)(2,1)} %copy-done.91, ...), custom_call_target="tpu_custom_call" | custom-call | flops 12079595520 | bytes 35000000 | tf_op jit(solution)/shard_map/in_grads/pallas_call | solution.py:392
  407.3 7.4 collective-permute-done.27
  424.2 19.3 %collective-permute-done.29.refs_2_ = bf16[320,1536]{1,0:T(8,128)(2,1)S(1)} collective-permute-done((bf16[320,1536]{1,0:T(8,128)(2,1)}, bf16[320,1536]{1,0:T(8,128)(2,1)S(1)}, u32[]{:S(2)}, u32[]{:S(2)}) %collective-permute-start.29) | collective-permute-done | bytes 983072 | tf_op jit(solution)/shard_map/ppermute | solution.py:605
  444.1 12.4 %result_rows.1 = (bf16[320,1536]{1,0:T(8,128)(2,1)}, bf16[320,1536]{1,0:T(8,128)(2,1)}, bf16[320,1536]{1,0:T(8,128)(2,1)}, bf16[320,1536]{1,0:T(8,128)(2,1)}, bf...) custom-call(bf16[4,640,768]{2,1,0:T(8,128)(2,1)} %get-tuple-element., ...), custom_call_target="tpu_custom_call" | custom-call | flops 6039797760 | bytes 22000000 | tf_op jit(solution)/shard_map/result_rows/pallas_call | solution.py:336
  468.1 19.1 %collective-permute-done.35 = f32[4,512]{1,0:T(4,128)S(1)} collective-permute-done((f32[4,512]{1,0:T(4,128)S(1)}, f32[4,512]{1,0:T(4,128)S(1)}, u32[]{:S(2)}, u32[]{:S(2)}) %collective-permute-start.35) | collective-permute-done | bytes 8224 | tf_op jit(solution)/shard_map/ppermute | solution.py:598
  506.8 17.4 %attend_back.1 = (bf16[512,1536]{1,0:T(8,128)(2,1)}, bf16[4,512,256]{2,1,0:T(8,128)(2,1)}, bf16[4,512,256]{2,1,0:T(8,128)(2,1)}) custom-call(s32[1]{0:T(128)} %bitcast.place, bf16[512,1536]{1,0:T(8,128)(2,1)} %get-tuple-element.247.query, bf16[4,512,512]{2,1,0:T(8,128)(2,1)} %pad_maximum_fusion.keys.values, ...), custom_call_target="tpu_custom_call" | custom-call | flops 1000000000 | bytes 1000000 | tf_op jit(solution)/shard_map/attend_back/pallas_call | solution.py:182
  530.4 6.0 core_grads.1
  540.6 11.7 %multiply_subtract_fusion.1 = (f32[4,768,384]{2,1,0:T(8,128)}, f32[4,768,384]{2,1,0:T(8,128)}, f32[4,768,384]{2,1,0:T(8,128)}) fusion(f32[4,768,384]{2,1,0:T(8,128)} %param.51, bf16[4,768,384]{2,1,0:T(8,128)(2,1)} %bitcast.218, f32[4,768,384]{2,1,0:T(8,128)} %param.52, f32[4,768,384]{2,1,0:T(8,128)} %param.53), kind=kLoop, calls=%fused_computation.25 | loop fusion | flops 18874368 | bytes 30670848 | tf_op jit(solution)/shard_map/sub | solution.py:549
  552.3 8.5 collective-permute-done.40.refs_2_
  560.8 14.5 %collective-permute-done.41.refs_3_ = bf16[512,1536]{1,0:T(8,128)(2,1)S(1)} collective-permute-done((bf16[512,1536]{1,0:T(8,128)(2,1)S(1)}, bf16[512,1536]{1,0:T(8,128)(2,1)S(1)}, u32[]{:S(2)}, u32[]{:S(2)}) %collective-permute-start.41) | collective-permute-done | bytes 1572896 | tf_op jit(solution)/shard_map/ppermute | solution.py:598
  581.3 19.2 %collective-permute-done.43 = bf16[512,512]{1,0:T(8,128)(2,1)S(1)} collective-permute-done((bf16[512,512]{1,0:T(8,128)(2,1)S(1)}, bf16[512,512]{1,0:T(8,128)(2,1)S(1)}, u32[]{:S(2)}, u32[]{:S(2)}) %collective-permute-start.43) | collective-permute-done | bytes 524320 | tf_op jit(solution)/shard_map/ppermute | solution.py:902
  602.7 7.3 weight_grads.1
  615.0 17.5 %collective-permute-start.42 = (bf16[384,1536]{1,0:T(8,128)(2,1)}, bf16[384,1536]{1,0:T(8,128)(2,1)}, u32[]{:S(2)}, u32[]{:S(2)}) collective-permute-start(bf16[384,1536]{1,0:T(8,128)(2,1)} %fusion.31), channel_id=1, source_target_pairs={{0,2},{1,3},{2,0},{3,1},{4,6},{5,7},{6,4},{7,5},{8,10},{9,11},{10,... | collective-permute-start | bytes 3538952 | tf_op jit(solution)/shard_map/ppermute | solution.py:623
  634.3 13.1 %collective-permute-done.44.refs_3_ = bf16[512,1536]{1,0:T(8,128)(2,1)S(1)} collective-permute-done((bf16[512,1536]{1,0:T(8,128)(2,1)S(1)}, bf16[512,1536]{1,0:T(8,128)(2,1)S(1)}, u32[]{:S(2)}, u32[]{:S(2)}) %collective-permute-start.44) | collective-permute-done | bytes 1572896 | tf_op jit(solution)/shard_map/ppermute | solution.py:598
  657.8 7.5 fusion.22
  671.2 16.2 %collective-permute-start.54 = (bf16[384,128]{1,0:T(8,128)(2,1)}, bf16[384,128]{1,0:T(8,128)(2,1)}, u32[]{:S(2)}, u32[]{:S(2)}) collective-permute-start(bf16[384,128]{1,0:T(8,128)(2,1)} %fusion.62), channel_id=1, source_target_pairs={{0,2},{1,3},{2,0},{3,1},{4,6},{5,7},{6,4},{7,5},{8,10},{9,11},{10,... | collective-permute-start | bytes 294920 | tf_op jit(solution)/shard_map/ppermute | solution.py:623
  692.3 24.5 %multiply_subtract_fusion = (f32[4,384,1536]{2,1,0:T(8,128)}, f32[4,384,1536]{2,1,0:T(8,128)}, f32[4,384,1536]{2,1,0:T(8,128)}) fusion(f32[4,384,1536]{2,1,0:T(8,128)} %param.48, bf16[4,384,1536]{2,1,0:T(8,128)(2,1)} %bitcast.211, f32[4,384,1536]{2,1,0:T(8,128)} %param.49, f32[4,384,1536]{2,1,0:T(8,128)} %param.50), kind=kLoop, calls=%fused_computation.4 | loop fusion | flops 37748736 | bytes 61341696 | tf_op jit(solution)/shard_map/sub | solution.py:549
  716.9 4.6 ring_rows.15
  724.1 4.6 collective-permute-start.48
  730.2 7.4 collective-permute-done.48
  750.1 5.1 collective-permute-done.51
  760.6 5.9 fusion.21
  767.0 13.5 %collective-permute-done.55 = bf16[192,2176]{1,0:T(8,128)(2,1)S(1)} collective-permute-done((bf16[192,2176]{1,0:T(8,128)(2,1)S(1)}, bf16[192,2176]{1,0:T(8,128)(2,1)S(1)}, u32[]{:S(2)}, u32[]{:S(2)}) %collective-permute-start.55) | collective-permute-done | bytes 835616 | tf_op jit(solution)/shard_map/ppermute | solution.py:605
  787.1 8.0 collective-permute-done.56
  807.6 10.3 %collective-permute-done.60 = bf16[48,2176]{1,0:T(8,128)(2,1)S(1)} collective-permute-done((bf16[48,2176]{1,0:T(8,128)(2,1)S(1)}, bf16[48,2176]{1,0:T(8,128)(2,1)S(1)}, u32[]{:S(2)}, u32[]{:S(2)}) %collective-permute-start.60) | collective-permute-done | bytes 208928 | tf_op jit(solution)/shard_map/ppermute | solution.py:598
  819.9 4.3 multiply_subtract_fusion.2
  824.4 14.4 %collective-permute-done.62 = bf16[192,2176]{1,0:T(8,128)(2,1)S(1)} collective-permute-done((bf16[192,2176]{1,0:T(8,128)(2,1)S(1)}, bf16[192,2176]{1,0:T(8,128)(2,1)S(1)}, u32[]{:S(2)}, u32[]{:S(2)}) %collective-permute-start.62) | collective-permute-done | bytes 835616 | tf_op jit(solution)/shard_map/ppermute | solution.py:605
  842.0 7.4 multiply_subtract_fusion.3
  (463 shorter events, 256.4 us)
Async XLA Ops:
  7.2 59.0 %all-gather.7.cloned.1.call-start = ((), (), s32[]{:S(2)}) async-start(), calls=%async_computation.3 | async-start | bytes 8355840 | tf_op jit(solution)/shard_map/all_gather | solution.py:636
  16.4 145.1 %all-gather.9.cloned.1.call-start = ((), (), s32[]{:S(2)}) async-start(), calls=%async_computation.4 | async-start | bytes 5898240 | tf_op jit(solution)/shard_map/all_gather | solution.py:644
  17.6 261.3 %all-gather.11.cloned.1.call-start = ((), (), s32[]{:S(2)}) async-start(), calls=%async_computation.8 | async-start | bytes 11796480 | tf_op jit(solution)/shard_map/all_gather | solution.py:762
  22.3 35.7 %collective-permute-start.3 = (bf16[512,1536]{1,0:T(8,128)(2,1)}, bf16[512,1536]{1,0:T(8,128)(2,1)}, u32[]{:S(2)}, u32[]{:S(2)}) collective-permute-start(bf16[512,1536]{1,0:T(8,128)(2,1)} %rows.1), channel_id=1, source_target_pairs={{0,8},{4,12},{8,16},{12,20},{16,24},{20,28},{24,0},{28,4},{1,9},{5... | collective-permute-start | bytes 4718600 | tf_op jit(solution)/shard_map/ppermute | solution.py:598
  30.4 22.4 %collective-permute-start.4 = (bf16[320,1536]{1,0:T(8,128)(2,1)}, bf16[320,1536]{1,0:T(8,128)(2,1)}, u32[]{:S(2)}, u32[]{:S(2)}) collective-permute-start(bf16[320,1536]{1,0:T(8,128)(2,1)} %bitcast.10), channel_id=1, source_target_pairs={{0,4},{4,0},{8,12},{12,8},{16,20},{20,16},{24,28},{28,24},{1,5},{5... | collective-permute-start | bytes 2949128 | tf_op jit(solution)/shard_map/ppermute | solution.py:605
  79.9 237.5 %all-gather.13.cloned.1.call-start = ((), (), s32[]{:S(2)}) async-start(), calls=%async_computation.9 | async-start | bytes 23592960 | tf_op jit(solution)/shard_map/all_gather | solution.py:763
  86.4 420.4 %reduce-scatter.6.cloned.1.call-start = ((), (), s32[]{:S(2)}) async-start(), calls=%async_computation.6 | async-start | bytes 11796480 | tf_op jit(solution)/shard_map/reduce_scatter | solution.py:823
  86.4 37.0 %collective-permute-start.8 = (bf16[512,1536]{1,0:T(8,128)(2,1)}, bf16[512,1536]{1,0:T(8,128)(2,1)}, u32[]{:S(2)}, u32[]{:S(2)}) collective-permute-start(bf16[512,1536]{1,0:T(8,128)(2,1)} %collective-permute-done.3.rows), channel_id=1, source_target_pairs={{0,8},{4,12},{8,16},{12,20},{16,24},{20,28},{24,0},{28,4},{1,9},{5... | collective-permute-start | bytes 4718600 | tf_op jit(solution)/shard_map/ppermute | solution.py:598
  88.0 25.7 %collective-permute-start.6 = (bf16[512,512]{1,0:T(8,128)(2,1)}, bf16[512,512]{1,0:T(8,128)(2,1)}, u32[]{:S(2)}, u32[]{:S(2)}) collective-permute-start(bf16[512,512]{1,0:T(8,128)(2,1)} %get-tuple-element.442), channel_id=1, source_target_pairs={{0,2},{1,3},{4,6},{5,7},{8,10},{9,11},{12,14},{13,15},{16,18},{17,... | collective-permute-start | bytes 1572872 | tf_op jit(solution)/shard_map/ppermute | solution.py:626
  91.2 22.5 %collective-permute-start.5 = (bf16[512,512]{1,0:T(8,128)(2,1)}, bf16[512,512]{1,0:T(8,128)(2,1)}, u32[]{:S(2)}, u32[]{:S(2)}) collective-permute-start(bf16[512,512]{1,0:T(8,128)(2,1)} %get-tuple-element.442), channel_id=1, source_target_pairs={{0,1},{1,0},{2,3},{3,2},{4,5},{5,4},{6,7},{7,6},{8,9},{9,8},{10,11... | collective-permute-start | bytes 1572872 | tf_op jit(solution)/shard_map/ppermute | solution.py:620
  123.5 36.8 %collective-permute-start.9 = (bf16[512,1536]{1,0:T(8,128)(2,1)}, bf16[512,1536]{1,0:T(8,128)(2,1)S(1)}, u32[]{:S(2)}, u32[]{:S(2)}) collective-permute-start(bf16[512,1536]{1,0:T(8,128)(2,1)} %collective-permute-done.8.rows), channel_id=1, source_target_pairs={{0,8},{4,12},{8,16},{12,20},{16,24},{20,28},{24,0},{28,4},{1,9},{5... | collective-permute-start | bytes 4718600 | tf_op jit(solution)/shard_map/ppermute | solution.py:598
  125.1 44.9 %collective-permute-start.10 = (bf16[320,1536]{1,0:T(8,128)(2,1)}, bf16[320,1536]{1,0:T(8,128)(2,1)}, u32[]{:S(2)}, u32[]{:S(2)}) collective-permute-start(bf16[320,1536]{1,0:T(8,128)(2,1)} %bitcast.17), channel_id=1, source_target_pairs={{0,4},{4,0},{8,12},{12,8},{16,20},{20,16},{24,28},{28,24},{1,5},{5... | collective-permute-start | bytes 2949128 | tf_op jit(solution)/shard_map/ppermute | solution.py:605
  169.2 36.8 %collective-permute-start.13 = (bf16[512,1536]{1,0:T(8,128)(2,1)S(1)}, bf16[512,1536]{1,0:T(8,128)(2,1)}, u32[]{:S(2)}, u32[]{:S(2)}) collective-permute-start(bf16[512,1536]{1,0:T(8,128)(2,1)S(1)} %multiply_convert_fusion.rows), channel_id=1, source_target_pairs={{0,8},{4,12},{8,16},{12,20},{16,24},{20,28},{24,0},{28,4},{1,9},{5... | collective-permute-start | bytes 4718600 | tf_op jit(solution)/shard_map/ppermute | solution.py:598
  173.3 22.4 %collective-permute-start.11 = (bf16[320,1536]{1,0:T(8,128)(2,1)S(1)}, bf16[320,1536]{1,0:T(8,128)(2,1)S(1)}, u32[]{:S(2)}, u32[]{:S(2)}) collective-permute-start(bf16[320,1536]{1,0:T(8,128)(2,1)S(1)} %bitcast.205), channel_id=1, source_target_pairs={{0,4},{4,0},{8,12},{12,8},{16,20},{20,16},{24,28},{28,24},{1,5},{5... | collective-permute-start | bytes 2949128 | tf_op jit(solution)/shard_map/ppermute | solution.py:605
  195.7 21.6 %collective-permute-start.12 = (bf16[320,1536]{1,0:T(8,128)(2,1)S(1)}, bf16[320,1536]{1,0:T(8,128)(2,1)S(1)}, u32[]{:S(2)}, u32[]{:S(2)}) collective-permute-start(bf16[320,1536]{1,0:T(8,128)(2,1)S(1)} %bitcast.203), channel_id=1, source_target_pairs={{0,4},{4,0},{8,12},{12,8},{16,20},{20,16},{24,28},{28,24},{1,5},{5... | collective-permute-start | bytes 2949128 | tf_op jit(solution)/shard_map/ppermute | solution.py:605
  206.1 36.3 %collective-permute-start.15 = (bf16[512,1536]{1,0:T(8,128)(2,1)}, bf16[512,1536]{1,0:T(8,128)(2,1)}, u32[]{:S(2)}, u32[]{:S(2)}) collective-permute-start(bf16[512,1536]{1,0:T(8,128)(2,1)} %collective-permute-done.13.rows), channel_id=1, source_target_pairs={{0,8},{4,12},{8,16},{12,20},{16,24},{20,28},{24,0},{28,4},{1,9},{5... | collective-permute-start | bytes 4718600 | tf_op jit(solution)/shard_map/ppermute | solution.py:598
  217.3 28.3 %collective-permute-start.14 = (bf16[320,1536]{1,0:T(8,128)(2,1)}, bf16[320,1536]{1,0:T(8,128)(2,1)}, u32[]{:S(2)}, u32[]{:S(2)}) collective-permute-start(bf16[320,1536]{1,0:T(8,128)(2,1)} %bitcast.18), channel_id=1, source_target_pairs={{0,4},{4,0},{8,12},{12,8},{16,20},{20,16},{24,28},{28,24},{1,5},{5... | collective-permute-start | bytes 2949128 | tf_op jit(solution)/shard_map/ppermute | solution.py:605
  220.5 21.9 %collective-permute-start.16 = (f32[4,512]{1,0:T(4,128)S(1)}, f32[4,512]{1,0:T(4,128)S(1)}, u32[]{:S(2)}, u32[]{:S(2)}) collective-permute-start(f32[4,512]{1,0:T(4,128)S(1)} %fusion.74), channel_id=1, source_target_pairs={{0,8},{4,12},{8,16},{12,20},{16,24},{20,28},{24,0},{28,4},{1,9},{5... | collective-permute-start | bytes 24584 | tf_op jit(solution)/shard_map/ppermute | solution.py:598
  242.3 35.3 %collective-permute-start.19 = (bf16[512,1536]{1,0:T(8,128)(2,1)}, bf16[512,1536]{1,0:T(8,128)(2,1)S(1)}, u32[]{:S(2)}, u32[]{:S(2)}) collective-permute-start(bf16[512,1536]{1,0:T(8,128)(2,1)} %collective-permute-done.15.rows), channel_id=1, source_target_pairs={{0,8},{4,12},{8,16},{12,20},{16,24},{20,28},{24,0},{28,4},{1,9},{5... | collective-permute-start | bytes 4718600 | tf_op jit(solution)/shard_map/ppermute | solution.py:598
  245.6 21.7 %collective-permute-start.17 = (bf16[320,1536]{1,0:T(8,128)(2,1)S(1)}, bf16[320,1536]{1,0:T(8,128)(2,1)S(1)}, u32[]{:S(2)}, u32[]{:S(2)}) collective-permute-start(bf16[320,1536]{1,0:T(8,128)(2,1)S(1)} %bitcast.204), channel_id=1, source_target_pairs={{0,4},{4,0},{8,12},{12,8},{16,20},{20,16},{24,28},{28,24},{1,5},{5... | collective-permute-start | bytes 2949128 | tf_op jit(solution)/shard_map/ppermute | solution.py:605
  267.2 27.5 %collective-permute-start.18 = (bf16[320,1536]{1,0:T(8,128)(2,1)}, bf16[320,1536]{1,0:T(8,128)(2,1)}, u32[]{:S(2)}, u32[]{:S(2)}) collective-permute-start(bf16[320,1536]{1,0:T(8,128)(2,1)} %bitcast.19), channel_id=1, source_target_pairs={{0,4},{4,0},{8,12},{12,8},{16,20},{20,16},{24,28},{28,24},{1,5},{5... | collective-permute-start | bytes 2949128 | tf_op jit(solution)/shard_map/ppermute | solution.py:605
  268.7 23.2 %collective-permute-start.20 = (f32[4,512]{1,0:T(4,128)S(1)}, f32[4,512]{1,0:T(4,128)S(1)}, u32[]{:S(2)}, u32[]{:S(2)}) collective-permute-start(f32[4,512]{1,0:T(4,128)S(1)} %collective-permute-done.16), channel_id=1, source_target_pairs={{0,8},{4,12},{8,16},{12,20},{16,24},{20,28},{24,0},{28,4},{1,9},{5... | collective-permute-start | bytes 24584 | tf_op jit(solution)/shard_map/ppermute | solution.py:598
  378.7 313.6 %reduce-scatter.4.cloned.1.call-start = ((), (), s32[]{:S(2)}) async-start(), calls=%async_computation.5 | async-start | bytes 23592960 | tf_op jit(solution)/shard_map/reduce_scatter | solution.py:832
  380.5 23.4 %collective-permute-start.26 = (f32[4,4,80]{2,1,0:T(4,128)S(1)}, f32[4,4,80]{2,1,0:T(4,128)S(1)}, u32[]{:S(2)}, u32[]{:S(2)}) collective-permute-start(f32[4,4,80]{2,1,0:T(4,128)S(1)} %get-tuple-element.448), channel_id=1, source_target_pairs={{0,4},{4,0},{8,12},{12,8},{16,20},{20,16},{24,28},{28,24},{1,5},{5... | collective-permute-start | bytes 15368 | tf_op jit(solution)/shard_map/ppermute | solution.py:605
  382.0 33.7 %collective-permute-start.28 = (bf16[512,1536]{1,0:T(8,128)(2,1)}, bf16[512,1536]{1,0:T(8,128)(2,1)S(1)}, u32[]{:S(2)}, u32[]{:S(2)}) collective-permute-start(bf16[512,1536]{1,0:T(8,128)(2,1)} %copy-done.9), channel_id=1, source_target_pairs={{0,8},{4,12},{8,16},{12,20},{16,24},{20,28},{24,0},{28,4},{1,9},{5... | collective-permute-start | bytes 4718600 | tf_op jit(solution)/shard_map/ppermute | solution.py:598
  382.4 32.3 %collective-permute-start.25 = (bf16[320,1536]{1,0:T(8,128)(2,1)}, bf16[320,1536]{1,0:T(8,128)(2,1)S(1)}, u32[]{:S(2)}, u32[]{:S(2)}) collective-permute-start(bf16[320,1536]{1,0:T(8,128)(2,1)} %get-tuple-element.212), channel_id=1, source_target_pairs={{0,4},{4,0},{8,12},{12,8},{16,20},{20,16},{24,28},{28,24},{1,5},{5... | collective-permute-start | bytes 2949128 | tf_op jit(solution)/shard_map/ppermute | solution.py:605
  421.3 335.9 %reduce-scatter.8.cloned.1.call-start = ((), (), s32[]{:S(2)}) async-start(), calls=%async_computation.7 | async-start | bytes 7864320 | tf_op jit(solution)/shard_map/reduce_scatter | solution.py:924
  421.3 35.2 %collective-permute-start.36 = (bf16[512,1536]{1,0:T(8,128)(2,1)S(1)}, bf16[512,1536]{1,0:T(8,128)(2,1)S(1)}, u32[]{:S(2)}, u32[]{:S(2)}) collective-permute-start(bf16[512,1536]{1,0:T(8,128)(2,1)S(1)} %ring_rows.9), channel_id=1, source_target_pairs={{0,8},{4,12},{8,16},{12,20},{16,24},{20,28},{24,0},{28,4},{1,9},{5... | collective-permute-start | bytes 4718600 | tf_op jit(solution)/shard_map/ppermute | solution.py:598
  421.4 22.1 %collective-permute-start.29 = (bf16[320,1536]{1,0:T(8,128)(2,1)}, bf16[320,1536]{1,0:T(8,128)(2,1)S(1)}, u32[]{:S(2)}, u32[]{:S(2)}) collective-permute-start(bf16[320,1536]{1,0:T(8,128)(2,1)} %get-tuple-element.232), channel_id=1, source_target_pairs={{0,4},{4,0},{8,12},{12,8},{16,20},{20,16},{24,28},{28,24},{1,5},{5... | collective-permute-start | bytes 2949128 | tf_op jit(solution)/shard_map/ppermute | solution.py:605
  422.1 34.4 %collective-permute-start.34 = (f32[4,512]{1,0:T(4,128)S(1)}, f32[4,512]{1,0:T(4,128)S(1)}, u32[]{:S(2)}, u32[]{:S(2)}) collective-permute-start(f32[4,512]{1,0:T(4,128)S(1)} %fusion.71), channel_id=1, source_target_pairs={{0,8},{4,12},{8,16},{12,20},{16,24},{20,28},{24,0},{28,4},{1,9},{5... | collective-permute-start | bytes 24584 | tf_op jit(solution)/shard_map/ppermute | solution.py:598
  443.5 21.8 %collective-permute-start.30 = (bf16[320,1536]{1,0:T(8,128)(2,1)S(1)}, bf16[320,1536]{1,0:T(8,128)(2,1)S(1)}, u32[]{:S(2)}, u32[]{:S(2)}) collective-permute-start(bf16[320,1536]{1,0:T(8,128)(2,1)S(1)} %copy-done.93), channel_id=1, source_target_pairs={{0,4},{4,0},{8,12},{12,8},{16,20},{20,16},{24,28},{28,24},{1,5},{5... | collective-permute-start | bytes 2949128 | tf_op jit(solution)/shard_map/ppermute | solution.py:605
  460.0 28.3 %collective-permute-start.37 = (bf16[512,1536]{1,0:T(8,128)(2,1)S(1)}, bf16[512,1536]{1,0:T(8,128)(2,1)S(1)}, u32[]{:S(2)}, u32[]{:S(2)}) collective-permute-start(bf16[512,1536]{1,0:T(8,128)(2,1)S(1)} %ring_rows.10), channel_id=1, source_target_pairs={{0,8},{4,12},{8,16},{12,20},{16,24},{20,28},{24,0},{28,4},{1,9},{5... | collective-permute-start | bytes 4718600 | tf_op jit(solution)/shard_map/ppermute | solution.py:598
  465.3 26.3 %collective-permute-start.31 = (bf16[320,1536]{1,0:T(8,128)(2,1)S(1)}, bf16[320,1536]{1,0:T(8,128)(2,1)S(1)}, u32[]{:S(2)}, u32[]{:S(2)}) collective-permute-start(bf16[320,1536]{1,0:T(8,128)(2,1)S(1)} %copy-done.96), channel_id=1, source_target_pairs={{0,4},{4,0},{8,12},{12,8},{16,20},{20,16},{24,28},{28,24},{1,5},{5... | collective-permute-start | bytes 2949128 | tf_op jit(solution)/shard_map/ppermute | solution.py:605
  465.9 21.2 %collective-permute-start.35 = (f32[4,512]{1,0:T(4,128)S(1)}, f32[4,512]{1,0:T(4,128)S(1)}, u32[]{:S(2)}, u32[]{:S(2)}) collective-permute-start(f32[4,512]{1,0:T(4,128)S(1)} %fusion.70), channel_id=1, source_target_pairs={{0,8},{4,12},{8,16},{12,20},{16,24},{20,28},{24,0},{28,4},{1,9},{5... | collective-permute-start | bytes 24584 | tf_op jit(solution)/shard_map/ppermute | solution.py:598
  536.5 42.1 %collective-permute-start.39 = (bf16[2,384,1536]{2,1,0:T(8,128)(2,1)}, bf16[2,384,1536]{2,1,0:T(8,128)(2,1)}, u32[]{:S(2)}, u32[]{:S(2)}) collective-permute-start(bf16[2,384,1536]{2,1,0:T(8,128)(2,1)} %get-tuple-element.257), channel_id=1, source_target_pairs={{0,1},{1,0},{2,3},{3,2},{4,5},{5,4},{6,7},{7,6},{8,9},{9,8},{10,11... | collective-permute-start | bytes 7077896 | tf_op jit(solution)/shard_map/ppermute | solution.py:620
  536.6 24.2 %collective-permute-start.40 = (bf16[320,1536]{1,0:T(8,128)(2,1)}, bf16[320,1536]{1,0:T(8,128)(2,1)S(1)}, u32[]{:S(2)}, u32[]{:S(2)}) collective-permute-start(bf16[320,1536]{1,0:T(8,128)(2,1)} %get-tuple-element.258), channel_id=1, source_target_pairs={{0,4},{4,0},{8,12},{12,8},{16,20},{20,16},{24,28},{28,24},{1,5},{5... | collective-permute-start | bytes 2949128 | tf_op jit(solution)/shard_map/ppermute | solution.py:605
  537.4 37.9 %collective-permute-start.41 = (bf16[512,1536]{1,0:T(8,128)(2,1)S(1)}, bf16[512,1536]{1,0:T(8,128)(2,1)S(1)}, u32[]{:S(2)}, u32[]{:S(2)}) collective-permute-start(bf16[512,1536]{1,0:T(8,128)(2,1)S(1)} %copy-done.6), channel_id=1, source_target_pairs={{0,8},{4,12},{8,16},{12,20},{16,24},{20,28},{24,0},{28,4},{1,9},{5... | collective-permute-start | bytes 4718600 | tf_op jit(solution)/shard_map/ppermute | solution.py:598
  539.0 61.5 %collective-permute-start.43 = (bf16[512,512]{1,0:T(8,128)(2,1)S(1)}, bf16[512,512]{1,0:T(8,128)(2,1)S(1)}, u32[]{:S(2)}, u32[]{:S(2)}) collective-permute-start(bf16[512,512]{1,0:T(8,128)(2,1)S(1)} %slice_bitcast_fusion.1), channel_id=1, source_target_pairs={{2,0},{3,1},{6,4},{7,5},{10,8},{11,9},{14,12},{15,13},{18,16},{19,... | collective-permute-start | bytes 1572872 | tf_op jit(solution)/shard_map/ppermute | solution.py:902
  610.0 37.5 %collective-permute-start.44 = (bf16[512,1536]{1,0:T(8,128)(2,1)S(1)}, bf16[512,1536]{1,0:T(8,128)(2,1)S(1)}, u32[]{:S(2)}, u32[]{:S(2)}) collective-permute-start(bf16[512,1536]{1,0:T(8,128)(2,1)S(1)} %ring_rows.13), channel_id=1, source_target_pairs={{0,8},{4,12},{8,16},{12,20},{16,24},{20,28},{24,0},{28,4},{1,9},{5... | collective-permute-start | bytes 4718600 | tf_op jit(solution)/shard_map/ppermute | solution.py:598
  611.3 23.0 %collective-permute-start.32 = (bf16[320,1536]{1,0:T(8,128)(2,1)}, bf16[320,1536]{1,0:T(8,128)(2,1)}, u32[]{:S(2)}, u32[]{:S(2)}) collective-permute-start(bf16[320,1536]{1,0:T(8,128)(2,1)} %get-tuple-element.235), channel_id=1, source_target_pairs={{0,4},{4,0},{8,12},{12,8},{16,20},{20,16},{24,28},{28,24},{1,5},{5... | collective-permute-start | bytes 2949128 | tf_op jit(solution)/shard_map/ppermute | solution.py:605
  615.0 72.4 %collective-permute-start.42 = (bf16[384,1536]{1,0:T(8,128)(2,1)}, bf16[384,1536]{1,0:T(8,128)(2,1)}, u32[]{:S(2)}, u32[]{:S(2)}) collective-permute-start(bf16[384,1536]{1,0:T(8,128)(2,1)} %fusion.31), channel_id=1, source_target_pairs={{0,2},{1,3},{2,0},{3,1},{4,6},{5,7},{6,4},{7,5},{8,10},{9,11},{10,... | collective-permute-start | bytes 3538952 | tf_op jit(solution)/shard_map/ppermute | solution.py:623
  666.6 50.2 %collective-permute-start.33 = (bf16[320,1536]{1,0:T(8,128)(2,1)}, bf16[320,1536]{1,0:T(8,128)(2,1)}, u32[]{:S(2)}, u32[]{:S(2)}) collective-permute-start(bf16[320,1536]{1,0:T(8,128)(2,1)} %get-tuple-element.236), channel_id=1, source_target_pairs={{0,4},{4,0},{8,12},{12,8},{16,20},{20,16},{24,28},{28,24},{1,5},{5... | collective-permute-start | bytes 2949128 | tf_op jit(solution)/shard_map/ppermute | solution.py:605
  668.4 48.5 %collective-permute-start.45 = (bf16[512,1536]{1,0:T(8,128)(2,1)S(1)}, bf16[512,1536]{1,0:T(8,128)(2,1)S(1)}, u32[]{:S(2)}, u32[]{:S(2)}) collective-permute-start(bf16[512,1536]{1,0:T(8,128)(2,1)S(1)} %ring_rows.14), channel_id=1, source_target_pairs={{0,8},{4,12},{8,16},{12,20},{16,24},{20,28},{24,0},{28,4},{1,9},{5... | collective-permute-start | bytes 4718600 | tf_op jit(solution)/shard_map/ppermute | solution.py:598
  671.2 58.7 %collective-permute-start.54 = (bf16[384,128]{1,0:T(8,128)(2,1)}, bf16[384,128]{1,0:T(8,128)(2,1)}, u32[]{:S(2)}, u32[]{:S(2)}) collective-permute-start(bf16[384,128]{1,0:T(8,128)(2,1)} %fusion.62), channel_id=1, source_target_pairs={{0,2},{1,3},{2,0},{3,1},{4,6},{5,7},{6,4},{7,5},{8,10},{9,11},{10,... | collective-permute-start | bytes 294920 | tf_op jit(solution)/shard_map/ppermute | solution.py:623
  690.9 30.5 %collective-permute-start.46 = (bf16[192,1536]{1,0:T(8,128)(2,1)}, bf16[192,1536]{1,0:T(8,128)(2,1)}, u32[]{:S(2)}, u32[]{:S(2)}) collective-permute-start(bf16[192,1536]{1,0:T(8,128)(2,1)} %get-tuple-element.429), channel_id=1, source_target_pairs={{0,4},{4,0},{8,12},{12,8},{16,20},{20,16},{24,28},{28,24},{1,5},{5... | collective-permute-start | bytes 1769480 | tf_op jit(solution)/shard_map/ppermute | solution.py:605
  759.0 21.5 %collective-permute-start.55 = (bf16[192,2176]{1,0:T(8,128)(2,1)S(1)}, bf16[192,2176]{1,0:T(8,128)(2,1)S(1)}, u32[]{:S(2)}, u32[]{:S(2)}) collective-permute-start(bf16[192,2176]{1,0:T(8,128)(2,1)S(1)} %dynamic-slice_bitcast_fusion), channel_id=1, source_target_pairs={{0,4},{4,0},{8,12},{12,8},{16,20},{20,16},{24,28},{28,24},{1,5},{5... | collective-permute-start | bytes 2506760 | tf_op jit(solution)/shard_map/ppermute | solution.py:605
  766.5 33.1 %collective-permute-start.63 = (bf16[192,1536]{1,0:T(8,128)(2,1)}, bf16[192,1536]{1,0:T(8,128)(2,1)S(1)}, u32[]{:S(2)}, u32[]{:S(2)}) collective-permute-start(bf16[192,1536]{1,0:T(8,128)(2,1)} %bitcast.61), channel_id=1, source_target_pairs={{0,4},{4,0},{8,12},{12,8},{16,20},{20,16},{24,28},{28,24},{1,5},{5... | collective-permute-start | bytes 1769480 | tf_op jit(solution)/shard_map/ppermute | solution.py:605
  818.3 20.6 %collective-permute-start.62 = (bf16[192,2176]{1,0:T(8,128)(2,1)S(1)}, bf16[192,2176]{1,0:T(8,128)(2,1)S(1)}, u32[]{:S(2)}, u32[]{:S(2)}) collective-permute-start(bf16[192,2176]{1,0:T(8,128)(2,1)S(1)} %bitcast.212), channel_id=1, source_target_pairs={{0,4},{4,0},{8,12},{12,8},{16,20},{20,16},{24,28},{28,24},{1,5},{5... | collective-permute-start | bytes 2506760 | tf_op jit(solution)/shard_map/ppermute | solution.py:605
  (124 other events, 1925.8 us)
Sparse Core Ops, SparseCore 0:
  16.5 49.7 all-gather.6
  68.4 45.2 all-gather.8
  115.8 67.7 all-gather.10
  185.6 119.9 all-gather.12
  378.8 88.0 reduce-scatter.5
  469.4 150.6 reduce-scatter.3
  622.8 72.5 reduce-scatter.7

commit v6 on v4

--- a/solution.py
+++ b/solution.py
@@ -941,34 +941,29 @@
     extra = extra.T.astype(bf16).reshape(chips, 2, shard_rows, 128)
     extra_mine = jnp.where(core == 0, extra[:, 0], extra[:, 1])
     extra_mate = core_shift(jnp.where(core == 0, extra[:, 1], extra[:, 0]), 1)
-    ring_step(result_held, after(result_steps[3], extra_mine), arrived)
-    arrived = ring_send(result_held)
-    back_mate, extra_mate = after((back_mate, extra_mate), result_held[2])
     back_mine = jnp.concatenate([back_mine, extra_mine], axis=2)
     back_mate = jnp.concatenate([back_mate, extra_mate], axis=2)
     back_low = chip_low(back_mine, back_mate)
     back_sent = chip_send(back_low)
+    ring_step(result_held, after(result_steps[3], back_low), arrived)
+    arrived = ring_send(result_held)
     in_state = adamw_update(
         expert_in,
         in_first,
         in_second,
-        after(in_part, back_low).astype(f32),
+        after(in_part, result_held[2]).astype(f32),
         0.5 / math.sqrt(MODEL_WIDTH),
         DECAY,
     )
     moe_out = ring_step(result_held, after(result_steps[0], in_state), arrived)
     layer_out = (residual + moe_out).astype(bf16)
     back_sent = after(back_sent, moe_out)
-    back_parts = x_parts(chip_total(back_mine, back_mate, back_sent).astype(bf16))
-    back_parts = z_parts(add_parts(back_parts))
-    back_low = add_parts(back_parts)
-    front_low = after(front_part, back_low)
-    front_parts = x_parts(front_low)
-    back_low = z_join(after(back_low, front_low))
-    front_low = add_parts(after(front_parts, back_low))
-    front_low = add_parts(z_parts(front_low))
-    back_sum = x_join(after(back_low, front_low))
-    front_sum = x_join(z_join(front_low))
+    back_part = chip_total(back_mine, back_mate, back_sent).astype(bf16)
+    part = jnp.concatenate([front_part, back_part], axis=1)
+    part = add_parts(x_parts(part))
+    part = add_parts(z_parts(part))
+    total = x_join(z_join(part))
+    front_sum, back_sum = total[:, :QKV], total[:, QKV:]
     output_sum = back_sum[:, :MODEL_WIDTH]
     router_sum = back_sum[:, MODEL_WIDTH : MODEL_WIDTH + experts_all]
     query_sum = front_sum[:, :MODEL_WIDTH]

time: 854 us -> 893 us (1.046)
  waiting for transfers between devices: 384 us -> 421 us
  starting transfers between devices: 76.1 us -> 63.4 us
    ppermute x22 -> x20, waiting for transfers between devices: 145 us -> 175 us  [x_shift(): lax.ppermute(value, 'expert', [(a * wide + b, a * wide + (b + by) % wide)...]
    ppermute x33 -> x27, waiting for transfers between devices: 166 us -> 186 us  [z_shift(): lax.ppermute(value, 'expert', [(a * wide + b, (a + by) % depth * wide + b...]
    ppermute x1, waiting for transfers between devices: 12.7 us -> 0.01 us  [y_shift(): lax.ppermute(value, 'fsdp', [(a, (a + 2 * by) % shards) for a in range(sh...]
    ppermute x33 -> x27, starting transfers between devices: 35.1 us -> 27.7 us  [z_shift(): lax.ppermute(value, 'expert', [(a * wide + b, (a + by) % depth * wide + b...]
    ppermute x22 -> x20, starting transfers between devices: 27.4 us -> 23.3 us  [x_shift(): lax.ppermute(value, 'expert', [(a * wide + b, a * wide + (b + by) % wide)...]
    unnamed x206 -> x192, local copies, waits for them, and re-layouts: 29.6 us -> 29 us
  transfers between devices with their start and end apart: 70 -> 62, of which waited for: 45 -> 36; matrix products, arithmetic and copies ran while one was open for 15% -> 14% of each run, Pallas kernels for 18% -> 18%
where the time goes in v6:
time: 893 us; the launch traced here: 876 us
  waiting for transfers between devices  421 us (47%)
  Pallas kernels  194 us (22%)
  other arithmetic  103 us (12%)
  starting transfers between devices  63.4 us (7%)
  local copies, waits for them, and re-layouts  45.7 us (5%)
  matrix products  33.1 us (4%)
  between operations  16 us (2%)
    ppermute x27, waiting for transfers between devices, z_shift(): lax.ppermute(value, 'expert', [(a * wide + b, (a + by) % depth * wide + b...  186 us
    ppermute x20, waiting for transfers between devices, x_shift(): lax.ppermute(value, 'expert', [(a * wide + b, a * wide + (b + by) % wide)...  175 us
    sub x6, other arithmetic, adamw_update(): weight - step_rate * (first_hat / (jnp.sqrt(second_hat) + ADAM_EPS) + dec...  52.1 us
    pallas_call x1, Pallas kernels, core_rows(): pl.pallas_call(functools.partial(core_kernel, count), out_shape=(low, low...  36.4 us
    ppermute x1, waiting for transfers between devices, body(): lax.ppermute(kv_low[s], 'fsdp', [(a + 2 * s, a) for a in range(shards - 2...  31.3 us
    unnamed x192, local copies, waits for them, and re-layouts  29 us
    ppermute x27, starting transfers between devices, z_shift(): lax.ppermute(value, 'expert', [(a * wide + b, (a + by) % depth * wide + b...  27.7 us
    pallas_call x8, Pallas kernels, ring_rows(): pl.pallas_call(functools.partial(ring_kernel, len(pieces)), out_shape=jax...  26.1 us
  transfers between devices with their start and end apart: 62, of which 36 were waited for; matrix products, arithmetic and copies ran while one was open for 14% of the time, Pallas kernels for 18%

profile of v6, /device:TPU:8, one launch (start us, length us, event | category | flops | bytes accessed | tf_op | source)
XLA Modules:
  0.0 876.5 jit_solution(10061837484977678161)
XLA Ops:
  24.8 4.5 pick_rows.8
  35.6 17.1 %collective-permute-done.4.refs_4_ = bf16[320,1536]{1,0:T(8,128)(2,1)} collective-permute-done((bf16[320,1536]{1,0:T(8,128)(2,1)}, bf16[320,1536]{1,0:T(8,128)(2,1)}, u32[]{:S(2)}, u32[]{:S(2)}) %collective-permute-start.4) | collective-permute-done | bytes 983072 | tf_op jit(solution)/shard_map/ppermute | solution.py:605
  52.7 5.3 collective-permute-done.3.rows
  68.8 6.1 fusion.2.pre
  79.9 6.5 convert_element_type.183
  91.3 22.4 %collective-permute-done.6 = bf16[512,512]{1,0:T(8,128)(2,1)} collective-permute-done((bf16[512,512]{1,0:T(8,128)(2,1)}, bf16[512,512]{1,0:T(8,128)(2,1)}, u32[]{:S(2)}, u32[]{:S(2)}) %collective-permute-start.6) | collective-permute-done | bytes 524320 | tf_op jit(solution)/shard_map/ppermute | solution.py:626
  126.6 14.3 %attend.1 = (bf16[512,1536]{1,0:T(8,128)(2,1)}, f32[12,1,512]{2,1,0:T(1,128)}, bf16[512,1536]{1,0:T(8,128)(2,1)}) custom-call(s32[1]{0:T(128)} %bitcast.place, f32[512,2048]{1,0:T(8,128)} %copy-done.45, f32[512,128]{1,0:T(8,128)} %get-tuple-element.458.cosine, f32[512,128]{1,0:T(8,128)} %copy-done.46, bf16[4,512,512]{2,1,0:T(8,128)(2,1)} %pad_maximum_fusion.1.keys.values, ...), custom_call_target="tpu_custom_call" | custom-call | flops 1000000000 | bytes 1000000 | tf_op jit(solution)/shard_map/attend/pallas_call | solution.py:106
  140.9 19.4 %collective-permute-done.9.rows = bf16[512,1536]{1,0:T(8,128)(2,1)S(1)} collective-permute-done((bf16[512,1536]{1,0:T(8,128)(2,1)}, bf16[512,1536]{1,0:T(8,128)(2,1)S(1)}, u32[]{:S(2)}, u32[]{:S(2)}) %collective-permute-start.9) | collective-permute-done | bytes 1572896 | tf_op jit(solution)/shard_map/ppermute | solution.py:598
  161.4 6.1 multiply_reduce_fusion.2
  175.7 19.4 %collective-permute-done.11.refs_6_ = bf16[320,1536]{1,0:T(8,128)(2,1)S(1)} collective-permute-done((bf16[320,1536]{1,0:T(8,128)(2,1)S(1)}, bf16[320,1536]{1,0:T(8,128)(2,1)S(1)}, u32[]{:S(2)}, u32[]{:S(2)}) %collective-permute-start.11) | collective-permute-done | bytes 983072 | tf_op jit(solution)/shard_map/ppermute | solution.py:605
  196.5 8.2 collective-permute-done.13.rows
  208.8 8.1 collective-permute-done.12.refs_4_
  220.5 20.5 %collective-permute-done.16 = f32[4,512]{1,0:T(4,128)S(1)} collective-permute-done((f32[4,512]{1,0:T(4,128)S(1)}, f32[4,512]{1,0:T(4,128)S(1)}, u32[]{:S(2)}, u32[]{:S(2)}) %collective-permute-start.16) | collective-permute-done | bytes 8224 | tf_op jit(solution)/shard_map/ppermute | solution.py:598
  250.7 15.4 %collective-permute-done.17.refs_7_ = bf16[320,1536]{1,0:T(8,128)(2,1)S(1)} collective-permute-done((bf16[320,1536]{1,0:T(8,128)(2,1)S(1)}, bf16[320,1536]{1,0:T(8,128)(2,1)S(1)}, u32[]{:S(2)}, u32[]{:S(2)}) %collective-permute-start.17) | collective-permute-done | bytes 983072 | tf_op jit(solution)/shard_map/ppermute | solution.py:605
  269.5 6.9 collective-permute-done.19.rows
  277.6 13.0 %inner_rows.1.refs_9_ = bf16[4,640,768]{2,1,0:T(8,128)(2,1)} custom-call(bf16[320,1536]{1,0:T(8,128)(2,1)} %copy-done.24, bf16[320,1536]{1,0:T(8,128)(2,1)} %copy-done.25, bf16[320,1536]{1,0:T(8,128)(2,1)} %copy-done.28, bf16[320,1536]{1,0:T(8,128)(2,1)} %copy-done.31, bf16[320,1536]{1,0:T(8,128)(2,1)} %collective-permute-done.4.refs_4_, ...), custom_call_target="tpu_custom_call" | custom-call | flops 6039797760 | bytes 20000000 | tf_op jit(solution)/shard_map/inner_rows/pallas_call | solution.py:248
  294.9 5.1 collective-permute-done.22
  301.5 11.9 %collective-permute-done.23 = f32[4,4,80]{2,0,1:T(4,128)S(1)} collective-permute-done((f32[4,4,80]{2,0,1:T(4,128)S(1)}, f32[4,4,80]{2,0,1:T(4,128)S(1)}, u32[]{:S(2)}, u32[]{:S(2)}) %collective-permute-start.23) | collective-permute-done | bytes 5152 | tf_op jit(solution)/shard_map/ppermute | solution.py:605
  316.1 36.4 %core_rows.1 = (bf16[4,640,768]{2,1,0:T(8,128)(2,1)}, bf16[4,640,768]{2,1,0:T(8,128)(2,1)}, bf16[4,640,768]{2,1,0:T(8,128)(2,1)}, f32[4,640,1]{2,1,0:T(8,128)}, ...) custom-call(bf16[320,1536]{1,0:T(8,128)(2,1)} %copy-done.26, ...), custom_call_target="tpu_custom_call" | custom-call | flops 24159191040 | bytes 60000000 | tf_op jit(solution)/shard_map/core_rows/pallas_call | solution.py:305
  353.9 13.8 %down_grads.1 = bf16[4,4,768,384]{3,2,1,0:T(8,128)(2,1)} custom-call(bf16[320,1536]{1,0:T(8,128)(2,1)} %copy-done.24, bf16[320,1536]{1,0:T(8,128)(2,1)} %copy-done.25, bf16[320,1536]{1,0:T(8,128)(2,1)} %copy-done.28, bf16[320,1536]{1,0:T(8,128)(2,1)} %copy-done.31, bf16[320,1536]{1,0:T(8,128)(2,1)} %collective-permute-done.4.refs_4_, ...), custom_call_target="tpu_custom_call" | custom-call | flops 6039797760 | bytes 22000000 | tf_op jit(solution)/shard_map/down_grads/pallas_call | solution.py:364
  381.9 20.8 %in_grads.1 = bf16[4,4,384,1536]{3,2,1,0:T(8,128)(2,1)} custom-call(bf16[320,1536]{1,0:T(8,128)(2,1)} %copy-done.26, bf16[320,1536]{1,0:T(8,128)(2,1)} %copy-done.27, bf16[320,1536]{1,0:T(8,128)(2,1)} %copy-done.29, bf16[320,1536]{1,0:T(8,128)(2,1)} %copy-done.30, bf16[320,1536]{1,0:T(8,128)(2,1)} %copy-done.82, ...), custom_call_target="tpu_custom_call" | custom-call | flops 12079595520 | bytes 35000000 | tf_op jit(solution)/shard_map/in_grads/pallas_call | solution.py:392
  406.6 6.0 collective-permute-done.27
  422.5 19.5 %collective-permute-done.29.refs_2_ = bf16[320,1536]{1,0:T(8,128)(2,1)S(1)} collective-permute-done((bf16[320,1536]{1,0:T(8,128)(2,1)S(1)}, bf16[320,1536]{1,0:T(8,128)(2,1)S(1)}, u32[]{:S(2)}, u32[]{:S(2)}) %collective-permute-start.29) | collective-permute-done | bytes 983072 | tf_op jit(solution)/shard_map/ppermute | solution.py:605
  442.8 12.4 %result_rows.1 = (bf16[320,1536]{1,0:T(8,128)(2,1)}, bf16[320,1536]{1,0:T(8,128)(2,1)}, bf16[320,1536]{1,0:T(8,128)(2,1)}, bf16[320,1536]{1,0:T(8,128)(2,1)}, bf...) custom-call(bf16[4,640,768]{2,1,0:T(8,128)(2,1)} %get-tuple-element., ...), custom_call_target="tpu_custom_call" | custom-call | flops 6039797760 | bytes 22000000 | tf_op jit(solution)/shard_map/result_rows/pallas_call | solution.py:336
  465.5 19.0 %collective-permute-done.35 = f32[4,512]{1,0:T(4,128)S(1)} collective-permute-done((f32[4,512]{1,0:T(4,128)S(1)}, f32[4,512]{1,0:T(4,128)S(1)}, u32[]{:S(2)}, u32[]{:S(2)}) %collective-permute-start.35) | collective-permute-done | bytes 8224 | tf_op jit(solution)/shard_map/ppermute | solution.py:598
  490.9 4.6 multiply_reduce_fusion
  502.9 17.9 %attend_back.1 = (bf16[512,1536]{1,0:T(8,128)(2,1)}, bf16[4,512,256]{2,1,0:T(8,128)(2,1)}, bf16[4,512,256]{2,1,0:T(8,128)(2,1)}) custom-call(s32[1]{0:T(128)} %bitcast.place, bf16[512,1536]{1,0:T(8,128)(2,1)} %get-tuple-element.243.query, bf16[4,512,512]{2,1,0:T(8,128)(2,1)} %pad_maximum_fusion.1.keys.values, ...), custom_call_target="tpu_custom_call" | custom-call | flops 1000000000 | bytes 1000000 | tf_op jit(solution)/shard_map/attend_back/pallas_call | solution.py:182
  525.7 6.7 core_grads.1
  534.1 12.0 %multiply_subtract_fusion.1 = (f32[4,768,384]{2,1,0:T(8,128)}, f32[4,768,384]{2,1,0:T(8,128)}, f32[4,768,384]{2,1,0:T(8,128)}) fusion(f32[4,768,384]{2,1,0:T(8,128)} %param.51, bf16[4,768,384]{2,1,0:T(8,128)(2,1)} %bitcast.177, f32[4,768,384]{2,1,0:T(8,128)} %param.52, f32[4,768,384]{2,1,0:T(8,128)} %param.53), kind=kLoop, calls=%fused_computation.25 | loop fusion | flops 18874368 | bytes 30670848 | tf_op jit(solution)/shard_map/sub | solution.py:549
  546.9 14.1 %collective-permute-done.41.refs_3_ = bf16[512,1536]{1,0:T(8,128)(2,1)S(1)} collective-permute-done((bf16[512,1536]{1,0:T(8,128)(2,1)S(1)}, bf16[512,1536]{1,0:T(8,128)(2,1)S(1)}, u32[]{:S(2)}, u32[]{:S(2)}) %collective-permute-start.41) | collective-permute-done | bytes 1572896 | tf_op jit(solution)/shard_map/ppermute | solution.py:598
  564.2 31.3 %collective-permute-done.39 = bf16[512,512]{1,0:T(8,128)(2,1)S(1)} collective-permute-done((bf16[512,512]{1,0:T(8,128)(2,1)S(1)}, bf16[512,512]{1,0:T(8,128)(2,1)S(1)}, u32[]{:S(2)}, u32[]{:S(2)}) %collective-permute-start.39) | collective-permute-done | bytes 524320 | tf_op jit(solution)/shard_map/ppermute | solution.py:902
  597.1 7.3 weight_grads.1
  605.7 22.5 %collective-permute-done.32.refs_2_ = bf16[320,1536]{1,0:T(8,128)(2,1)S(1)} collective-permute-done((bf16[320,1536]{1,0:T(8,128)(2,1)}, bf16[320,1536]{1,0:T(8,128)(2,1)S(1)}, u32[]{:S(2)}, u32[]{:S(2)}) %collective-permute-start.32) | collective-permute-done | bytes 983072 | tf_op jit(solution)/shard_map/ppermute | solution.py:605
  630.5 6.0 fusion.11
  636.6 4.4 fusion.15
  646.4 7.0 collective-permute-start.46
  653.4 12.8 %collective-permute-done.44.refs_3_ = bf16[512,1536]{1,0:T(8,128)(2,1)S(1)} collective-permute-done((bf16[512,1536]{1,0:T(8,128)(2,1)S(1)}, bf16[512,1536]{1,0:T(8,128)(2,1)S(1)}, u32[]{:S(2)}, u32[]{:S(2)}) %collective-permute-start.44) | collective-permute-done | bytes 1572896 | tf_op jit(solution)/shard_map/ppermute | solution.py:598
  671.0 24.4 %multiply_subtract_fusion = (f32[4,384,1536]{2,1,0:T(8,128)}, f32[4,384,1536]{2,1,0:T(8,128)}, f32[4,384,1536]{2,1,0:T(8,128)}) fusion(f32[4,384,1536]{2,1,0:T(8,128)} %param.48, bf16[4,384,1536]{2,1,0:T(8,128)(2,1)} %bitcast.176, f32[4,384,1536]{2,1,0:T(8,128)} %param.49, f32[4,384,1536]{2,1,0:T(8,128)} %param.50), kind=kLoop, calls=%fused_computation.4 | loop fusion | flops 37748736 | bytes 61341696 | tf_op jit(solution)/shard_map/sub | solution.py:549
  695.4 10.2 %collective-permute-done.45.refs_3_ = bf16[512,1536]{1,0:T(8,128)(2,1)S(1)} collective-permute-done((bf16[512,1536]{1,0:T(8,128)(2,1)S(1)}, bf16[512,1536]{1,0:T(8,128)(2,1)S(1)}, u32[]{:S(2)}, u32[]{:S(2)}) %collective-permute-start.45) | collective-permute-done | bytes 1572896 | tf_op jit(solution)/shard_map/ppermute | solution.py:598
  705.6 4.5 ring_rows.15
  717.2 29.7 %collective-permute-done.47 = bf16[192,3712]{1,0:T(8,128)(2,1)} collective-permute-done((bf16[192,3712]{1,0:T(8,128)(2,1)}, bf16[192,3712]{1,0:T(8,128)(2,1)}, u32[]{:S(2)}, u32[]{:S(2)}) %collective-permute-start.47) | collective-permute-done | bytes 1425440 | tf_op jit(solution)/shard_map/ppermute | solution.py:605
  749.9 5.5 collective-permute-start.49
  755.4 18.3 %collective-permute-done.48 = bf16[48,3712]{1,0:T(8,128)(2,1)S(1)} collective-permute-done((bf16[48,3712]{1,0:T(8,128)(2,1)S(1)}, bf16[48,3712]{1,0:T(8,128)(2,1)S(1)}, u32[]{:S(2)}, u32[]{:S(2)}) %collective-permute-start.48) | collective-permute-done | bytes 356384 | tf_op jit(solution)/shard_map/ppermute | solution.py:598
  788.2 9.4 %collective-permute-done.51 = bf16[48,3712]{1,0:T(8,128)(2,1)S(1)} collective-permute-done((bf16[48,3712]{1,0:T(8,128)(2,1)}, bf16[48,3712]{1,0:T(8,128)(2,1)S(1)}, u32[]{:S(2)}, u32[]{:S(2)}) %collective-permute-start.51) | collective-permute-done | bytes 356384 | tf_op jit(solution)/shard_map/ppermute | solution.py:598
  798.3 18.2 %collective-permute-done.52 = bf16[48,3712]{1,0:T(8,128)(2,1)S(1)} collective-permute-done((bf16[48,3712]{1,0:T(8,128)(2,1)}, bf16[48,3712]{1,0:T(8,128)(2,1)S(1)}, u32[]{:S(2)}, u32[]{:S(2)}) %collective-permute-start.52) | collective-permute-done | bytes 356384 | tf_op jit(solution)/shard_map/ppermute | solution.py:598
  819.0 6.7 fusion.19
  827.4 22.4 %collective-permute-done.54 = bf16[192,3712]{1,0:T(8,128)(2,1)S(1)} collective-permute-done((bf16[192,3712]{1,0:T(8,128)(2,1)}, bf16[192,3712]{1,0:T(8,128)(2,1)S(1)}, u32[]{:S(2)}, u32[]{:S(2)}) %collective-permute-start.54) | collective-permute-done | bytes 1425440 | tf_op jit(solution)/shard_map/ppermute | solution.py:605
  854.7 11.5 %multiply_subtract_fusion.2 = (f32[384,1536]{1,0:T(8,128)}, f32[384,1536]{1,0:T(8,128)}, f32[384,1536]{1,0:T(8,128)}, f32[384,1536]{1,0:T(8,128)}, f32[384,1536]{1,0:T(8,128)}, /*index=5*/f32[384,1536]{1,0:T(8,128)}) fusion(f32[384,1536]{1,0:T(8,128)} %param.42, f32[384,3712]{1,0:T(8,128)} %copy-done.36, f32[384,1536]{1,0:T(8,128)} %param.43, ...), kind=kLoop, calls=%fused_computation.56 | loop fusion | flops 17694720 | bytes 33030144 | tf_op jit(solution)/shard_map/sub | solution.py:549
  (417 shorter events, 215.1 us)
Async XLA Ops:
  7.2 59.0 %all-gather.7.cloned.1.call-start = ((), (), s32[]{:S(2)}) async-start(), calls=%async_computation.3 | async-start | bytes 8355840 | tf_op jit(solution)/shard_map/all_gather | solution.py:636
  16.4 145.1 %all-gather.9.cloned.1.call-start = ((), (), s32[]{:S(2)}) async-start(), calls=%async_computation.4 | async-start | bytes 5898240 | tf_op jit(solution)/shard_map/all_gather | solution.py:644
  17.6 260.0 %all-gather.11.cloned.1.call-start = ((), (), s32[]{:S(2)}) async-start(), calls=%async_computation.8 | async-start | bytes 11796480 | tf_op jit(solution)/shard_map/all_gather | solution.py:762
  22.3 35.7 %collective-permute-start.3 = (bf16[512,1536]{1,0:T(8,128)(2,1)}, bf16[512,1536]{1,0:T(8,128)(2,1)}, u32[]{:S(2)}, u32[]{:S(2)}) collective-permute-start(bf16[512,1536]{1,0:T(8,128)(2,1)} %rows.1), channel_id=1, source_target_pairs={{0,8},{4,12},{8,16},{12,20},{16,24},{20,28},{24,0},{28,4},{1,9},{5... | collective-permute-start | bytes 4718600 | tf_op jit(solution)/shard_map/ppermute | solution.py:598
  30.3 22.4 %collective-permute-start.4 = (bf16[320,1536]{1,0:T(8,128)(2,1)}, bf16[320,1536]{1,0:T(8,128)(2,1)}, u32[]{:S(2)}, u32[]{:S(2)}) collective-permute-start(bf16[320,1536]{1,0:T(8,128)(2,1)} %bitcast.10), channel_id=1, source_target_pairs={{0,4},{4,0},{8,12},{12,8},{16,20},{20,16},{24,28},{28,24},{1,5},{5... | collective-permute-start | bytes 2949128 | tf_op jit(solution)/shard_map/ppermute | solution.py:605
  79.9 236.2 %all-gather.13.cloned.1.call-start = ((), (), s32[]{:S(2)}) async-start(), calls=%async_computation.9 | async-start | bytes 23592960 | tf_op jit(solution)/shard_map/all_gather | solution.py:763
  86.4 416.5 %reduce-scatter.6.cloned.1.call-start = ((), (), s32[]{:S(2)}) async-start(), calls=%async_computation.6 | async-start | bytes 11796480 | tf_op jit(solution)/shard_map/reduce_scatter | solution.py:823
  86.4 37.0 %collective-permute-start.8 = (bf16[512,1536]{1,0:T(8,128)(2,1)}, bf16[512,1536]{1,0:T(8,128)(2,1)}, u32[]{:S(2)}, u32[]{:S(2)}) collective-permute-start(bf16[512,1536]{1,0:T(8,128)(2,1)} %collective-permute-done.3.rows), channel_id=1, source_target_pairs={{0,8},{4,12},{8,16},{12,20},{16,24},{20,28},{24,0},{28,4},{1,9},{5... | collective-permute-start | bytes 4718600 | tf_op jit(solution)/shard_map/ppermute | solution.py:598
  88.0 25.7 %collective-permute-start.6 = (bf16[512,512]{1,0:T(8,128)(2,1)}, bf16[512,512]{1,0:T(8,128)(2,1)}, u32[]{:S(2)}, u32[]{:S(2)}) collective-permute-start(bf16[512,512]{1,0:T(8,128)(2,1)} %get-tuple-element.454), channel_id=1, source_target_pairs={{0,2},{1,3},{4,6},{5,7},{8,10},{9,11},{12,14},{13,15},{16,18},{17,... | collective-permute-start | bytes 1572872 | tf_op jit(solution)/shard_map/ppermute | solution.py:626
  91.3 22.5 %collective-permute-start.5 = (bf16[512,512]{1,0:T(8,128)(2,1)}, bf16[512,512]{1,0:T(8,128)(2,1)}, u32[]{:S(2)}, u32[]{:S(2)}) collective-permute-start(bf16[512,512]{1,0:T(8,128)(2,1)} %get-tuple-element.454), channel_id=1, source_target_pairs={{0,1},{1,0},{2,3},{3,2},{4,5},{5,4},{6,7},{7,6},{8,9},{9,8},{10,11... | collective-permute-start | bytes 1572872 | tf_op jit(solution)/shard_map/ppermute | solution.py:620
  123.5 36.8 %collective-permute-start.9 = (bf16[512,1536]{1,0:T(8,128)(2,1)}, bf16[512,1536]{1,0:T(8,128)(2,1)S(1)}, u32[]{:S(2)}, u32[]{:S(2)}) collective-permute-start(bf16[512,1536]{1,0:T(8,128)(2,1)} %collective-permute-done.8.rows), channel_id=1, source_target_pairs={{0,8},{4,12},{8,16},{12,20},{16,24},{20,28},{24,0},{28,4},{1,9},{5... | collective-permute-start | bytes 4718600 | tf_op jit(solution)/shard_map/ppermute | solution.py:598
  125.1 44.1 %collective-permute-start.10 = (bf16[320,1536]{1,0:T(8,128)(2,1)}, bf16[320,1536]{1,0:T(8,128)(2,1)}, u32[]{:S(2)}, u32[]{:S(2)}) collective-permute-start(bf16[320,1536]{1,0:T(8,128)(2,1)} %bitcast.17), channel_id=1, source_target_pairs={{0,4},{4,0},{8,12},{12,8},{16,20},{20,16},{24,28},{28,24},{1,5},{5... | collective-permute-start | bytes 2949128 | tf_op jit(solution)/shard_map/ppermute | solution.py:605
  167.9 36.9 %collective-permute-start.13 = (bf16[512,1536]{1,0:T(8,128)(2,1)S(1)}, bf16[512,1536]{1,0:T(8,128)(2,1)}, u32[]{:S(2)}, u32[]{:S(2)}) collective-permute-start(bf16[512,1536]{1,0:T(8,128)(2,1)S(1)} %multiply_convert_fusion.rows), channel_id=1, source_target_pairs={{0,8},{4,12},{8,16},{12,20},{16,24},{20,28},{24,0},{28,4},{1,9},{5... | collective-permute-start | bytes 4718600 | tf_op jit(solution)/shard_map/ppermute | solution.py:598
  172.5 22.7 %collective-permute-start.11 = (bf16[320,1536]{1,0:T(8,128)(2,1)S(1)}, bf16[320,1536]{1,0:T(8,128)(2,1)S(1)}, u32[]{:S(2)}, u32[]{:S(2)}) collective-permute-start(bf16[320,1536]{1,0:T(8,128)(2,1)S(1)} %bitcast.169), channel_id=1, source_target_pairs={{0,4},{4,0},{8,12},{12,8},{16,20},{20,16},{24,28},{28,24},{1,5},{5... | collective-permute-start | bytes 2949128 | tf_op jit(solution)/shard_map/ppermute | solution.py:605
  195.1 21.8 %collective-permute-start.12 = (bf16[320,1536]{1,0:T(8,128)(2,1)S(1)}, bf16[320,1536]{1,0:T(8,128)(2,1)S(1)}, u32[]{:S(2)}, u32[]{:S(2)}) collective-permute-start(bf16[320,1536]{1,0:T(8,128)(2,1)S(1)} %bitcast.167), channel_id=1, source_target_pairs={{0,4},{4,0},{8,12},{12,8},{16,20},{20,16},{24,28},{28,24},{1,5},{5... | collective-permute-start | bytes 2949128 | tf_op jit(solution)/shard_map/ppermute | solution.py:605
  204.8 36.3 %collective-permute-start.15 = (bf16[512,1536]{1,0:T(8,128)(2,1)}, bf16[512,1536]{1,0:T(8,128)(2,1)}, u32[]{:S(2)}, u32[]{:S(2)}) collective-permute-start(bf16[512,1536]{1,0:T(8,128)(2,1)} %collective-permute-done.13.rows), channel_id=1, source_target_pairs={{0,8},{4,12},{8,16},{12,20},{16,24},{20,28},{24,0},{28,4},{1,9},{5... | collective-permute-start | bytes 4718600 | tf_op jit(solution)/shard_map/ppermute | solution.py:598
  216.9 27.5 %collective-permute-start.14 = (bf16[320,1536]{1,0:T(8,128)(2,1)}, bf16[320,1536]{1,0:T(8,128)(2,1)}, u32[]{:S(2)}, u32[]{:S(2)}) collective-permute-start(bf16[320,1536]{1,0:T(8,128)(2,1)} %bitcast.18), channel_id=1, source_target_pairs={{0,4},{4,0},{8,12},{12,8},{16,20},{20,16},{24,28},{28,24},{1,5},{5... | collective-permute-start | bytes 2949128 | tf_op jit(solution)/shard_map/ppermute | solution.py:605
  241.1 35.3 %collective-permute-start.19 = (bf16[512,1536]{1,0:T(8,128)(2,1)}, bf16[512,1536]{1,0:T(8,128)(2,1)S(1)}, u32[]{:S(2)}, u32[]{:S(2)}) collective-permute-start(bf16[512,1536]{1,0:T(8,128)(2,1)} %collective-permute-done.15.rows), channel_id=1, source_target_pairs={{0,8},{4,12},{8,16},{12,20},{16,24},{20,28},{24,0},{28,4},{1,9},{5... | collective-permute-start | bytes 4718600 | tf_op jit(solution)/shard_map/ppermute | solution.py:598
  244.4 21.7 %collective-permute-start.17 = (bf16[320,1536]{1,0:T(8,128)(2,1)S(1)}, bf16[320,1536]{1,0:T(8,128)(2,1)S(1)}, u32[]{:S(2)}, u32[]{:S(2)}) collective-permute-start(bf16[320,1536]{1,0:T(8,128)(2,1)S(1)} %bitcast.168), channel_id=1, source_target_pairs={{0,4},{4,0},{8,12},{12,8},{16,20},{20,16},{24,28},{28,24},{1,5},{5... | collective-permute-start | bytes 2949128 | tf_op jit(solution)/shard_map/ppermute | solution.py:605
  266.1 27.3 %collective-permute-start.18 = (bf16[320,1536]{1,0:T(8,128)(2,1)}, bf16[320,1536]{1,0:T(8,128)(2,1)}, u32[]{:S(2)}, u32[]{:S(2)}) collective-permute-start(bf16[320,1536]{1,0:T(8,128)(2,1)} %bitcast.19), channel_id=1, source_target_pairs={{0,4},{4,0},{8,12},{12,8},{16,20},{20,16},{24,28},{28,24},{1,5},{5... | collective-permute-start | bytes 2949128 | tf_op jit(solution)/shard_map/ppermute | solution.py:605
  267.4 23.2 %collective-permute-start.20 = (f32[4,512]{1,0:T(4,128)S(1)}, f32[4,512]{1,0:T(4,128)S(1)}, u32[]{:S(2)}, u32[]{:S(2)}) collective-permute-start(f32[4,512]{1,0:T(4,128)S(1)} %collective-permute-done.16), channel_id=1, source_target_pairs={{0,8},{4,12},{8,16},{12,20},{16,24},{20,28},{24,0},{28,4},{1,9},{5... | collective-permute-start | bytes 24584 | tf_op jit(solution)/shard_map/ppermute | solution.py:598
  377.4 293.5 %reduce-scatter.4.cloned.1.call-start = ((), (), s32[]{:S(2)}) async-start(), calls=%async_computation.5 | async-start | bytes 23592960 | tf_op jit(solution)/shard_map/reduce_scatter | solution.py:832
  379.3 23.4 %collective-permute-start.26 = (f32[4,4,80]{2,1,0:T(4,128)S(1)}, f32[4,4,80]{2,1,0:T(4,128)S(1)}, u32[]{:S(2)}, u32[]{:S(2)}) collective-permute-start(f32[4,4,80]{2,1,0:T(4,128)S(1)} %get-tuple-element.460), channel_id=1, source_target_pairs={{0,4},{4,0},{8,12},{12,8},{16,20},{20,16},{24,28},{28,24},{1,5},{5... | collective-permute-start | bytes 15368 | tf_op jit(solution)/shard_map/ppermute | solution.py:605
  380.7 32.8 %collective-permute-start.28 = (bf16[512,1536]{1,0:T(8,128)(2,1)}, bf16[512,1536]{1,0:T(8,128)(2,1)S(1)}, u32[]{:S(2)}, u32[]{:S(2)}) collective-permute-start(bf16[512,1536]{1,0:T(8,128)(2,1)} %copy-done.9), channel_id=1, source_target_pairs={{0,8},{4,12},{8,16},{12,20},{16,24},{20,28},{24,0},{28,4},{1,9},{5... | collective-permute-start | bytes 4718600 | tf_op jit(solution)/shard_map/ppermute | solution.py:598
  381.2 31.4 %collective-permute-start.25 = (bf16[320,1536]{1,0:T(8,128)(2,1)}, bf16[320,1536]{1,0:T(8,128)(2,1)S(1)}, u32[]{:S(2)}, u32[]{:S(2)}) collective-permute-start(bf16[320,1536]{1,0:T(8,128)(2,1)} %get-tuple-element.208), channel_id=1, source_target_pairs={{0,4},{4,0},{8,12},{12,8},{16,20},{20,16},{24,28},{28,24},{1,5},{5... | collective-permute-start | bytes 2949128 | tf_op jit(solution)/shard_map/ppermute | solution.py:605
  419.2 293.8 %reduce-scatter.8.cloned.1.call-start = ((), (), s32[]{:S(2)}) async-start(), calls=%async_computation.7 | async-start | bytes 7864320 | tf_op jit(solution)/shard_map/reduce_scatter | solution.py:922
  419.2 35.9 %collective-permute-start.36 = (bf16[512,1536]{1,0:T(8,128)(2,1)S(1)}, bf16[512,1536]{1,0:T(8,128)(2,1)S(1)}, u32[]{:S(2)}, u32[]{:S(2)}) collective-permute-start(bf16[512,1536]{1,0:T(8,128)(2,1)S(1)} %ring_rows.9), channel_id=1, source_target_pairs={{0,8},{4,12},{8,16},{12,20},{16,24},{20,28},{24,0},{28,4},{1,9},{5... | collective-permute-start | bytes 4718600 | tf_op jit(solution)/shard_map/ppermute | solution.py:598
  420.4 21.6 %collective-permute-start.29 = (bf16[320,1536]{1,0:T(8,128)(2,1)S(1)}, bf16[320,1536]{1,0:T(8,128)(2,1)S(1)}, u32[]{:S(2)}, u32[]{:S(2)}) collective-permute-start(bf16[320,1536]{1,0:T(8,128)(2,1)S(1)} %copy-done.85), channel_id=1, source_target_pairs={{0,4},{4,0},{8,12},{12,8},{16,20},{20,16},{24,28},{28,24},{1,5},{5... | collective-permute-start | bytes 2949128 | tf_op jit(solution)/shard_map/ppermute | solution.py:605
  421.2 34.0 %collective-permute-start.34 = (f32[4,512]{1,0:T(4,128)S(1)}, f32[4,512]{1,0:T(4,128)S(1)}, u32[]{:S(2)}, u32[]{:S(2)}) collective-permute-start(f32[4,512]{1,0:T(4,128)S(1)} %fusion.61), channel_id=1, source_target_pairs={{0,8},{4,12},{8,16},{12,20},{16,24},{20,28},{24,0},{28,4},{1,9},{5... | collective-permute-start | bytes 24584 | tf_op jit(solution)/shard_map/ppermute | solution.py:598
  442.0 22.0 %collective-permute-start.30 = (bf16[320,1536]{1,0:T(8,128)(2,1)}, bf16[320,1536]{1,0:T(8,128)(2,1)S(1)}, u32[]{:S(2)}, u32[]{:S(2)}) collective-permute-start(bf16[320,1536]{1,0:T(8,128)(2,1)} %get-tuple-element.229), channel_id=1, source_target_pairs={{0,4},{4,0},{8,12},{12,8},{16,20},{20,16},{24,28},{28,24},{1,5},{5... | collective-permute-start | bytes 2949128 | tf_op jit(solution)/shard_map/ppermute | solution.py:605
  458.6 26.4 %collective-permute-start.37 = (bf16[512,1536]{1,0:T(8,128)(2,1)S(1)}, bf16[512,1536]{1,0:T(8,128)(2,1)S(1)}, u32[]{:S(2)}, u32[]{:S(2)}) collective-permute-start(bf16[512,1536]{1,0:T(8,128)(2,1)S(1)} %ring_rows.10), channel_id=1, source_target_pairs={{0,8},{4,12},{8,16},{12,20},{16,24},{20,28},{24,0},{28,4},{1,9},{5... | collective-permute-start | bytes 4718600 | tf_op jit(solution)/shard_map/ppermute | solution.py:598
  464.0 24.3 %collective-permute-start.31 = (bf16[320,1536]{1,0:T(8,128)(2,1)S(1)}, bf16[320,1536]{1,0:T(8,128)(2,1)S(1)}, u32[]{:S(2)}, u32[]{:S(2)}) collective-permute-start(bf16[320,1536]{1,0:T(8,128)(2,1)S(1)} %copy-done.88), channel_id=1, source_target_pairs={{0,4},{4,0},{8,12},{12,8},{16,20},{20,16},{24,28},{28,24},{1,5},{5... | collective-permute-start | bytes 2949128 | tf_op jit(solution)/shard_map/ppermute | solution.py:605
  523.6 23.3 %collective-permute-start.40 = (bf16[320,1536]{1,0:T(8,128)(2,1)S(1)}, bf16[320,1536]{1,0:T(8,128)(2,1)S(1)}, u32[]{:S(2)}, u32[]{:S(2)}) collective-permute-start(bf16[320,1536]{1,0:T(8,128)(2,1)S(1)} %copy-done.84), channel_id=1, source_target_pairs={{0,4},{4,0},{8,12},{12,8},{16,20},{20,16},{24,28},{28,24},{1,5},{5... | collective-permute-start | bytes 2949128 | tf_op jit(solution)/shard_map/ppermute | solution.py:605
  524.8 36.2 %collective-permute-start.41 = (bf16[512,1536]{1,0:T(8,128)(2,1)S(1)}, bf16[512,1536]{1,0:T(8,128)(2,1)S(1)}, u32[]{:S(2)}, u32[]{:S(2)}) collective-permute-start(bf16[512,1536]{1,0:T(8,128)(2,1)S(1)} %copy-done.8), channel_id=1, source_target_pairs={{0,8},{4,12},{8,16},{12,20},{16,24},{20,28},{24,0},{28,4},{1,9},{5... | collective-permute-start | bytes 4718600 | tf_op jit(solution)/shard_map/ppermute | solution.py:598
  532.5 63.1 %collective-permute-start.39 = (bf16[512,512]{1,0:T(8,128)(2,1)S(1)}, bf16[512,512]{1,0:T(8,128)(2,1)S(1)}, u32[]{:S(2)}, u32[]{:S(2)}) collective-permute-start(bf16[512,512]{1,0:T(8,128)(2,1)S(1)} %fusion.36), channel_id=1, source_target_pairs={{2,0},{3,1},{6,4},{7,5},{10,8},{11,9},{14,12},{15,13},{18,16},{19,... | collective-permute-start | bytes 1572872 | tf_op jit(solution)/shard_map/ppermute | solution.py:902
  604.4 23.8 %collective-permute-start.32 = (bf16[320,1536]{1,0:T(8,128)(2,1)}, bf16[320,1536]{1,0:T(8,128)(2,1)S(1)}, u32[]{:S(2)}, u32[]{:S(2)}) collective-permute-start(bf16[320,1536]{1,0:T(8,128)(2,1)} %get-tuple-element.231), channel_id=1, source_target_pairs={{0,4},{4,0},{8,12},{12,8},{16,20},{20,16},{24,28},{28,24},{1,5},{5... | collective-permute-start | bytes 2949128 | tf_op jit(solution)/shard_map/ppermute | solution.py:605
  605.4 36.4 %collective-permute-start.42 = (bf16[2,384,1536]{2,1,0:T(8,128)(2,1)}, bf16[2,384,1536]{2,1,0:T(8,128)(2,1)}, u32[]{:S(2)}, u32[]{:S(2)}) collective-permute-start(bf16[2,384,1536]{2,1,0:T(8,128)(2,1)} %get-tuple-element.261), channel_id=1, source_target_pairs={{0,1},{1,0},{2,3},{3,2},{4,5},{5,4},{6,7},{7,6},{8,9},{9,8},{10,11... | collective-permute-start | bytes 7077896 | tf_op jit(solution)/shard_map/ppermute | solution.py:620
  628.1 67.2 %collective-permute-start.33 = (bf16[320,1536]{1,0:T(8,128)(2,1)}, bf16[320,1536]{1,0:T(8,128)(2,1)}, u32[]{:S(2)}, u32[]{:S(2)}) collective-permute-start(bf16[320,1536]{1,0:T(8,128)(2,1)} %get-tuple-element.232), channel_id=1, source_target_pairs={{0,4},{4,0},{8,12},{12,8},{16,20},{20,16},{24,28},{28,24},{1,5},{5... | collective-permute-start | bytes 2949128 | tf_op jit(solution)/shard_map/ppermute | solution.py:605
  629.4 36.8 %collective-permute-start.44 = (bf16[512,1536]{1,0:T(8,128)(2,1)S(1)}, bf16[512,1536]{1,0:T(8,128)(2,1)S(1)}, u32[]{:S(2)}, u32[]{:S(2)}) collective-permute-start(bf16[512,1536]{1,0:T(8,128)(2,1)S(1)} %ring_rows.13), channel_id=1, source_target_pairs={{0,8},{4,12},{8,16},{12,20},{16,24},{20,28},{24,0},{28,4},{1,9},{5... | collective-permute-start | bytes 4718600 | tf_op jit(solution)/shard_map/ppermute | solution.py:598
  646.4 63.7 %collective-permute-start.46 = (bf16[384,1664]{1,0:T(8,128)(2,1)}, bf16[384,1664]{1,0:T(8,128)(2,1)}, u32[]{:S(2)}, u32[]{:S(2)}) collective-permute-start(bf16[384,1664]{1,0:T(8,128)(2,1)} %fusion.28), channel_id=1, source_target_pairs={{0,2},{1,3},{2,0},{3,1},{4,6},{5,7},{6,4},{7,5},{8,10},{9,11},{10,... | collective-permute-start | bytes 3833864 | tf_op jit(solution)/shard_map/ppermute | solution.py:623
  669.4 36.2 %collective-permute-start.45 = (bf16[512,1536]{1,0:T(8,128)(2,1)S(1)}, bf16[512,1536]{1,0:T(8,128)(2,1)S(1)}, u32[]{:S(2)}, u32[]{:S(2)}) collective-permute-start(bf16[512,1536]{1,0:T(8,128)(2,1)S(1)} %ring_rows.14), channel_id=1, source_target_pairs={{0,8},{4,12},{8,16},{12,20},{16,24},{20,28},{24,0},{28,4},{1,9},{5... | collective-permute-start | bytes 4718600 | tf_op jit(solution)/shard_map/ppermute | solution.py:598
  716.2 30.7 %collective-permute-start.47 = (bf16[192,3712]{1,0:T(8,128)(2,1)}, bf16[192,3712]{1,0:T(8,128)(2,1)}, u32[]{:S(2)}, u32[]{:S(2)}) collective-permute-start(bf16[192,3712]{1,0:T(8,128)(2,1)} %dynamic-slice_bitcast_fusion), channel_id=1, source_target_pairs={{0,4},{4,0},{8,12},{12,8},{16,20},{20,16},{24,28},{28,24},{1,5},{5... | collective-permute-start | bytes 4276232 | tf_op jit(solution)/shard_map/ppermute | solution.py:605
  749.8 23.8 %collective-permute-start.48 = (bf16[48,3712]{1,0:T(8,128)(2,1)S(1)}, bf16[48,3712]{1,0:T(8,128)(2,1)S(1)}, u32[]{:S(2)}, u32[]{:S(2)}) collective-permute-start(bf16[48,3712]{1,0:T(8,128)(2,1)S(1)} %get-tuple-element.446), channel_id=1, source_target_pairs={{0,8},{4,12},{8,16},{12,20},{16,24},{20,28},{24,0},{28,4},{1,9},{5... | collective-permute-start | bytes 1069064 | tf_op jit(solution)/shard_map/ppermute | solution.py:598
  749.9 27.8 %collective-permute-start.49 = (bf16[48,3712]{1,0:T(8,128)(2,1)S(1)}, bf16[48,3712]{1,0:T(8,128)(2,1)S(1)}, u32[]{:S(2)}, u32[]{:S(2)}) collective-permute-start(bf16[48,3712]{1,0:T(8,128)(2,1)S(1)} %get-tuple-element.448), channel_id=1, source_target_pairs={{0,16},{4,20},{8,24},{12,28},{16,0},{20,4},{24,8},{28,12},{1,17},{... | collective-permute-start | bytes 1069064 | tf_op jit(solution)/shard_map/ppermute | solution.py:598
  755.4 26.3 %collective-permute-start.50 = (bf16[48,3712]{1,0:T(8,128)(2,1)S(1)}, bf16[48,3712]{1,0:T(8,128)(2,1)S(1)}, u32[]{:S(2)}, u32[]{:S(2)}) collective-permute-start(bf16[48,3712]{1,0:T(8,128)(2,1)S(1)} %get-tuple-element.447), channel_id=1, source_target_pairs={{0,24},{4,28},{8,0},{12,4},{16,8},{20,12},{24,16},{28,20},{1,25},{... | collective-permute-start | bytes 1069064 | tf_op jit(solution)/shard_map/ppermute | solution.py:598
  786.1 30.4 %collective-permute-start.52 = (bf16[48,3712]{1,0:T(8,128)(2,1)}, bf16[48,3712]{1,0:T(8,128)(2,1)S(1)}, u32[]{:S(2)}, u32[]{:S(2)}) collective-permute-start(bf16[48,3712]{1,0:T(8,128)(2,1)} %get-tuple-element.423), channel_id=1, source_target_pairs={{0,16},{4,20},{8,24},{12,28},{16,0},{20,4},{24,8},{28,12},{1,17},{... | collective-permute-start | bytes 1069064 | tf_op jit(solution)/shard_map/ppermute | solution.py:598
  786.2 31.0 %collective-permute-start.53 = (bf16[48,3712]{1,0:T(8,128)(2,1)}, bf16[48,3712]{1,0:T(8,128)(2,1)S(1)}, u32[]{:S(2)}, u32[]{:S(2)}) collective-permute-start(bf16[48,3712]{1,0:T(8,128)(2,1)} %get-tuple-element.423), channel_id=1, source_target_pairs={{0,24},{4,28},{8,0},{12,4},{16,8},{20,12},{24,16},{28,20},{1,25},{... | collective-permute-start | bytes 1069064 | tf_op jit(solution)/shard_map/ppermute | solution.py:598
  818.0 31.8 %collective-permute-start.54 = (bf16[192,3712]{1,0:T(8,128)(2,1)}, bf16[192,3712]{1,0:T(8,128)(2,1)S(1)}, u32[]{:S(2)}, u32[]{:S(2)}) collective-permute-start(bf16[192,3712]{1,0:T(8,128)(2,1)} %bitcast.67), channel_id=1, source_target_pairs={{0,4},{4,0},{8,12},{12,8},{16,20},{20,16},{24,28},{28,24},{1,5},{5... | collective-permute-start | bytes 4276232 | tf_op jit(solution)/shard_map/ppermute | solution.py:605
  (107 other events, 1466.8 us)
Sparse Core Ops, SparseCore 0:
  16.5 49.7 all-gather.6
  68.4 45.2 all-gather.8
  115.8 67.7 all-gather.10
  185.6 120.0 all-gather.12
  377.6 88.1 reduce-scatter.5
  468.2 150.7 reduce-scatter.3
  621.7 82.0 reduce-scatter.7

commit v7 on v4

--- a/solution.py
+++ b/solution.py
@@ -962,10 +962,10 @@
     back_parts = x_parts(chip_total(back_mine, back_mate, back_sent).astype(bf16))
     back_parts = z_parts(add_parts(back_parts))
     back_low = add_parts(back_parts)
-    front_low = after(front_part, back_low)
+    front_low = after(front_part, moe_out)
     front_parts = x_parts(front_low)
     back_low = z_join(after(back_low, front_low))
-    front_low = add_parts(after(front_parts, back_low))
+    front_low = add_parts(front_parts)
     front_low = add_parts(z_parts(front_low))
     back_sum = x_join(after(back_low, front_low))
     front_sum = x_join(z_join(front_low))

time: 854 us -> 864 us (1.012)
  waiting for transfers between devices: 384 us -> 400 us
    ppermute x33, waiting for transfers between devices: 166 us -> 184 us  [z_shift(): lax.ppermute(value, 'expert', [(a * wide + b, (a + by) % depth * wide + b...]
    ppermute x1, waiting for transfers between devices: 12.7 us -> 0.01 us  [y_shift(): lax.ppermute(value, 'fsdp', [(a, (a + 2 * by) % shards) for a in range(sh...]
    ppermute x22, waiting for transfers between devices: 145 us -> 156 us  [x_shift(): lax.ppermute(value, 'expert', [(a * wide + b, a * wide + (b + by) % wide)...]
    unnamed x206 -> x184, local copies, waits for them, and re-layouts: 29.6 us -> 26.2 us
  transfers between devices with their start and end apart: 70 -> 70, of which waited for: 45 -> 40; matrix products, arithmetic and copies ran while one was open for 15% -> 15% of each run, Pallas kernels for 18% -> 18%
where the time goes in v7:
time: 864 us; the launch traced here: 852 us
  waiting for transfers between devices  400 us (46%)
  Pallas kernels  194 us (22%)
  other arithmetic  95.8 us (11%)
  starting transfers between devices  72.1 us (8%)
  local copies, waits for them, and re-layouts  41.2 us (5%)
  matrix products  33.2 us (4%)
  between operations  16.2 us (2%)
    ppermute x33, waiting for transfers between devices, z_shift(): lax.ppermute(value, 'expert', [(a * wide + b, (a + by) % depth * wide + b...  184 us
    ppermute x22, waiting for transfers between devices, x_shift(): lax.ppermute(value, 'expert', [(a * wide + b, a * wide + (b + by) % wide)...  156 us
    sub x6, other arithmetic, adamw_update(): weight - step_rate * (first_hat / (jnp.sqrt(second_hat) + ADAM_EPS) + dec...  49.2 us
    pallas_call x1, Pallas kernels, core_rows(): pl.pallas_call(functools.partial(core_kernel, count), out_shape=(low, low...  36.4 us
    ppermute x33, starting transfers between devices, z_shift(): lax.ppermute(value, 'expert', [(a * wide + b, (a + by) % depth * wide + b...  34 us
    ppermute x1, waiting for transfers between devices, body(): lax.ppermute(kv_low[s], 'fsdp', [(a + 2 * s, a) for a in range(shards - 2...  31.2 us
    unnamed x184, local copies, waits for them, and re-layouts  26.2 us
    pallas_call x8, Pallas kernels, ring_rows(): pl.pallas_call(functools.partial(ring_kernel, len(pieces)), out_shape=jax...  26.2 us
  transfers between devices with their start and end apart: 70, of which 40 were waited for; matrix products, arithmetic and copies ran while one was open for 15% of the time, Pallas kernels for 18%

profile of v7, /device:TPU:8, one launch (start us, length us, event | category | flops | bytes accessed | tf_op | source)
XLA Modules:
  0.0 852.1 jit_solution(16575166894275204898)
XLA Ops:
  24.8 4.5 pick_rows.8
  35.6 17.1 %collective-permute-done.4.refs_4_ = bf16[320,1536]{1,0:T(8,128)(2,1)} collective-permute-done((bf16[320,1536]{1,0:T(8,128)(2,1)}, bf16[320,1536]{1,0:T(8,128)(2,1)}, u32[]{:S(2)}, u32[]{:S(2)}) %collective-permute-start.4) | collective-permute-done | bytes 983072 | tf_op jit(solution)/shard_map/ppermute | solution.py:605
  52.7 5.3 collective-permute-done.3.rows
  68.8 6.1 fusion.2.pre
  79.9 6.5 convert_element_type.219
  91.3 22.4 %collective-permute-done.6 = bf16[512,512]{1,0:T(8,128)(2,1)} collective-permute-done((bf16[512,512]{1,0:T(8,128)(2,1)}, bf16[512,512]{1,0:T(8,128)(2,1)}, u32[]{:S(2)}, u32[]{:S(2)}) %collective-permute-start.6) | collective-permute-done | bytes 524320 | tf_op jit(solution)/shard_map/ppermute | solution.py:626
  126.6 14.3 %attend.1 = (bf16[512,1536]{1,0:T(8,128)(2,1)}, f32[12,1,512]{2,1,0:T(1,128)}, bf16[512,1536]{1,0:T(8,128)(2,1)}) custom-call(s32[1]{0:T(128)} %bitcast.place, f32[512,2048]{1,0:T(8,128)} %copy-done.45, f32[512,128]{1,0:T(8,128)} %get-tuple-element.468.cosine, f32[512,128]{1,0:T(8,128)} %copy-done.46, bf16[4,512,512]{2,1,0:T(8,128)(2,1)} %pad_maximum_fusion.keys.values, ...), custom_call_target="tpu_custom_call" | custom-call | flops 1000000000 | bytes 1000000 | tf_op jit(solution)/shard_map/attend/pallas_call | solution.py:106
  140.9 19.4 %collective-permute-done.9.rows = bf16[512,1536]{1,0:T(8,128)(2,1)S(1)} collective-permute-done((bf16[512,1536]{1,0:T(8,128)(2,1)}, bf16[512,1536]{1,0:T(8,128)(2,1)S(1)}, u32[]{:S(2)}, u32[]{:S(2)}) %collective-permute-start.9) | collective-permute-done | bytes 1572896 | tf_op jit(solution)/shard_map/ppermute | solution.py:598
  161.4 6.1 multiply_reduce_fusion.2
  175.7 19.4 %collective-permute-done.11.refs_6_ = bf16[320,1536]{1,0:T(8,128)(2,1)S(1)} collective-permute-done((bf16[320,1536]{1,0:T(8,128)(2,1)S(1)}, bf16[320,1536]{1,0:T(8,128)(2,1)S(1)}, u32[]{:S(2)}, u32[]{:S(2)}) %collective-permute-start.11) | collective-permute-done | bytes 983072 | tf_op jit(solution)/shard_map/ppermute | solution.py:605
  196.5 8.2 collective-permute-done.13.rows
  208.8 8.1 collective-permute-done.12.refs_4_
  220.5 20.5 %collective-permute-done.16 = f32[4,512]{1,0:T(4,128)S(1)} collective-permute-done((f32[4,512]{1,0:T(4,128)S(1)}, f32[4,512]{1,0:T(4,128)S(1)}, u32[]{:S(2)}, u32[]{:S(2)}) %collective-permute-start.16) | collective-permute-done | bytes 8224 | tf_op jit(solution)/shard_map/ppermute | solution.py:598
  250.7 15.4 %collective-permute-done.17.refs_7_ = bf16[320,1536]{1,0:T(8,128)(2,1)S(1)} collective-permute-done((bf16[320,1536]{1,0:T(8,128)(2,1)S(1)}, bf16[320,1536]{1,0:T(8,128)(2,1)S(1)}, u32[]{:S(2)}, u32[]{:S(2)}) %collective-permute-start.17) | collective-permute-done | bytes 983072 | tf_op jit(solution)/shard_map/ppermute | solution.py:605
  269.5 6.9 collective-permute-done.19.rows
  277.6 13.0 %inner_rows.1.refs_9_ = bf16[4,640,768]{2,1,0:T(8,128)(2,1)} custom-call(bf16[320,1536]{1,0:T(8,128)(2,1)} %copy-done.24, bf16[320,1536]{1,0:T(8,128)(2,1)} %copy-done.25, bf16[320,1536]{1,0:T(8,128)(2,1)} %copy-done.28, bf16[320,1536]{1,0:T(8,128)(2,1)} %copy-done.31, bf16[320,1536]{1,0:T(8,128)(2,1)} %collective-permute-done.4.refs_4_, ...), custom_call_target="tpu_custom_call" | custom-call | flops 6039797760 | bytes 20000000 | tf_op jit(solution)/shard_map/inner_rows/pallas_call | solution.py:248
  294.9 5.1 collective-permute-done.22
  301.5 11.9 %collective-permute-done.23 = f32[4,4,80]{2,0,1:T(4,128)S(1)} collective-permute-done((f32[4,4,80]{2,0,1:T(4,128)S(1)}, f32[4,4,80]{2,0,1:T(4,128)S(1)}, u32[]{:S(2)}, u32[]{:S(2)}) %collective-permute-start.23) | collective-permute-done | bytes 5152 | tf_op jit(solution)/shard_map/ppermute | solution.py:605
  316.1 36.4 %core_rows.1 = (bf16[4,640,768]{2,1,0:T(8,128)(2,1)}, bf16[4,640,768]{2,1,0:T(8,128)(2,1)}, bf16[4,640,768]{2,1,0:T(8,128)(2,1)}, f32[4,640,1]{2,1,0:T(8,128)}, ...) custom-call(bf16[320,1536]{1,0:T(8,128)(2,1)} %copy-done.26, ...), custom_call_target="tpu_custom_call" | custom-call | flops 24159191040 | bytes 60000000 | tf_op jit(solution)/shard_map/core_rows/pallas_call | solution.py:305
  353.9 13.8 %down_grads.1 = bf16[4,4,768,384]{3,2,1,0:T(8,128)(2,1)} custom-call(bf16[320,1536]{1,0:T(8,128)(2,1)} %copy-done.24, bf16[320,1536]{1,0:T(8,128)(2,1)} %copy-done.25, bf16[320,1536]{1,0:T(8,128)(2,1)} %copy-done.28, bf16[320,1536]{1,0:T(8,128)(2,1)} %copy-done.31, bf16[320,1536]{1,0:T(8,128)(2,1)} %collective-permute-done.4.refs_4_, ...), custom_call_target="tpu_custom_call" | custom-call | flops 6039797760 | bytes 22000000 | tf_op jit(solution)/shard_map/down_grads/pallas_call | solution.py:364
  381.9 20.8 %in_grads.1 = bf16[4,4,384,1536]{3,2,1,0:T(8,128)(2,1)} custom-call(bf16[320,1536]{1,0:T(8,128)(2,1)} %copy-done.26, bf16[320,1536]{1,0:T(8,128)(2,1)} %copy-done.27, bf16[320,1536]{1,0:T(8,128)(2,1)} %copy-done.29, bf16[320,1536]{1,0:T(8,128)(2,1)} %copy-done.30, bf16[320,1536]{1,0:T(8,128)(2,1)} %copy-done.78, ...), custom_call_target="tpu_custom_call" | custom-call | flops 12079595520 | bytes 35000000 | tf_op jit(solution)/shard_map/in_grads/pallas_call | solution.py:392
  406.7 6.0 collective-permute-done.27
  422.5 19.5 %collective-permute-done.29.refs_2_ = bf16[320,1536]{1,0:T(8,128)(2,1)S(1)} collective-permute-done((bf16[320,1536]{1,0:T(8,128)(2,1)S(1)}, bf16[320,1536]{1,0:T(8,128)(2,1)S(1)}, u32[]{:S(2)}, u32[]{:S(2)}) %collective-permute-start.29) | collective-permute-done | bytes 983072 | tf_op jit(solution)/shard_map/ppermute | solution.py:605
  442.8 12.4 %result_rows.1 = (bf16[320,1536]{1,0:T(8,128)(2,1)}, bf16[320,1536]{1,0:T(8,128)(2,1)}, bf16[320,1536]{1,0:T(8,128)(2,1)}, bf16[320,1536]{1,0:T(8,128)(2,1)}, bf...) custom-call(bf16[4,640,768]{2,1,0:T(8,128)(2,1)} %get-tuple-element., ...), custom_call_target="tpu_custom_call" | custom-call | flops 6039797760 | bytes 22000000 | tf_op jit(solution)/shard_map/result_rows/pallas_call | solution.py:336
  465.5 19.0 %collective-permute-done.35 = f32[4,512]{1,0:T(4,128)S(1)} collective-permute-done((f32[4,512]{1,0:T(4,128)S(1)}, f32[4,512]{1,0:T(4,128)S(1)}, u32[]{:S(2)}, u32[]{:S(2)}) %collective-permute-start.35) | collective-permute-done | bytes 8224 | tf_op jit(solution)/shard_map/ppermute | solution.py:598
  490.9 4.7 multiply_reduce_fusion
  503.0 17.9 %attend_back.1 = (bf16[512,1536]{1,0:T(8,128)(2,1)}, bf16[4,512,256]{2,1,0:T(8,128)(2,1)}, bf16[4,512,256]{2,1,0:T(8,128)(2,1)}) custom-call(s32[1]{0:T(128)} %bitcast.place, bf16[512,1536]{1,0:T(8,128)(2,1)} %get-tuple-element.248.query, bf16[4,512,512]{2,1,0:T(8,128)(2,1)} %pad_maximum_fusion.keys.values, ...), custom_call_target="tpu_custom_call" | custom-call | flops 1000000000 | bytes 1000000 | tf_op jit(solution)/shard_map/attend_back/pallas_call | solution.py:182
  525.8 6.7 core_grads.1
  534.2 12.0 %multiply_subtract_fusion.1 = (f32[4,768,384]{2,1,0:T(8,128)}, f32[4,768,384]{2,1,0:T(8,128)}, f32[4,768,384]{2,1,0:T(8,128)}) fusion(f32[4,768,384]{2,1,0:T(8,128)} %param.51, bf16[4,768,384]{2,1,0:T(8,128)(2,1)} %bitcast.215, f32[4,768,384]{2,1,0:T(8,128)} %param.52, f32[4,768,384]{2,1,0:T(8,128)} %param.53), kind=kLoop, calls=%fused_computation.25 | loop fusion | flops 18874368 | bytes 30670848 | tf_op jit(solution)/shard_map/sub | solution.py:549
  546.9 14.1 %collective-permute-done.41.refs_3_ = bf16[512,1536]{1,0:T(8,128)(2,1)S(1)} collective-permute-done((bf16[512,1536]{1,0:T(8,128)(2,1)S(1)}, bf16[512,1536]{1,0:T(8,128)(2,1)S(1)}, u32[]{:S(2)}, u32[]{:S(2)}) %collective-permute-start.41) | collective-permute-done | bytes 1572896 | tf_op jit(solution)/shard_map/ppermute | solution.py:598
  564.3 31.2 %collective-permute-done.39 = bf16[512,512]{1,0:T(8,128)(2,1)S(1)} collective-permute-done((bf16[512,512]{1,0:T(8,128)(2,1)S(1)}, bf16[512,512]{1,0:T(8,128)(2,1)S(1)}, u32[]{:S(2)}, u32[]{:S(2)}) %collective-permute-start.39) | collective-permute-done | bytes 524320 | tf_op jit(solution)/shard_map/ppermute | solution.py:902
  597.0 7.3 weight_grads.1
  605.7 22.4 %collective-permute-done.32.refs_2_ = bf16[320,1536]{1,0:T(8,128)(2,1)S(1)} collective-permute-done((bf16[320,1536]{1,0:T(8,128)(2,1)}, bf16[320,1536]{1,0:T(8,128)(2,1)S(1)}, u32[]{:S(2)}, u32[]{:S(2)}) %collective-permute-start.32) | collective-permute-done | bytes 983072 | tf_op jit(solution)/shard_map/ppermute | solution.py:605
  630.5 6.1 fusion.11
  636.6 4.4 fusion.15
  641.8 24.4 %collective-permute-done.44.refs_3_ = bf16[512,1536]{1,0:T(8,128)(2,1)S(1)} collective-permute-done((bf16[512,1536]{1,0:T(8,128)(2,1)S(1)}, bf16[512,1536]{1,0:T(8,128)(2,1)S(1)}, u32[]{:S(2)}, u32[]{:S(2)}) %collective-permute-start.44) | collective-permute-done | bytes 1572896 | tf_op jit(solution)/shard_map/ppermute | solution.py:598
  674.9 7.8 collective-permute-start.46
  682.7 24.4 %multiply_subtract_fusion = (f32[4,384,1536]{2,1,0:T(8,128)}, f32[4,384,1536]{2,1,0:T(8,128)}, f32[4,384,1536]{2,1,0:T(8,128)}) fusion(f32[4,384,1536]{2,1,0:T(8,128)} %param.48, bf16[4,384,1536]{2,1,0:T(8,128)(2,1)} %bitcast.206, f32[4,384,1536]{2,1,0:T(8,128)} %param.49, f32[4,384,1536]{2,1,0:T(8,128)} %param.50), kind=kLoop, calls=%fused_computation.4 | loop fusion | flops 37748736 | bytes 61341696 | tf_op jit(solution)/shard_map/sub | solution.py:549
  707.1 4.5 ring_rows.15
  718.2 5.5 fusion.19
  723.7 20.4 %collective-permute-done.47 = bf16[192,1664]{1,0:T(8,128)(2,1)S(1)} collective-permute-done((bf16[192,1664]{1,0:T(8,128)(2,1)S(1)}, bf16[192,1664]{1,0:T(8,128)(2,1)S(1)}, u32[]{:S(2)}, u32[]{:S(2)}) %collective-permute-start.47) | collective-permute-done | bytes 639008 | tf_op jit(solution)/shard_map/ppermute | solution.py:605
  756.6 11.4 %collective-permute-done.49 = bf16[48,1664]{1,0:T(8,128)(2,1)S(1)} collective-permute-done((bf16[48,1664]{1,0:T(8,128)(2,1)S(1)}, bf16[48,1664]{1,0:T(8,128)(2,1)S(1)}, u32[]{:S(2)}, u32[]{:S(2)}) %collective-permute-start.49) | collective-permute-done | bytes 159776 | tf_op jit(solution)/shard_map/ppermute | solution.py:598
  768.0 7.5 collective-permute-done.50
  775.8 11.6 %collective-permute-done.51 = bf16[48,1664]{1,0:T(8,128)(2,1)S(1)} collective-permute-done((bf16[48,1664]{1,0:T(8,128)(2,1)S(1)}, bf16[48,1664]{1,0:T(8,128)(2,1)S(1)}, u32[]{:S(2)}, u32[]{:S(2)}) %collective-permute-start.51) | collective-permute-done | bytes 159776 | tf_op jit(solution)/shard_map/ppermute | solution.py:598
  789.1 10.0 %collective-permute-done.53 = bf16[48,1664]{1,0:T(8,128)(2,1)S(1)} collective-permute-done((bf16[48,1664]{1,0:T(8,128)(2,1)S(1)}, bf16[48,1664]{1,0:T(8,128)(2,1)S(1)}, u32[]{:S(2)}, u32[]{:S(2)}) %collective-permute-start.53) | collective-permute-done | bytes 159776 | tf_op jit(solution)/shard_map/ppermute | solution.py:598
  811.3 6.4 collective-permute-done.58
  822.9 6.2 collective-permute-done.62
  834.0 8.9 %multiply_subtract_fusion.2 = (f32[384,1536]{1,0:T(8,128)}, f32[384,1536]{1,0:T(8,128)}, f32[384,1536]{1,0:T(8,128)}, f32[384,1536]{1,0:T(8,128)}, f32[384,1536]{1,0:T(8,128)}, /*index=5*/f32[384,1536]{1,0:T(8,128)}) fusion(f32[384,1536]{1,0:T(8,128)S(1)} %copy-done.43, f32[384,1664]{1,0:T(8,128)S(1)} %bitcast_convert_fusion.1, f32[384,1536]{1,0:T(8,128)} %param.43, ...), kind=kLoop, calls=%fused_computation.52 | loop fusion | flops 17694720 | bytes 33030144 | tf_op jit(solution)/shard_map/sub | solution.py:549
  (437 shorter events, 222.1 us)
Async XLA Ops:
  7.2 59.0 %all-gather.7.cloned.1.call-start = ((), (), s32[]{:S(2)}) async-start(), calls=%async_computation.3 | async-start | bytes 8355840 | tf_op jit(solution)/shard_map/all_gather | solution.py:636
  16.4 145.1 %all-gather.9.cloned.1.call-start = ((), (), s32[]{:S(2)}) async-start(), calls=%async_computation.4 | async-start | bytes 5898240 | tf_op jit(solution)/shard_map/all_gather | solution.py:644
  17.6 260.0 %all-gather.11.cloned.1.call-start = ((), (), s32[]{:S(2)}) async-start(), calls=%async_computation.8 | async-start | bytes 11796480 | tf_op jit(solution)/shard_map/all_gather | solution.py:762
  22.3 35.7 %collective-permute-start.3 = (bf16[512,1536]{1,0:T(8,128)(2,1)}, bf16[512,1536]{1,0:T(8,128)(2,1)}, u32[]{:S(2)}, u32[]{:S(2)}) collective-permute-start(bf16[512,1536]{1,0:T(8,128)(2,1)} %rows.1), channel_id=1, source_target_pairs={{0,8},{4,12},{8,16},{12,20},{16,24},{20,28},{24,0},{28,4},{1,9},{5... | collective-permute-start | bytes 4718600 | tf_op jit(solution)/shard_map/ppermute | solution.py:598
  30.3 22.4 %collective-permute-start.4 = (bf16[320,1536]{1,0:T(8,128)(2,1)}, bf16[320,1536]{1,0:T(8,128)(2,1)}, u32[]{:S(2)}, u32[]{:S(2)}) collective-permute-start(bf16[320,1536]{1,0:T(8,128)(2,1)} %bitcast.10), channel_id=1, source_target_pairs={{0,4},{4,0},{8,12},{12,8},{16,20},{20,16},{24,28},{28,24},{1,5},{5... | collective-permute-start | bytes 2949128 | tf_op jit(solution)/shard_map/ppermute | solution.py:605
  79.9 236.2 %all-gather.13.cloned.1.call-start = ((), (), s32[]{:S(2)}) async-start(), calls=%async_computation.9 | async-start | bytes 23592960 | tf_op jit(solution)/shard_map/all_gather | solution.py:763
  86.4 416.6 %reduce-scatter.6.cloned.1.call-start = ((), (), s32[]{:S(2)}) async-start(), calls=%async_computation.6 | async-start | bytes 11796480 | tf_op jit(solution)/shard_map/reduce_scatter | solution.py:823
  86.4 37.0 %collective-permute-start.8 = (bf16[512,1536]{1,0:T(8,128)(2,1)}, bf16[512,1536]{1,0:T(8,128)(2,1)}, u32[]{:S(2)}, u32[]{:S(2)}) collective-permute-start(bf16[512,1536]{1,0:T(8,128)(2,1)} %collective-permute-done.3.rows), channel_id=1, source_target_pairs={{0,8},{4,12},{8,16},{12,20},{16,24},{20,28},{24,0},{28,4},{1,9},{5... | collective-permute-start | bytes 4718600 | tf_op jit(solution)/shard_map/ppermute | solution.py:598
  88.0 25.7 %collective-permute-start.6 = (bf16[512,512]{1,0:T(8,128)(2,1)}, bf16[512,512]{1,0:T(8,128)(2,1)}, u32[]{:S(2)}, u32[]{:S(2)}) collective-permute-start(bf16[512,512]{1,0:T(8,128)(2,1)} %get-tuple-element.464), channel_id=1, source_target_pairs={{0,2},{1,3},{4,6},{5,7},{8,10},{9,11},{12,14},{13,15},{16,18},{17,... | collective-permute-start | bytes 1572872 | tf_op jit(solution)/shard_map/ppermute | solution.py:626
  91.3 22.4 %collective-permute-start.5 = (bf16[512,512]{1,0:T(8,128)(2,1)}, bf16[512,512]{1,0:T(8,128)(2,1)}, u32[]{:S(2)}, u32[]{:S(2)}) collective-permute-start(bf16[512,512]{1,0:T(8,128)(2,1)} %get-tuple-element.464), channel_id=1, source_target_pairs={{0,1},{1,0},{2,3},{3,2},{4,5},{5,4},{6,7},{7,6},{8,9},{9,8},{10,11... | collective-permute-start | bytes 1572872 | tf_op jit(solution)/shard_map/ppermute | solution.py:620
  123.5 36.8 %collective-permute-start.9 = (bf16[512,1536]{1,0:T(8,128)(2,1)}, bf16[512,1536]{1,0:T(8,128)(2,1)S(1)}, u32[]{:S(2)}, u32[]{:S(2)}) collective-permute-start(bf16[512,1536]{1,0:T(8,128)(2,1)} %collective-permute-done.8.rows), channel_id=1, source_target_pairs={{0,8},{4,12},{8,16},{12,20},{16,24},{20,28},{24,0},{28,4},{1,9},{5... | collective-permute-start | bytes 4718600 | tf_op jit(solution)/shard_map/ppermute | solution.py:598
  125.1 44.1 %collective-permute-start.10 = (bf16[320,1536]{1,0:T(8,128)(2,1)}, bf16[320,1536]{1,0:T(8,128)(2,1)}, u32[]{:S(2)}, u32[]{:S(2)}) collective-permute-start(bf16[320,1536]{1,0:T(8,128)(2,1)} %bitcast.17), channel_id=1, source_target_pairs={{0,4},{4,0},{8,12},{12,8},{16,20},{20,16},{24,28},{28,24},{1,5},{5... | collective-permute-start | bytes 2949128 | tf_op jit(solution)/shard_map/ppermute | solution.py:605
  167.9 36.9 %collective-permute-start.13 = (bf16[512,1536]{1,0:T(8,128)(2,1)S(1)}, bf16[512,1536]{1,0:T(8,128)(2,1)}, u32[]{:S(2)}, u32[]{:S(2)}) collective-permute-start(bf16[512,1536]{1,0:T(8,128)(2,1)S(1)} %multiply_convert_fusion.rows), channel_id=1, source_target_pairs={{0,8},{4,12},{8,16},{12,20},{16,24},{20,28},{24,0},{28,4},{1,9},{5... | collective-permute-start | bytes 4718600 | tf_op jit(solution)/shard_map/ppermute | solution.py:598
  172.5 22.7 %collective-permute-start.11 = (bf16[320,1536]{1,0:T(8,128)(2,1)S(1)}, bf16[320,1536]{1,0:T(8,128)(2,1)S(1)}, u32[]{:S(2)}, u32[]{:S(2)}) collective-permute-start(bf16[320,1536]{1,0:T(8,128)(2,1)S(1)} %bitcast.201), channel_id=1, source_target_pairs={{0,4},{4,0},{8,12},{12,8},{16,20},{20,16},{24,28},{28,24},{1,5},{5... | collective-permute-start | bytes 2949128 | tf_op jit(solution)/shard_map/ppermute | solution.py:605
  195.1 21.8 %collective-permute-start.12 = (bf16[320,1536]{1,0:T(8,128)(2,1)S(1)}, bf16[320,1536]{1,0:T(8,128)(2,1)S(1)}, u32[]{:S(2)}, u32[]{:S(2)}) collective-permute-start(bf16[320,1536]{1,0:T(8,128)(2,1)S(1)} %bitcast.199), channel_id=1, source_target_pairs={{0,4},{4,0},{8,12},{12,8},{16,20},{20,16},{24,28},{28,24},{1,5},{5... | collective-permute-start | bytes 2949128 | tf_op jit(solution)/shard_map/ppermute | solution.py:605
  204.8 36.3 %collective-permute-start.15 = (bf16[512,1536]{1,0:T(8,128)(2,1)}, bf16[512,1536]{1,0:T(8,128)(2,1)}, u32[]{:S(2)}, u32[]{:S(2)}) collective-permute-start(bf16[512,1536]{1,0:T(8,128)(2,1)} %collective-permute-done.13.rows), channel_id=1, source_target_pairs={{0,8},{4,12},{8,16},{12,20},{16,24},{20,28},{24,0},{28,4},{1,9},{5... | collective-permute-start | bytes 4718600 | tf_op jit(solution)/shard_map/ppermute | solution.py:598
  216.9 27.5 %collective-permute-start.14 = (bf16[320,1536]{1,0:T(8,128)(2,1)}, bf16[320,1536]{1,0:T(8,128)(2,1)}, u32[]{:S(2)}, u32[]{:S(2)}) collective-permute-start(bf16[320,1536]{1,0:T(8,128)(2,1)} %bitcast.18), channel_id=1, source_target_pairs={{0,4},{4,0},{8,12},{12,8},{16,20},{20,16},{24,28},{28,24},{1,5},{5... | collective-permute-start | bytes 2949128 | tf_op jit(solution)/shard_map/ppermute | solution.py:605
  241.1 35.3 %collective-permute-start.19 = (bf16[512,1536]{1,0:T(8,128)(2,1)}, bf16[512,1536]{1,0:T(8,128)(2,1)S(1)}, u32[]{:S(2)}, u32[]{:S(2)}) collective-permute-start(bf16[512,1536]{1,0:T(8,128)(2,1)} %collective-permute-done.15.rows), channel_id=1, source_target_pairs={{0,8},{4,12},{8,16},{12,20},{16,24},{20,28},{24,0},{28,4},{1,9},{5... | collective-permute-start | bytes 4718600 | tf_op jit(solution)/shard_map/ppermute | solution.py:598
  244.4 21.7 %collective-permute-start.17 = (bf16[320,1536]{1,0:T(8,128)(2,1)S(1)}, bf16[320,1536]{1,0:T(8,128)(2,1)S(1)}, u32[]{:S(2)}, u32[]{:S(2)}) collective-permute-start(bf16[320,1536]{1,0:T(8,128)(2,1)S(1)} %bitcast.200), channel_id=1, source_target_pairs={{0,4},{4,0},{8,12},{12,8},{16,20},{20,16},{24,28},{28,24},{1,5},{5... | collective-permute-start | bytes 2949128 | tf_op jit(solution)/shard_map/ppermute | solution.py:605
  266.1 27.3 %collective-permute-start.18 = (bf16[320,1536]{1,0:T(8,128)(2,1)}, bf16[320,1536]{1,0:T(8,128)(2,1)}, u32[]{:S(2)}, u32[]{:S(2)}) collective-permute-start(bf16[320,1536]{1,0:T(8,128)(2,1)} %bitcast.19), channel_id=1, source_target_pairs={{0,4},{4,0},{8,12},{12,8},{16,20},{20,16},{24,28},{28,24},{1,5},{5... | collective-permute-start | bytes 2949128 | tf_op jit(solution)/shard_map/ppermute | solution.py:605
  267.4 23.2 %collective-permute-start.20 = (f32[4,512]{1,0:T(4,128)S(1)}, f32[4,512]{1,0:T(4,128)S(1)}, u32[]{:S(2)}, u32[]{:S(2)}) collective-permute-start(f32[4,512]{1,0:T(4,128)S(1)} %collective-permute-done.16), channel_id=1, source_target_pairs={{0,8},{4,12},{8,16},{12,20},{16,24},{20,28},{24,0},{28,4},{1,9},{5... | collective-permute-start | bytes 24584 | tf_op jit(solution)/shard_map/ppermute | solution.py:598
  377.5 305.2 %reduce-scatter.4.cloned.1.call-start = ((), (), s32[]{:S(2)}) async-start(), calls=%async_computation.5 | async-start | bytes 23592960 | tf_op jit(solution)/shard_map/reduce_scatter | solution.py:832
  379.3 23.4 %collective-permute-start.26 = (f32[4,4,80]{2,1,0:T(4,128)S(1)}, f32[4,4,80]{2,1,0:T(4,128)S(1)}, u32[]{:S(2)}, u32[]{:S(2)}) collective-permute-start(f32[4,4,80]{2,1,0:T(4,128)S(1)} %get-tuple-element.470), channel_id=1, source_target_pairs={{0,4},{4,0},{8,12},{12,8},{16,20},{20,16},{24,28},{28,24},{1,5},{5... | collective-permute-start | bytes 15368 | tf_op jit(solution)/shard_map/ppermute | solution.py:605
  380.7 32.8 %collective-permute-start.28 = (bf16[512,1536]{1,0:T(8,128)(2,1)}, bf16[512,1536]{1,0:T(8,128)(2,1)S(1)}, u32[]{:S(2)}, u32[]{:S(2)}) collective-permute-start(bf16[512,1536]{1,0:T(8,128)(2,1)} %copy-done.9), channel_id=1, source_target_pairs={{0,8},{4,12},{8,16},{12,20},{16,24},{20,28},{24,0},{28,4},{1,9},{5... | collective-permute-start | bytes 4718600 | tf_op jit(solution)/shard_map/ppermute | solution.py:598
  381.2 31.4 %collective-permute-start.25 = (bf16[320,1536]{1,0:T(8,128)(2,1)}, bf16[320,1536]{1,0:T(8,128)(2,1)S(1)}, u32[]{:S(2)}, u32[]{:S(2)}) collective-permute-start(bf16[320,1536]{1,0:T(8,128)(2,1)} %get-tuple-element.213), channel_id=1, source_target_pairs={{0,4},{4,0},{8,12},{12,8},{16,20},{20,16},{24,28},{28,24},{1,5},{5... | collective-permute-start | bytes 2949128 | tf_op jit(solution)/shard_map/ppermute | solution.py:605
  419.2 292.4 %reduce-scatter.8.cloned.1.call-start = ((), (), s32[]{:S(2)}) async-start(), calls=%async_computation.7 | async-start | bytes 7864320 | tf_op jit(solution)/shard_map/reduce_scatter | solution.py:922
  419.3 35.9 %collective-permute-start.36 = (bf16[512,1536]{1,0:T(8,128)(2,1)S(1)}, bf16[512,1536]{1,0:T(8,128)(2,1)S(1)}, u32[]{:S(2)}, u32[]{:S(2)}) collective-permute-start(bf16[512,1536]{1,0:T(8,128)(2,1)S(1)} %ring_rows.9), channel_id=1, source_target_pairs={{0,8},{4,12},{8,16},{12,20},{16,24},{20,28},{24,0},{28,4},{1,9},{5... | collective-permute-start | bytes 4718600 | tf_op jit(solution)/shard_map/ppermute | solution.py:598
  421.2 34.0 %collective-permute-start.34 = (f32[4,512]{1,0:T(4,128)S(1)}, f32[4,512]{1,0:T(4,128)S(1)}, u32[]{:S(2)}, u32[]{:S(2)}) collective-permute-start(f32[4,512]{1,0:T(4,128)S(1)} %fusion.65), channel_id=1, source_target_pairs={{0,8},{4,12},{8,16},{12,20},{16,24},{20,28},{24,0},{28,4},{1,9},{5... | collective-permute-start | bytes 24584 | tf_op jit(solution)/shard_map/ppermute | solution.py:598
  442.0 22.0 %collective-permute-start.30 = (bf16[320,1536]{1,0:T(8,128)(2,1)}, bf16[320,1536]{1,0:T(8,128)(2,1)S(1)}, u32[]{:S(2)}, u32[]{:S(2)}) collective-permute-start(bf16[320,1536]{1,0:T(8,128)(2,1)} %get-tuple-element.234), channel_id=1, source_target_pairs={{0,4},{4,0},{8,12},{12,8},{16,20},{20,16},{24,28},{28,24},{1,5},{5... | collective-permute-start | bytes 2949128 | tf_op jit(solution)/shard_map/ppermute | solution.py:605
  458.6 26.4 %collective-permute-start.37 = (bf16[512,1536]{1,0:T(8,128)(2,1)S(1)}, bf16[512,1536]{1,0:T(8,128)(2,1)S(1)}, u32[]{:S(2)}, u32[]{:S(2)}) collective-permute-start(bf16[512,1536]{1,0:T(8,128)(2,1)S(1)} %ring_rows.10), channel_id=1, source_target_pairs={{0,8},{4,12},{8,16},{12,20},{16,24},{20,28},{24,0},{28,4},{1,9},{5... | collective-permute-start | bytes 4718600 | tf_op jit(solution)/shard_map/ppermute | solution.py:598
  464.0 24.3 %collective-permute-start.31 = (bf16[320,1536]{1,0:T(8,128)(2,1)S(1)}, bf16[320,1536]{1,0:T(8,128)(2,1)S(1)}, u32[]{:S(2)}, u32[]{:S(2)}) collective-permute-start(bf16[320,1536]{1,0:T(8,128)(2,1)S(1)} %copy-done.84), channel_id=1, source_target_pairs={{0,4},{4,0},{8,12},{12,8},{16,20},{20,16},{24,28},{28,24},{1,5},{5... | collective-permute-start | bytes 2949128 | tf_op jit(solution)/shard_map/ppermute | solution.py:605
  523.7 23.3 %collective-permute-start.40 = (bf16[320,1536]{1,0:T(8,128)(2,1)S(1)}, bf16[320,1536]{1,0:T(8,128)(2,1)S(1)}, u32[]{:S(2)}, u32[]{:S(2)}) collective-permute-start(bf16[320,1536]{1,0:T(8,128)(2,1)S(1)} %copy-done.80), channel_id=1, source_target_pairs={{0,4},{4,0},{8,12},{12,8},{16,20},{20,16},{24,28},{28,24},{1,5},{5... | collective-permute-start | bytes 2949128 | tf_op jit(solution)/shard_map/ppermute | solution.py:605
  524.9 36.2 %collective-permute-start.41 = (bf16[512,1536]{1,0:T(8,128)(2,1)S(1)}, bf16[512,1536]{1,0:T(8,128)(2,1)S(1)}, u32[]{:S(2)}, u32[]{:S(2)}) collective-permute-start(bf16[512,1536]{1,0:T(8,128)(2,1)S(1)} %copy-done.8), channel_id=1, source_target_pairs={{0,8},{4,12},{8,16},{12,20},{16,24},{20,28},{24,0},{28,4},{1,9},{5... | collective-permute-start | bytes 4718600 | tf_op jit(solution)/shard_map/ppermute | solution.py:598
  532.5 63.0 %collective-permute-start.39 = (bf16[512,512]{1,0:T(8,128)(2,1)S(1)}, bf16[512,512]{1,0:T(8,128)(2,1)S(1)}, u32[]{:S(2)}, u32[]{:S(2)}) collective-permute-start(bf16[512,512]{1,0:T(8,128)(2,1)S(1)} %fusion.34), channel_id=1, source_target_pairs={{2,0},{3,1},{6,4},{7,5},{10,8},{11,9},{14,12},{15,13},{18,16},{19,... | collective-permute-start | bytes 1572872 | tf_op jit(solution)/shard_map/ppermute | solution.py:902
  604.4 23.8 %collective-permute-start.32 = (bf16[320,1536]{1,0:T(8,128)(2,1)}, bf16[320,1536]{1,0:T(8,128)(2,1)S(1)}, u32[]{:S(2)}, u32[]{:S(2)}) collective-permute-start(bf16[320,1536]{1,0:T(8,128)(2,1)} %get-tuple-element.236), channel_id=1, source_target_pairs={{0,4},{4,0},{8,12},{12,8},{16,20},{20,16},{24,28},{28,24},{1,5},{5... | collective-permute-start | bytes 2949128 | tf_op jit(solution)/shard_map/ppermute | solution.py:605
  605.4 65.6 %collective-permute-start.42 = (bf16[2,384,1536]{2,1,0:T(8,128)(2,1)}, bf16[2,384,1536]{2,1,0:T(8,128)(2,1)}, u32[]{:S(2)}, u32[]{:S(2)}) collective-permute-start(bf16[2,384,1536]{2,1,0:T(8,128)(2,1)} %get-tuple-element.266), channel_id=1, source_target_pairs={{0,1},{1,0},{2,3},{3,2},{4,5},{5,4},{6,7},{7,6},{8,9},{9,8},{10,11... | collective-permute-start | bytes 7077896 | tf_op jit(solution)/shard_map/ppermute | solution.py:620
  628.1 78.9 %collective-permute-start.33 = (bf16[320,1536]{1,0:T(8,128)(2,1)}, bf16[320,1536]{1,0:T(8,128)(2,1)}, u32[]{:S(2)}, u32[]{:S(2)}) collective-permute-start(bf16[320,1536]{1,0:T(8,128)(2,1)} %get-tuple-element.237), channel_id=1, source_target_pairs={{0,4},{4,0},{8,12},{12,8},{16,20},{20,16},{24,28},{28,24},{1,5},{5... | collective-permute-start | bytes 2949128 | tf_op jit(solution)/shard_map/ppermute | solution.py:605
  629.4 36.8 %collective-permute-start.44 = (bf16[512,1536]{1,0:T(8,128)(2,1)S(1)}, bf16[512,1536]{1,0:T(8,128)(2,1)S(1)}, u32[]{:S(2)}, u32[]{:S(2)}) collective-permute-start(bf16[512,1536]{1,0:T(8,128)(2,1)S(1)} %ring_rows.13), channel_id=1, source_target_pairs={{0,8},{4,12},{8,16},{12,20},{16,24},{20,28},{24,0},{28,4},{1,9},{5... | collective-permute-start | bytes 4718600 | tf_op jit(solution)/shard_map/ppermute | solution.py:598
  641.7 29.2 %collective-permute-start.43 = (bf16[2,384,128]{2,1,0:T(8,128)(2,1)S(1)}, bf16[2,384,128]{2,1,0:T(8,128)(2,1)S(1)}, u32[]{:S(2)}, u32[]{:S(2)}) collective-permute-start(bf16[2,384,128]{2,1,0:T(8,128)(2,1)S(1)} %get-tuple-element.465), channel_id=1, source_target_pairs={{0,1},{1,0},{2,3},{3,2},{4,5},{5,4},{6,7},{7,6},{8,9},{9,8},{10,11... | collective-permute-start | bytes 589832 | tf_op jit(solution)/shard_map/ppermute | solution.py:620
  669.5 37.6 %collective-permute-start.45 = (bf16[512,1536]{1,0:T(8,128)(2,1)S(1)}, bf16[512,1536]{1,0:T(8,128)(2,1)S(1)}, u32[]{:S(2)}, u32[]{:S(2)}) collective-permute-start(bf16[512,1536]{1,0:T(8,128)(2,1)S(1)} %ring_rows.14), channel_id=1, source_target_pairs={{0,8},{4,12},{8,16},{12,20},{16,24},{20,28},{24,0},{28,4},{1,9},{5... | collective-permute-start | bytes 4718600 | tf_op jit(solution)/shard_map/ppermute | solution.py:598
  674.9 39.1 %collective-permute-start.46 = (bf16[384,1664]{1,0:T(8,128)(2,1)}, bf16[384,1664]{1,0:T(8,128)(2,1)}, u32[]{:S(2)}, u32[]{:S(2)}) collective-permute-start(bf16[384,1664]{1,0:T(8,128)(2,1)} %fusion.28), channel_id=1, source_target_pairs={{0,2},{1,3},{2,0},{3,1},{4,6},{5,7},{6,4},{7,5},{8,10},{9,11},{10,... | collective-permute-start | bytes 3833864 | tf_op jit(solution)/shard_map/ppermute | solution.py:623
  712.9 38.6 %collective-permute-start.54 = (bf16[192,2048]{1,0:T(8,128)(2,1)S(1)}, bf16[192,2048]{1,0:T(8,128)(2,1)S(1)}, u32[]{:S(2)}, u32[]{:S(2)}) collective-permute-start(bf16[192,2048]{1,0:T(8,128)(2,1)S(1)} %dynamic-slice_bitcast_fusion), channel_id=1, source_target_pairs={{0,4},{4,0},{8,12},{12,8},{16,20},{20,16},{24,28},{28,24},{1,5},{5... | collective-permute-start | bytes 2359304 | tf_op jit(solution)/shard_map/ppermute | solution.py:605
  717.0 27.1 %collective-permute-start.47 = (bf16[192,1664]{1,0:T(8,128)(2,1)S(1)}, bf16[192,1664]{1,0:T(8,128)(2,1)S(1)}, u32[]{:S(2)}, u32[]{:S(2)}) collective-permute-start(bf16[192,1664]{1,0:T(8,128)(2,1)S(1)} %dynamic-slice_bitcast_fusion.1), channel_id=1, source_target_pairs={{0,4},{4,0},{8,12},{12,8},{16,20},{20,16},{24,28},{28,24},{1,5},{5... | collective-permute-start | bytes 1916936 | tf_op jit(solution)/shard_map/ppermute | solution.py:605
  745.7 22.3 %collective-permute-start.49 = (bf16[48,1664]{1,0:T(8,128)(2,1)S(1)}, bf16[48,1664]{1,0:T(8,128)(2,1)S(1)}, u32[]{:S(2)}, u32[]{:S(2)}) collective-permute-start(bf16[48,1664]{1,0:T(8,128)(2,1)S(1)} %get-tuple-element.462), channel_id=1, source_target_pairs={{0,16},{4,20},{8,24},{12,28},{16,0},{20,4},{24,8},{28,12},{1,17},{... | collective-permute-start | bytes 479240 | tf_op jit(solution)/shard_map/ppermute | solution.py:598
  750.0 25.5 %collective-permute-start.50 = (bf16[48,1664]{1,0:T(8,128)(2,1)S(1)}, bf16[48,1664]{1,0:T(8,128)(2,1)S(1)}, u32[]{:S(2)}, u32[]{:S(2)}) collective-permute-start(bf16[48,1664]{1,0:T(8,128)(2,1)S(1)} %get-tuple-element.461), channel_id=1, source_target_pairs={{0,24},{4,28},{8,0},{12,4},{16,8},{20,12},{24,16},{28,20},{1,25},{... | collective-permute-start | bytes 479240 | tf_op jit(solution)/shard_map/ppermute | solution.py:598
  751.8 47.3 %collective-permute-start.55 = (bf16[48,2048]{1,0:T(8,128)(2,1)S(1)}, bf16[48,2048]{1,0:T(8,128)(2,1)S(1)}, u32[]{:S(2)}, u32[]{:S(2)}) collective-permute-start(bf16[48,2048]{1,0:T(8,128)(2,1)S(1)} %get-tuple-element.457), channel_id=1, source_target_pairs={{0,8},{4,12},{8,16},{12,20},{16,24},{20,28},{24,0},{28,4},{1,9},{5... | collective-permute-start | bytes 589832 | tf_op jit(solution)/shard_map/ppermute | solution.py:598
  752.4 46.7 %collective-permute-start.56 = (bf16[48,2048]{1,0:T(8,128)(2,1)S(1)}, bf16[48,2048]{1,0:T(8,128)(2,1)S(1)}, u32[]{:S(2)}, u32[]{:S(2)}) collective-permute-start(bf16[48,2048]{1,0:T(8,128)(2,1)S(1)} %get-tuple-element.459), channel_id=1, source_target_pairs={{0,16},{4,20},{8,24},{12,28},{16,0},{20,4},{24,8},{28,12},{1,17},{... | collective-permute-start | bytes 589832 | tf_op jit(solution)/shard_map/ppermute | solution.py:598
  754.6 44.5 %collective-permute-start.57 = (bf16[48,2048]{1,0:T(8,128)(2,1)S(1)}, bf16[48,2048]{1,0:T(8,128)(2,1)S(1)}, u32[]{:S(2)}, u32[]{:S(2)}) collective-permute-start(bf16[48,2048]{1,0:T(8,128)(2,1)S(1)} %get-tuple-element.458), channel_id=1, source_target_pairs={{0,24},{4,28},{8,0},{12,4},{16,8},{20,12},{24,16},{28,20},{1,25},{... | collective-permute-start | bytes 589832 | tf_op jit(solution)/shard_map/ppermute | solution.py:598
  (111 other events, 1519.5 us)
Sparse Core Ops, SparseCore 0:
  16.5 49.7 all-gather.6
  68.4 45.2 all-gather.8
  115.8 67.7 all-gather.10
  185.6 119.9 all-gather.12
  377.6 88.1 reduce-scatter.5
  468.3 150.6 reduce-scatter.3
  621.7 58.3 reduce-scatter.7
